TPU v7x, 32 devices: a whole 2x2x4 slice. The times are simulated.
32 devices in a mesh: seq: 4 (over y, x), head: 8 (over z, core).
Axes of the slice: x: 2, y: 2, z: 4, core: 2. Of those that a mesh axis runs over, the one named last changes fastest.
Arguments:
- queries: bfloat16 [6144, 4096], P(('seq', 'head')), may hold values from -48 to 48
- keys: bfloat16 [6144, 2048], P(('seq', 'head')), may hold values from -4 to 4
- values: bfloat16 [6144, 2048], P(('seq', 'head')), may hold values from -6 to 6
- grad_out: bfloat16 [6144, 4096], P(('seq', 'head')), may hold values from -6 to 6
- doc_lengths: int32 [16], replicated, may hold values from 1 to 1536, 6144 in all
Outputs:
- grad_queries: bfloat16 [6144, 4096], P(('seq', 'head'))
- grad_keys: bfloat16 [6144, 2048], P(('seq', 'head'))
- grad_values: bfloat16 [6144, 2048], P(('seq', 'head'))
Inputs may be any that keep to these rules, and one draw needn't show every extreme that they name: `doc_lengths`: the lengths sum to 6144.
All inputs are finite; a program needn't handle non-finite values.
Results may differ from a plain program's by a relative error of at most 0.012.
Values may be sent and summed in bfloat16 or wider, within the bound.
No kernel may reach another device: no remote copies, remote signals or barrier semaphores. Data moves between devices by JAX's collectives and lax.ppermute only.
A program may use at most 128 MiB of HBM per device.

v0:
```python
import functools
import math

import jax
import jax.numpy as jnp
from jax import lax
from jax.experimental import pallas as pl
from jax.experimental.pallas import tpu as pltpu
from jax.sharding import PartitionSpec as P

HD = 128
WINDOW = 1024
TQ = 256
TK = 256
SCALING = HD ** (-0.5)
EXP2_SCALE = SCALING * math.log2(math.e)
MASKED = -1e30


def passed_along(shard, axis, by):
    count = lax.axis_size(axis)
    pairs = [(i, i + by) for i in range(count) if 0 <= i + by < count]
    return lax.ppermute(shard, axis, pairs)


def dot_nt(a, b):
    return lax.dot_general(a, b, (((1,), (1,)), ((), ())), preferred_element_type=jnp.float32)


def dot_nn(a, b):
    return lax.dot_general(a, b, (((1,), (0,)), ((), ())), preferred_element_type=jnp.float32)


def partner_rows(me_ref, k, tokens):
    return pl.ds(pl.multiple_of((me_ref[0] ^ k) * tokens, tokens), tokens)


def gather_rows(me_ref, blocks, out_ref):
    for k, block in enumerate(blocks):
        out_ref[partner_rows(me_ref, k, block.shape[0]), :] = block[...]


def attend_kernel(per_group, ways, me_ref, first_tile, low_ref, halo_k, halo_v, own_k, own_v, *refs):
    blocks, refs = refs[:ways], refs[ways:]
    dq_ref, own_ref, rim_ref, qd_ref, k_ext, v_ext, k_t, dk_ext, dv_ext, s_buf, dp_buf = refs
    if ways == 1:
        qd_ref = blocks[0]
    else:
        gather_rows(me_ref, blocks, qd_ref)
    group = qd_ref.shape[0]
    reach = WINDOW // TK
    k_ext[:WINDOW, :] = halo_k[...]
    k_ext[WINDOW:, :] = own_k[...]
    v_ext[:WINDOW, :] = halo_v[...]
    v_ext[WINDOW:, :] = own_v[...]
    dk_ext[...] = jnp.zeros_like(dk_ext)
    dv_ext[...] = jnp.zeros_like(dv_ext)

    def turn(t, carry):
        rows = pl.ds(pl.multiple_of(t * TK, TK), TK)
        k_t[t] = jnp.transpose(k_ext[rows, :].astype(jnp.float32)).astype(jnp.bfloat16)
        return carry

    lax.fori_loop(0, (group + WINDOW) // TK, turn, 0)
    wide = per_group * TQ
    key_iota = lax.broadcasted_iota(jnp.int32, (TK, wide), 0)

    def q_block(b, carry):
        q_rows = pl.ds(pl.multiple_of(b * TQ, TQ), TQ)
        start = first_tile[b]
        stop = b * (TQ // TK) + (TQ // TK - 1) + reach + 1
        q = jnp.concatenate(
            [qd_ref[q_rows, i * HD : (i + 1) * HD] for i in range(per_group)], axis=0
        )
        d_out = jnp.concatenate(
            [qd_ref[q_rows, i * HD : (i + 1) * HD] for i in range(per_group, 2 * per_group)],
            axis=0,
        )
        low = low_ref[:, q_rows]
        low = jnp.concatenate([low] * per_group, axis=1)
        high = b * TQ + WINDOW + lax.broadcasted_iota(jnp.int32, (1, TQ), 1)
        high = jnp.concatenate([high] * per_group, axis=1)

        def score(t, top):
            rows = pl.ds(pl.multiple_of(t * TK, TK), TK)
            slot = pl.ds(pl.multiple_of((t - start) * TK, TK), TK)
            s = dot_nt(k_ext[rows, :], q)
            j = key_iota + t * TK
            s = jnp.where((j >= low) & (j <= high), s, MASKED)
            s_buf[slot, :] = s
            return jnp.maximum(top, jnp.max(s, axis=0, keepdims=True))

        top = lax.fori_loop(start, stop, score, jnp.full((1, wide), MASKED, jnp.float32))

        def weigh(t, sums):
            total, dotted = sums
            rows = pl.ds(pl.multiple_of(t * TK, TK), TK)
            slot = pl.ds(pl.multiple_of((t - start) * TK, TK), TK)
            p = jnp.exp2((s_buf[slot, :] - top) * EXP2_SCALE)
            dp = dot_nt(v_ext[rows, :], d_out)
            s_buf[slot, :] = p
            dp_buf[slot, :] = dp
            return (
                total + jnp.sum(p, axis=0, keepdims=True),
                dotted + jnp.sum(p * dp, axis=0, keepdims=True),
            )

        zero = jnp.zeros((1, wide), jnp.float32)
        total, dotted = lax.fori_loop(start, stop, weigh, (zero, zero))
        inverse = 1.0 / total
        row_dot = dotted * inverse
        inverse_scaled = inverse * SCALING

        def grads(t, dq_t):
            rows = pl.ds(pl.multiple_of(t * TK, TK), TK)
            slot = pl.ds(pl.multiple_of((t - start) * TK, TK), TK)
            p = s_buf[slot, :]
            ds = ((p * inverse_scaled) * (dp_buf[slot, :] - row_dot)).astype(jnp.bfloat16)
            weights = (p * inverse).astype(jnp.bfloat16)
            dv_ext[rows, :] += dot_nn(weights, d_out)
            dk_ext[rows, :] += dot_nn(ds, q)
            return dq_t + dot_nn(k_t[t], ds)

        dq_t = lax.fori_loop(start, stop, grads, jnp.zeros((HD, wide), jnp.float32))
        dq = jnp.transpose(dq_t).astype(jnp.bfloat16)
        for i in range(per_group):
            dq_ref[q_rows, i * HD : (i + 1) * HD] = dq[i * TQ : (i + 1) * TQ, :]
        return carry

    lax.fori_loop(0, group // TQ, q_block, 0)
    rim_ref[:, :HD] = dk_ext[:WINDOW, :].astype(jnp.bfloat16)
    rim_ref[:, HD:] = dv_ext[:WINDOW, :].astype(jnp.bfloat16)
    own_ref[:, :HD] = dk_ext[WINDOW:, :]
    own_ref[:, HD:] = dv_ext[WINDOW:, :]


def attend(me, qd_blocks, halo, own, chunk, kv_local, low, first_tile):
    group = own.shape[0]
    tokens, qd_lanes = qd_blocks[0].shape
    ways = len(qd_blocks)
    per_group = qd_lanes // (2 * HD)
    ext = group + WINDOW
    wide = per_group * TQ
    span = WINDOW + TQ

    def vmem(shape, lane_block=0):
        return pl.BlockSpec(shape, lambda i: (0, lane_block))

    area = group * (WINDOW + TQ) * per_group
    return pl.pallas_call(
        functools.partial(attend_kernel, per_group, ways),
        grid=(1,),
        out_shape=(
            jax.ShapeDtypeStruct((group, per_group * HD), jnp.bfloat16),
            jax.ShapeDtypeStruct((group, 2 * HD), jnp.float32),
            jax.ShapeDtypeStruct((WINDOW, 2 * HD), jnp.bfloat16),
        ),
        in_specs=[
            pl.BlockSpec(memory_space=pltpu.SMEM),
            pl.BlockSpec(memory_space=pltpu.SMEM),
            vmem((1, group)),
            vmem((WINDOW, HD), chunk),
            vmem((WINDOW, HD), kv_local + chunk),
            vmem((group, HD), chunk),
            vmem((group, HD), kv_local + chunk),
        ]
        + [vmem((tokens, qd_lanes))] * ways,
        out_specs=(
            vmem((group, per_group * HD)),
            vmem((group, 2 * HD)),
            vmem((WINDOW, 2 * HD)),
        ),
        scratch_shapes=[
            pltpu.VMEM((group, qd_lanes), jnp.bfloat16),
            pltpu.VMEM((ext, HD), jnp.bfloat16),
            pltpu.VMEM((ext, HD), jnp.bfloat16),
            pltpu.VMEM((ext // TK, HD, TK), jnp.bfloat16),
            pltpu.VMEM((ext, HD), jnp.float32),
            pltpu.VMEM((ext, HD), jnp.float32),
            pltpu.VMEM((span, wide), jnp.float32),
            pltpu.VMEM((span, wide), jnp.float32),
        ],
        compiler_params=pltpu.CompilerParams(vmem_limit_bytes=40 * 1024 * 1024),
        cost_estimate=pl.CostEstimate(
            flops=area * HD * 2 * 5, bytes_accessed=group * HD * 24, transcendentals=area
        ),
        name="attend",
    )(me, first_tile, low, halo, halo, own, own, *qd_blocks)


SMEM = pl.BlockSpec(memory_space=pltpu.SMEM)
VMEM = pl.BlockSpec(memory_space=pltpu.VMEM)
ANYWHERE = pl.BlockSpec(memory_space=pl.ANY)


def on_chip(kernel, me, arrays, shapes, name, scratch=(), earlier=()):
    moved = sum(a.size * a.dtype.itemsize for a in arrays) + sum(2 * math.prod(s) for s in shapes)

    def body(me_ref, *refs):
        kernel(me_ref, *refs[len(earlier) :])

    return pl.pallas_call(
        body,
        out_shape=tuple(jax.ShapeDtypeStruct(s, jnp.bfloat16) for s in shapes),
        in_specs=[SMEM] + [ANYWHERE] * len(earlier) + [VMEM] * len(arrays),
        out_specs=(VMEM,) * len(shapes),
        scratch_shapes=list(scratch),
        compiler_params=pltpu.CompilerParams(vmem_limit_bytes=40 * 1024 * 1024),
        cost_estimate=pl.CostEstimate(flops=0, bytes_accessed=moved, transcendentals=0),
        name=name,
    )(me, *earlier, *arrays)


def packed(me, arrays, ways, chunk, chunks, by_partner, earlier=()):
    tokens = arrays[0].shape[0]
    lanes = [a.shape[1] // (ways * chunks) for a in arrays]
    total = sum(lanes)

    def kernel(me_ref, *refs):
        ins, outs = refs[: len(arrays)], refs[len(arrays) :]
        for k in range(ways):
            out = outs[k] if by_partner else outs[0].at[k]
            first = 0
            for ref, width in zip(ins, lanes):
                if by_partner:
                    at = pl.multiple_of(((me_ref[0] ^ k) * chunks + chunk) * width, width)
                else:
                    at = (k * chunks + chunk) * width
                out[:, first : first + width] = ref[:, pl.ds(at, width)]
                first += width

    shapes = [(tokens, total)] * ways if by_partner else [(ways, tokens, total)]
    return on_chip(kernel, me, arrays, shapes, "packed", earlier=earlier)


def unpacked(me, grads, ways, q_lanes):
    chunks = len(grads)
    tokens = grads[0][0].shape[-2]
    lanes = (q_lanes, HD, HD)
    counts = [len(blocks) for blocks in grads]

    def kernel(me_ref, *refs):
        outs = refs[sum(counts) :]
        for c in range(chunks):
            ins = refs[sum(counts[:c]) : sum(counts[: c + 1])]
            for k in range(ways):
                block = ins[k] if len(ins) > 1 else ins[0].at[k]
                first = 0
                for out, width in zip(outs, lanes):
                    if len(ins) > 1:
                        at = pl.multiple_of(((me_ref[0] ^ k) * chunks + c) * width, width)
                    else:
                        at = (k * chunks + c) * width
                    out[:, pl.ds(at, width)] = block[:, first : first + width]
                    first += width

    shapes = [(tokens, ways * chunks * width) for width in lanes]
    return on_chip(kernel, me, [g for blocks in grads for g in blocks], shapes, "unpacked")


def gathered(me, blocks):
    tokens, lanes = blocks[0].shape
    ways = len(blocks)
    group = ways * tokens

    def kernel(me_ref, *refs):
        all_ref, tail_ref = refs[ways:]
        gather_rows(me_ref, refs[:ways], all_ref)
        tail_ref[...] = all_ref[group - WINDOW :, :]

    return on_chip(kernel, me, blocks, [(group, lanes), (WINDOW, lanes)], "gathered")


def settled(me, dq, own, returned, ways, by_partner):
    group, q_lanes = dq.shape
    tokens = group // ways
    total_lanes = q_lanes + 2 * HD

    def kernel(me_ref, dq_ref, own_ref, back_ref, *refs):
        cut = group - WINDOW
        total = refs[-1] if by_partner else refs[0].at[:, q_lanes:]
        total[:cut, :] = own_ref[:cut, :].astype(jnp.bfloat16)
        total[cut:, :] = (own_ref[cut:, :] + back_ref[...].astype(jnp.float32)).astype(jnp.bfloat16)
        if not by_partner:
            refs[0][:, :q_lanes] = dq_ref[...]
            return
        for k, out in enumerate(refs[:ways]):
            rows = partner_rows(me_ref, k, tokens)
            out[:, :q_lanes] = dq_ref[rows, :]
            out[:, q_lanes:] = total[rows, :]

    shapes = [(tokens, total_lanes)] * ways if by_partner else [(group, total_lanes)]
    scratch = [pltpu.VMEM((group, 2 * HD), jnp.bfloat16)] if by_partner else []
    return on_chip(kernel, me, (dq, own, returned), shapes, "settled", scratch)


def exchanged(blocks):
    ways = len(blocks)
    came = {0: blocks[0]}
    for k in reversed(range(1, ways)):
        came[k] = lax.ppermute(blocks[k], "head", [(i, i ^ k) for i in range(ways)])
    return [came[k] for k in range(ways)]


def exchanged_at_once(sent):
    return lax.all_to_all(sent, "head", split_axis=0, concat_axis=0, tiled=True)


def local(queries, keys, values, grad_out, doc_lengths):
    ways = lax.axis_size("head")
    tokens = queries.shape[0]
    group = tokens * ways
    kv_local = keys.shape[1] // (ways * HD)
    per_group = queries.shape[1] // keys.shape[1]
    q_lanes = per_group * HD
    group_first = lax.axis_index("seq") * group
    me = lax.axis_index("head").astype(jnp.int32).reshape(1)

    came = exchanged(packed(me, (keys, values), ways, 0, 1, True))
    kv, tail = gathered(me, came)
    halo = passed_along(tail, "seq", 1)
    qds = [
        exchanged(packed(me, (queries, grad_out), ways, 0, kv_local, True, [came[ways - 2]]))
    ]
    for c in range(1, kv_local):
        earlier = [qds[-1][-2] if c == 1 else qds[-1][0], halo]
        sent = packed(me, (queries, grad_out), ways, c, kv_local, False, earlier)[0]
        qds.append([exchanged_at_once(sent).reshape(group, 2 * q_lanes)])

    position = group_first + jnp.arange(group, dtype=jnp.int32)
    ends = jnp.cumsum(doc_lengths)
    doc_start = jnp.sum(
        jnp.where(position[:, None] >= ends[None, :], doc_lengths[None, :], 0), axis=1
    )
    low = jnp.maximum(doc_start, position - (WINDOW - 1)) - (group_first - WINDOW)
    low = low.astype(jnp.int32)
    first_tile = low[::TQ] // TK

    grads = []
    for c in range(kv_local):
        dq, own, rim = attend(me, qds[c], halo, kv, c, kv_local, low.reshape(1, group), first_tile)
        returned = passed_along(rim, "seq", -1)
        last = c == kv_local - 1
        settled_now = settled(me, dq, own, returned, ways, last)
        if last:
            grads.append(exchanged(settled_now))
        else:
            sent = settled_now[0].reshape(ways, tokens, q_lanes + 2 * HD)
            grads.append([exchanged_at_once(sent)])
    return unpacked(me, grads, ways, q_lanes)


def solution(mesh):
    rows = P(("seq", "head"), None)
    return jax.shard_map(
        local,
        mesh=mesh,
        in_specs=(rows, rows, rows, rows, P()),
        out_specs=(rows, rows, rows),
        check_vma=False,
    )
```

profile of v0, /device:TPU:13, one launch (start us, length us, event | category | flops | bytes accessed | tf_op | source)
XLA Modules:
  0.0 260.0 jit_solution(9792653494393660097)
XLA Ops:
  5.6 2.3 collective-permute-start.3
  9.6 6.5 %collective-permute-done.1.refs_2_ = bf16[192,512]{1,0:T(8,128)(2,1)S(1)} collective-permute-done((bf16[192,512]{1,0:T(8,128)(2,1)S(1)}, bf16[192,512]{1,0:T(8,128)(2,1)S(1)}, u32[]{:S(2)}, u32[]{:S(2)}) %collective-permute-start.1) | collective-permute-done | bytes 196640 | tf_op jit(solution)/shard_map/ppermute | solution.py:301
  17.6 2.8 %collective-permute-done.2.refs_3_ = bf16[192,512]{1,0:T(8,128)(2,1)S(1)} collective-permute-done((bf16[192,512]{1,0:T(8,128)(2,1)S(1)}, bf16[192,512]{1,0:T(8,128)(2,1)S(1)}, u32[]{:S(2)}, u32[]{:S(2)}) %collective-permute-start.2) | collective-permute-done | bytes 196640 | tf_op jit(solution)/shard_map/ppermute | solution.py:301
  20.4 12.7 %collective-permute-done.4.refs_5_ = bf16[192,512]{1,0:T(8,128)(2,1)S(1)} collective-permute-done((bf16[192,512]{1,0:T(8,128)(2,1)S(1)}, bf16[192,512]{1,0:T(8,128)(2,1)S(1)}, u32[]{:S(2)}, u32[]{:S(2)}) %collective-permute-start.4) | collective-permute-done | bytes 196640 | tf_op jit(solution)/shard_map/ppermute | solution.py:301
  33.2 4.2 %collective-permute-done.5.refs_6_.refs_0_ = bf16[192,512]{1,0:T(8,128)(2,1)S(1)} collective-permute-done((bf16[192,512]{1,0:T(8,128)(2,1)S(1)}, bf16[192,512]{1,0:T(8,128)(2,1)S(1)}, u32[]{:S(2)}, u32[]{:S(2)}) %collective-permute-start.5) | collective-permute-done | bytes 196640 | tf_op jit(solution)/shard_map/ppermute | solution.py:301
  37.4 4.3 %collective-permute-done.6.refs_7_ = bf16[192,512]{1,0:T(8,128)(2,1)S(1)} collective-permute-done((bf16[192,512]{1,0:T(8,128)(2,1)S(1)}, bf16[192,512]{1,0:T(8,128)(2,1)S(1)}, u32[]{:S(2)}, u32[]{:S(2)}) %collective-permute-start.6) | collective-permute-done | bytes 196640 | tf_op jit(solution)/shard_map/ppermute | solution.py:301
  41.8 3.1 %collective-permute-start.7 = (bf16[1024,512]{1,0:T(8,128)(2,1)S(1)}, bf16[1024,512]{1,0:T(8,128)(2,1)S(1)}, u32[]{:S(2)}, u32[]{:S(2)}) collective-permute-start(bf16[1024,512]{1,0:T(8,128)(2,1)S(1)} %get-tuple-element.43), channel_id=1, source_target_pairs={{0,8},{8,16},{16,24},{1,9},{9,17},{17,25},{2,10},{10,18},{18,26},{... | collective-permute-start | bytes 3145736 | tf_op jit(solution)/shard_map/ppermute | solution.py:23
  47.9 2.4 collective-permute-start.13
  50.3 4.8 %collective-permute-done.13.refs_6_.refs_0_ = bf16[192,512]{1,0:T(8,128)(2,1)S(1)} collective-permute-done((bf16[192,512]{1,0:T(8,128)(2,1)S(1)}, bf16[192,512]{1,0:T(8,128)(2,1)S(1)}, u32[]{:S(2)}, u32[]{:S(2)}) %collective-permute-start.13) | collective-permute-done | bytes 196640 | tf_op jit(solution)/shard_map/ppermute | solution.py:301
  55.2 13.2 %collective-permute-done.7.halo_k.halo_v.refs_1_ = bf16[1024,512]{1,0:T(8,128)(2,1)S(1)} collective-permute-done((bf16[1024,512]{1,0:T(8,128)(2,1)S(1)}, bf16[1024,512]{1,0:T(8,128)(2,1)S(1)}, u32[]{:S(2)}, u32[]{:S(2)}) %collective-permute-start.7) | collective-permute-done | bytes 1048608 | tf_op jit(solution)/shard_map/ppermute | solution.py:23
  69.8 7.0 %all-to-all-start.1 = ((bf16[8,192,512]{2,1,0:T(8,128)(2,1)}), bf16[8,192,512]{2,1,0:T(8,128)(2,1)S(1)}, u32[]{:S(2)}, u32[]{:S(2)}) async-start(bf16[8,192,512]{2,1,0:T(8,128)(2,1)} %packed.5), calls=%async_computation.1 | async-start | bytes 3145728 | tf_op jit(solution)/shard_map/all_to_all | solution.py:306
  77.7 1.8 collective-permute-start.10
  79.5 2.1 collective-permute-start.11
  83.3 24.3 %collective-permute-done.9.refs_2_ = bf16[192,512]{1,0:T(8,128)(2,1)S(1)} collective-permute-done((bf16[192,512]{1,0:T(8,128)(2,1)}, bf16[192,512]{1,0:T(8,128)(2,1)S(1)}, u32[]{:S(2)}, u32[]{:S(2)}) %collective-permute-start.9) | collective-permute-done | bytes 196640 | tf_op jit(solution)/shard_map/ppermute | solution.py:301
  107.7 4.3 %collective-permute-done.10.refs_3_ = bf16[192,512]{1,0:T(8,128)(2,1)S(1)} collective-permute-done((bf16[192,512]{1,0:T(8,128)(2,1)}, bf16[192,512]{1,0:T(8,128)(2,1)S(1)}, u32[]{:S(2)}, u32[]{:S(2)}) %collective-permute-start.10) | collective-permute-done | bytes 196640 | tf_op jit(solution)/shard_map/ppermute | solution.py:301
  112.0 16.0 %collective-permute-done.11.refs_4_ = bf16[192,512]{1,0:T(8,128)(2,1)S(1)} collective-permute-done((bf16[192,512]{1,0:T(8,128)(2,1)}, bf16[192,512]{1,0:T(8,128)(2,1)S(1)}, u32[]{:S(2)}, u32[]{:S(2)}) %collective-permute-start.11) | collective-permute-done | bytes 196640 | tf_op jit(solution)/shard_map/ppermute | solution.py:301
  128.0 4.1 %collective-permute-done.12.refs_5_ = bf16[192,512]{1,0:T(8,128)(2,1)S(1)} collective-permute-done((bf16[192,512]{1,0:T(8,128)(2,1)S(1)}, bf16[192,512]{1,0:T(8,128)(2,1)S(1)}, u32[]{:S(2)}, u32[]{:S(2)}) %collective-permute-start.12) | collective-permute-done | bytes 196640 | tf_op jit(solution)/shard_map/ppermute | solution.py:301
  132.1 6.0 %collective-permute-done.14.refs_7_ = bf16[192,512]{1,0:T(8,128)(2,1)S(1)} collective-permute-done((bf16[192,512]{1,0:T(8,128)(2,1)S(1)}, bf16[192,512]{1,0:T(8,128)(2,1)S(1)}, u32[]{:S(2)}, u32[]{:S(2)}) %collective-permute-start.14) | collective-permute-done | bytes 196640 | tf_op jit(solution)/shard_map/ppermute | solution.py:301
  139.5 14.6 %attend.2 = (bf16[1536,256]{1,0:T(8,128)(2,1)S(1)}, f32[1536,256]{1,0:T(8,128)S(1)}, bf16[1024,256]{1,0:T(8,128)(2,1)S(1)}) custom-call(s32[1]{0:T(128)} %bitcast.me_ref, s32[6]{0:T(128)S(1)} %and_select_fusion.first_tile, s32[1,1536]{1,0:T(1,128)S(1)} %maximum_subtract_fusion.1.low_ref, bf16[1024,512]{1,0:T(8,128)(2,1)S(1)} %collective-permute-done.7.halo_k.halo_v.refs_1_, ...), custom_call_target="tpu_custom_call" | custom-call | flops 5033164800 | bytes 4718592 | tf_op jit(solution)/shard_map/attend/pallas_call | solution.py:150
  154.1 8.0 %collective-permute-start.15 = (bf16[1024,256]{1,0:T(8,128)(2,1)S(1)}, bf16[1024,256]{1,0:T(8,128)(2,1)S(1)}, u32[]{:S(2)}, u32[]{:S(2)}) collective-permute-start(bf16[1024,256]{1,0:T(8,128)(2,1)S(1)} %get-tuple-element.55), channel_id=1, source_target_pairs={{8,0},{16,8},{24,16},{9,1},{17,9},{25,17},{10,2},{18,10},{26,18},{... | collective-permute-start | bytes 1572872 | tf_op jit(solution)/shard_map/ppermute | solution.py:23
  162.1 13.2 %collective-permute-done.15.refs_2_ = bf16[1024,256]{1,0:T(8,128)(2,1)S(1)} collective-permute-done((bf16[1024,256]{1,0:T(8,128)(2,1)S(1)}, bf16[1024,256]{1,0:T(8,128)(2,1)S(1)}, u32[]{:S(2)}, u32[]{:S(2)}) %collective-permute-start.15) | collective-permute-done | bytes 524320 | tf_op jit(solution)/shard_map/ppermute | solution.py:23
  176.7 3.7 %all-to-all-start = ((bf16[8,192,512]{2,1,0:T(8,128)(2,1)}), bf16[8,192,512]{2,1,0:T(8,128)(2,1)S(1)}, u32[]{:S(2)}, u32[]{:S(2)}) async-start(bf16[8,192,512]{2,1,0:T(8,128)(2,1)} %bitcast.2), calls=%async_computation | async-start | bytes 3145728 | tf_op jit(solution)/shard_map/all_to_all | solution.py:306
  183.0 14.6 %attend.3 = (bf16[1536,256]{1,0:T(8,128)(2,1)S(1)}, f32[1536,256]{1,0:T(8,128)S(1)}, bf16[1024,256]{1,0:T(8,128)(2,1)S(1)}) custom-call(s32[1]{0:T(128)} %bitcast.me_ref, s32[6]{0:T(128)S(1)} %and_select_fusion.first_tile, s32[1,1536]{1,0:T(1,128)S(1)} %maximum_subtract_fusion.1.low_ref, bf16[1024,512]{1,0:T(8,128)(2,1)S(1)} %copy-done.3, ...), custom_call_target="tpu_custom_call" | custom-call | flops 5033164800 | bytes 4718592 | tf_op jit(solution)/shard_map/attend/pallas_call | solution.py:150
  197.7 9.0 %collective-permute-start.16 = (bf16[1024,256]{1,0:T(8,128)(2,1)S(1)}, bf16[1024,256]{1,0:T(8,128)(2,1)S(1)}, u32[]{:S(2)}, u32[]{:S(2)}) collective-permute-start(bf16[1024,256]{1,0:T(8,128)(2,1)S(1)} %get-tuple-element.58), channel_id=1, source_target_pairs={{8,0},{16,8},{24,16},{9,1},{17,9},{25,17},{10,2},{18,10},{26,18},{... | collective-permute-start | bytes 1572872 | tf_op jit(solution)/shard_map/ppermute | solution.py:23
  206.7 10.8 %collective-permute-done.16.refs_2_ = bf16[1024,256]{1,0:T(8,128)(2,1)S(1)} collective-permute-done((bf16[1024,256]{1,0:T(8,128)(2,1)S(1)}, bf16[1024,256]{1,0:T(8,128)(2,1)S(1)}, u32[]{:S(2)}, u32[]{:S(2)}) %collective-permute-start.16) | collective-permute-done | bytes 524320 | tf_op jit(solution)/shard_map/ppermute | solution.py:23
  221.5 2.1 collective-permute-start.20
  225.5 6.4 %collective-permute-done.18.refs_3_ = bf16[192,512]{1,0:T(8,128)(2,1)S(1)} collective-permute-done((bf16[192,512]{1,0:T(8,128)(2,1)S(1)}, bf16[192,512]{1,0:T(8,128)(2,1)S(1)}, u32[]{:S(2)}, u32[]{:S(2)}) %collective-permute-start.18) | collective-permute-done | bytes 196640 | tf_op jit(solution)/shard_map/ppermute | solution.py:301
  233.4 3.0 %collective-permute-done.19.refs_4_ = bf16[192,512]{1,0:T(8,128)(2,1)S(1)} collective-permute-done((bf16[192,512]{1,0:T(8,128)(2,1)}, bf16[192,512]{1,0:T(8,128)(2,1)S(1)}, u32[]{:S(2)}, u32[]{:S(2)}) %collective-permute-start.19) | collective-permute-done | bytes 196640 | tf_op jit(solution)/shard_map/ppermute | solution.py:301
  236.3 12.8 %collective-permute-done.21.refs_6_ = bf16[192,512]{1,0:T(8,128)(2,1)S(1)} collective-permute-done((bf16[192,512]{1,0:T(8,128)(2,1)}, bf16[192,512]{1,0:T(8,128)(2,1)S(1)}, u32[]{:S(2)}, u32[]{:S(2)}) %collective-permute-start.21) | collective-permute-done | bytes 196640 | tf_op jit(solution)/shard_map/ppermute | solution.py:301
  249.1 4.1 %collective-permute-done.22.refs_7_ = bf16[192,512]{1,0:T(8,128)(2,1)S(1)} collective-permute-done((bf16[192,512]{1,0:T(8,128)(2,1)S(1)}, bf16[192,512]{1,0:T(8,128)(2,1)S(1)}, u32[]{:S(2)}, u32[]{:S(2)}) %collective-permute-start.22) | collective-permute-done | bytes 196640 | tf_op jit(solution)/shard_map/ppermute | solution.py:301
  253.2 4.5 %collective-permute-done.23.refs_8_ = bf16[192,512]{1,0:T(8,128)(2,1)S(1)} collective-permute-done((bf16[192,512]{1,0:T(8,128)(2,1)S(1)}, bf16[192,512]{1,0:T(8,128)(2,1)S(1)}, u32[]{:S(2)}, u32[]{:S(2)}) %collective-permute-start.23) | collective-permute-done | bytes 196640 | tf_op jit(solution)/shard_map/ppermute | solution.py:301
  257.7 2.3 unpacked.1
  (66 shorter events, 28.0 us)
Async XLA Ops:
  2.9 42.0 %copy-start = (bf16[192,4096]{1,0:T(8,128)(2,1)S(1)}, bf16[192,4096]{1,0:T(8,128)(2,1)}, u32[]{:S(2)}) copy-start(bf16[192,4096]{1,0:T(8,128)(2,1)} %refs_2_.3) | copy-start | bytes 4718596
  2.9 42.1 %copy-start.1 = (bf16[192,4096]{1,0:T(8,128)(2,1)S(1)}, bf16[192,4096]{1,0:T(8,128)(2,1)}, u32[]{:S(2)}) copy-start(bf16[192,4096]{1,0:T(8,128)(2,1)} %refs_3_.1) | copy-start | bytes 4718596
  3.1 5.2 %collective-permute-start = (bf16[192,512]{1,0:T(8,128)(2,1)S(1)}, bf16[192,512]{1,0:T(8,128)(2,1)S(1)}, u32[]{:S(2)}, u32[]{:S(2)}) collective-permute-start(bf16[192,512]{1,0:T(8,128)(2,1)S(1)} %get-tuple-element.36), channel_id=1, source_target_pairs={{0,1},{1,0},{2,3},{3,2},{4,5},{5,4},{6,7},{7,6},{8,9},{9,8},{10,11... | collective-permute-start | bytes 589832 | tf_op jit(solution)/shard_map/ppermute | solution.py:301
  3.9 12.2 %collective-permute-start.1 = (bf16[192,512]{1,0:T(8,128)(2,1)S(1)}, bf16[192,512]{1,0:T(8,128)(2,1)S(1)}, u32[]{:S(2)}, u32[]{:S(2)}) collective-permute-start(bf16[192,512]{1,0:T(8,128)(2,1)S(1)} %get-tuple-element.37), channel_id=1, source_target_pairs={{0,2},{1,3},{2,0},{3,1},{4,6},{5,7},{6,4},{7,5},{8,10},{9,11},{10,... | collective-permute-start | bytes 589832 | tf_op jit(solution)/shard_map/ppermute | solution.py:301
  4.1 16.4 %collective-permute-start.2 = (bf16[192,512]{1,0:T(8,128)(2,1)S(1)}, bf16[192,512]{1,0:T(8,128)(2,1)S(1)}, u32[]{:S(2)}, u32[]{:S(2)}) collective-permute-start(bf16[192,512]{1,0:T(8,128)(2,1)S(1)} %get-tuple-element.38), channel_id=1, source_target_pairs={{0,3},{1,2},{2,1},{3,0},{4,7},{5,6},{6,5},{7,4},{8,11},{9,10},{10,... | collective-permute-start | bytes 589832 | tf_op jit(solution)/shard_map/ppermute | solution.py:301
  5.6 14.8 %collective-permute-start.3 = (bf16[192,512]{1,0:T(8,128)(2,1)S(1)}, bf16[192,512]{1,0:T(8,128)(2,1)S(1)}, u32[]{:S(2)}, u32[]{:S(2)}) collective-permute-start(bf16[192,512]{1,0:T(8,128)(2,1)S(1)} %get-tuple-element.39), channel_id=1, source_target_pairs={{0,4},{1,5},{2,6},{3,7},{4,0},{5,1},{6,2},{7,3},{8,12},{9,13},{10,... | collective-permute-start | bytes 589832 | tf_op jit(solution)/shard_map/ppermute | solution.py:301
  7.9 25.3 %collective-permute-start.4 = (bf16[192,512]{1,0:T(8,128)(2,1)S(1)}, bf16[192,512]{1,0:T(8,128)(2,1)S(1)}, u32[]{:S(2)}, u32[]{:S(2)}) collective-permute-start(bf16[192,512]{1,0:T(8,128)(2,1)S(1)} %get-tuple-element.40), channel_id=1, source_target_pairs={{0,5},{1,4},{2,7},{3,6},{4,1},{5,0},{6,3},{7,2},{8,13},{9,12},{10,... | collective-permute-start | bytes 589832 | tf_op jit(solution)/shard_map/ppermute | solution.py:301
  8.3 29.1 %collective-permute-start.5 = (bf16[192,512]{1,0:T(8,128)(2,1)S(1)}, bf16[192,512]{1,0:T(8,128)(2,1)S(1)}, u32[]{:S(2)}, u32[]{:S(2)}) collective-permute-start(bf16[192,512]{1,0:T(8,128)(2,1)S(1)} %get-tuple-element.41), channel_id=1, source_target_pairs={{0,6},{1,7},{2,4},{3,5},{4,2},{5,3},{6,0},{7,1},{8,14},{9,15},{10,... | collective-permute-start | bytes 589832 | tf_op jit(solution)/shard_map/ppermute | solution.py:301
  16.1 25.6 %collective-permute-start.6 = (bf16[192,512]{1,0:T(8,128)(2,1)S(1)}, bf16[192,512]{1,0:T(8,128)(2,1)S(1)}, u32[]{:S(2)}, u32[]{:S(2)}) collective-permute-start(bf16[192,512]{1,0:T(8,128)(2,1)S(1)} %get-tuple-element.42), channel_id=1, source_target_pairs={{0,7},{1,6},{2,5},{3,4},{4,3},{5,2},{6,1},{7,0},{8,15},{9,14},{10,... | collective-permute-start | bytes 589832 | tf_op jit(solution)/shard_map/ppermute | solution.py:301
  41.8 3.4 %copy-start.6 = (bf16[1536,512]{1,0:T(8,128)(2,1)}, bf16[1536,512]{1,0:T(8,128)(2,1)S(1)}, u32[]{:S(2)}) copy-start(bf16[1536,512]{1,0:T(8,128)(2,1)S(1)} %get-tuple-element.44.own_k.own_v) | copy-start | bytes 4718596
  41.8 26.6 %collective-permute-start.7 = (bf16[1024,512]{1,0:T(8,128)(2,1)S(1)}, bf16[1024,512]{1,0:T(8,128)(2,1)S(1)}, u32[]{:S(2)}, u32[]{:S(2)}) collective-permute-start(bf16[1024,512]{1,0:T(8,128)(2,1)S(1)} %get-tuple-element.43), channel_id=1, source_target_pairs={{0,8},{8,16},{16,24},{1,9},{9,17},{17,25},{2,10},{10,18},{18,26},{... | collective-permute-start | bytes 3145736 | tf_op jit(solution)/shard_map/ppermute | solution.py:23
  47.9 7.2 %collective-permute-start.13 = (bf16[192,512]{1,0:T(8,128)(2,1)S(1)}, bf16[192,512]{1,0:T(8,128)(2,1)S(1)}, u32[]{:S(2)}, u32[]{:S(2)}) collective-permute-start(bf16[192,512]{1,0:T(8,128)(2,1)S(1)} %get-tuple-element.51), channel_id=1, source_target_pairs={{0,6},{1,7},{2,4},{3,5},{4,2},{5,3},{6,0},{7,1},{8,14},{9,15},{10,... | collective-permute-start | bytes 589832 | tf_op jit(solution)/shard_map/ppermute | solution.py:301
  68.4 69.8 %copy-start.2 = (bf16[1024,512]{1,0:T(8,128)(2,1)}, bf16[1024,512]{1,0:T(8,128)(2,1)S(1)}, u32[]{:S(2)}) copy-start(bf16[1024,512]{1,0:T(8,128)(2,1)S(1)} %collective-permute-done.7.halo_k.halo_v.refs_1_) | copy-start | bytes 3145732
  69.8 7.0 %copy-start.13 = (s32[16]{0:T(128)S(1)}, s32[16]{0:T(128)}, u32[]{:S(2)}) copy-start(s32[16]{0:T(128)} %param.9) | copy-start | bytes 196
  69.8 106.9 %all-to-all-start.1 = ((bf16[8,192,512]{2,1,0:T(8,128)(2,1)}), bf16[8,192,512]{2,1,0:T(8,128)(2,1)S(1)}, u32[]{:S(2)}, u32[]{:S(2)}) async-start(bf16[8,192,512]{2,1,0:T(8,128)(2,1)} %packed.5), calls=%async_computation.1 | async-start | bytes 3145728 | tf_op jit(solution)/shard_map/all_to_all | solution.py:306
  77.3 4.8 %collective-permute-start.8 = (bf16[192,512]{1,0:T(8,128)(2,1)}, bf16[192,512]{1,0:T(8,128)(2,1)S(1)}, u32[]{:S(2)}, u32[]{:S(2)}) collective-permute-start(bf16[192,512]{1,0:T(8,128)(2,1)} %copy-done.12), channel_id=1, source_target_pairs={{0,1},{1,0},{2,3},{3,2},{4,5},{5,4},{6,7},{7,6},{8,9},{9,8},{10,11... | collective-permute-start | bytes 589832 | tf_op jit(solution)/shard_map/ppermute | solution.py:301
  77.6 30.0 %collective-permute-start.9 = (bf16[192,512]{1,0:T(8,128)(2,1)}, bf16[192,512]{1,0:T(8,128)(2,1)S(1)}, u32[]{:S(2)}, u32[]{:S(2)}) collective-permute-start(bf16[192,512]{1,0:T(8,128)(2,1)} %copy-done.11), channel_id=1, source_target_pairs={{0,2},{1,3},{2,0},{3,1},{4,6},{5,7},{6,4},{7,5},{8,10},{9,11},{10,... | collective-permute-start | bytes 589832 | tf_op jit(solution)/shard_map/ppermute | solution.py:301
  77.7 34.2 %collective-permute-start.10 = (bf16[192,512]{1,0:T(8,128)(2,1)}, bf16[192,512]{1,0:T(8,128)(2,1)S(1)}, u32[]{:S(2)}, u32[]{:S(2)}) collective-permute-start(bf16[192,512]{1,0:T(8,128)(2,1)} %copy-done.10), channel_id=1, source_target_pairs={{0,3},{1,2},{2,1},{3,0},{4,7},{5,6},{6,5},{7,4},{8,11},{9,10},{10,... | collective-permute-start | bytes 589832 | tf_op jit(solution)/shard_map/ppermute | solution.py:301
  79.5 48.5 %collective-permute-start.11 = (bf16[192,512]{1,0:T(8,128)(2,1)}, bf16[192,512]{1,0:T(8,128)(2,1)S(1)}, u32[]{:S(2)}, u32[]{:S(2)}) collective-permute-start(bf16[192,512]{1,0:T(8,128)(2,1)} %copy-done.9), channel_id=1, source_target_pairs={{0,4},{1,5},{2,6},{3,7},{4,0},{5,1},{6,2},{7,3},{8,12},{9,13},{10,... | collective-permute-start | bytes 589832 | tf_op jit(solution)/shard_map/ppermute | solution.py:301
  81.6 50.5 %collective-permute-start.12 = (bf16[192,512]{1,0:T(8,128)(2,1)S(1)}, bf16[192,512]{1,0:T(8,128)(2,1)S(1)}, u32[]{:S(2)}, u32[]{:S(2)}) collective-permute-start(bf16[192,512]{1,0:T(8,128)(2,1)S(1)} %get-tuple-element.50), channel_id=1, source_target_pairs={{0,5},{1,4},{2,7},{3,6},{4,1},{5,0},{6,3},{7,2},{8,13},{9,12},{10,... | collective-permute-start | bytes 589832 | tf_op jit(solution)/shard_map/ppermute | solution.py:301
  82.1 56.0 %collective-permute-start.14 = (bf16[192,512]{1,0:T(8,128)(2,1)S(1)}, bf16[192,512]{1,0:T(8,128)(2,1)S(1)}, u32[]{:S(2)}, u32[]{:S(2)}) collective-permute-start(bf16[192,512]{1,0:T(8,128)(2,1)S(1)} %get-tuple-element.52), channel_id=1, source_target_pairs={{0,7},{1,6},{2,5},{3,4},{4,3},{5,2},{6,1},{7,0},{8,15},{9,14},{10,... | collective-permute-start | bytes 589832 | tf_op jit(solution)/shard_map/ppermute | solution.py:301
  138.1 1.4 copy-start.7
  154.1 21.2 %collective-permute-start.15 = (bf16[1024,256]{1,0:T(8,128)(2,1)S(1)}, bf16[1024,256]{1,0:T(8,128)(2,1)S(1)}, u32[]{:S(2)}, u32[]{:S(2)}) collective-permute-start(bf16[1024,256]{1,0:T(8,128)(2,1)S(1)} %get-tuple-element.55), channel_id=1, source_target_pairs={{8,0},{16,8},{24,16},{9,1},{17,9},{25,17},{10,2},{18,10},{26,18},{... | collective-permute-start | bytes 1572872 | tf_op jit(solution)/shard_map/ppermute | solution.py:23
  176.7 56.7 %all-to-all-start = ((bf16[8,192,512]{2,1,0:T(8,128)(2,1)}), bf16[8,192,512]{2,1,0:T(8,128)(2,1)S(1)}, u32[]{:S(2)}, u32[]{:S(2)}) async-start(bf16[8,192,512]{2,1,0:T(8,128)(2,1)} %bitcast.2), calls=%async_computation | async-start | bytes 3145728 | tf_op jit(solution)/shard_map/all_to_all | solution.py:306
  197.7 19.9 %collective-permute-start.16 = (bf16[1024,256]{1,0:T(8,128)(2,1)S(1)}, bf16[1024,256]{1,0:T(8,128)(2,1)S(1)}, u32[]{:S(2)}, u32[]{:S(2)}) collective-permute-start(bf16[1024,256]{1,0:T(8,128)(2,1)S(1)} %get-tuple-element.58), channel_id=1, source_target_pairs={{8,0},{16,8},{24,16},{9,1},{17,9},{25,17},{10,2},{18,10},{26,18},{... | collective-permute-start | bytes 1572872 | tf_op jit(solution)/shard_map/ppermute | solution.py:23
  218.6 5.7 %collective-permute-start.17 = (bf16[192,512]{1,0:T(8,128)(2,1)S(1)}, bf16[192,512]{1,0:T(8,128)(2,1)S(1)}, u32[]{:S(2)}, u32[]{:S(2)}) collective-permute-start(bf16[192,512]{1,0:T(8,128)(2,1)S(1)} %get-tuple-element.60), channel_id=1, source_target_pairs={{0,1},{1,0},{2,3},{3,2},{4,5},{5,4},{6,7},{7,6},{8,9},{9,8},{10,11... | collective-permute-start | bytes 589832 | tf_op jit(solution)/shard_map/ppermute | solution.py:301
  219.9 12.0 %collective-permute-start.18 = (bf16[192,512]{1,0:T(8,128)(2,1)S(1)}, bf16[192,512]{1,0:T(8,128)(2,1)S(1)}, u32[]{:S(2)}, u32[]{:S(2)}) collective-permute-start(bf16[192,512]{1,0:T(8,128)(2,1)S(1)} %get-tuple-element.61), channel_id=1, source_target_pairs={{0,2},{1,3},{2,0},{3,1},{4,6},{5,7},{6,4},{7,5},{8,10},{9,11},{10,... | collective-permute-start | bytes 589832 | tf_op jit(solution)/shard_map/ppermute | solution.py:301
  219.9 16.4 %collective-permute-start.19 = (bf16[192,512]{1,0:T(8,128)(2,1)}, bf16[192,512]{1,0:T(8,128)(2,1)S(1)}, u32[]{:S(2)}, u32[]{:S(2)}) collective-permute-start(bf16[192,512]{1,0:T(8,128)(2,1)} %get-tuple-element.62), channel_id=1, source_target_pairs={{0,3},{1,2},{2,1},{3,0},{4,7},{5,6},{6,5},{7,4},{8,11},{9,10},{10,... | collective-permute-start | bytes 589832 | tf_op jit(solution)/shard_map/ppermute | solution.py:301
  221.5 14.8 %collective-permute-start.20 = (bf16[192,512]{1,0:T(8,128)(2,1)}, bf16[192,512]{1,0:T(8,128)(2,1)S(1)}, u32[]{:S(2)}, u32[]{:S(2)}) collective-permute-start(bf16[192,512]{1,0:T(8,128)(2,1)} %get-tuple-element.63), channel_id=1, source_target_pairs={{0,4},{1,5},{2,6},{3,7},{4,0},{5,1},{6,2},{7,3},{8,12},{9,13},{10,... | collective-permute-start | bytes 589832 | tf_op jit(solution)/shard_map/ppermute | solution.py:301
  223.6 25.5 %collective-permute-start.21 = (bf16[192,512]{1,0:T(8,128)(2,1)}, bf16[192,512]{1,0:T(8,128)(2,1)S(1)}, u32[]{:S(2)}, u32[]{:S(2)}) collective-permute-start(bf16[192,512]{1,0:T(8,128)(2,1)} %get-tuple-element.64), channel_id=1, source_target_pairs={{0,5},{1,4},{2,7},{3,6},{4,1},{5,0},{6,3},{7,2},{8,13},{9,12},{10,... | collective-permute-start | bytes 589832 | tf_op jit(solution)/shard_map/ppermute | solution.py:301
  224.3 28.9 %collective-permute-start.22 = (bf16[192,512]{1,0:T(8,128)(2,1)S(1)}, bf16[192,512]{1,0:T(8,128)(2,1)S(1)}, u32[]{:S(2)}, u32[]{:S(2)}) collective-permute-start(bf16[192,512]{1,0:T(8,128)(2,1)S(1)} %get-tuple-element.65), channel_id=1, source_target_pairs={{0,6},{1,7},{2,4},{3,5},{4,2},{5,3},{6,0},{7,1},{8,14},{9,15},{10,... | collective-permute-start | bytes 589832 | tf_op jit(solution)/shard_map/ppermute | solution.py:301
  231.9 25.8 %collective-permute-start.23 = (bf16[192,512]{1,0:T(8,128)(2,1)S(1)}, bf16[192,512]{1,0:T(8,128)(2,1)S(1)}, u32[]{:S(2)}, u32[]{:S(2)}) collective-permute-start(bf16[192,512]{1,0:T(8,128)(2,1)S(1)} %get-tuple-element.66), channel_id=1, source_target_pairs={{0,7},{1,6},{2,5},{3,4},{4,3},{5,2},{6,1},{7,0},{8,15},{9,14},{10,... | collective-permute-start | bytes 589832 | tf_op jit(solution)/shard_map/ppermute | solution.py:301
  (8 other events, 7.6 us)
where the time goes:
time: 263 us; the launch traced here: 260 us
  waiting for transfers between devices  158 us (60%)
  starting transfers between devices  55.7 us (21%)
  Pallas kernels  35.8 us (14%)
  local copies, waits for them, and re-layouts  9.2 us (3%)
    ppermute x21, waiting for transfers between devices, exchanged(): came[k] = lax.ppermute(blocks[k], 'head', [(i, i ^ k) for i in range(ways)])  121 us
    ppermute x3, waiting for transfers between devices, passed_along(): return lax.ppermute(shard, axis, pairs)  37.3 us
    pallas_call x2, Pallas kernels, attend(): pl.pallas_call(functools.partial(attend_kernel, per_group, ways), grid=(1...  29.2 us
    ppermute x21, starting transfers between devices, exchanged(): came[k] = lax.ppermute(blocks[k], 'head', [(i, i ^ k) for i in range(ways)])  24.8 us
    ppermute x3, starting transfers between devices, passed_along(): return lax.ppermute(shard, axis, pairs)  20.1 us
    all_to_all x2, starting transfers between devices, exchanged_at_once(): return lax.all_to_all(sent, 'head', split_axis=0, concat_axis=0, tiled=True)  10.8 us
    unnamed x28, local copies, waits for them, and re-layouts  9.02 us
    pallas_call x7, Pallas kernels, on_chip(): pl.pallas_call(body, out_shape=tuple((jax.ShapeDtypeStruct(s, jnp.bfloat1...  6.65 us
  transfers between devices with their start and end apart: 26, of which 19 were waited for; matrix products, arithmetic and copies ran while one was open for 0% of the time, Pallas kernels for 12%

commit v1 on v0

--- a/solution.py
+++ b/solution.py
@@ -15,6 +15,14 @@
 SCALING = HD ** (-0.5)
 EXP2_SCALE = SCALING * math.log2(math.e)
 MASKED = -1e30
+SPARE = 4 * 1024 * 1024
+SMEM = pl.BlockSpec(memory_space=pltpu.SMEM)
+VMEM = pl.BlockSpec(memory_space=pltpu.VMEM)
+ANYWHERE = pl.BlockSpec(memory_space=pl.ANY)
+
+
+def array_bytes(arrays):
+    return sum(math.prod(a.shape) * a.dtype.itemsize for a in arrays)
 
 
 def passed_along(shard, axis, by):
@@ -40,7 +48,9 @@
         out_ref[partner_rows(me_ref, k, block.shape[0]), :] = block[...]
 
 
-def attend_kernel(per_group, ways, me_ref, first_tile, low_ref, halo_k, halo_v, own_k, own_v, *refs):
+def attend_kernel(
+    per_group, ways, chunk, kv_local, me_ref, first_tile, low_ref, halo_ref, kv_ref, *refs
+):
     blocks, refs = refs[:ways], refs[ways:]
     dq_ref, own_ref, rim_ref, qd_ref, k_ext, v_ext, k_t, dk_ext, dv_ext, s_buf, dp_buf = refs
     if ways == 1:
@@ -49,10 +59,9 @@
         gather_rows(me_ref, blocks, qd_ref)
     group = qd_ref.shape[0]
     reach = WINDOW // TK
-    k_ext[:WINDOW, :] = halo_k[...]
-    k_ext[WINDOW:, :] = own_k[...]
-    v_ext[:WINDOW, :] = halo_v[...]
-    v_ext[WINDOW:, :] = own_v[...]
+    for ref, at in ((k_ext, chunk * HD), (v_ext, (kv_local + chunk) * HD)):
+        ref[:WINDOW, :] = halo_ref[:, at : at + HD]
+        ref[WINDOW:, :] = kv_ref[:, at : at + HD]
     dk_ext[...] = jnp.zeros_like(dk_ext)
     dv_ext[...] = jnp.zeros_like(dv_ext)
 
@@ -143,69 +152,51 @@
     wide = per_group * TQ
     span = WINDOW + TQ
 
-    def vmem(shape, lane_block=0):
-        return pl.BlockSpec(shape, lambda i: (0, lane_block))
-
     area = group * (WINDOW + TQ) * per_group
+    outs = [
+        jax.ShapeDtypeStruct((group, per_group * HD), jnp.bfloat16),
+        jax.ShapeDtypeStruct((group, 2 * HD), jnp.float32),
+        jax.ShapeDtypeStruct((WINDOW, 2 * HD), jnp.bfloat16),
+    ]
+    scratch = [
+        jax.ShapeDtypeStruct((group, qd_lanes) if ways > 1 else (16, 128), jnp.bfloat16),
+        jax.ShapeDtypeStruct((ext, HD), jnp.bfloat16),
+        jax.ShapeDtypeStruct((ext, HD), jnp.bfloat16),
+        jax.ShapeDtypeStruct((ext // TK, HD, TK), jnp.bfloat16),
+        jax.ShapeDtypeStruct((ext, HD), jnp.float32),
+        jax.ShapeDtypeStruct((ext, HD), jnp.float32),
+        jax.ShapeDtypeStruct((span, wide), jnp.float32),
+        jax.ShapeDtypeStruct((span, wide), jnp.float32),
+    ]
+    needed = array_bytes([low, halo, own, *qd_blocks, *outs, *scratch])
     return pl.pallas_call(
-        functools.partial(attend_kernel, per_group, ways),
-        grid=(1,),
-        out_shape=(
-            jax.ShapeDtypeStruct((group, per_group * HD), jnp.bfloat16),
-            jax.ShapeDtypeStruct((group, 2 * HD), jnp.float32),
-            jax.ShapeDtypeStruct((WINDOW, 2 * HD), jnp.bfloat16),
-        ),
-        in_specs=[
-            pl.BlockSpec(memory_space=pltpu.SMEM),
-            pl.BlockSpec(memory_space=pltpu.SMEM),
-            vmem((1, group)),
-            vmem((WINDOW, HD), chunk),
-            vmem((WINDOW, HD), kv_local + chunk),
-            vmem((group, HD), chunk),
-            vmem((group, HD), kv_local + chunk),
-        ]
-        + [vmem((tokens, qd_lanes))] * ways,
-        out_specs=(
-            vmem((group, per_group * HD)),
-            vmem((group, 2 * HD)),
-            vmem((WINDOW, 2 * HD)),
-        ),
-        scratch_shapes=[
-            pltpu.VMEM((group, qd_lanes), jnp.bfloat16),
-            pltpu.VMEM((ext, HD), jnp.bfloat16),
-            pltpu.VMEM((ext, HD), jnp.bfloat16),
-            pltpu.VMEM((ext // TK, HD, TK), jnp.bfloat16),
-            pltpu.VMEM((ext, HD), jnp.float32),
-            pltpu.VMEM((ext, HD), jnp.float32),
-            pltpu.VMEM((span, wide), jnp.float32),
-            pltpu.VMEM((span, wide), jnp.float32),
-        ],
-        compiler_params=pltpu.CompilerParams(vmem_limit_bytes=40 * 1024 * 1024),
+        functools.partial(attend_kernel, per_group, ways, chunk, kv_local),
+        out_shape=tuple(outs),
+        in_specs=[SMEM, SMEM] + [VMEM] * (3 + ways),
+        out_specs=(VMEM,) * 3,
+        scratch_shapes=[pltpu.VMEM(s.shape, s.dtype) for s in scratch],
+        compiler_params=pltpu.CompilerParams(vmem_limit_bytes=needed + SPARE),
         cost_estimate=pl.CostEstimate(
             flops=area * HD * 2 * 5, bytes_accessed=group * HD * 24, transcendentals=area
         ),
         name="attend",
-    )(me, first_tile, low, halo, halo, own, own, *qd_blocks)
-
-
-SMEM = pl.BlockSpec(memory_space=pltpu.SMEM)
-VMEM = pl.BlockSpec(memory_space=pltpu.VMEM)
-ANYWHERE = pl.BlockSpec(memory_space=pl.ANY)
+    )(me, first_tile, low, halo, own, *qd_blocks)
 
 
 def on_chip(kernel, me, arrays, shapes, name, scratch=(), earlier=()):
-    moved = sum(a.size * a.dtype.itemsize for a in arrays) + sum(2 * math.prod(s) for s in shapes)
+    outs = tuple(jax.ShapeDtypeStruct(s, jnp.bfloat16) for s in shapes)
+    moved = array_bytes([*arrays, *outs])
 
     def body(me_ref, *refs):
         kernel(me_ref, *refs[len(earlier) :])
 
     return pl.pallas_call(
         body,
-        out_shape=tuple(jax.ShapeDtypeStruct(s, jnp.bfloat16) for s in shapes),
+        out_shape=outs,
         in_specs=[SMEM] + [ANYWHERE] * len(earlier) + [VMEM] * len(arrays),
         out_specs=(VMEM,) * len(shapes),
         scratch_shapes=list(scratch),
-        compiler_params=pltpu.CompilerParams(vmem_limit_bytes=40 * 1024 * 1024),
+        compiler_params=pltpu.CompilerParams(vmem_limit_bytes=moved + SPARE),
         cost_estimate=pl.CostEstimate(flops=0, bytes_accessed=moved, transcendentals=0),
         name=name,
     )(me, *earlier, *arrays)
@@ -323,7 +314,7 @@
         exchanged(packed(me, (queries, grad_out), ways, 0, kv_local, True, [came[ways - 2]]))
     ]
     for c in range(1, kv_local):
-        earlier = [qds[-1][-2] if c == 1 else qds[-1][0], halo]
+        earlier = [*qds[-1][min(1, len(qds[-1]) - 1) :], halo]
         sent = packed(me, (queries, grad_out), ways, c, kv_local, False, earlier)[0]
         qds.append([exchanged_at_once(sent).reshape(group, 2 * q_lanes)])
 

time: 263 us -> 228 us (0.87)
  waiting for transfers between devices: 158 us -> 115 us
  Pallas kernels: 35.8 us -> 47.8 us
  starting transfers between devices: 55.7 us -> 49.1 us
    ppermute x21, waiting for transfers between devices: 121 us -> 93.5 us  [exchanged(): came[k] = lax.ppermute(blocks[k], 'head', [(i, i ^ k) for i in range(ways)])]
    ppermute x3, waiting for transfers between devices: 37.3 us -> 21.9 us  [passed_along(): return lax.ppermute(shard, axis, pairs)]
    pallas_call x9, Pallas kernels: 35.8 us -> 47.8 us  [the longest x2 41.1 us: attend(): pl.pallas_call(functools.partial(attend_kernel, per_group, ways, chunk, k...]
    ppermute x3, starting transfers between devices: 20.1 us -> 16.1 us  [passed_along(): return lax.ppermute(shard, axis, pairs)]
    unnamed x28 -> x36, local copies, waits for them, and re-layouts: 9.02 us -> 10.7 us
  transfers between devices with their start and end apart: 26 -> 26, of which waited for: 19 -> 17; matrix products, arithmetic and copies ran while one was open for 0% -> 0% of each run, Pallas kernels for 12% -> 20%
where the time goes in v1:
time: 228 us; the launch traced here: 224 us
  waiting for transfers between devices  115 us (50%)
  starting transfers between devices  49.1 us (22%)
  Pallas kernels  47.8 us (21%)
  local copies, waits for them, and re-layouts  10.9 us (5%)
    ppermute x21, waiting for transfers between devices, exchanged(): came[k] = lax.ppermute(blocks[k], 'head', [(i, i ^ k) for i in range(ways)])  93.5 us
    pallas_call x2, Pallas kernels, attend(): pl.pallas_call(functools.partial(attend_kernel, per_group, ways, chunk, k...  41.1 us
    ppermute x21, starting transfers between devices, exchanged(): came[k] = lax.ppermute(blocks[k], 'head', [(i, i ^ k) for i in range(ways)])  23.3 us
    ppermute x3, waiting for transfers between devices, passed_along(): return lax.ppermute(shard, axis, pairs)  21.9 us
    ppermute x3, starting transfers between devices, passed_along(): return lax.ppermute(shard, axis, pairs)  16.1 us
    unnamed x36, local copies, waits for them, and re-layouts  10.7 us
    all_to_all x2, starting transfers between devices, exchanged_at_once(): return lax.all_to_all(sent, 'head', split_axis=0, concat_axis=0, tiled=True)  9.62 us
    pallas_call x7, Pallas kernels, on_chip(): pl.pallas_call(body, out_shape=outs, in_specs=[SMEM] + [ANYWHERE] * len(e...  6.71 us
  transfers between devices with their start and end apart: 26, of which 17 were waited for; matrix products, arithmetic and copies ran while one was open for 0% of the time, Pallas kernels for 20%

profile of v1, /device:TPU:13, one launch (start us, length us, event | category | flops | bytes accessed | tf_op | source)
XLA Modules:
  0.0 224.3 jit_solution(5127497966437814357)
XLA Ops:
  4.0 1.5 collective-permute-start.2
  5.6 2.3 %collective-permute-start.3 = (bf16[192,512]{1,0:T(8,128)(2,1)S(1)}, bf16[192,512]{1,0:T(8,128)(2,1)S(1)}, u32[]{:S(2)}, u32[]{:S(2)}) collective-permute-start(bf16[192,512]{1,0:T(8,128)(2,1)S(1)} %get-tuple-element.39), channel_id=1, source_target_pairs={{0,4},{1,5},{2,6},{3,7},{4,0},{5,1},{6,2},{7,3},{8,12},{9,13},{10,... | collective-permute-start | bytes 589832 | tf_op jit(solution)/shard_map/ppermute | solution.py:292
  9.6 6.5 %collective-permute-done.1.refs_2_ = bf16[192,512]{1,0:T(8,128)(2,1)S(1)} collective-permute-done((bf16[192,512]{1,0:T(8,128)(2,1)S(1)}, bf16[192,512]{1,0:T(8,128)(2,1)S(1)}, u32[]{:S(2)}, u32[]{:S(2)}) %collective-permute-start.1) | collective-permute-done | bytes 196640 | tf_op jit(solution)/shard_map/ppermute | solution.py:292
  16.1 1.5 collective-permute-start.6
  17.6 2.8 %collective-permute-done.2.refs_3_ = bf16[192,512]{1,0:T(8,128)(2,1)S(1)} collective-permute-done((bf16[192,512]{1,0:T(8,128)(2,1)S(1)}, bf16[192,512]{1,0:T(8,128)(2,1)S(1)}, u32[]{:S(2)}, u32[]{:S(2)}) %collective-permute-start.2) | collective-permute-done | bytes 196640 | tf_op jit(solution)/shard_map/ppermute | solution.py:292
  20.4 12.7 %collective-permute-done.4.refs_5_ = bf16[192,512]{1,0:T(8,128)(2,1)S(1)} collective-permute-done((bf16[192,512]{1,0:T(8,128)(2,1)S(1)}, bf16[192,512]{1,0:T(8,128)(2,1)S(1)}, u32[]{:S(2)}, u32[]{:S(2)}) %collective-permute-start.4) | collective-permute-done | bytes 196640 | tf_op jit(solution)/shard_map/ppermute | solution.py:292
  33.2 4.2 %collective-permute-done.5.refs_6_.refs_0_ = bf16[192,512]{1,0:T(8,128)(2,1)S(1)} collective-permute-done((bf16[192,512]{1,0:T(8,128)(2,1)S(1)}, bf16[192,512]{1,0:T(8,128)(2,1)S(1)}, u32[]{:S(2)}, u32[]{:S(2)}) %collective-permute-start.5) | collective-permute-done | bytes 196640 | tf_op jit(solution)/shard_map/ppermute | solution.py:292
  37.4 4.3 %collective-permute-done.6.refs_7_ = bf16[192,512]{1,0:T(8,128)(2,1)S(1)} collective-permute-done((bf16[192,512]{1,0:T(8,128)(2,1)S(1)}, bf16[192,512]{1,0:T(8,128)(2,1)S(1)}, u32[]{:S(2)}, u32[]{:S(2)}) %collective-permute-start.6) | collective-permute-done | bytes 196640 | tf_op jit(solution)/shard_map/ppermute | solution.py:292
  41.8 3.1 %collective-permute-start.7 = (bf16[1024,512]{1,0:T(8,128)(2,1)S(1)}, bf16[1024,512]{1,0:T(8,128)(2,1)S(1)}, u32[]{:S(2)}, u32[]{:S(2)}) collective-permute-start(bf16[1024,512]{1,0:T(8,128)(2,1)S(1)} %get-tuple-element.43), channel_id=1, source_target_pairs={{0,8},{8,16},{16,24},{1,9},{9,17},{17,25},{2,10},{10,18},{18,26},{... | collective-permute-start | bytes 3145736 | tf_op jit(solution)/shard_map/ppermute | solution.py:31
  47.1 1.6 collective-permute-start.10
  49.9 1.5 collective-permute-start.12
  51.5 8.0 %collective-permute-done.9.refs_2_.refs_1_ = bf16[192,512]{1,0:T(8,128)(2,1)S(1)} collective-permute-done((bf16[192,512]{1,0:T(8,128)(2,1)S(1)}, bf16[192,512]{1,0:T(8,128)(2,1)S(1)}, u32[]{:S(2)}, u32[]{:S(2)}) %collective-permute-start.9) | collective-permute-done | bytes 196640 | tf_op jit(solution)/shard_map/ppermute | solution.py:292
  60.0 3.8 %collective-permute-done.10.refs_3_.refs_2_ = bf16[192,512]{1,0:T(8,128)(2,1)S(1)} collective-permute-done((bf16[192,512]{1,0:T(8,128)(2,1)S(1)}, bf16[192,512]{1,0:T(8,128)(2,1)S(1)}, u32[]{:S(2)}, u32[]{:S(2)}) %collective-permute-start.10) | collective-permute-done | bytes 196640 | tf_op jit(solution)/shard_map/ppermute | solution.py:292
  64.8 10.0 %collective-permute-done.12.refs_5_.refs_4_ = bf16[192,512]{1,0:T(8,128)(2,1)S(1)} collective-permute-done((bf16[192,512]{1,0:T(8,128)(2,1)S(1)}, bf16[192,512]{1,0:T(8,128)(2,1)S(1)}, u32[]{:S(2)}, u32[]{:S(2)}) %collective-permute-start.12) | collective-permute-done | bytes 196640 | tf_op jit(solution)/shard_map/ppermute | solution.py:292
  74.8 6.2 %collective-permute-done.13.refs_6_.refs_5_ = bf16[192,512]{1,0:T(8,128)(2,1)S(1)} collective-permute-done((bf16[192,512]{1,0:T(8,128)(2,1)S(1)}, bf16[192,512]{1,0:T(8,128)(2,1)S(1)}, u32[]{:S(2)}, u32[]{:S(2)}) %collective-permute-start.13) | collective-permute-done | bytes 196640 | tf_op jit(solution)/shard_map/ppermute | solution.py:292
  81.0 4.2 %collective-permute-done.14.refs_7_.refs_6_ = bf16[192,512]{1,0:T(8,128)(2,1)S(1)} collective-permute-done((bf16[192,512]{1,0:T(8,128)(2,1)S(1)}, bf16[192,512]{1,0:T(8,128)(2,1)S(1)}, u32[]{:S(2)}, u32[]{:S(2)}) %collective-permute-start.14) | collective-permute-done | bytes 196640 | tf_op jit(solution)/shard_map/ppermute | solution.py:292
  86.6 3.7 %all-to-all-start.1 = ((bf16[8,192,512]{2,1,0:T(8,128)(2,1)}), bf16[8,192,512]{2,1,0:T(8,128)(2,1)S(1)}, u32[]{:S(2)}, u32[]{:S(2)}) async-start(bf16[8,192,512]{2,1,0:T(8,128)(2,1)} %packed.5), calls=%async_computation.1 | async-start | bytes 3145728 | tf_op jit(solution)/shard_map/all_to_all | solution.py:297
  95.9 20.5 %attend.2 = (bf16[1536,256]{1,0:T(8,128)(2,1)S(1)}, f32[1536,256]{1,0:T(8,128)S(1)}, bf16[1024,256]{1,0:T(8,128)(2,1)S(1)}) custom-call(s32[1]{0:T(128)} %bitcast.me_ref, s32[6]{0:T(128)S(1)} %and_select_fusion.first_tile, s32[1,1536]{1,0:T(1,128)S(1)} %maximum_subtract_fusion.1.low_ref, bf16[1024,512]{1,0:T(8,128)(2,1)S(1)} %collective-permute-done.7.halo_ref.refs_7_, ...), custom_call_target="tpu_custom_call" | custom-call | flops 5033164800 | bytes 4718592 | tf_op jit(solution)/shard_map/attend/pallas_call | solution.py:172
  116.5 5.6 %collective-permute-start.15 = (bf16[1024,256]{1,0:T(8,128)(2,1)S(1)}, bf16[1024,256]{1,0:T(8,128)(2,1)S(1)}, u32[]{:S(2)}, u32[]{:S(2)}) collective-permute-start(bf16[1024,256]{1,0:T(8,128)(2,1)S(1)} %get-tuple-element.55), channel_id=1, source_target_pairs={{8,0},{16,8},{24,16},{9,1},{17,9},{25,17},{10,2},{18,10},{26,18},{... | collective-permute-start | bytes 1572872 | tf_op jit(solution)/shard_map/ppermute | solution.py:31
  122.0 10.9 %collective-permute-done.15.refs_2_ = bf16[1024,256]{1,0:T(8,128)(2,1)S(1)} collective-permute-done((bf16[1024,256]{1,0:T(8,128)(2,1)S(1)}, bf16[1024,256]{1,0:T(8,128)(2,1)S(1)}, u32[]{:S(2)}, u32[]{:S(2)}) %collective-permute-start.15) | collective-permute-done | bytes 524320 | tf_op jit(solution)/shard_map/ppermute | solution.py:31
  134.3 5.9 %all-to-all-start = ((bf16[8,192,512]{2,1,0:T(8,128)(2,1)}), bf16[8,192,512]{2,1,0:T(8,128)(2,1)S(1)}, u32[]{:S(2)}, u32[]{:S(2)}) async-start(bf16[8,192,512]{2,1,0:T(8,128)(2,1)} %bitcast.2), calls=%async_computation | async-start | bytes 3145728 | tf_op jit(solution)/shard_map/all_to_all | solution.py:297
  142.9 20.6 %attend.3 = (bf16[1536,256]{1,0:T(8,128)(2,1)S(1)}, f32[1536,256]{1,0:T(8,128)S(1)}, bf16[1024,256]{1,0:T(8,128)(2,1)S(1)}) custom-call(s32[1]{0:T(128)} %bitcast.me_ref, s32[6]{0:T(128)S(1)} %and_select_fusion.first_tile, s32[1,1536]{1,0:T(1,128)S(1)} %maximum_subtract_fusion.1.low_ref, bf16[1024,512]{1,0:T(8,128)(2,1)S(1)} %copy-done.3, ...), custom_call_target="tpu_custom_call" | custom-call | flops 5033164800 | bytes 4718592 | tf_op jit(solution)/shard_map/attend/pallas_call | solution.py:172
  163.5 7.5 %collective-permute-start.16 = (bf16[1024,256]{1,0:T(8,128)(2,1)S(1)}, bf16[1024,256]{1,0:T(8,128)(2,1)S(1)}, u32[]{:S(2)}, u32[]{:S(2)}) collective-permute-start(bf16[1024,256]{1,0:T(8,128)(2,1)S(1)} %get-tuple-element.58), channel_id=1, source_target_pairs={{8,0},{16,8},{24,16},{9,1},{17,9},{25,17},{10,2},{18,10},{26,18},{... | collective-permute-start | bytes 1572872 | tf_op jit(solution)/shard_map/ppermute | solution.py:31
  171.0 10.9 %collective-permute-done.16.refs_2_ = bf16[1024,256]{1,0:T(8,128)(2,1)S(1)} collective-permute-done((bf16[1024,256]{1,0:T(8,128)(2,1)S(1)}, bf16[1024,256]{1,0:T(8,128)(2,1)S(1)}, u32[]{:S(2)}, u32[]{:S(2)}) %collective-permute-start.16) | collective-permute-done | bytes 524320 | tf_op jit(solution)/shard_map/ppermute | solution.py:31
  184.3 1.5 collective-permute-start.19
  185.8 2.1 collective-permute-start.20
  189.8 6.4 %collective-permute-done.18.refs_3_ = bf16[192,512]{1,0:T(8,128)(2,1)S(1)} collective-permute-done((bf16[192,512]{1,0:T(8,128)(2,1)S(1)}, bf16[192,512]{1,0:T(8,128)(2,1)S(1)}, u32[]{:S(2)}, u32[]{:S(2)}) %collective-permute-start.18) | collective-permute-done | bytes 196640 | tf_op jit(solution)/shard_map/ppermute | solution.py:292
  197.6 3.0 %collective-permute-done.19.refs_4_ = bf16[192,512]{1,0:T(8,128)(2,1)S(1)} collective-permute-done((bf16[192,512]{1,0:T(8,128)(2,1)}, bf16[192,512]{1,0:T(8,128)(2,1)S(1)}, u32[]{:S(2)}, u32[]{:S(2)}) %collective-permute-start.19) | collective-permute-done | bytes 196640 | tf_op jit(solution)/shard_map/ppermute | solution.py:292
  200.7 12.7 %collective-permute-done.21.refs_6_ = bf16[192,512]{1,0:T(8,128)(2,1)S(1)} collective-permute-done((bf16[192,512]{1,0:T(8,128)(2,1)}, bf16[192,512]{1,0:T(8,128)(2,1)S(1)}, u32[]{:S(2)}, u32[]{:S(2)}) %collective-permute-start.21) | collective-permute-done | bytes 196640 | tf_op jit(solution)/shard_map/ppermute | solution.py:292
  213.4 4.1 %collective-permute-done.22.refs_7_ = bf16[192,512]{1,0:T(8,128)(2,1)S(1)} collective-permute-done((bf16[192,512]{1,0:T(8,128)(2,1)S(1)}, bf16[192,512]{1,0:T(8,128)(2,1)S(1)}, u32[]{:S(2)}, u32[]{:S(2)}) %collective-permute-start.22) | collective-permute-done | bytes 196640 | tf_op jit(solution)/shard_map/ppermute | solution.py:292
  217.5 4.5 %collective-permute-done.23.refs_8_ = bf16[192,512]{1,0:T(8,128)(2,1)S(1)} collective-permute-done((bf16[192,512]{1,0:T(8,128)(2,1)S(1)}, bf16[192,512]{1,0:T(8,128)(2,1)S(1)}, u32[]{:S(2)}, u32[]{:S(2)}) %collective-permute-start.23) | collective-permute-done | bytes 196640 | tf_op jit(solution)/shard_map/ppermute | solution.py:292
  222.0 2.3 %unpacked.1 = (bf16[192,4096]{1,0:T(8,128)(2,1)}, bf16[192,2048]{1,0:T(8,128)(2,1)}, bf16[192,2048]{1,0:T(8,128)(2,1)}) custom-call(s32[1]{0:T(128)} %bitcast.me_ref, bf16[8,192,512]{2,1,0:T(8,128)(2,1)S(1)} %all-to-all-done.refs_0_, bf16[192,512]{1,0:T(8,128)(2,1)S(1)} %get-tuple-element.59.refs_1_, bf16[192,512]{1,0:T(8,128)(2,1)S(1)} %collective-permute-done.17.refs_2_, ...), custom_call_target="tpu_custom_call" | custom-call | bytes 6291456 | tf_op jit(solution)/shard_map/unpacked/pallas_call | solution.py:193
  (74 shorter events, 26.8 us)
Async XLA Ops:
  2.9 42.0 %copy-start = (bf16[192,4096]{1,0:T(8,128)(2,1)S(1)}, bf16[192,4096]{1,0:T(8,128)(2,1)}, u32[]{:S(2)}) copy-start(bf16[192,4096]{1,0:T(8,128)(2,1)} %refs_8_.1) | copy-start | bytes 4718596
  2.9 42.1 %copy-start.1 = (bf16[192,4096]{1,0:T(8,128)(2,1)S(1)}, bf16[192,4096]{1,0:T(8,128)(2,1)}, u32[]{:S(2)}) copy-start(bf16[192,4096]{1,0:T(8,128)(2,1)} %refs_9_.1) | copy-start | bytes 4718596
  3.1 5.2 %collective-permute-start = (bf16[192,512]{1,0:T(8,128)(2,1)S(1)}, bf16[192,512]{1,0:T(8,128)(2,1)S(1)}, u32[]{:S(2)}, u32[]{:S(2)}) collective-permute-start(bf16[192,512]{1,0:T(8,128)(2,1)S(1)} %get-tuple-element.36), channel_id=1, source_target_pairs={{0,1},{1,0},{2,3},{3,2},{4,5},{5,4},{6,7},{7,6},{8,9},{9,8},{10,11... | collective-permute-start | bytes 589832 | tf_op jit(solution)/shard_map/ppermute | solution.py:292
  3.9 12.2 %collective-permute-start.1 = (bf16[192,512]{1,0:T(8,128)(2,1)S(1)}, bf16[192,512]{1,0:T(8,128)(2,1)S(1)}, u32[]{:S(2)}, u32[]{:S(2)}) collective-permute-start(bf16[192,512]{1,0:T(8,128)(2,1)S(1)} %get-tuple-element.37), channel_id=1, source_target_pairs={{0,2},{1,3},{2,0},{3,1},{4,6},{5,7},{6,4},{7,5},{8,10},{9,11},{10,... | collective-permute-start | bytes 589832 | tf_op jit(solution)/shard_map/ppermute | solution.py:292
  4.0 16.4 %collective-permute-start.2 = (bf16[192,512]{1,0:T(8,128)(2,1)S(1)}, bf16[192,512]{1,0:T(8,128)(2,1)S(1)}, u32[]{:S(2)}, u32[]{:S(2)}) collective-permute-start(bf16[192,512]{1,0:T(8,128)(2,1)S(1)} %get-tuple-element.38), channel_id=1, source_target_pairs={{0,3},{1,2},{2,1},{3,0},{4,7},{5,6},{6,5},{7,4},{8,11},{9,10},{10,... | collective-permute-start | bytes 589832 | tf_op jit(solution)/shard_map/ppermute | solution.py:292
  5.6 14.8 %collective-permute-start.3 = (bf16[192,512]{1,0:T(8,128)(2,1)S(1)}, bf16[192,512]{1,0:T(8,128)(2,1)S(1)}, u32[]{:S(2)}, u32[]{:S(2)}) collective-permute-start(bf16[192,512]{1,0:T(8,128)(2,1)S(1)} %get-tuple-element.39), channel_id=1, source_target_pairs={{0,4},{1,5},{2,6},{3,7},{4,0},{5,1},{6,2},{7,3},{8,12},{9,13},{10,... | collective-permute-start | bytes 589832 | tf_op jit(solution)/shard_map/ppermute | solution.py:292
  7.9 25.3 %collective-permute-start.4 = (bf16[192,512]{1,0:T(8,128)(2,1)S(1)}, bf16[192,512]{1,0:T(8,128)(2,1)S(1)}, u32[]{:S(2)}, u32[]{:S(2)}) collective-permute-start(bf16[192,512]{1,0:T(8,128)(2,1)S(1)} %get-tuple-element.40), channel_id=1, source_target_pairs={{0,5},{1,4},{2,7},{3,6},{4,1},{5,0},{6,3},{7,2},{8,13},{9,12},{10,... | collective-permute-start | bytes 589832 | tf_op jit(solution)/shard_map/ppermute | solution.py:292
  8.3 29.1 %collective-permute-start.5 = (bf16[192,512]{1,0:T(8,128)(2,1)S(1)}, bf16[192,512]{1,0:T(8,128)(2,1)S(1)}, u32[]{:S(2)}, u32[]{:S(2)}) collective-permute-start(bf16[192,512]{1,0:T(8,128)(2,1)S(1)} %get-tuple-element.41), channel_id=1, source_target_pairs={{0,6},{1,7},{2,4},{3,5},{4,2},{5,3},{6,0},{7,1},{8,14},{9,15},{10,... | collective-permute-start | bytes 589832 | tf_op jit(solution)/shard_map/ppermute | solution.py:292
  16.1 25.6 %collective-permute-start.6 = (bf16[192,512]{1,0:T(8,128)(2,1)S(1)}, bf16[192,512]{1,0:T(8,128)(2,1)S(1)}, u32[]{:S(2)}, u32[]{:S(2)}) collective-permute-start(bf16[192,512]{1,0:T(8,128)(2,1)S(1)} %get-tuple-element.42), channel_id=1, source_target_pairs={{0,7},{1,6},{2,5},{3,4},{4,3},{5,2},{6,1},{7,0},{8,15},{9,14},{10,... | collective-permute-start | bytes 589832 | tf_op jit(solution)/shard_map/ppermute | solution.py:292
  41.8 43.4 %collective-permute-start.7 = (bf16[1024,512]{1,0:T(8,128)(2,1)S(1)}, bf16[1024,512]{1,0:T(8,128)(2,1)S(1)}, u32[]{:S(2)}, u32[]{:S(2)}) collective-permute-start(bf16[1024,512]{1,0:T(8,128)(2,1)S(1)} %get-tuple-element.43), channel_id=1, source_target_pairs={{0,8},{8,16},{16,24},{1,9},{9,17},{17,25},{2,10},{10,18},{18,26},{... | collective-permute-start | bytes 3145736 | tf_op jit(solution)/shard_map/ppermute | solution.py:31
  45.9 4.1 %collective-permute-start.8 = (bf16[192,512]{1,0:T(8,128)(2,1)S(1)}, bf16[192,512]{1,0:T(8,128)(2,1)S(1)}, u32[]{:S(2)}, u32[]{:S(2)}) collective-permute-start(bf16[192,512]{1,0:T(8,128)(2,1)S(1)} %get-tuple-element.46), channel_id=1, source_target_pairs={{0,1},{1,0},{2,3},{3,2},{4,5},{5,4},{6,7},{7,6},{8,9},{9,8},{10,11... | collective-permute-start | bytes 589832 | tf_op jit(solution)/shard_map/ppermute | solution.py:292
  47.1 12.4 %collective-permute-start.9 = (bf16[192,512]{1,0:T(8,128)(2,1)S(1)}, bf16[192,512]{1,0:T(8,128)(2,1)S(1)}, u32[]{:S(2)}, u32[]{:S(2)}) collective-permute-start(bf16[192,512]{1,0:T(8,128)(2,1)S(1)} %get-tuple-element.47), channel_id=1, source_target_pairs={{0,2},{1,3},{2,0},{3,1},{4,6},{5,7},{6,4},{7,5},{8,10},{9,11},{10,... | collective-permute-start | bytes 589832 | tf_op jit(solution)/shard_map/ppermute | solution.py:292
  47.1 16.7 %collective-permute-start.10 = (bf16[192,512]{1,0:T(8,128)(2,1)S(1)}, bf16[192,512]{1,0:T(8,128)(2,1)S(1)}, u32[]{:S(2)}, u32[]{:S(2)}) collective-permute-start(bf16[192,512]{1,0:T(8,128)(2,1)S(1)} %get-tuple-element.48), channel_id=1, source_target_pairs={{0,3},{1,2},{2,1},{3,0},{4,7},{5,6},{6,5},{7,4},{8,11},{9,10},{10,... | collective-permute-start | bytes 589832 | tf_op jit(solution)/shard_map/ppermute | solution.py:292
  48.7 16.0 %collective-permute-start.11 = (bf16[192,512]{1,0:T(8,128)(2,1)S(1)}, bf16[192,512]{1,0:T(8,128)(2,1)S(1)}, u32[]{:S(2)}, u32[]{:S(2)}) collective-permute-start(bf16[192,512]{1,0:T(8,128)(2,1)S(1)} %get-tuple-element.49), channel_id=1, source_target_pairs={{0,4},{1,5},{2,6},{3,7},{4,0},{5,1},{6,2},{7,3},{8,12},{9,13},{10,... | collective-permute-start | bytes 589832 | tf_op jit(solution)/shard_map/ppermute | solution.py:292
  49.9 24.8 %collective-permute-start.12 = (bf16[192,512]{1,0:T(8,128)(2,1)S(1)}, bf16[192,512]{1,0:T(8,128)(2,1)S(1)}, u32[]{:S(2)}, u32[]{:S(2)}) collective-permute-start(bf16[192,512]{1,0:T(8,128)(2,1)S(1)} %get-tuple-element.50), channel_id=1, source_target_pairs={{0,5},{1,4},{2,7},{3,6},{4,1},{5,0},{6,3},{7,2},{8,13},{9,12},{10,... | collective-permute-start | bytes 589832 | tf_op jit(solution)/shard_map/ppermute | solution.py:292
  59.4 21.5 %collective-permute-start.13 = (bf16[192,512]{1,0:T(8,128)(2,1)S(1)}, bf16[192,512]{1,0:T(8,128)(2,1)S(1)}, u32[]{:S(2)}, u32[]{:S(2)}) collective-permute-start(bf16[192,512]{1,0:T(8,128)(2,1)S(1)} %get-tuple-element.51), channel_id=1, source_target_pairs={{0,6},{1,7},{2,4},{3,5},{4,2},{5,3},{6,0},{7,1},{8,14},{9,15},{10,... | collective-permute-start | bytes 589832 | tf_op jit(solution)/shard_map/ppermute | solution.py:292
  63.8 21.4 %collective-permute-start.14 = (bf16[192,512]{1,0:T(8,128)(2,1)S(1)}, bf16[192,512]{1,0:T(8,128)(2,1)S(1)}, u32[]{:S(2)}, u32[]{:S(2)}) collective-permute-start(bf16[192,512]{1,0:T(8,128)(2,1)S(1)} %get-tuple-element.52), channel_id=1, source_target_pairs={{0,7},{1,6},{2,5},{3,4},{4,3},{5,2},{6,1},{7,0},{8,15},{9,14},{10,... | collective-permute-start | bytes 589832 | tf_op jit(solution)/shard_map/ppermute | solution.py:292
  74.8 11.8 %copy-start.6 = (bf16[192,512]{1,0:T(8,128)(2,1)}, bf16[192,512]{1,0:T(8,128)(2,1)S(1)}, u32[]{:S(2)}) copy-start(bf16[192,512]{1,0:T(8,128)(2,1)S(1)} %collective-permute-done.12.refs_5_.refs_4_) | copy-start | bytes 589828
  81.0 5.6 %copy-start.8 = (bf16[192,512]{1,0:T(8,128)(2,1)}, bf16[192,512]{1,0:T(8,128)(2,1)S(1)}, u32[]{:S(2)}) copy-start(bf16[192,512]{1,0:T(8,128)(2,1)S(1)} %collective-permute-done.13.refs_6_.refs_5_) | copy-start | bytes 589828
  85.2 5.6 %copy-start.2 = (bf16[1024,512]{1,0:T(8,128)(2,1)}, bf16[1024,512]{1,0:T(8,128)(2,1)S(1)}, u32[]{:S(2)}) copy-start(bf16[1024,512]{1,0:T(8,128)(2,1)S(1)} %collective-permute-done.7.halo_ref.refs_7_) | copy-start | bytes 3145732
  86.6 3.7 %copy-start.17 = (s32[16]{0:T(128)S(1)}, s32[16]{0:T(128)}, u32[]{:S(2)}) copy-start(s32[16]{0:T(128)} %param.9) | copy-start | bytes 196
  86.6 47.7 %all-to-all-start.1 = ((bf16[8,192,512]{2,1,0:T(8,128)(2,1)}), bf16[8,192,512]{2,1,0:T(8,128)(2,1)S(1)}, u32[]{:S(2)}, u32[]{:S(2)}) async-start(bf16[8,192,512]{2,1,0:T(8,128)(2,1)} %packed.5), calls=%async_computation.1 | async-start | bytes 3145728 | tf_op jit(solution)/shard_map/all_to_all | solution.py:297
  116.5 16.5 %collective-permute-start.15 = (bf16[1024,256]{1,0:T(8,128)(2,1)S(1)}, bf16[1024,256]{1,0:T(8,128)(2,1)S(1)}, u32[]{:S(2)}, u32[]{:S(2)}) collective-permute-start(bf16[1024,256]{1,0:T(8,128)(2,1)S(1)} %get-tuple-element.55), channel_id=1, source_target_pairs={{8,0},{16,8},{24,16},{9,1},{17,9},{25,17},{10,2},{18,10},{26,18},{... | collective-permute-start | bytes 1572872 | tf_op jit(solution)/shard_map/ppermute | solution.py:31
  134.3 63.4 %all-to-all-start = ((bf16[8,192,512]{2,1,0:T(8,128)(2,1)}), bf16[8,192,512]{2,1,0:T(8,128)(2,1)S(1)}, u32[]{:S(2)}, u32[]{:S(2)}) async-start(bf16[8,192,512]{2,1,0:T(8,128)(2,1)} %bitcast.2), calls=%async_computation | async-start | bytes 3145728 | tf_op jit(solution)/shard_map/all_to_all | solution.py:297
  163.5 18.4 %collective-permute-start.16 = (bf16[1024,256]{1,0:T(8,128)(2,1)S(1)}, bf16[1024,256]{1,0:T(8,128)(2,1)S(1)}, u32[]{:S(2)}, u32[]{:S(2)}) collective-permute-start(bf16[1024,256]{1,0:T(8,128)(2,1)S(1)} %get-tuple-element.58), channel_id=1, source_target_pairs={{8,0},{16,8},{24,16},{9,1},{17,9},{25,17},{10,2},{18,10},{26,18},{... | collective-permute-start | bytes 1572872 | tf_op jit(solution)/shard_map/ppermute | solution.py:31
  183.0 5.6 %collective-permute-start.17 = (bf16[192,512]{1,0:T(8,128)(2,1)S(1)}, bf16[192,512]{1,0:T(8,128)(2,1)S(1)}, u32[]{:S(2)}, u32[]{:S(2)}) collective-permute-start(bf16[192,512]{1,0:T(8,128)(2,1)S(1)} %get-tuple-element.60), channel_id=1, source_target_pairs={{0,1},{1,0},{2,3},{3,2},{4,5},{5,4},{6,7},{7,6},{8,9},{9,8},{10,11... | collective-permute-start | bytes 589832 | tf_op jit(solution)/shard_map/ppermute | solution.py:292
  184.2 12.0 %collective-permute-start.18 = (bf16[192,512]{1,0:T(8,128)(2,1)S(1)}, bf16[192,512]{1,0:T(8,128)(2,1)S(1)}, u32[]{:S(2)}, u32[]{:S(2)}) collective-permute-start(bf16[192,512]{1,0:T(8,128)(2,1)S(1)} %get-tuple-element.61), channel_id=1, source_target_pairs={{0,2},{1,3},{2,0},{3,1},{4,6},{5,7},{6,4},{7,5},{8,10},{9,11},{10,... | collective-permute-start | bytes 589832 | tf_op jit(solution)/shard_map/ppermute | solution.py:292
  184.3 16.4 %collective-permute-start.19 = (bf16[192,512]{1,0:T(8,128)(2,1)}, bf16[192,512]{1,0:T(8,128)(2,1)S(1)}, u32[]{:S(2)}, u32[]{:S(2)}) collective-permute-start(bf16[192,512]{1,0:T(8,128)(2,1)} %get-tuple-element.62), channel_id=1, source_target_pairs={{0,3},{1,2},{2,1},{3,0},{4,7},{5,6},{6,5},{7,4},{8,11},{9,10},{10,... | collective-permute-start | bytes 589832 | tf_op jit(solution)/shard_map/ppermute | solution.py:292
  185.8 14.9 %collective-permute-start.20 = (bf16[192,512]{1,0:T(8,128)(2,1)}, bf16[192,512]{1,0:T(8,128)(2,1)S(1)}, u32[]{:S(2)}, u32[]{:S(2)}) collective-permute-start(bf16[192,512]{1,0:T(8,128)(2,1)} %get-tuple-element.63), channel_id=1, source_target_pairs={{0,4},{1,5},{2,6},{3,7},{4,0},{5,1},{6,2},{7,3},{8,12},{9,13},{10,... | collective-permute-start | bytes 589832 | tf_op jit(solution)/shard_map/ppermute | solution.py:292
  187.9 25.5 %collective-permute-start.21 = (bf16[192,512]{1,0:T(8,128)(2,1)}, bf16[192,512]{1,0:T(8,128)(2,1)S(1)}, u32[]{:S(2)}, u32[]{:S(2)}) collective-permute-start(bf16[192,512]{1,0:T(8,128)(2,1)} %get-tuple-element.64), channel_id=1, source_target_pairs={{0,5},{1,4},{2,7},{3,6},{4,1},{5,0},{6,3},{7,2},{8,13},{9,12},{10,... | collective-permute-start | bytes 589832 | tf_op jit(solution)/shard_map/ppermute | solution.py:292
  188.6 28.9 %collective-permute-start.22 = (bf16[192,512]{1,0:T(8,128)(2,1)S(1)}, bf16[192,512]{1,0:T(8,128)(2,1)S(1)}, u32[]{:S(2)}, u32[]{:S(2)}) collective-permute-start(bf16[192,512]{1,0:T(8,128)(2,1)S(1)} %get-tuple-element.65), channel_id=1, source_target_pairs={{0,6},{1,7},{2,4},{3,5},{4,2},{5,3},{6,0},{7,1},{8,14},{9,15},{10,... | collective-permute-start | bytes 589832 | tf_op jit(solution)/shard_map/ppermute | solution.py:292
  196.2 25.8 %collective-permute-start.23 = (bf16[192,512]{1,0:T(8,128)(2,1)S(1)}, bf16[192,512]{1,0:T(8,128)(2,1)S(1)}, u32[]{:S(2)}, u32[]{:S(2)}) collective-permute-start(bf16[192,512]{1,0:T(8,128)(2,1)S(1)} %get-tuple-element.66), channel_id=1, source_target_pairs={{0,7},{1,6},{2,5},{3,4},{4,3},{5,2},{6,1},{7,0},{8,15},{9,14},{10,... | collective-permute-start | bytes 589832 | tf_op jit(solution)/shard_map/ppermute | solution.py:292
  (12 other events, 15.5 us)

commit v2 on v1

--- a/solution.py
+++ b/solution.py
@@ -10,15 +10,13 @@
 
 HD = 128
 WINDOW = 1024
-TQ = 256
-TK = 256
+TQ = TK = 256
 SCALING = HD ** (-0.5)
 EXP2_SCALE = SCALING * math.log2(math.e)
 MASKED = -1e30
 SPARE = 4 * 1024 * 1024
 SMEM = pl.BlockSpec(memory_space=pltpu.SMEM)
 VMEM = pl.BlockSpec(memory_space=pltpu.VMEM)
-ANYWHERE = pl.BlockSpec(memory_space=pl.ANY)
 
 
 def array_bytes(arrays):
@@ -73,11 +71,12 @@
     lax.fori_loop(0, (group + WINDOW) // TK, turn, 0)
     wide = per_group * TQ
     key_iota = lax.broadcasted_iota(jnp.int32, (TK, wide), 0)
-
-    def q_block(b, carry):
+    query_iota = lax.broadcasted_iota(jnp.int32, (1, TQ), 1)
+    diagonal = jnp.concatenate([query_iota] * per_group, axis=1)
+
+    def q_block(b, tiles):
         q_rows = pl.ds(pl.multiple_of(b * TQ, TQ), TQ)
-        start = first_tile[b]
-        stop = b * (TQ // TK) + (TQ // TK - 1) + reach + 1
+        first = b + reach + 1 - tiles
         q = jnp.concatenate(
             [qd_ref[q_rows, i * HD : (i + 1) * HD] for i in range(per_group)], axis=0
         )
@@ -85,61 +84,54 @@
             [qd_ref[q_rows, i * HD : (i + 1) * HD] for i in range(per_group, 2 * per_group)],
             axis=0,
         )
-        low = low_ref[:, q_rows]
-        low = jnp.concatenate([low] * per_group, axis=1)
-        high = b * TQ + WINDOW + lax.broadcasted_iota(jnp.int32, (1, TQ), 1)
-        high = jnp.concatenate([high] * per_group, axis=1)
-
-        def score(t, top):
-            rows = pl.ds(pl.multiple_of(t * TK, TK), TK)
-            slot = pl.ds(pl.multiple_of((t - start) * TK, TK), TK)
-            s = dot_nt(k_ext[rows, :], q)
-            j = key_iota + t * TK
-            s = jnp.where((j >= low) & (j <= high), s, MASKED)
-            s_buf[slot, :] = s
-            return jnp.maximum(top, jnp.max(s, axis=0, keepdims=True))
-
-        top = lax.fori_loop(start, stop, score, jnp.full((1, wide), MASKED, jnp.float32))
-
-        def weigh(t, sums):
-            total, dotted = sums
-            rows = pl.ds(pl.multiple_of(t * TK, TK), TK)
-            slot = pl.ds(pl.multiple_of((t - start) * TK, TK), TK)
-            p = jnp.exp2((s_buf[slot, :] - top) * EXP2_SCALE)
-            dp = dot_nt(v_ext[rows, :], d_out)
-            s_buf[slot, :] = p
-            dp_buf[slot, :] = dp
-            return (
-                total + jnp.sum(p, axis=0, keepdims=True),
-                dotted + jnp.sum(p * dp, axis=0, keepdims=True),
-            )
-
-        zero = jnp.zeros((1, wide), jnp.float32)
-        total, dotted = lax.fori_loop(start, stop, weigh, (zero, zero))
+        low = jnp.concatenate([low_ref[:, q_rows]] * per_group, axis=1) - first * TK
+        key_rows = [pl.ds(pl.multiple_of((first + t) * TK, TK), TK) for t in range(tiles)]
+        slots = [slice(t * TK, (t + 1) * TK) for t in range(tiles)]
+
+        top = jnp.full((1, wide), MASKED, jnp.float32)
+        for t in range(tiles):
+            s = dot_nt(k_ext[key_rows[t], :], q)
+            allowed = key_iota >= low - t * TK
+            if t == tiles - 1:
+                allowed = allowed & (key_iota <= diagonal)
+            s = jnp.where(allowed, s, MASKED)
+            s_buf[slots[t], :] = s
+            top = jnp.maximum(top, jnp.max(s, axis=0, keepdims=True))
+
+        total = jnp.zeros((1, wide), jnp.float32)
+        dotted = jnp.zeros((1, wide), jnp.float32)
+        for t in range(tiles):
+            p = jnp.exp2((s_buf[slots[t], :] - top) * EXP2_SCALE)
+            dp = dot_nt(v_ext[key_rows[t], :], d_out)
+            s_buf[slots[t], :] = p
+            dp_buf[slots[t], :] = dp
+            total += jnp.sum(p, axis=0, keepdims=True)
+            dotted += jnp.sum(p * dp, axis=0, keepdims=True)
         inverse = 1.0 / total
         row_dot = dotted * inverse
-        inverse_scaled = inverse * SCALING
-
-        def grads(t, dq_t):
-            rows = pl.ds(pl.multiple_of(t * TK, TK), TK)
-            slot = pl.ds(pl.multiple_of((t - start) * TK, TK), TK)
-            p = s_buf[slot, :]
-            ds = ((p * inverse_scaled) * (dp_buf[slot, :] - row_dot)).astype(jnp.bfloat16)
-            weights = (p * inverse).astype(jnp.bfloat16)
-            dv_ext[rows, :] += dot_nn(weights, d_out)
-            dk_ext[rows, :] += dot_nn(ds, q)
-            return dq_t + dot_nn(k_t[t], ds)
-
-        dq_t = lax.fori_loop(start, stop, grads, jnp.zeros((HD, wide), jnp.float32))
-        dq = jnp.transpose(dq_t).astype(jnp.bfloat16)
+
+        dq_t = jnp.zeros((HD, wide), jnp.float32)
+        for t in range(tiles):
+            weights = s_buf[slots[t], :] * inverse
+            ds = (weights * (dp_buf[slots[t], :] - row_dot)).astype(jnp.bfloat16)
+            dv_ext[key_rows[t], :] += dot_nn(weights.astype(jnp.bfloat16), d_out)
+            dk_ext[key_rows[t], :] += dot_nn(ds, q)
+            dq_t += dot_nn(k_t[first + t], ds)
+
+        dq = jnp.transpose(dq_t * SCALING).astype(jnp.bfloat16)
         for i in range(per_group):
             dq_ref[q_rows, i * HD : (i + 1) * HD] = dq[i * TQ : (i + 1) * TQ, :]
+
+    def any_block(b, carry):
+        tiles = b + reach + 1 - first_tile[b]
+        for count in range(1, reach + 2):
+            pl.when(tiles == count)(functools.partial(q_block, b, count))
         return carry
 
-    lax.fori_loop(0, group // TQ, q_block, 0)
-    rim_ref[:, :HD] = dk_ext[:WINDOW, :].astype(jnp.bfloat16)
+    lax.fori_loop(0, group // TQ, any_block, 0)
+    rim_ref[:, :HD] = (dk_ext[:WINDOW, :] * SCALING).astype(jnp.bfloat16)
     rim_ref[:, HD:] = dv_ext[:WINDOW, :].astype(jnp.bfloat16)
-    own_ref[:, :HD] = dk_ext[WINDOW:, :]
+    own_ref[:, :HD] = dk_ext[WINDOW:, :] * SCALING
     own_ref[:, HD:] = dv_ext[WINDOW:, :]
 
 
@@ -185,7 +177,7 @@
 
 def on_chip(kernel, me, arrays, shapes, name, scratch=(), earlier=()):
     outs = tuple(jax.ShapeDtypeStruct(s, jnp.bfloat16) for s in shapes)
-    moved = array_bytes([*arrays, *outs])
+    moved = array_bytes([*arrays, *earlier, *outs])
 
     def body(me_ref, *refs):
         kernel(me_ref, *refs[len(earlier) :])
@@ -193,7 +185,7 @@
     return pl.pallas_call(
         body,
         out_shape=outs,
-        in_specs=[SMEM] + [ANYWHERE] * len(earlier) + [VMEM] * len(arrays),
+        in_specs=[SMEM] + [VMEM] * (len(earlier) + len(arrays)),
         out_specs=(VMEM,) * len(shapes),
         scratch_shapes=list(scratch),
         compiler_params=pltpu.CompilerParams(vmem_limit_bytes=moved + SPARE),
@@ -311,10 +303,10 @@
     kv, tail = gathered(me, came)
     halo = passed_along(tail, "seq", 1)
     qds = [
-        exchanged(packed(me, (queries, grad_out), ways, 0, kv_local, True, [came[ways - 2]]))
+        exchanged(packed(me, (queries, grad_out), ways, 0, kv_local, True, [came[1]]))
     ]
     for c in range(1, kv_local):
-        earlier = [*qds[-1][min(1, len(qds[-1]) - 1) :], halo]
+        earlier = [*qds[-1][-2:], halo]
         sent = packed(me, (queries, grad_out), ways, c, kv_local, False, earlier)[0]
         qds.append([exchanged_at_once(sent).reshape(group, 2 * q_lanes)])
 

time: 228 us -> 240 us (1.053)
  waiting for transfers between devices: 115 us -> 153 us
  Pallas kernels: 47.8 us -> 26.5 us
  starting transfers between devices: 49.1 us -> 45.5 us
    ppermute x21, waiting for transfers between devices: 93.5 us -> 121 us  [exchanged(): came[k] = lax.ppermute(blocks[k], 'head', [(i, i ^ k) for i in range(ways)])]
    pallas_call x2, Pallas kernels: 41.1 us -> 19.8 us  [attend(): pl.pallas_call(functools.partial(attend_kernel, per_group, ways, chunk, k...]
    ppermute x3, waiting for transfers between devices: 21.9 us -> 32.5 us  [passed_along(): return lax.ppermute(shard, axis, pairs)]
    ppermute x3, starting transfers between devices: 16.1 us -> 7.37 us  [passed_along(): return lax.ppermute(shard, axis, pairs)]
    all_to_all x2, starting transfers between devices: 9.62 us -> 14.7 us  [exchanged_at_once(): return lax.all_to_all(sent, 'head', split_axis=0, concat_axis=0, tiled=True)]
    unnamed x36 -> x28, local copies, waits for them, and re-layouts: 10.7 us -> 9.02 us
  transfers between devices with their start and end apart: 26 -> 26, of which waited for: 17 -> 19; matrix products, arithmetic and copies ran while one was open for 0% -> 0% of each run, Pallas kernels for 20% -> 10%
where the time goes in v2:
time: 240 us; the launch traced here: 235 us
  waiting for transfers between devices  153 us (64%)
  starting transfers between devices  45.5 us (19%)
  Pallas kernels  26.5 us (11%)
  local copies, waits for them, and re-layouts  9.2 us (4%)
    ppermute x21, waiting for transfers between devices, exchanged(): came[k] = lax.ppermute(blocks[k], 'head', [(i, i ^ k) for i in range(ways)])  121 us
    ppermute x3, waiting for transfers between devices, passed_along(): return lax.ppermute(shard, axis, pairs)  32.5 us
    ppermute x21, starting transfers between devices, exchanged(): came[k] = lax.ppermute(blocks[k], 'head', [(i, i ^ k) for i in range(ways)])  23.4 us
    pallas_call x2, Pallas kernels, attend(): pl.pallas_call(functools.partial(attend_kernel, per_group, ways, chunk, k...  19.8 us
    all_to_all x2, starting transfers between devices, exchanged_at_once(): return lax.all_to_all(sent, 'head', split_axis=0, concat_axis=0, tiled=True)  14.7 us
    unnamed x28, local copies, waits for them, and re-layouts  9.02 us
    ppermute x3, starting transfers between devices, passed_along(): return lax.ppermute(shard, axis, pairs)  7.37 us
    pallas_call x7, Pallas kernels, on_chip(): pl.pallas_call(body, out_shape=outs, in_specs=[SMEM] + [VMEM] * (len(earl...  6.69 us
  transfers between devices with their start and end apart: 26, of which 19 were waited for; matrix products, arithmetic and copies ran while one was open for 0% of the time, Pallas kernels for 10%

profile of v2, /device:TPU:13, one launch (start us, length us, event | category | flops | bytes accessed | tf_op | source)
XLA Modules:
  0.0 235.4 jit_solution(13682339385454276759)
XLA Ops:
  5.6 2.3 collective-permute-start.3
  9.6 6.5 %collective-permute-done.1.refs_2_ = bf16[192,512]{1,0:T(8,128)(2,1)S(1)} collective-permute-done((bf16[192,512]{1,0:T(8,128)(2,1)S(1)}, bf16[192,512]{1,0:T(8,128)(2,1)S(1)}, u32[]{:S(2)}, u32[]{:S(2)}) %collective-permute-start.1) | collective-permute-done | bytes 196640 | tf_op jit(solution)/shard_map/ppermute | solution.py:284
  17.6 2.8 %collective-permute-done.2.refs_3_ = bf16[192,512]{1,0:T(8,128)(2,1)S(1)} collective-permute-done((bf16[192,512]{1,0:T(8,128)(2,1)S(1)}, bf16[192,512]{1,0:T(8,128)(2,1)S(1)}, u32[]{:S(2)}, u32[]{:S(2)}) %collective-permute-start.2) | collective-permute-done | bytes 196640 | tf_op jit(solution)/shard_map/ppermute | solution.py:284
  20.4 12.7 %collective-permute-done.4.refs_5_ = bf16[192,512]{1,0:T(8,128)(2,1)S(1)} collective-permute-done((bf16[192,512]{1,0:T(8,128)(2,1)S(1)}, bf16[192,512]{1,0:T(8,128)(2,1)S(1)}, u32[]{:S(2)}, u32[]{:S(2)}) %collective-permute-start.4) | collective-permute-done | bytes 196640 | tf_op jit(solution)/shard_map/ppermute | solution.py:284
  33.2 4.2 %collective-permute-done.5.refs_6_ = bf16[192,512]{1,0:T(8,128)(2,1)S(1)} collective-permute-done((bf16[192,512]{1,0:T(8,128)(2,1)S(1)}, bf16[192,512]{1,0:T(8,128)(2,1)S(1)}, u32[]{:S(2)}, u32[]{:S(2)}) %collective-permute-start.5) | collective-permute-done | bytes 196640 | tf_op jit(solution)/shard_map/ppermute | solution.py:284
  37.4 4.3 %collective-permute-done.6.refs_7_ = bf16[192,512]{1,0:T(8,128)(2,1)S(1)} collective-permute-done((bf16[192,512]{1,0:T(8,128)(2,1)S(1)}, bf16[192,512]{1,0:T(8,128)(2,1)S(1)}, u32[]{:S(2)}, u32[]{:S(2)}) %collective-permute-start.6) | collective-permute-done | bytes 196640 | tf_op jit(solution)/shard_map/ppermute | solution.py:284
  41.8 3.1 %collective-permute-start.7 = (bf16[1024,512]{1,0:T(8,128)(2,1)S(1)}, bf16[1024,512]{1,0:T(8,128)(2,1)S(1)}, u32[]{:S(2)}, u32[]{:S(2)}) collective-permute-start(bf16[1024,512]{1,0:T(8,128)(2,1)S(1)} %get-tuple-element.43), channel_id=1, source_target_pairs={{0,8},{8,16},{16,24},{1,9},{9,17},{17,25},{2,10},{10,18},{18,26},{... | collective-permute-start | bytes 3145736 | tf_op jit(solution)/shard_map/ppermute | solution.py:29
  47.9 2.4 %collective-permute-start.13 = (bf16[192,512]{1,0:T(8,128)(2,1)S(1)}, bf16[192,512]{1,0:T(8,128)(2,1)S(1)}, u32[]{:S(2)}, u32[]{:S(2)}) collective-permute-start(bf16[192,512]{1,0:T(8,128)(2,1)S(1)} %get-tuple-element.51), channel_id=1, source_target_pairs={{0,6},{1,7},{2,4},{3,5},{4,2},{5,3},{6,0},{7,1},{8,14},{9,15},{10,... | collective-permute-start | bytes 589832 | tf_op jit(solution)/shard_map/ppermute | solution.py:284
  50.7 6.6 %collective-permute-done.13.refs_6_.refs_0_ = bf16[192,512]{1,0:T(8,128)(2,1)S(1)} collective-permute-done((bf16[192,512]{1,0:T(8,128)(2,1)S(1)}, bf16[192,512]{1,0:T(8,128)(2,1)S(1)}, u32[]{:S(2)}, u32[]{:S(2)}) %collective-permute-start.13) | collective-permute-done | bytes 196640 | tf_op jit(solution)/shard_map/ppermute | solution.py:284
  57.3 4.2 %collective-permute-done.14.refs_7_.refs_1_ = bf16[192,512]{1,0:T(8,128)(2,1)S(1)} collective-permute-done((bf16[192,512]{1,0:T(8,128)(2,1)S(1)}, bf16[192,512]{1,0:T(8,128)(2,1)S(1)}, u32[]{:S(2)}, u32[]{:S(2)}) %collective-permute-start.14) | collective-permute-done | bytes 196640 | tf_op jit(solution)/shard_map/ppermute | solution.py:284
  61.6 6.8 %collective-permute-done.7.halo_ref.refs_2_ = bf16[1024,512]{1,0:T(8,128)(2,1)S(1)} collective-permute-done((bf16[1024,512]{1,0:T(8,128)(2,1)S(1)}, bf16[1024,512]{1,0:T(8,128)(2,1)S(1)}, u32[]{:S(2)}, u32[]{:S(2)}) %collective-permute-start.7) | collective-permute-done | bytes 1048608 | tf_op jit(solution)/shard_map/ppermute | solution.py:29
  69.8 7.0 %all-to-all-start.1 = ((bf16[8,192,512]{2,1,0:T(8,128)(2,1)}), bf16[8,192,512]{2,1,0:T(8,128)(2,1)S(1)}, u32[]{:S(2)}, u32[]{:S(2)}) async-start(bf16[8,192,512]{2,1,0:T(8,128)(2,1)} %packed.5), calls=%async_computation.1 | async-start | bytes 3145728 | tf_op jit(solution)/shard_map/all_to_all | solution.py:289
  77.7 1.8 collective-permute-start.10
  79.5 2.1 collective-permute-start.11
  82.1 25.6 %collective-permute-done.9.refs_2_ = bf16[192,512]{1,0:T(8,128)(2,1)S(1)} collective-permute-done((bf16[192,512]{1,0:T(8,128)(2,1)}, bf16[192,512]{1,0:T(8,128)(2,1)S(1)}, u32[]{:S(2)}, u32[]{:S(2)}) %collective-permute-start.9) | collective-permute-done | bytes 196640 | tf_op jit(solution)/shard_map/ppermute | solution.py:284
  107.7 4.3 %collective-permute-done.10.refs_3_ = bf16[192,512]{1,0:T(8,128)(2,1)S(1)} collective-permute-done((bf16[192,512]{1,0:T(8,128)(2,1)}, bf16[192,512]{1,0:T(8,128)(2,1)S(1)}, u32[]{:S(2)}, u32[]{:S(2)}) %collective-permute-start.10) | collective-permute-done | bytes 196640 | tf_op jit(solution)/shard_map/ppermute | solution.py:284
  112.0 11.8 %collective-permute-done.11.refs_4_ = bf16[192,512]{1,0:T(8,128)(2,1)S(1)} collective-permute-done((bf16[192,512]{1,0:T(8,128)(2,1)}, bf16[192,512]{1,0:T(8,128)(2,1)S(1)}, u32[]{:S(2)}, u32[]{:S(2)}) %collective-permute-start.11) | collective-permute-done | bytes 196640 | tf_op jit(solution)/shard_map/ppermute | solution.py:284
  123.8 4.1 %collective-permute-done.12.refs_5_ = bf16[192,512]{1,0:T(8,128)(2,1)S(1)} collective-permute-done((bf16[192,512]{1,0:T(8,128)(2,1)S(1)}, bf16[192,512]{1,0:T(8,128)(2,1)S(1)}, u32[]{:S(2)}, u32[]{:S(2)}) %collective-permute-start.12) | collective-permute-done | bytes 196640 | tf_op jit(solution)/shard_map/ppermute | solution.py:284
  129.3 10.0 %attend.2 = (bf16[1536,256]{1,0:T(8,128)(2,1)S(1)}, f32[1536,256]{1,0:T(8,128)S(1)}, bf16[1024,256]{1,0:T(8,128)(2,1)S(1)}) custom-call(s32[1]{0:T(128)} %bitcast.me_ref, s32[6]{0:T(128)S(1)} %and_select_fusion.first_tile, s32[1,1536]{1,0:T(1,128)S(1)} %maximum_subtract_fusion.1.low_ref, bf16[1024,512]{1,0:T(8,128)(2,1)S(1)} %collective-permute-done.7.halo_ref.refs_2_, ...), custom_call_target="tpu_custom_call" | custom-call | flops 5033164800 | bytes 4718592 | tf_op jit(solution)/shard_map/attend/pallas_call | solution.py:164
  139.3 1.9 collective-permute-start.15
  141.2 13.0 %collective-permute-done.15.refs_2_ = bf16[1024,256]{1,0:T(8,128)(2,1)S(1)} collective-permute-done((bf16[1024,256]{1,0:T(8,128)(2,1)S(1)}, bf16[1024,256]{1,0:T(8,128)(2,1)S(1)}, u32[]{:S(2)}, u32[]{:S(2)}) %collective-permute-start.15) | collective-permute-done | bytes 524320 | tf_op jit(solution)/shard_map/ppermute | solution.py:29
  155.6 7.7 %all-to-all-start = ((bf16[8,192,512]{2,1,0:T(8,128)(2,1)}), bf16[8,192,512]{2,1,0:T(8,128)(2,1)S(1)}, u32[]{:S(2)}, u32[]{:S(2)}) async-start(bf16[8,192,512]{2,1,0:T(8,128)(2,1)} %bitcast.2), calls=%async_computation | async-start | bytes 3145728 | tf_op jit(solution)/shard_map/all_to_all | solution.py:289
  165.9 9.8 %attend.3 = (bf16[1536,256]{1,0:T(8,128)(2,1)S(1)}, f32[1536,256]{1,0:T(8,128)S(1)}, bf16[1024,256]{1,0:T(8,128)(2,1)S(1)}) custom-call(s32[1]{0:T(128)} %bitcast.me_ref, s32[6]{0:T(128)S(1)} %and_select_fusion.first_tile, s32[1,1536]{1,0:T(1,128)S(1)} %maximum_subtract_fusion.1.low_ref, bf16[1024,512]{1,0:T(8,128)(2,1)S(1)} %copy-done.3, ...), custom_call_target="tpu_custom_call" | custom-call | flops 5033164800 | bytes 4718592 | tf_op jit(solution)/shard_map/attend/pallas_call | solution.py:164
  175.8 2.3 collective-permute-start.16
  178.1 12.7 %collective-permute-done.16.refs_2_ = bf16[1024,256]{1,0:T(8,128)(2,1)S(1)} collective-permute-done((bf16[1024,256]{1,0:T(8,128)(2,1)S(1)}, bf16[1024,256]{1,0:T(8,128)(2,1)S(1)}, u32[]{:S(2)}, u32[]{:S(2)}) %collective-permute-start.16) | collective-permute-done | bytes 524320 | tf_op jit(solution)/shard_map/ppermute | solution.py:29
  194.7 2.1 collective-permute-start.20
  198.6 9.3 %collective-permute-done.18.refs_3_ = bf16[192,512]{1,0:T(8,128)(2,1)S(1)} collective-permute-done((bf16[192,512]{1,0:T(8,128)(2,1)S(1)}, bf16[192,512]{1,0:T(8,128)(2,1)S(1)}, u32[]{:S(2)}, u32[]{:S(2)}) %collective-permute-start.18) | collective-permute-done | bytes 196640 | tf_op jit(solution)/shard_map/ppermute | solution.py:284
  209.0 3.3 %collective-permute-done.19.refs_4_ = bf16[192,512]{1,0:T(8,128)(2,1)S(1)} collective-permute-done((bf16[192,512]{1,0:T(8,128)(2,1)}, bf16[192,512]{1,0:T(8,128)(2,1)S(1)}, u32[]{:S(2)}, u32[]{:S(2)}) %collective-permute-start.19) | collective-permute-done | bytes 196640 | tf_op jit(solution)/shard_map/ppermute | solution.py:284
  212.3 10.1 %collective-permute-done.21.refs_6_ = bf16[192,512]{1,0:T(8,128)(2,1)S(1)} collective-permute-done((bf16[192,512]{1,0:T(8,128)(2,1)}, bf16[192,512]{1,0:T(8,128)(2,1)S(1)}, u32[]{:S(2)}, u32[]{:S(2)}) %collective-permute-start.21) | collective-permute-done | bytes 196640 | tf_op jit(solution)/shard_map/ppermute | solution.py:284
  222.3 6.4 %collective-permute-done.22.refs_7_ = bf16[192,512]{1,0:T(8,128)(2,1)S(1)} collective-permute-done((bf16[192,512]{1,0:T(8,128)(2,1)S(1)}, bf16[192,512]{1,0:T(8,128)(2,1)S(1)}, u32[]{:S(2)}, u32[]{:S(2)}) %collective-permute-start.22) | collective-permute-done | bytes 196640 | tf_op jit(solution)/shard_map/ppermute | solution.py:284
  228.7 4.4 %collective-permute-done.23.refs_8_ = bf16[192,512]{1,0:T(8,128)(2,1)S(1)} collective-permute-done((bf16[192,512]{1,0:T(8,128)(2,1)S(1)}, bf16[192,512]{1,0:T(8,128)(2,1)S(1)}, u32[]{:S(2)}, u32[]{:S(2)}) %collective-permute-start.23) | collective-permute-done | bytes 196640 | tf_op jit(solution)/shard_map/ppermute | solution.py:284
  233.1 2.3 unpacked.1
  (66 shorter events, 26.6 us)
Async XLA Ops:
  2.9 42.0 %copy-start = (bf16[192,4096]{1,0:T(8,128)(2,1)S(1)}, bf16[192,4096]{1,0:T(8,128)(2,1)}, u32[]{:S(2)}) copy-start(bf16[192,4096]{1,0:T(8,128)(2,1)} %refs_3_.1) | copy-start | bytes 4718596
  2.9 42.1 %copy-start.1 = (bf16[192,4096]{1,0:T(8,128)(2,1)S(1)}, bf16[192,4096]{1,0:T(8,128)(2,1)}, u32[]{:S(2)}) copy-start(bf16[192,4096]{1,0:T(8,128)(2,1)} %refs_4_.1) | copy-start | bytes 4718596
  3.1 5.2 %collective-permute-start = (bf16[192,512]{1,0:T(8,128)(2,1)S(1)}, bf16[192,512]{1,0:T(8,128)(2,1)S(1)}, u32[]{:S(2)}, u32[]{:S(2)}) collective-permute-start(bf16[192,512]{1,0:T(8,128)(2,1)S(1)} %get-tuple-element.36), channel_id=1, source_target_pairs={{0,1},{1,0},{2,3},{3,2},{4,5},{5,4},{6,7},{7,6},{8,9},{9,8},{10,11... | collective-permute-start | bytes 589832 | tf_op jit(solution)/shard_map/ppermute | solution.py:284
  3.9 12.2 %collective-permute-start.1 = (bf16[192,512]{1,0:T(8,128)(2,1)S(1)}, bf16[192,512]{1,0:T(8,128)(2,1)S(1)}, u32[]{:S(2)}, u32[]{:S(2)}) collective-permute-start(bf16[192,512]{1,0:T(8,128)(2,1)S(1)} %get-tuple-element.37), channel_id=1, source_target_pairs={{0,2},{1,3},{2,0},{3,1},{4,6},{5,7},{6,4},{7,5},{8,10},{9,11},{10,... | collective-permute-start | bytes 589832 | tf_op jit(solution)/shard_map/ppermute | solution.py:284
  4.0 16.4 %collective-permute-start.2 = (bf16[192,512]{1,0:T(8,128)(2,1)S(1)}, bf16[192,512]{1,0:T(8,128)(2,1)S(1)}, u32[]{:S(2)}, u32[]{:S(2)}) collective-permute-start(bf16[192,512]{1,0:T(8,128)(2,1)S(1)} %get-tuple-element.38), channel_id=1, source_target_pairs={{0,3},{1,2},{2,1},{3,0},{4,7},{5,6},{6,5},{7,4},{8,11},{9,10},{10,... | collective-permute-start | bytes 589832 | tf_op jit(solution)/shard_map/ppermute | solution.py:284
  5.6 14.8 %collective-permute-start.3 = (bf16[192,512]{1,0:T(8,128)(2,1)S(1)}, bf16[192,512]{1,0:T(8,128)(2,1)S(1)}, u32[]{:S(2)}, u32[]{:S(2)}) collective-permute-start(bf16[192,512]{1,0:T(8,128)(2,1)S(1)} %get-tuple-element.39), channel_id=1, source_target_pairs={{0,4},{1,5},{2,6},{3,7},{4,0},{5,1},{6,2},{7,3},{8,12},{9,13},{10,... | collective-permute-start | bytes 589832 | tf_op jit(solution)/shard_map/ppermute | solution.py:284
  7.9 25.3 %collective-permute-start.4 = (bf16[192,512]{1,0:T(8,128)(2,1)S(1)}, bf16[192,512]{1,0:T(8,128)(2,1)S(1)}, u32[]{:S(2)}, u32[]{:S(2)}) collective-permute-start(bf16[192,512]{1,0:T(8,128)(2,1)S(1)} %get-tuple-element.40), channel_id=1, source_target_pairs={{0,5},{1,4},{2,7},{3,6},{4,1},{5,0},{6,3},{7,2},{8,13},{9,12},{10,... | collective-permute-start | bytes 589832 | tf_op jit(solution)/shard_map/ppermute | solution.py:284
  8.3 29.1 %collective-permute-start.5 = (bf16[192,512]{1,0:T(8,128)(2,1)S(1)}, bf16[192,512]{1,0:T(8,128)(2,1)S(1)}, u32[]{:S(2)}, u32[]{:S(2)}) collective-permute-start(bf16[192,512]{1,0:T(8,128)(2,1)S(1)} %get-tuple-element.41), channel_id=1, source_target_pairs={{0,6},{1,7},{2,4},{3,5},{4,2},{5,3},{6,0},{7,1},{8,14},{9,15},{10,... | collective-permute-start | bytes 589832 | tf_op jit(solution)/shard_map/ppermute | solution.py:284
  16.1 25.6 %collective-permute-start.6 = (bf16[192,512]{1,0:T(8,128)(2,1)S(1)}, bf16[192,512]{1,0:T(8,128)(2,1)S(1)}, u32[]{:S(2)}, u32[]{:S(2)}) collective-permute-start(bf16[192,512]{1,0:T(8,128)(2,1)S(1)} %get-tuple-element.42), channel_id=1, source_target_pairs={{0,7},{1,6},{2,5},{3,4},{4,3},{5,2},{6,1},{7,0},{8,15},{9,14},{10,... | collective-permute-start | bytes 589832 | tf_op jit(solution)/shard_map/ppermute | solution.py:284
  41.8 3.4 %copy-start.6 = (bf16[1536,512]{1,0:T(8,128)(2,1)}, bf16[1536,512]{1,0:T(8,128)(2,1)S(1)}, u32[]{:S(2)}) copy-start(bf16[1536,512]{1,0:T(8,128)(2,1)S(1)} %get-tuple-element.44.kv_ref) | copy-start | bytes 4718596
  41.8 26.6 %collective-permute-start.7 = (bf16[1024,512]{1,0:T(8,128)(2,1)S(1)}, bf16[1024,512]{1,0:T(8,128)(2,1)S(1)}, u32[]{:S(2)}, u32[]{:S(2)}) collective-permute-start(bf16[1024,512]{1,0:T(8,128)(2,1)S(1)} %get-tuple-element.43), channel_id=1, source_target_pairs={{0,8},{8,16},{16,24},{1,9},{9,17},{17,25},{2,10},{10,18},{18,26},{... | collective-permute-start | bytes 3145736 | tf_op jit(solution)/shard_map/ppermute | solution.py:29
  47.9 9.4 %collective-permute-start.13 = (bf16[192,512]{1,0:T(8,128)(2,1)S(1)}, bf16[192,512]{1,0:T(8,128)(2,1)S(1)}, u32[]{:S(2)}, u32[]{:S(2)}) collective-permute-start(bf16[192,512]{1,0:T(8,128)(2,1)S(1)} %get-tuple-element.51), channel_id=1, source_target_pairs={{0,6},{1,7},{2,4},{3,5},{4,2},{5,3},{6,0},{7,1},{8,14},{9,15},{10,... | collective-permute-start | bytes 589832 | tf_op jit(solution)/shard_map/ppermute | solution.py:284
  50.3 11.2 %collective-permute-start.14 = (bf16[192,512]{1,0:T(8,128)(2,1)S(1)}, bf16[192,512]{1,0:T(8,128)(2,1)S(1)}, u32[]{:S(2)}, u32[]{:S(2)}) collective-permute-start(bf16[192,512]{1,0:T(8,128)(2,1)S(1)} %get-tuple-element.52), channel_id=1, source_target_pairs={{0,7},{1,6},{2,5},{3,4},{4,3},{5,2},{6,1},{7,0},{8,15},{9,14},{10,... | collective-permute-start | bytes 589832 | tf_op jit(solution)/shard_map/ppermute | solution.py:284
  68.4 59.5 %copy-start.2 = (bf16[1024,512]{1,0:T(8,128)(2,1)}, bf16[1024,512]{1,0:T(8,128)(2,1)S(1)}, u32[]{:S(2)}) copy-start(bf16[1024,512]{1,0:T(8,128)(2,1)S(1)} %collective-permute-done.7.halo_ref.refs_2_) | copy-start | bytes 3145732
  69.8 7.0 %copy-start.13 = (s32[16]{0:T(128)S(1)}, s32[16]{0:T(128)}, u32[]{:S(2)}) copy-start(s32[16]{0:T(128)} %param.9) | copy-start | bytes 196
  69.8 85.8 %all-to-all-start.1 = ((bf16[8,192,512]{2,1,0:T(8,128)(2,1)}), bf16[8,192,512]{2,1,0:T(8,128)(2,1)S(1)}, u32[]{:S(2)}, u32[]{:S(2)}) async-start(bf16[8,192,512]{2,1,0:T(8,128)(2,1)} %packed.5), calls=%async_computation.1 | async-start | bytes 3145728 | tf_op jit(solution)/shard_map/all_to_all | solution.py:289
  77.3 4.8 %collective-permute-start.8 = (bf16[192,512]{1,0:T(8,128)(2,1)}, bf16[192,512]{1,0:T(8,128)(2,1)S(1)}, u32[]{:S(2)}, u32[]{:S(2)}) collective-permute-start(bf16[192,512]{1,0:T(8,128)(2,1)} %copy-done.12), channel_id=1, source_target_pairs={{0,1},{1,0},{2,3},{3,2},{4,5},{5,4},{6,7},{7,6},{8,9},{9,8},{10,11... | collective-permute-start | bytes 589832 | tf_op jit(solution)/shard_map/ppermute | solution.py:284
  77.7 30.0 %collective-permute-start.9 = (bf16[192,512]{1,0:T(8,128)(2,1)}, bf16[192,512]{1,0:T(8,128)(2,1)S(1)}, u32[]{:S(2)}, u32[]{:S(2)}) collective-permute-start(bf16[192,512]{1,0:T(8,128)(2,1)} %copy-done.11), channel_id=1, source_target_pairs={{0,2},{1,3},{2,0},{3,1},{4,6},{5,7},{6,4},{7,5},{8,10},{9,11},{10,... | collective-permute-start | bytes 589832 | tf_op jit(solution)/shard_map/ppermute | solution.py:284
  77.7 34.3 %collective-permute-start.10 = (bf16[192,512]{1,0:T(8,128)(2,1)}, bf16[192,512]{1,0:T(8,128)(2,1)S(1)}, u32[]{:S(2)}, u32[]{:S(2)}) collective-permute-start(bf16[192,512]{1,0:T(8,128)(2,1)} %copy-done.10), channel_id=1, source_target_pairs={{0,3},{1,2},{2,1},{3,0},{4,7},{5,6},{6,5},{7,4},{8,11},{9,10},{10,... | collective-permute-start | bytes 589832 | tf_op jit(solution)/shard_map/ppermute | solution.py:284
  79.5 44.3 %collective-permute-start.11 = (bf16[192,512]{1,0:T(8,128)(2,1)}, bf16[192,512]{1,0:T(8,128)(2,1)S(1)}, u32[]{:S(2)}, u32[]{:S(2)}) collective-permute-start(bf16[192,512]{1,0:T(8,128)(2,1)} %copy-done.9), channel_id=1, source_target_pairs={{0,4},{1,5},{2,6},{3,7},{4,0},{5,1},{6,2},{7,3},{8,12},{9,13},{10,... | collective-permute-start | bytes 589832 | tf_op jit(solution)/shard_map/ppermute | solution.py:284
  81.6 46.3 %collective-permute-start.12 = (bf16[192,512]{1,0:T(8,128)(2,1)S(1)}, bf16[192,512]{1,0:T(8,128)(2,1)S(1)}, u32[]{:S(2)}, u32[]{:S(2)}) collective-permute-start(bf16[192,512]{1,0:T(8,128)(2,1)S(1)} %get-tuple-element.50), channel_id=1, source_target_pairs={{0,5},{1,4},{2,7},{3,6},{4,1},{5,0},{6,3},{7,2},{8,13},{9,12},{10,... | collective-permute-start | bytes 589832 | tf_op jit(solution)/shard_map/ppermute | solution.py:284
  127.9 1.4 copy-start.7
  139.3 14.9 %collective-permute-start.15 = (bf16[1024,256]{1,0:T(8,128)(2,1)S(1)}, bf16[1024,256]{1,0:T(8,128)(2,1)S(1)}, u32[]{:S(2)}, u32[]{:S(2)}) collective-permute-start(bf16[1024,256]{1,0:T(8,128)(2,1)S(1)} %get-tuple-element.55), channel_id=1, source_target_pairs={{8,0},{16,8},{24,16},{9,1},{17,9},{25,17},{10,2},{18,10},{26,18},{... | collective-permute-start | bytes 1572872 | tf_op jit(solution)/shard_map/ppermute | solution.py:29
  155.6 53.4 %all-to-all-start = ((bf16[8,192,512]{2,1,0:T(8,128)(2,1)}), bf16[8,192,512]{2,1,0:T(8,128)(2,1)S(1)}, u32[]{:S(2)}, u32[]{:S(2)}) async-start(bf16[8,192,512]{2,1,0:T(8,128)(2,1)} %bitcast.2), calls=%async_computation | async-start | bytes 3145728 | tf_op jit(solution)/shard_map/all_to_all | solution.py:289
  175.8 15.0 %collective-permute-start.16 = (bf16[1024,256]{1,0:T(8,128)(2,1)S(1)}, bf16[1024,256]{1,0:T(8,128)(2,1)S(1)}, u32[]{:S(2)}, u32[]{:S(2)}) collective-permute-start(bf16[1024,256]{1,0:T(8,128)(2,1)S(1)} %get-tuple-element.58), channel_id=1, source_target_pairs={{8,0},{16,8},{24,16},{9,1},{17,9},{25,17},{10,2},{18,10},{26,18},{... | collective-permute-start | bytes 1572872 | tf_op jit(solution)/shard_map/ppermute | solution.py:29
  191.9 5.6 %collective-permute-start.17 = (bf16[192,512]{1,0:T(8,128)(2,1)S(1)}, bf16[192,512]{1,0:T(8,128)(2,1)S(1)}, u32[]{:S(2)}, u32[]{:S(2)}) collective-permute-start(bf16[192,512]{1,0:T(8,128)(2,1)S(1)} %get-tuple-element.60), channel_id=1, source_target_pairs={{0,1},{1,0},{2,3},{3,2},{4,5},{5,4},{6,7},{7,6},{8,9},{9,8},{10,11... | collective-permute-start | bytes 589832 | tf_op jit(solution)/shard_map/ppermute | solution.py:284
  193.1 14.9 %collective-permute-start.18 = (bf16[192,512]{1,0:T(8,128)(2,1)S(1)}, bf16[192,512]{1,0:T(8,128)(2,1)S(1)}, u32[]{:S(2)}, u32[]{:S(2)}) collective-permute-start(bf16[192,512]{1,0:T(8,128)(2,1)S(1)} %get-tuple-element.61), channel_id=1, source_target_pairs={{0,2},{1,3},{2,0},{3,1},{4,6},{5,7},{6,4},{7,5},{8,10},{9,11},{10,... | collective-permute-start | bytes 589832 | tf_op jit(solution)/shard_map/ppermute | solution.py:284
  193.1 19.1 %collective-permute-start.19 = (bf16[192,512]{1,0:T(8,128)(2,1)}, bf16[192,512]{1,0:T(8,128)(2,1)S(1)}, u32[]{:S(2)}, u32[]{:S(2)}) collective-permute-start(bf16[192,512]{1,0:T(8,128)(2,1)} %get-tuple-element.62), channel_id=1, source_target_pairs={{0,3},{1,2},{2,1},{3,0},{4,7},{5,6},{6,5},{7,4},{8,11},{9,10},{10,... | collective-permute-start | bytes 589832 | tf_op jit(solution)/shard_map/ppermute | solution.py:284
  194.7 17.6 %collective-permute-start.20 = (bf16[192,512]{1,0:T(8,128)(2,1)}, bf16[192,512]{1,0:T(8,128)(2,1)S(1)}, u32[]{:S(2)}, u32[]{:S(2)}) collective-permute-start(bf16[192,512]{1,0:T(8,128)(2,1)} %get-tuple-element.63), channel_id=1, source_target_pairs={{0,4},{1,5},{2,6},{3,7},{4,0},{5,1},{6,2},{7,3},{8,12},{9,13},{10,... | collective-permute-start | bytes 589832 | tf_op jit(solution)/shard_map/ppermute | solution.py:284
  196.8 25.5 %collective-permute-start.21 = (bf16[192,512]{1,0:T(8,128)(2,1)}, bf16[192,512]{1,0:T(8,128)(2,1)S(1)}, u32[]{:S(2)}, u32[]{:S(2)}) collective-permute-start(bf16[192,512]{1,0:T(8,128)(2,1)} %get-tuple-element.64), channel_id=1, source_target_pairs={{0,5},{1,4},{2,7},{3,6},{4,1},{5,0},{6,3},{7,2},{8,13},{9,12},{10,... | collective-permute-start | bytes 589832 | tf_op jit(solution)/shard_map/ppermute | solution.py:284
  197.5 31.3 %collective-permute-start.22 = (bf16[192,512]{1,0:T(8,128)(2,1)S(1)}, bf16[192,512]{1,0:T(8,128)(2,1)S(1)}, u32[]{:S(2)}, u32[]{:S(2)}) collective-permute-start(bf16[192,512]{1,0:T(8,128)(2,1)S(1)} %get-tuple-element.65), channel_id=1, source_target_pairs={{0,6},{1,7},{2,4},{3,5},{4,2},{5,3},{6,0},{7,1},{8,14},{9,15},{10,... | collective-permute-start | bytes 589832 | tf_op jit(solution)/shard_map/ppermute | solution.py:284
  207.9 25.2 %collective-permute-start.23 = (bf16[192,512]{1,0:T(8,128)(2,1)S(1)}, bf16[192,512]{1,0:T(8,128)(2,1)S(1)}, u32[]{:S(2)}, u32[]{:S(2)}) collective-permute-start(bf16[192,512]{1,0:T(8,128)(2,1)S(1)} %get-tuple-element.66), channel_id=1, source_target_pairs={{0,7},{1,6},{2,5},{3,4},{4,3},{5,2},{6,1},{7,0},{8,15},{9,14},{10,... | collective-permute-start | bytes 589832 | tf_op jit(solution)/shard_map/ppermute | solution.py:284
  (8 other events, 7.6 us)

commit v3 on v2

--- a/solution.py
+++ b/solution.py
@@ -306,7 +306,7 @@
         exchanged(packed(me, (queries, grad_out), ways, 0, kv_local, True, [came[1]]))
     ]
     for c in range(1, kv_local):
-        earlier = [*qds[-1][-2:], halo]
+        earlier = [*qds[-1][-(ways - 1) :], halo]
         sent = packed(me, (queries, grad_out), ways, c, kv_local, False, earlier)[0]
         qds.append([exchanged_at_once(sent).reshape(group, 2 * q_lanes)])
 

time: 240 us -> 205 us (0.85); the launches traced: 235 us -> 204 us
  waiting for transfers between devices: 153 us -> 120 us
  starting transfers between devices: 45.5 us -> 42.6 us
  Pallas kernels: 26.5 us -> 29.1 us
    ppermute x21, waiting for transfers between devices: 121 us -> 95.9 us  [exchanged(): came[k] = lax.ppermute(blocks[k], 'head', [(i, i ^ k) for i in range(ways)])]
    ppermute x3, waiting for transfers between devices: 32.5 us -> 23.1 us  [passed_along(): return lax.ppermute(shard, axis, pairs)]
    all_to_all x2, starting transfers between devices: 14.7 us -> 10.7 us  [exchanged_at_once(): return lax.all_to_all(sent, 'head', split_axis=0, concat_axis=0, tiled=True)]
    ppermute x3, starting transfers between devices: 7.37 us -> 10.1 us  [passed_along(): return lax.ppermute(shard, axis, pairs)]
    pallas_call x2, Pallas kernels: 19.8 us -> 22.4 us  [attend(): pl.pallas_call(functools.partial(attend_kernel, per_group, ways, chunk, k...]
    unnamed x28 -> x36, local copies, waits for them, and re-layouts: 9.02 us -> 10.7 us
  transfers between devices with their start and end apart: 26 -> 26, of which waited for: 19 -> 18; matrix products, arithmetic and copies ran while one was open for 0% -> 0% of each run, Pallas kernels for 10% -> 12%
where the time goes in v3:
time: 205 us; the launch traced here: 204 us
  waiting for transfers between devices  120 us (59%)
  starting transfers between devices  42.6 us (21%)
  Pallas kernels  29.1 us (14%)
  local copies, waits for them, and re-layouts  10.9 us (5%)
    ppermute x21, waiting for transfers between devices, exchanged(): came[k] = lax.ppermute(blocks[k], 'head', [(i, i ^ k) for i in range(ways)])  95.9 us
    ppermute x3, waiting for transfers between devices, passed_along(): return lax.ppermute(shard, axis, pairs)  23.1 us
    pallas_call x2, Pallas kernels, attend(): pl.pallas_call(functools.partial(attend_kernel, per_group, ways, chunk, k...  22.4 us
    ppermute x21, starting transfers between devices, exchanged(): came[k] = lax.ppermute(blocks[k], 'head', [(i, i ^ k) for i in range(ways)])  21.8 us
    all_to_all x2, starting transfers between devices, exchanged_at_once(): return lax.all_to_all(sent, 'head', split_axis=0, concat_axis=0, tiled=True)  10.7 us
    unnamed x36, local copies, waits for them, and re-layouts  10.7 us
    ppermute x3, starting transfers between devices, passed_along(): return lax.ppermute(shard, axis, pairs)  10.1 us
    pallas_call x7, Pallas kernels, on_chip(): pl.pallas_call(body, out_shape=outs, in_specs=[SMEM] + [VMEM] * (len(earl...  6.71 us
  transfers between devices with their start and end apart: 26, of which 18 were waited for; matrix products, arithmetic and copies ran while one was open for 0% of the time, Pallas kernels for 12%

profile of v3, /device:TPU:13, one launch (start us, length us, event | category | flops | bytes accessed | tf_op | source)
XLA Modules:
  0.0 203.7 jit_solution(11219015135153167435)
XLA Ops:
  4.0 1.5 collective-permute-start.2
  5.6 2.3 %collective-permute-start.3 = (bf16[192,512]{1,0:T(8,128)(2,1)S(1)}, bf16[192,512]{1,0:T(8,128)(2,1)S(1)}, u32[]{:S(2)}, u32[]{:S(2)}) collective-permute-start(bf16[192,512]{1,0:T(8,128)(2,1)S(1)} %get-tuple-element.39), channel_id=1, source_target_pairs={{0,4},{1,5},{2,6},{3,7},{4,0},{5,1},{6,2},{7,3},{8,12},{9,13},{10,... | collective-permute-start | bytes 589832 | tf_op jit(solution)/shard_map/ppermute | solution.py:284
  9.6 6.5 %collective-permute-done.1.refs_2_ = bf16[192,512]{1,0:T(8,128)(2,1)S(1)} collective-permute-done((bf16[192,512]{1,0:T(8,128)(2,1)S(1)}, bf16[192,512]{1,0:T(8,128)(2,1)S(1)}, u32[]{:S(2)}, u32[]{:S(2)}) %collective-permute-start.1) | collective-permute-done | bytes 196640 | tf_op jit(solution)/shard_map/ppermute | solution.py:284
  16.1 1.5 collective-permute-start.6
  17.6 2.8 %collective-permute-done.2.refs_3_ = bf16[192,512]{1,0:T(8,128)(2,1)S(1)} collective-permute-done((bf16[192,512]{1,0:T(8,128)(2,1)S(1)}, bf16[192,512]{1,0:T(8,128)(2,1)S(1)}, u32[]{:S(2)}, u32[]{:S(2)}) %collective-permute-start.2) | collective-permute-done | bytes 196640 | tf_op jit(solution)/shard_map/ppermute | solution.py:284
  20.4 12.7 %collective-permute-done.4.refs_5_ = bf16[192,512]{1,0:T(8,128)(2,1)S(1)} collective-permute-done((bf16[192,512]{1,0:T(8,128)(2,1)S(1)}, bf16[192,512]{1,0:T(8,128)(2,1)S(1)}, u32[]{:S(2)}, u32[]{:S(2)}) %collective-permute-start.4) | collective-permute-done | bytes 196640 | tf_op jit(solution)/shard_map/ppermute | solution.py:284
  33.2 4.2 %collective-permute-done.5.refs_6_ = bf16[192,512]{1,0:T(8,128)(2,1)S(1)} collective-permute-done((bf16[192,512]{1,0:T(8,128)(2,1)S(1)}, bf16[192,512]{1,0:T(8,128)(2,1)S(1)}, u32[]{:S(2)}, u32[]{:S(2)}) %collective-permute-start.5) | collective-permute-done | bytes 196640 | tf_op jit(solution)/shard_map/ppermute | solution.py:284
  37.4 4.3 %collective-permute-done.6.refs_7_ = bf16[192,512]{1,0:T(8,128)(2,1)S(1)} collective-permute-done((bf16[192,512]{1,0:T(8,128)(2,1)S(1)}, bf16[192,512]{1,0:T(8,128)(2,1)S(1)}, u32[]{:S(2)}, u32[]{:S(2)}) %collective-permute-start.6) | collective-permute-done | bytes 196640 | tf_op jit(solution)/shard_map/ppermute | solution.py:284
  41.8 3.1 %collective-permute-start.7 = (bf16[1024,512]{1,0:T(8,128)(2,1)S(1)}, bf16[1024,512]{1,0:T(8,128)(2,1)S(1)}, u32[]{:S(2)}, u32[]{:S(2)}) collective-permute-start(bf16[1024,512]{1,0:T(8,128)(2,1)S(1)} %get-tuple-element.43), channel_id=1, source_target_pairs={{0,8},{8,16},{16,24},{1,9},{9,17},{17,25},{2,10},{10,18},{18,26},{... | collective-permute-start | bytes 3145736 | tf_op jit(solution)/shard_map/ppermute | solution.py:29
  47.1 1.6 collective-permute-start.10
  49.9 1.5 collective-permute-start.12
  51.5 8.0 %collective-permute-done.9.refs_2_.refs_1_ = bf16[192,512]{1,0:T(8,128)(2,1)S(1)} collective-permute-done((bf16[192,512]{1,0:T(8,128)(2,1)S(1)}, bf16[192,512]{1,0:T(8,128)(2,1)S(1)}, u32[]{:S(2)}, u32[]{:S(2)}) %collective-permute-start.9) | collective-permute-done | bytes 196640 | tf_op jit(solution)/shard_map/ppermute | solution.py:284
  60.0 3.8 %collective-permute-done.10.refs_3_.refs_2_ = bf16[192,512]{1,0:T(8,128)(2,1)S(1)} collective-permute-done((bf16[192,512]{1,0:T(8,128)(2,1)S(1)}, bf16[192,512]{1,0:T(8,128)(2,1)S(1)}, u32[]{:S(2)}, u32[]{:S(2)}) %collective-permute-start.10) | collective-permute-done | bytes 196640 | tf_op jit(solution)/shard_map/ppermute | solution.py:284
  64.8 10.0 %collective-permute-done.12.refs_5_.refs_4_ = bf16[192,512]{1,0:T(8,128)(2,1)S(1)} collective-permute-done((bf16[192,512]{1,0:T(8,128)(2,1)S(1)}, bf16[192,512]{1,0:T(8,128)(2,1)S(1)}, u32[]{:S(2)}, u32[]{:S(2)}) %collective-permute-start.12) | collective-permute-done | bytes 196640 | tf_op jit(solution)/shard_map/ppermute | solution.py:284
  74.8 6.2 %collective-permute-done.13.refs_6_.refs_5_ = bf16[192,512]{1,0:T(8,128)(2,1)S(1)} collective-permute-done((bf16[192,512]{1,0:T(8,128)(2,1)S(1)}, bf16[192,512]{1,0:T(8,128)(2,1)S(1)}, u32[]{:S(2)}, u32[]{:S(2)}) %collective-permute-start.13) | collective-permute-done | bytes 196640 | tf_op jit(solution)/shard_map/ppermute | solution.py:284
  81.0 4.2 %collective-permute-done.14.refs_7_.refs_6_ = bf16[192,512]{1,0:T(8,128)(2,1)S(1)} collective-permute-done((bf16[192,512]{1,0:T(8,128)(2,1)S(1)}, bf16[192,512]{1,0:T(8,128)(2,1)S(1)}, u32[]{:S(2)}, u32[]{:S(2)}) %collective-permute-start.14) | collective-permute-done | bytes 196640 | tf_op jit(solution)/shard_map/ppermute | solution.py:284
  86.6 3.7 %all-to-all-start.1 = ((bf16[8,192,512]{2,1,0:T(8,128)(2,1)}), bf16[8,192,512]{2,1,0:T(8,128)(2,1)S(1)}, u32[]{:S(2)}, u32[]{:S(2)}) async-start(bf16[8,192,512]{2,1,0:T(8,128)(2,1)} %packed.5), calls=%async_computation.1 | async-start | bytes 3145728 | tf_op jit(solution)/shard_map/all_to_all | solution.py:289
  95.9 11.3 %attend.2 = (bf16[1536,256]{1,0:T(8,128)(2,1)S(1)}, f32[1536,256]{1,0:T(8,128)S(1)}, bf16[1024,256]{1,0:T(8,128)(2,1)S(1)}) custom-call(s32[1]{0:T(128)} %bitcast.me_ref, s32[6]{0:T(128)S(1)} %and_select_fusion.first_tile, s32[1,1536]{1,0:T(1,128)S(1)} %maximum_subtract_fusion.1.low_ref, bf16[1024,512]{1,0:T(8,128)(2,1)S(1)} %collective-permute-done.7.halo_ref.refs_7_, ...), custom_call_target="tpu_custom_call" | custom-call | flops 5033164800 | bytes 4718592 | tf_op jit(solution)/shard_map/attend/pallas_call | solution.py:164
  107.2 3.5 %collective-permute-start.15 = (bf16[1024,256]{1,0:T(8,128)(2,1)S(1)}, bf16[1024,256]{1,0:T(8,128)(2,1)S(1)}, u32[]{:S(2)}, u32[]{:S(2)}) collective-permute-start(bf16[1024,256]{1,0:T(8,128)(2,1)S(1)} %get-tuple-element.55), channel_id=1, source_target_pairs={{8,0},{16,8},{24,16},{9,1},{17,9},{25,17},{10,2},{18,10},{26,18},{... | collective-permute-start | bytes 1572872 | tf_op jit(solution)/shard_map/ppermute | solution.py:29
  110.7 11.6 %collective-permute-done.15.refs_2_ = bf16[1024,256]{1,0:T(8,128)(2,1)S(1)} collective-permute-done((bf16[1024,256]{1,0:T(8,128)(2,1)S(1)}, bf16[1024,256]{1,0:T(8,128)(2,1)S(1)}, u32[]{:S(2)}, u32[]{:S(2)}) %collective-permute-start.15) | collective-permute-done | bytes 524320 | tf_op jit(solution)/shard_map/ppermute | solution.py:29
  124.6 7.0 %all-to-all-start = ((bf16[8,192,512]{2,1,0:T(8,128)(2,1)}), bf16[8,192,512]{2,1,0:T(8,128)(2,1)S(1)}, u32[]{:S(2)}, u32[]{:S(2)}) async-start(bf16[8,192,512]{2,1,0:T(8,128)(2,1)} %bitcast.2), calls=%async_computation | async-start | bytes 3145728 | tf_op jit(solution)/shard_map/all_to_all | solution.py:289
  134.3 11.1 %attend.3 = (bf16[1536,256]{1,0:T(8,128)(2,1)S(1)}, f32[1536,256]{1,0:T(8,128)S(1)}, bf16[1024,256]{1,0:T(8,128)(2,1)S(1)}) custom-call(s32[1]{0:T(128)} %bitcast.me_ref, s32[6]{0:T(128)S(1)} %and_select_fusion.first_tile, s32[1,1536]{1,0:T(1,128)S(1)} %maximum_subtract_fusion.1.low_ref, bf16[1024,512]{1,0:T(8,128)(2,1)S(1)} %copy-done.3, ...), custom_call_target="tpu_custom_call" | custom-call | flops 5033164800 | bytes 4718592 | tf_op jit(solution)/shard_map/attend/pallas_call | solution.py:164
  145.4 3.5 %collective-permute-start.16 = (bf16[1024,256]{1,0:T(8,128)(2,1)S(1)}, bf16[1024,256]{1,0:T(8,128)(2,1)S(1)}, u32[]{:S(2)}, u32[]{:S(2)}) collective-permute-start(bf16[1024,256]{1,0:T(8,128)(2,1)S(1)} %get-tuple-element.58), channel_id=1, source_target_pairs={{8,0},{16,8},{24,16},{9,1},{17,9},{25,17},{10,2},{18,10},{26,18},{... | collective-permute-start | bytes 1572872 | tf_op jit(solution)/shard_map/ppermute | solution.py:29
  148.8 11.5 %collective-permute-done.16.refs_2_ = bf16[1024,256]{1,0:T(8,128)(2,1)S(1)} collective-permute-done((bf16[1024,256]{1,0:T(8,128)(2,1)S(1)}, bf16[1024,256]{1,0:T(8,128)(2,1)S(1)}, u32[]{:S(2)}, u32[]{:S(2)}) %collective-permute-start.16) | collective-permute-done | bytes 524320 | tf_op jit(solution)/shard_map/ppermute | solution.py:29
  162.7 1.6 collective-permute-start.19
  164.3 2.1 %collective-permute-start.20 = (bf16[192,512]{1,0:T(8,128)(2,1)}, bf16[192,512]{1,0:T(8,128)(2,1)S(1)}, u32[]{:S(2)}, u32[]{:S(2)}) collective-permute-start(bf16[192,512]{1,0:T(8,128)(2,1)} %get-tuple-element.63), channel_id=1, source_target_pairs={{0,4},{1,5},{2,6},{3,7},{4,0},{5,1},{6,2},{7,3},{8,12},{9,13},{10,... | collective-permute-start | bytes 589832 | tf_op jit(solution)/shard_map/ppermute | solution.py:284
  168.2 9.7 %collective-permute-done.18.refs_3_ = bf16[192,512]{1,0:T(8,128)(2,1)S(1)} collective-permute-done((bf16[192,512]{1,0:T(8,128)(2,1)S(1)}, bf16[192,512]{1,0:T(8,128)(2,1)S(1)}, u32[]{:S(2)}, u32[]{:S(2)}) %collective-permute-start.18) | collective-permute-done | bytes 196640 | tf_op jit(solution)/shard_map/ppermute | solution.py:284
  177.9 4.2 %collective-permute-done.19.refs_4_ = bf16[192,512]{1,0:T(8,128)(2,1)S(1)} collective-permute-done((bf16[192,512]{1,0:T(8,128)(2,1)}, bf16[192,512]{1,0:T(8,128)(2,1)S(1)}, u32[]{:S(2)}, u32[]{:S(2)}) %collective-permute-start.19) | collective-permute-done | bytes 196640 | tf_op jit(solution)/shard_map/ppermute | solution.py:284
  182.1 9.8 %collective-permute-done.21.refs_6_ = bf16[192,512]{1,0:T(8,128)(2,1)S(1)} collective-permute-done((bf16[192,512]{1,0:T(8,128)(2,1)}, bf16[192,512]{1,0:T(8,128)(2,1)S(1)}, u32[]{:S(2)}, u32[]{:S(2)}) %collective-permute-start.21) | collective-permute-done | bytes 196640 | tf_op jit(solution)/shard_map/ppermute | solution.py:284
  191.9 5.2 %collective-permute-done.22.refs_7_ = bf16[192,512]{1,0:T(8,128)(2,1)S(1)} collective-permute-done((bf16[192,512]{1,0:T(8,128)(2,1)S(1)}, bf16[192,512]{1,0:T(8,128)(2,1)S(1)}, u32[]{:S(2)}, u32[]{:S(2)}) %collective-permute-start.22) | collective-permute-done | bytes 196640 | tf_op jit(solution)/shard_map/ppermute | solution.py:284
  197.1 4.4 %collective-permute-done.23.refs_8_ = bf16[192,512]{1,0:T(8,128)(2,1)S(1)} collective-permute-done((bf16[192,512]{1,0:T(8,128)(2,1)S(1)}, bf16[192,512]{1,0:T(8,128)(2,1)S(1)}, u32[]{:S(2)}, u32[]{:S(2)}) %collective-permute-start.23) | collective-permute-done | bytes 196640 | tf_op jit(solution)/shard_map/ppermute | solution.py:284
  201.5 2.3 %unpacked.1 = (bf16[192,4096]{1,0:T(8,128)(2,1)}, bf16[192,2048]{1,0:T(8,128)(2,1)}, bf16[192,2048]{1,0:T(8,128)(2,1)}) custom-call(s32[1]{0:T(128)} %bitcast.me_ref, bf16[8,192,512]{2,1,0:T(8,128)(2,1)S(1)} %all-to-all-done.refs_0_, bf16[192,512]{1,0:T(8,128)(2,1)S(1)} %get-tuple-element.59.refs_1_, bf16[192,512]{1,0:T(8,128)(2,1)S(1)} %collective-permute-done.17.refs_2_, ...), custom_call_target="tpu_custom_call" | custom-call | bytes 6291456 | tf_op jit(solution)/shard_map/unpacked/pallas_call | solution.py:185
  (74 shorter events, 26.2 us)
Async XLA Ops:
  2.9 42.0 %copy-start = (bf16[192,4096]{1,0:T(8,128)(2,1)S(1)}, bf16[192,4096]{1,0:T(8,128)(2,1)}, u32[]{:S(2)}) copy-start(bf16[192,4096]{1,0:T(8,128)(2,1)} %refs_8_.1) | copy-start | bytes 4718596
  2.9 42.1 %copy-start.1 = (bf16[192,4096]{1,0:T(8,128)(2,1)S(1)}, bf16[192,4096]{1,0:T(8,128)(2,1)}, u32[]{:S(2)}) copy-start(bf16[192,4096]{1,0:T(8,128)(2,1)} %refs_9_.1) | copy-start | bytes 4718596
  3.1 5.2 %collective-permute-start = (bf16[192,512]{1,0:T(8,128)(2,1)S(1)}, bf16[192,512]{1,0:T(8,128)(2,1)S(1)}, u32[]{:S(2)}, u32[]{:S(2)}) collective-permute-start(bf16[192,512]{1,0:T(8,128)(2,1)S(1)} %get-tuple-element.36), channel_id=1, source_target_pairs={{0,1},{1,0},{2,3},{3,2},{4,5},{5,4},{6,7},{7,6},{8,9},{9,8},{10,11... | collective-permute-start | bytes 589832 | tf_op jit(solution)/shard_map/ppermute | solution.py:284
  3.9 12.2 %collective-permute-start.1 = (bf16[192,512]{1,0:T(8,128)(2,1)S(1)}, bf16[192,512]{1,0:T(8,128)(2,1)S(1)}, u32[]{:S(2)}, u32[]{:S(2)}) collective-permute-start(bf16[192,512]{1,0:T(8,128)(2,1)S(1)} %get-tuple-element.37), channel_id=1, source_target_pairs={{0,2},{1,3},{2,0},{3,1},{4,6},{5,7},{6,4},{7,5},{8,10},{9,11},{10,... | collective-permute-start | bytes 589832 | tf_op jit(solution)/shard_map/ppermute | solution.py:284
  4.0 16.4 %collective-permute-start.2 = (bf16[192,512]{1,0:T(8,128)(2,1)S(1)}, bf16[192,512]{1,0:T(8,128)(2,1)S(1)}, u32[]{:S(2)}, u32[]{:S(2)}) collective-permute-start(bf16[192,512]{1,0:T(8,128)(2,1)S(1)} %get-tuple-element.38), channel_id=1, source_target_pairs={{0,3},{1,2},{2,1},{3,0},{4,7},{5,6},{6,5},{7,4},{8,11},{9,10},{10,... | collective-permute-start | bytes 589832 | tf_op jit(solution)/shard_map/ppermute | solution.py:284
  5.6 14.8 %collective-permute-start.3 = (bf16[192,512]{1,0:T(8,128)(2,1)S(1)}, bf16[192,512]{1,0:T(8,128)(2,1)S(1)}, u32[]{:S(2)}, u32[]{:S(2)}) collective-permute-start(bf16[192,512]{1,0:T(8,128)(2,1)S(1)} %get-tuple-element.39), channel_id=1, source_target_pairs={{0,4},{1,5},{2,6},{3,7},{4,0},{5,1},{6,2},{7,3},{8,12},{9,13},{10,... | collective-permute-start | bytes 589832 | tf_op jit(solution)/shard_map/ppermute | solution.py:284
  7.9 25.3 %collective-permute-start.4 = (bf16[192,512]{1,0:T(8,128)(2,1)S(1)}, bf16[192,512]{1,0:T(8,128)(2,1)S(1)}, u32[]{:S(2)}, u32[]{:S(2)}) collective-permute-start(bf16[192,512]{1,0:T(8,128)(2,1)S(1)} %get-tuple-element.40), channel_id=1, source_target_pairs={{0,5},{1,4},{2,7},{3,6},{4,1},{5,0},{6,3},{7,2},{8,13},{9,12},{10,... | collective-permute-start | bytes 589832 | tf_op jit(solution)/shard_map/ppermute | solution.py:284
  8.3 29.1 %collective-permute-start.5 = (bf16[192,512]{1,0:T(8,128)(2,1)S(1)}, bf16[192,512]{1,0:T(8,128)(2,1)S(1)}, u32[]{:S(2)}, u32[]{:S(2)}) collective-permute-start(bf16[192,512]{1,0:T(8,128)(2,1)S(1)} %get-tuple-element.41), channel_id=1, source_target_pairs={{0,6},{1,7},{2,4},{3,5},{4,2},{5,3},{6,0},{7,1},{8,14},{9,15},{10,... | collective-permute-start | bytes 589832 | tf_op jit(solution)/shard_map/ppermute | solution.py:284
  16.1 25.6 %collective-permute-start.6 = (bf16[192,512]{1,0:T(8,128)(2,1)S(1)}, bf16[192,512]{1,0:T(8,128)(2,1)S(1)}, u32[]{:S(2)}, u32[]{:S(2)}) collective-permute-start(bf16[192,512]{1,0:T(8,128)(2,1)S(1)} %get-tuple-element.42), channel_id=1, source_target_pairs={{0,7},{1,6},{2,5},{3,4},{4,3},{5,2},{6,1},{7,0},{8,15},{9,14},{10,... | collective-permute-start | bytes 589832 | tf_op jit(solution)/shard_map/ppermute | solution.py:284
  41.8 43.4 %collective-permute-start.7 = (bf16[1024,512]{1,0:T(8,128)(2,1)S(1)}, bf16[1024,512]{1,0:T(8,128)(2,1)S(1)}, u32[]{:S(2)}, u32[]{:S(2)}) collective-permute-start(bf16[1024,512]{1,0:T(8,128)(2,1)S(1)} %get-tuple-element.43), channel_id=1, source_target_pairs={{0,8},{8,16},{16,24},{1,9},{9,17},{17,25},{2,10},{10,18},{18,26},{... | collective-permute-start | bytes 3145736 | tf_op jit(solution)/shard_map/ppermute | solution.py:29
  45.9 4.1 %collective-permute-start.8 = (bf16[192,512]{1,0:T(8,128)(2,1)S(1)}, bf16[192,512]{1,0:T(8,128)(2,1)S(1)}, u32[]{:S(2)}, u32[]{:S(2)}) collective-permute-start(bf16[192,512]{1,0:T(8,128)(2,1)S(1)} %get-tuple-element.46), channel_id=1, source_target_pairs={{0,1},{1,0},{2,3},{3,2},{4,5},{5,4},{6,7},{7,6},{8,9},{9,8},{10,11... | collective-permute-start | bytes 589832 | tf_op jit(solution)/shard_map/ppermute | solution.py:284
  47.1 12.4 %collective-permute-start.9 = (bf16[192,512]{1,0:T(8,128)(2,1)S(1)}, bf16[192,512]{1,0:T(8,128)(2,1)S(1)}, u32[]{:S(2)}, u32[]{:S(2)}) collective-permute-start(bf16[192,512]{1,0:T(8,128)(2,1)S(1)} %get-tuple-element.47), channel_id=1, source_target_pairs={{0,2},{1,3},{2,0},{3,1},{4,6},{5,7},{6,4},{7,5},{8,10},{9,11},{10,... | collective-permute-start | bytes 589832 | tf_op jit(solution)/shard_map/ppermute | solution.py:284
  47.1 16.7 %collective-permute-start.10 = (bf16[192,512]{1,0:T(8,128)(2,1)S(1)}, bf16[192,512]{1,0:T(8,128)(2,1)S(1)}, u32[]{:S(2)}, u32[]{:S(2)}) collective-permute-start(bf16[192,512]{1,0:T(8,128)(2,1)S(1)} %get-tuple-element.48), channel_id=1, source_target_pairs={{0,3},{1,2},{2,1},{3,0},{4,7},{5,6},{6,5},{7,4},{8,11},{9,10},{10,... | collective-permute-start | bytes 589832 | tf_op jit(solution)/shard_map/ppermute | solution.py:284
  48.7 16.0 %collective-permute-start.11 = (bf16[192,512]{1,0:T(8,128)(2,1)S(1)}, bf16[192,512]{1,0:T(8,128)(2,1)S(1)}, u32[]{:S(2)}, u32[]{:S(2)}) collective-permute-start(bf16[192,512]{1,0:T(8,128)(2,1)S(1)} %get-tuple-element.49), channel_id=1, source_target_pairs={{0,4},{1,5},{2,6},{3,7},{4,0},{5,1},{6,2},{7,3},{8,12},{9,13},{10,... | collective-permute-start | bytes 589832 | tf_op jit(solution)/shard_map/ppermute | solution.py:284
  49.9 24.8 %collective-permute-start.12 = (bf16[192,512]{1,0:T(8,128)(2,1)S(1)}, bf16[192,512]{1,0:T(8,128)(2,1)S(1)}, u32[]{:S(2)}, u32[]{:S(2)}) collective-permute-start(bf16[192,512]{1,0:T(8,128)(2,1)S(1)} %get-tuple-element.50), channel_id=1, source_target_pairs={{0,5},{1,4},{2,7},{3,6},{4,1},{5,0},{6,3},{7,2},{8,13},{9,12},{10,... | collective-permute-start | bytes 589832 | tf_op jit(solution)/shard_map/ppermute | solution.py:284
  59.4 21.5 %collective-permute-start.13 = (bf16[192,512]{1,0:T(8,128)(2,1)S(1)}, bf16[192,512]{1,0:T(8,128)(2,1)S(1)}, u32[]{:S(2)}, u32[]{:S(2)}) collective-permute-start(bf16[192,512]{1,0:T(8,128)(2,1)S(1)} %get-tuple-element.51), channel_id=1, source_target_pairs={{0,6},{1,7},{2,4},{3,5},{4,2},{5,3},{6,0},{7,1},{8,14},{9,15},{10,... | collective-permute-start | bytes 589832 | tf_op jit(solution)/shard_map/ppermute | solution.py:284
  63.8 21.4 %collective-permute-start.14 = (bf16[192,512]{1,0:T(8,128)(2,1)S(1)}, bf16[192,512]{1,0:T(8,128)(2,1)S(1)}, u32[]{:S(2)}, u32[]{:S(2)}) collective-permute-start(bf16[192,512]{1,0:T(8,128)(2,1)S(1)} %get-tuple-element.52), channel_id=1, source_target_pairs={{0,7},{1,6},{2,5},{3,4},{4,3},{5,2},{6,1},{7,0},{8,15},{9,14},{10,... | collective-permute-start | bytes 589832 | tf_op jit(solution)/shard_map/ppermute | solution.py:284
  74.8 11.8 %copy-start.6 = (bf16[192,512]{1,0:T(8,128)(2,1)}, bf16[192,512]{1,0:T(8,128)(2,1)S(1)}, u32[]{:S(2)}) copy-start(bf16[192,512]{1,0:T(8,128)(2,1)S(1)} %collective-permute-done.12.refs_5_.refs_4_) | copy-start | bytes 589828
  81.0 5.6 %copy-start.8 = (bf16[192,512]{1,0:T(8,128)(2,1)}, bf16[192,512]{1,0:T(8,128)(2,1)S(1)}, u32[]{:S(2)}) copy-start(bf16[192,512]{1,0:T(8,128)(2,1)S(1)} %collective-permute-done.13.refs_6_.refs_5_) | copy-start | bytes 589828
  85.2 5.6 %copy-start.2 = (bf16[1024,512]{1,0:T(8,128)(2,1)}, bf16[1024,512]{1,0:T(8,128)(2,1)S(1)}, u32[]{:S(2)}) copy-start(bf16[1024,512]{1,0:T(8,128)(2,1)S(1)} %collective-permute-done.7.halo_ref.refs_7_) | copy-start | bytes 3145732
  86.6 3.7 %copy-start.17 = (s32[16]{0:T(128)S(1)}, s32[16]{0:T(128)}, u32[]{:S(2)}) copy-start(s32[16]{0:T(128)} %param.9) | copy-start | bytes 196
  86.6 38.0 %all-to-all-start.1 = ((bf16[8,192,512]{2,1,0:T(8,128)(2,1)}), bf16[8,192,512]{2,1,0:T(8,128)(2,1)S(1)}, u32[]{:S(2)}, u32[]{:S(2)}) async-start(bf16[8,192,512]{2,1,0:T(8,128)(2,1)} %packed.5), calls=%async_computation.1 | async-start | bytes 3145728 | tf_op jit(solution)/shard_map/all_to_all | solution.py:289
  107.2 15.0 %collective-permute-start.15 = (bf16[1024,256]{1,0:T(8,128)(2,1)S(1)}, bf16[1024,256]{1,0:T(8,128)(2,1)S(1)}, u32[]{:S(2)}, u32[]{:S(2)}) collective-permute-start(bf16[1024,256]{1,0:T(8,128)(2,1)S(1)} %get-tuple-element.55), channel_id=1, source_target_pairs={{8,0},{16,8},{24,16},{9,1},{17,9},{25,17},{10,2},{18,10},{26,18},{... | collective-permute-start | bytes 1572872 | tf_op jit(solution)/shard_map/ppermute | solution.py:29
  124.6 53.3 %all-to-all-start = ((bf16[8,192,512]{2,1,0:T(8,128)(2,1)}), bf16[8,192,512]{2,1,0:T(8,128)(2,1)S(1)}, u32[]{:S(2)}, u32[]{:S(2)}) async-start(bf16[8,192,512]{2,1,0:T(8,128)(2,1)} %bitcast.2), calls=%async_computation | async-start | bytes 3145728 | tf_op jit(solution)/shard_map/all_to_all | solution.py:289
  145.4 15.0 %collective-permute-start.16 = (bf16[1024,256]{1,0:T(8,128)(2,1)S(1)}, bf16[1024,256]{1,0:T(8,128)(2,1)S(1)}, u32[]{:S(2)}, u32[]{:S(2)}) collective-permute-start(bf16[1024,256]{1,0:T(8,128)(2,1)S(1)} %get-tuple-element.58), channel_id=1, source_target_pairs={{8,0},{16,8},{24,16},{9,1},{17,9},{25,17},{10,2},{18,10},{26,18},{... | collective-permute-start | bytes 1572872 | tf_op jit(solution)/shard_map/ppermute | solution.py:29
  161.5 5.6 %collective-permute-start.17 = (bf16[192,512]{1,0:T(8,128)(2,1)S(1)}, bf16[192,512]{1,0:T(8,128)(2,1)S(1)}, u32[]{:S(2)}, u32[]{:S(2)}) collective-permute-start(bf16[192,512]{1,0:T(8,128)(2,1)S(1)} %get-tuple-element.60), channel_id=1, source_target_pairs={{0,1},{1,0},{2,3},{3,2},{4,5},{5,4},{6,7},{7,6},{8,9},{9,8},{10,11... | collective-permute-start | bytes 589832 | tf_op jit(solution)/shard_map/ppermute | solution.py:284
  162.7 15.3 %collective-permute-start.18 = (bf16[192,512]{1,0:T(8,128)(2,1)S(1)}, bf16[192,512]{1,0:T(8,128)(2,1)S(1)}, u32[]{:S(2)}, u32[]{:S(2)}) collective-permute-start(bf16[192,512]{1,0:T(8,128)(2,1)S(1)} %get-tuple-element.61), channel_id=1, source_target_pairs={{0,2},{1,3},{2,0},{3,1},{4,6},{5,7},{6,4},{7,5},{8,10},{9,11},{10,... | collective-permute-start | bytes 589832 | tf_op jit(solution)/shard_map/ppermute | solution.py:284
  162.7 19.4 %collective-permute-start.19 = (bf16[192,512]{1,0:T(8,128)(2,1)}, bf16[192,512]{1,0:T(8,128)(2,1)S(1)}, u32[]{:S(2)}, u32[]{:S(2)}) collective-permute-start(bf16[192,512]{1,0:T(8,128)(2,1)} %get-tuple-element.62), channel_id=1, source_target_pairs={{0,3},{1,2},{2,1},{3,0},{4,7},{5,6},{6,5},{7,4},{8,11},{9,10},{10,... | collective-permute-start | bytes 589832 | tf_op jit(solution)/shard_map/ppermute | solution.py:284
  164.3 17.9 %collective-permute-start.20 = (bf16[192,512]{1,0:T(8,128)(2,1)}, bf16[192,512]{1,0:T(8,128)(2,1)S(1)}, u32[]{:S(2)}, u32[]{:S(2)}) collective-permute-start(bf16[192,512]{1,0:T(8,128)(2,1)} %get-tuple-element.63), channel_id=1, source_target_pairs={{0,4},{1,5},{2,6},{3,7},{4,0},{5,1},{6,2},{7,3},{8,12},{9,13},{10,... | collective-permute-start | bytes 589832 | tf_op jit(solution)/shard_map/ppermute | solution.py:284
  166.4 25.5 %collective-permute-start.21 = (bf16[192,512]{1,0:T(8,128)(2,1)}, bf16[192,512]{1,0:T(8,128)(2,1)S(1)}, u32[]{:S(2)}, u32[]{:S(2)}) collective-permute-start(bf16[192,512]{1,0:T(8,128)(2,1)} %get-tuple-element.64), channel_id=1, source_target_pairs={{0,5},{1,4},{2,7},{3,6},{4,1},{5,0},{6,3},{7,2},{8,13},{9,12},{10,... | collective-permute-start | bytes 589832 | tf_op jit(solution)/shard_map/ppermute | solution.py:284
  167.1 30.0 %collective-permute-start.22 = (bf16[192,512]{1,0:T(8,128)(2,1)S(1)}, bf16[192,512]{1,0:T(8,128)(2,1)S(1)}, u32[]{:S(2)}, u32[]{:S(2)}) collective-permute-start(bf16[192,512]{1,0:T(8,128)(2,1)S(1)} %get-tuple-element.65), channel_id=1, source_target_pairs={{0,6},{1,7},{2,4},{3,5},{4,2},{5,3},{6,0},{7,1},{8,14},{9,15},{10,... | collective-permute-start | bytes 589832 | tf_op jit(solution)/shard_map/ppermute | solution.py:284
  177.9 23.5 %collective-permute-start.23 = (bf16[192,512]{1,0:T(8,128)(2,1)S(1)}, bf16[192,512]{1,0:T(8,128)(2,1)S(1)}, u32[]{:S(2)}, u32[]{:S(2)}) collective-permute-start(bf16[192,512]{1,0:T(8,128)(2,1)S(1)} %get-tuple-element.66), channel_id=1, source_target_pairs={{0,7},{1,6},{2,5},{3,4},{4,3},{5,2},{6,1},{7,0},{8,15},{9,14},{10,... | collective-permute-start | bytes 589832 | tf_op jit(solution)/shard_map/ppermute | solution.py:284
  (12 other events, 15.5 us)

commit v4 on v3

--- a/solution.py
+++ b/solution.py
@@ -51,10 +51,7 @@
 ):
     blocks, refs = refs[:ways], refs[ways:]
     dq_ref, own_ref, rim_ref, qd_ref, k_ext, v_ext, k_t, dk_ext, dv_ext, s_buf, dp_buf = refs
-    if ways == 1:
-        qd_ref = blocks[0]
-    else:
-        gather_rows(me_ref, blocks, qd_ref)
+    gather_rows(me_ref, blocks, qd_ref)
     group = qd_ref.shape[0]
     reach = WINDOW // TK
     for ref, at in ((k_ext, chunk * HD), (v_ext, (kv_local + chunk) * HD)):
@@ -151,7 +148,7 @@
         jax.ShapeDtypeStruct((WINDOW, 2 * HD), jnp.bfloat16),
     ]
     scratch = [
-        jax.ShapeDtypeStruct((group, qd_lanes) if ways > 1 else (16, 128), jnp.bfloat16),
+        jax.ShapeDtypeStruct((group, qd_lanes), jnp.bfloat16),
         jax.ShapeDtypeStruct((ext, HD), jnp.bfloat16),
         jax.ShapeDtypeStruct((ext, HD), jnp.bfloat16),
         jax.ShapeDtypeStruct((ext // TK, HD, TK), jnp.bfloat16),
@@ -194,47 +191,36 @@
     )(me, *earlier, *arrays)
 
 
-def packed(me, arrays, ways, chunk, chunks, by_partner, earlier=()):
+def packed(me, arrays, ways, places, chunk=0, chunks=1, earlier=()):
     tokens = arrays[0].shape[0]
     lanes = [a.shape[1] // (ways * chunks) for a in arrays]
-    total = sum(lanes)
 
     def kernel(me_ref, *refs):
         ins, outs = refs[: len(arrays)], refs[len(arrays) :]
-        for k in range(ways):
-            out = outs[k] if by_partner else outs[0].at[k]
+        for k, out in zip(places, outs):
             first = 0
             for ref, width in zip(ins, lanes):
-                if by_partner:
-                    at = pl.multiple_of(((me_ref[0] ^ k) * chunks + chunk) * width, width)
-                else:
-                    at = (k * chunks + chunk) * width
+                at = pl.multiple_of(((me_ref[0] ^ k) * chunks + chunk) * width, width)
                 out[:, first : first + width] = ref[:, pl.ds(at, width)]
                 first += width
 
-    shapes = [(tokens, total)] * ways if by_partner else [(ways, tokens, total)]
+    shapes = [(tokens, sum(lanes))] * len(places)
     return on_chip(kernel, me, arrays, shapes, "packed", earlier=earlier)
 
 
-def unpacked(me, grads, ways, q_lanes):
-    chunks = len(grads)
-    tokens = grads[0][0].shape[-2]
+def unpacked(me, grads, q_lanes):
+    chunks, ways = len(grads), len(grads[0])
+    tokens = grads[0][0].shape[0]
     lanes = (q_lanes, HD, HD)
-    counts = [len(blocks) for blocks in grads]
 
     def kernel(me_ref, *refs):
-        outs = refs[sum(counts) :]
+        ins, outs = refs[: chunks * ways], refs[chunks * ways :]
         for c in range(chunks):
-            ins = refs[sum(counts[:c]) : sum(counts[: c + 1])]
             for k in range(ways):
-                block = ins[k] if len(ins) > 1 else ins[0].at[k]
                 first = 0
                 for out, width in zip(outs, lanes):
-                    if len(ins) > 1:
-                        at = pl.multiple_of(((me_ref[0] ^ k) * chunks + c) * width, width)
-                    else:
-                        at = (k * chunks + c) * width
-                    out[:, pl.ds(at, width)] = block[:, first : first + width]
+                    at = pl.multiple_of(((me_ref[0] ^ k) * chunks + c) * width, width)
+                    out[:, pl.ds(at, width)] = ins[c * ways + k][:, first : first + width]
                     first += width
 
     shapes = [(tokens, ways * chunks * width) for width in lanes]
@@ -254,39 +240,30 @@
     return on_chip(kernel, me, blocks, [(group, lanes), (WINDOW, lanes)], "gathered")
 
 
-def settled(me, dq, own, returned, ways, by_partner):
+def settled(me, dq, own, returned, ways, places, earlier=()):
     group, q_lanes = dq.shape
     tokens = group // ways
-    total_lanes = q_lanes + 2 * HD
 
     def kernel(me_ref, dq_ref, own_ref, back_ref, *refs):
+        outs, total = refs[:-1], refs[-1]
         cut = group - WINDOW
-        total = refs[-1] if by_partner else refs[0].at[:, q_lanes:]
         total[:cut, :] = own_ref[:cut, :].astype(jnp.bfloat16)
         total[cut:, :] = (own_ref[cut:, :] + back_ref[...].astype(jnp.float32)).astype(jnp.bfloat16)
-        if not by_partner:
-            refs[0][:, :q_lanes] = dq_ref[...]
-            return
-        for k, out in enumerate(refs[:ways]):
+        for k, out in zip(places, outs):
             rows = partner_rows(me_ref, k, tokens)
             out[:, :q_lanes] = dq_ref[rows, :]
             out[:, q_lanes:] = total[rows, :]
 
-    shapes = [(tokens, total_lanes)] * ways if by_partner else [(group, total_lanes)]
-    scratch = [pltpu.VMEM((group, 2 * HD), jnp.bfloat16)] if by_partner else []
-    return on_chip(kernel, me, (dq, own, returned), shapes, "settled", scratch)
+    shapes = [(tokens, q_lanes + 2 * HD)] * len(places)
+    scratch = [pltpu.VMEM((group, 2 * HD), jnp.bfloat16)]
+    return on_chip(kernel, me, (dq, own, returned), shapes, "settled", scratch, earlier)
 
 
 def exchanged(blocks):
     ways = len(blocks)
-    came = {0: blocks[0]}
-    for k in reversed(range(1, ways)):
-        came[k] = lax.ppermute(blocks[k], "head", [(i, i ^ k) for i in range(ways)])
-    return [came[k] for k in range(ways)]
-
-
-def exchanged_at_once(sent):
-    return lax.all_to_all(sent, "head", split_axis=0, concat_axis=0, tiled=True)
+    return [blocks[0]] + [
+        lax.ppermute(blocks[k], "head", [(i, i ^ k) for i in range(ways)]) for k in range(1, ways)
+    ]
 
 
 def local(queries, keys, values, grad_out, doc_lengths):
@@ -298,17 +275,9 @@
     q_lanes = per_group * HD
     group_first = lax.axis_index("seq") * group
     me = lax.axis_index("head").astype(jnp.int32).reshape(1)
-
-    came = exchanged(packed(me, (keys, values), ways, 0, 1, True))
-    kv, tail = gathered(me, came)
-    halo = passed_along(tail, "seq", 1)
-    qds = [
-        exchanged(packed(me, (queries, grad_out), ways, 0, kv_local, True, [came[1]]))
-    ]
-    for c in range(1, kv_local):
-        earlier = [*qds[-1][-(ways - 1) :], halo]
-        sent = packed(me, (queries, grad_out), ways, c, kv_local, False, earlier)[0]
-        qds.append([exchanged_at_once(sent).reshape(group, 2 * q_lanes)])
+    places = list(range(ways))
+    early = places[: ways - ways // 4]
+    late = places[ways - ways // 4 :]
 
     position = group_first + jnp.arange(group, dtype=jnp.int32)
     ends = jnp.cumsum(doc_lengths)
@@ -319,18 +288,31 @@
     low = low.astype(jnp.int32)
     first_tile = low[::TQ] // TK
 
+    came = exchanged(packed(me, (keys, values), ways, places))
+    kv, tail = gathered(me, came)
+    halo = passed_along(tail, "seq", 1)
+
+    parts, returned = [], []
+    for c in range(kv_local):
+        sent = []
+        for k in places:
+            earlier = [parts[-1][0]] if parts and k in late else [came[k]] if k else []
+            sent += packed(me, (queries, grad_out), ways, [k], c, kv_local, earlier)
+        came = exchanged(sent)
+        parts.append(attend(me, came, halo, kv, c, kv_local, low.reshape(1, group), first_tile))
+        returned.append(passed_along(parts[-1][2], "seq", -1))
+
     grads = []
-    for c in range(kv_local):
-        dq, own, rim = attend(me, qds[c], halo, kv, c, kv_local, low.reshape(1, group), first_tile)
-        returned = passed_along(rim, "seq", -1)
-        last = c == kv_local - 1
-        settled_now = settled(me, dq, own, returned, ways, last)
-        if last:
-            grads.append(exchanged(settled_now))
+    for c, (dq, own, _) in enumerate(parts):
+        if c < kv_local - 1:
+            sent = [
+                *settled(me, dq, own, returned[c], ways, early),
+                *settled(me, dq, own, returned[c], ways, late, [parts[c + 1][0]]),
+            ]
         else:
-            sent = settled_now[0].reshape(ways, tokens, q_lanes + 2 * HD)
-            grads.append([exchanged_at_once(sent)])
-    return unpacked(me, grads, ways, q_lanes)
+            sent = settled(me, dq, own, returned[c], ways, places)
+        grads.append(exchanged(sent))
+    return unpacked(me, grads, q_lanes)
 
 
 def solution(mesh):

time: 205 us -> 213 us (1.039); the launches traced: 204 us -> 214 us
  starting transfers between devices: 42.6 us -> 59.8 us
  local copies, waits for them, and re-layouts: 10.9 us -> 6.59 us
  Pallas kernels: 29.1 us -> 26.2 us
    ppermute x21 -> x35, starting transfers between devices: 21.8 us -> 46.1 us  [exchanged(): lax.ppermute(blocks[k], 'head', [(i, i ^ k) for i in range(ways)])]
    ppermute x21 -> x35, waiting for transfers between devices: 95.9 us -> 109 us  [exchanged(): lax.ppermute(blocks[k], 'head', [(i, i ^ k) for i in range(ways)])]
    ppermute x3, waiting for transfers between devices: 23.1 us -> 10.8 us  [passed_along(): return lax.ppermute(shard, axis, pairs)]
    all_to_all x2 -> x0, starting transfers between devices: 10.7 us -> none  [exchanged_at_once(): return lax.all_to_all(sent, 'head', split_axis=0, concat_axis=0, tiled=True)]
    unnamed x36, local copies, waits for them, and re-layouts: 10.7 us -> 5.9 us
    ppermute x3, starting transfers between devices: 10.1 us -> 13.7 us  [passed_along(): return lax.ppermute(shard, axis, pairs)]
    pallas_call x7 -> x22, Pallas kernels: 6.71 us -> 4.97 us  [on_chip(): pl.pallas_call(body, out_shape=outs, in_specs=[SMEM] + [VMEM] * (len(earl...]
  transfers between devices with their start and end apart: 26 -> 38, of which waited for: 18 -> 20; matrix products, arithmetic and copies ran while one was open for 0% -> 1% of each run, Pallas kernels for 12% -> 11%
where the time goes in v4:
time: 213 us; the launch traced here: 214 us
  waiting for transfers between devices  120 us (56%)
  starting transfers between devices  59.8 us (28%)
  Pallas kernels  26.2 us (12%)
  local copies, waits for them, and re-layouts  6.59 us (3%)
    ppermute x35, waiting for transfers between devices, exchanged(): lax.ppermute(blocks[k], 'head', [(i, i ^ k) for i in range(ways)])  109 us
    ppermute x35, starting transfers between devices, exchanged(): lax.ppermute(blocks[k], 'head', [(i, i ^ k) for i in range(ways)])  46.1 us
    pallas_call x2, Pallas kernels, attend(): pl.pallas_call(functools.partial(attend_kernel, per_group, ways, chunk, k...  21.3 us
    ppermute x3, starting transfers between devices, passed_along(): return lax.ppermute(shard, axis, pairs)  13.7 us
    ppermute x3, waiting for transfers between devices, passed_along(): return lax.ppermute(shard, axis, pairs)  10.8 us
    unnamed x36, local copies, waits for them, and re-layouts  5.9 us
    pallas_call x22, Pallas kernels, on_chip(): pl.pallas_call(body, out_shape=outs, in_specs=[SMEM] + [VMEM] * (len(earl...  4.97 us
  transfers between devices with their start and end apart: 38, of which 20 were waited for; matrix products, arithmetic and copies ran while one was open for 1% of the time, Pallas kernels for 11%

profile of v4, /device:TPU:13, one launch (start us, length us, event | category | flops | bytes accessed | tf_op | source)
XLA Modules:
  0.0 214.2 jit_solution(5993460207521958044)
XLA Ops:
  5.6 2.3 %collective-permute-start.3 = (bf16[192,512]{1,0:T(8,128)(2,1)S(1)}, bf16[192,512]{1,0:T(8,128)(2,1)S(1)}, u32[]{:S(2)}, u32[]{:S(2)}) collective-permute-start(bf16[192,512]{1,0:T(8,128)(2,1)S(1)} %get-tuple-element.39), channel_id=1, source_target_pairs={{0,4},{1,5},{2,6},{3,7},{4,0},{5,1},{6,2},{7,3},{8,12},{9,13},{10,... | collective-permute-start | bytes 589832 | tf_op jit(solution)/shard_map/ppermute | solution.py:265
  9.6 6.5 %collective-permute-done.1.refs_2_.refs_0_ = bf16[192,512]{1,0:T(8,128)(2,1)S(1)} collective-permute-done((bf16[192,512]{1,0:T(8,128)(2,1)S(1)}, bf16[192,512]{1,0:T(8,128)(2,1)S(1)}, u32[]{:S(2)}, u32[]{:S(2)}) %collective-permute-start.1) | collective-permute-done | bytes 196640 | tf_op jit(solution)/shard_map/ppermute | solution.py:265
  17.6 2.8 %collective-permute-done.2.refs_3_.refs_0_ = bf16[192,512]{1,0:T(8,128)(2,1)S(1)} collective-permute-done((bf16[192,512]{1,0:T(8,128)(2,1)S(1)}, bf16[192,512]{1,0:T(8,128)(2,1)S(1)}, u32[]{:S(2)}, u32[]{:S(2)}) %collective-permute-start.2) | collective-permute-done | bytes 196640 | tf_op jit(solution)/shard_map/ppermute | solution.py:265
  20.4 12.7 %collective-permute-done.4.refs_5_.refs_0_ = bf16[192,512]{1,0:T(8,128)(2,1)S(1)} collective-permute-done((bf16[192,512]{1,0:T(8,128)(2,1)S(1)}, bf16[192,512]{1,0:T(8,128)(2,1)S(1)}, u32[]{:S(2)}, u32[]{:S(2)}) %collective-permute-start.4) | collective-permute-done | bytes 196640 | tf_op jit(solution)/shard_map/ppermute | solution.py:265
  33.2 4.2 %collective-permute-done.5.refs_6_.refs_0_ = bf16[192,512]{1,0:T(8,128)(2,1)S(1)} collective-permute-done((bf16[192,512]{1,0:T(8,128)(2,1)S(1)}, bf16[192,512]{1,0:T(8,128)(2,1)S(1)}, u32[]{:S(2)}, u32[]{:S(2)}) %collective-permute-start.5) | collective-permute-done | bytes 196640 | tf_op jit(solution)/shard_map/ppermute | solution.py:265
  37.4 4.3 %collective-permute-done.6.refs_7_.refs_0_ = bf16[192,512]{1,0:T(8,128)(2,1)S(1)} collective-permute-done((bf16[192,512]{1,0:T(8,128)(2,1)S(1)}, bf16[192,512]{1,0:T(8,128)(2,1)S(1)}, u32[]{:S(2)}, u32[]{:S(2)}) %collective-permute-start.6) | collective-permute-done | bytes 196640 | tf_op jit(solution)/shard_map/ppermute | solution.py:265
  44.6 3.1 %collective-permute-start.7 = (bf16[1024,512]{1,0:T(8,128)(2,1)}, bf16[1024,512]{1,0:T(8,128)(2,1)}, u32[]{:S(2)}, u32[]{:S(2)}) collective-permute-start(bf16[1024,512]{1,0:T(8,128)(2,1)} %get-tuple-element.43), channel_id=1, source_target_pairs={{0,8},{8,16},{16,24},{1,9},{9,17},{17,25},{2,10},{10,18},{18,26},{... | collective-permute-start | bytes 3145736 | tf_op jit(solution)/shard_map/ppermute | solution.py:29
  51.8 2.5 %collective-permute-start.10 = (bf16[192,512]{1,0:T(8,128)(2,1)S(1)}, bf16[192,512]{1,0:T(8,128)(2,1)S(1)}, u32[]{:S(2)}, u32[]{:S(2)}) collective-permute-start(bf16[192,512]{1,0:T(8,128)(2,1)S(1)} %packed.21), channel_id=1, source_target_pairs={{0,3},{1,2},{2,1},{3,0},{4,7},{5,6},{6,5},{7,4},{8,11},{9,10},{10,... | collective-permute-start | bytes 589832 | tf_op jit(solution)/shard_map/ppermute | solution.py:265
  57.7 4.9 %collective-permute-start.13 = (bf16[192,512]{1,0:T(8,128)(2,1)S(1)}, bf16[192,512]{1,0:T(8,128)(2,1)S(1)}, u32[]{:S(2)}, u32[]{:S(2)}) collective-permute-start(bf16[192,512]{1,0:T(8,128)(2,1)S(1)} %packed.24), channel_id=1, source_target_pairs={{0,6},{1,7},{2,4},{3,5},{4,2},{5,3},{6,0},{7,1},{8,14},{9,15},{10,... | collective-permute-start | bytes 589832 | tf_op jit(solution)/shard_map/ppermute | solution.py:265
  62.6 4.5 %collective-permute-done.10.refs_3_.refs_0_ = bf16[192,512]{1,0:T(8,128)(2,1)S(1)} collective-permute-done((bf16[192,512]{1,0:T(8,128)(2,1)S(1)}, bf16[192,512]{1,0:T(8,128)(2,1)S(1)}, u32[]{:S(2)}, u32[]{:S(2)}) %collective-permute-start.10) | collective-permute-done | bytes 196640 | tf_op jit(solution)/shard_map/ppermute | solution.py:265
  70.3 10.3 %collective-permute-done.12.refs_5_.refs_0_ = bf16[192,512]{1,0:T(8,128)(2,1)S(1)} collective-permute-done((bf16[192,512]{1,0:T(8,128)(2,1)S(1)}, bf16[192,512]{1,0:T(8,128)(2,1)S(1)}, u32[]{:S(2)}, u32[]{:S(2)}) %collective-permute-start.12) | collective-permute-done | bytes 196640 | tf_op jit(solution)/shard_map/ppermute | solution.py:265
  80.5 3.2 %collective-permute-start.22 = (bf16[192,512]{1,0:T(8,128)(2,1)S(1)}, bf16[192,512]{1,0:T(8,128)(2,1)S(1)}, u32[]{:S(2)}, u32[]{:S(2)}) collective-permute-start(bf16[192,512]{1,0:T(8,128)(2,1)S(1)} %packed.28), channel_id=1, source_target_pairs={{0,2},{1,3},{2,0},{3,1},{4,6},{5,7},{6,4},{7,5},{8,10},{9,11},{10,... | collective-permute-start | bytes 589832 | tf_op jit(solution)/shard_map/ppermute | solution.py:265
  83.7 3.0 %collective-permute-done.13.refs_6_ = bf16[192,512]{1,0:T(8,128)(2,1)S(1)} collective-permute-done((bf16[192,512]{1,0:T(8,128)(2,1)S(1)}, bf16[192,512]{1,0:T(8,128)(2,1)S(1)}, u32[]{:S(2)}, u32[]{:S(2)}) %collective-permute-start.13) | collective-permute-done | bytes 196640 | tf_op jit(solution)/shard_map/ppermute | solution.py:265
  86.8 4.3 %collective-permute-done.14.refs_7_ = bf16[192,512]{1,0:T(8,128)(2,1)S(1)} collective-permute-done((bf16[192,512]{1,0:T(8,128)(2,1)S(1)}, bf16[192,512]{1,0:T(8,128)(2,1)S(1)}, u32[]{:S(2)}, u32[]{:S(2)}) %collective-permute-start.14) | collective-permute-done | bytes 196640 | tf_op jit(solution)/shard_map/ppermute | solution.py:265
  91.1 2.8 %collective-permute-start.25 = (bf16[192,512]{1,0:T(8,128)(2,1)S(1)}, bf16[192,512]{1,0:T(8,128)(2,1)S(1)}, u32[]{:S(2)}, u32[]{:S(2)}) collective-permute-start(bf16[192,512]{1,0:T(8,128)(2,1)S(1)} %packed.31), channel_id=1, source_target_pairs={{0,5},{1,4},{2,7},{3,6},{4,1},{5,0},{6,3},{7,2},{8,13},{9,12},{10,... | collective-permute-start | bytes 589832 | tf_op jit(solution)/shard_map/ppermute | solution.py:265
  93.9 10.6 %attend.2 = (bf16[1536,256]{1,0:T(8,128)(2,1)S(1)}, f32[1536,256]{1,0:T(8,128)S(1)}, bf16[1024,256]{1,0:T(8,128)(2,1)S(1)}) custom-call(s32[1]{0:T(128)} %bitcast.me_ref, s32[6]{0:T(128)S(1)} %and_select_fusion.first_tile, s32[1,1536]{1,0:T(1,128)S(1)} %maximum_subtract_fusion.1.low_ref, bf16[1024,512]{1,0:T(8,128)(2,1)} %collective-permute-done.7.halo_ref, ...), custom_call_target="tpu_custom_call" | custom-call | flops 5033164800 | bytes 4718592 | tf_op jit(solution)/shard_map/attend/pallas_call | solution.py:161
  106.3 5.4 %collective-permute-start.15 = (bf16[1024,256]{1,0:T(8,128)(2,1)S(1)}, bf16[1024,256]{1,0:T(8,128)(2,1)S(1)}, u32[]{:S(2)}, u32[]{:S(2)}) collective-permute-start(bf16[1024,256]{1,0:T(8,128)(2,1)S(1)} %get-tuple-element.47), channel_id=1, source_target_pairs={{8,0},{16,8},{24,16},{9,1},{17,9},{25,17},{10,2},{18,10},{26,18},{... | collective-permute-start | bytes 1572872 | tf_op jit(solution)/shard_map/ppermute | solution.py:29
  111.7 4.8 %collective-permute-done.25.refs_5_ = bf16[192,512]{1,0:T(8,128)(2,1)S(1)} collective-permute-done((bf16[192,512]{1,0:T(8,128)(2,1)S(1)}, bf16[192,512]{1,0:T(8,128)(2,1)S(1)}, u32[]{:S(2)}, u32[]{:S(2)}) %collective-permute-start.25) | collective-permute-done | bytes 196640 | tf_op jit(solution)/shard_map/ppermute | solution.py:265
  116.5 6.3 %collective-permute-done.26.refs_6_ = bf16[192,512]{1,0:T(8,128)(2,1)S(1)} collective-permute-done((bf16[192,512]{1,0:T(8,128)(2,1)S(1)}, bf16[192,512]{1,0:T(8,128)(2,1)S(1)}, u32[]{:S(2)}, u32[]{:S(2)}) %collective-permute-start.26) | collective-permute-done | bytes 196640 | tf_op jit(solution)/shard_map/ppermute | solution.py:265
  122.8 3.7 %collective-permute-done.27.refs_7_ = bf16[192,512]{1,0:T(8,128)(2,1)S(1)} collective-permute-done((bf16[192,512]{1,0:T(8,128)(2,1)S(1)}, bf16[192,512]{1,0:T(8,128)(2,1)S(1)}, u32[]{:S(2)}, u32[]{:S(2)}) %collective-permute-start.27) | collective-permute-done | bytes 196640 | tf_op jit(solution)/shard_map/ppermute | solution.py:265
  126.5 10.6 %attend.3 = (bf16[1536,256]{1,0:T(8,128)(2,1)S(1)}, f32[1536,256]{1,0:T(8,128)S(1)}, bf16[1024,256]{1,0:T(8,128)(2,1)S(1)}) custom-call(s32[1]{0:T(128)} %bitcast.me_ref, s32[6]{0:T(128)S(1)} %and_select_fusion.first_tile, s32[1,1536]{1,0:T(1,128)S(1)} %maximum_subtract_fusion.1.low_ref, bf16[1024,512]{1,0:T(8,128)(2,1)} %collective-permute-done.7.halo_ref, ...), custom_call_target="tpu_custom_call" | custom-call | flops 5033164800 | bytes 4718592 | tf_op jit(solution)/shard_map/attend/pallas_call | solution.py:161
  137.1 5.2 %collective-permute-start.30 = (bf16[1024,256]{1,0:T(8,128)(2,1)S(1)}, bf16[1024,256]{1,0:T(8,128)(2,1)S(1)}, u32[]{:S(2)}, u32[]{:S(2)}) collective-permute-start(bf16[1024,256]{1,0:T(8,128)(2,1)S(1)} %get-tuple-element.58), channel_id=1, source_target_pairs={{8,0},{16,8},{24,16},{9,1},{17,9},{25,17},{10,2},{18,10},{26,18},{... | collective-permute-start | bytes 1572872 | tf_op jit(solution)/shard_map/ppermute | solution.py:29
  145.7 10.7 %collective-permute-done.30.refs_2_ = bf16[1024,256]{1,0:T(8,128)(2,1)S(1)} collective-permute-done((bf16[1024,256]{1,0:T(8,128)(2,1)S(1)}, bf16[1024,256]{1,0:T(8,128)(2,1)S(1)}, u32[]{:S(2)}, u32[]{:S(2)}) %collective-permute-start.30) | collective-permute-done | bytes 524320 | tf_op jit(solution)/shard_map/ppermute | solution.py:29
  156.8 2.2 %collective-permute-start.19 = (bf16[192,512]{1,0:T(8,128)(2,1)S(1)}, bf16[192,512]{1,0:T(8,128)(2,1)S(1)}, u32[]{:S(2)}, u32[]{:S(2)}) collective-permute-start(bf16[192,512]{1,0:T(8,128)(2,1)S(1)} %get-tuple-element.52), channel_id=1, source_target_pairs={{0,4},{1,5},{2,6},{3,7},{4,0},{5,1},{6,2},{7,3},{8,12},{9,13},{10,... | collective-permute-start | bytes 589832 | tf_op jit(solution)/shard_map/ppermute | solution.py:265
  163.7 8.1 %collective-permute-done.19.refs_4_ = bf16[192,512]{1,0:T(8,128)(2,1)S(1)} collective-permute-done((bf16[192,512]{1,0:T(8,128)(2,1)S(1)}, bf16[192,512]{1,0:T(8,128)(2,1)S(1)}, u32[]{:S(2)}, u32[]{:S(2)}) %collective-permute-start.19) | collective-permute-done | bytes 196640 | tf_op jit(solution)/shard_map/ppermute | solution.py:265
  171.8 3.3 %collective-permute-start.34 = (bf16[192,512]{1,0:T(8,128)(2,1)S(1)}, bf16[192,512]{1,0:T(8,128)(2,1)S(1)}, u32[]{:S(2)}, u32[]{:S(2)}) collective-permute-start(bf16[192,512]{1,0:T(8,128)(2,1)S(1)} %get-tuple-element.63), channel_id=1, source_target_pairs={{0,4},{1,5},{2,6},{3,7},{4,0},{5,1},{6,2},{7,3},{8,12},{9,13},{10,... | collective-permute-start | bytes 589832 | tf_op jit(solution)/shard_map/ppermute | solution.py:265
  176.2 3.4 %collective-permute-start.35 = (bf16[192,512]{1,0:T(8,128)(2,1)S(1)}, bf16[192,512]{1,0:T(8,128)(2,1)S(1)}, u32[]{:S(2)}, u32[]{:S(2)}) collective-permute-start(bf16[192,512]{1,0:T(8,128)(2,1)S(1)} %get-tuple-element.64), channel_id=1, source_target_pairs={{0,5},{1,4},{2,7},{3,6},{4,1},{5,0},{6,3},{7,2},{8,13},{9,12},{10,... | collective-permute-start | bytes 589832 | tf_op jit(solution)/shard_map/ppermute | solution.py:265
  181.5 3.5 %collective-permute-done.34.refs_12_ = bf16[192,512]{1,0:T(8,128)(2,1)S(1)} collective-permute-done((bf16[192,512]{1,0:T(8,128)(2,1)S(1)}, bf16[192,512]{1,0:T(8,128)(2,1)S(1)}, u32[]{:S(2)}, u32[]{:S(2)}) %collective-permute-start.34) | collective-permute-done | bytes 196640 | tf_op jit(solution)/shard_map/ppermute | solution.py:265
  185.0 16.1 %collective-permute-done.35.refs_13_ = bf16[192,512]{1,0:T(8,128)(2,1)S(1)} collective-permute-done((bf16[192,512]{1,0:T(8,128)(2,1)S(1)}, bf16[192,512]{1,0:T(8,128)(2,1)S(1)}, u32[]{:S(2)}, u32[]{:S(2)}) %collective-permute-start.35) | collective-permute-done | bytes 196640 | tf_op jit(solution)/shard_map/ppermute | solution.py:265
  201.1 6.4 %collective-permute-done.36.refs_14_ = bf16[192,512]{1,0:T(8,128)(2,1)S(1)} collective-permute-done((bf16[192,512]{1,0:T(8,128)(2,1)S(1)}, bf16[192,512]{1,0:T(8,128)(2,1)S(1)}, u32[]{:S(2)}, u32[]{:S(2)}) %collective-permute-start.36) | collective-permute-done | bytes 196640 | tf_op jit(solution)/shard_map/ppermute | solution.py:265
  207.5 4.3 %collective-permute-done.37.refs_15_ = bf16[192,512]{1,0:T(8,128)(2,1)S(1)} collective-permute-done((bf16[192,512]{1,0:T(8,128)(2,1)S(1)}, bf16[192,512]{1,0:T(8,128)(2,1)S(1)}, u32[]{:S(2)}, u32[]{:S(2)}) %collective-permute-start.37) | collective-permute-done | bytes 196640 | tf_op jit(solution)/shard_map/ppermute | solution.py:265
  211.9 2.3 %unpacked.1 = (bf16[192,4096]{1,0:T(8,128)(2,1)}, bf16[192,2048]{1,0:T(8,128)(2,1)}, bf16[192,2048]{1,0:T(8,128)(2,1)}) custom-call(s32[1]{0:T(128)} %bitcast.me_ref, bf16[192,512]{1,0:T(8,128)(2,1)S(1)} %get-tuple-element.48.refs_0_, bf16[192,512]{1,0:T(8,128)(2,1)S(1)} %collective-permute-done.16.refs_1_, ...), custom_call_target="tpu_custom_call" | custom-call | bytes 6291456 | tf_op jit(solution)/shard_map/unpacked/pallas_call | solution.py:182
  (113 shorter events, 34.8 us)
Async XLA Ops:
  4.1 16.4 %collective-permute-start.2 = (bf16[192,512]{1,0:T(8,128)(2,1)S(1)}, bf16[192,512]{1,0:T(8,128)(2,1)S(1)}, u32[]{:S(2)}, u32[]{:S(2)}) collective-permute-start(bf16[192,512]{1,0:T(8,128)(2,1)S(1)} %get-tuple-element.38), channel_id=1, source_target_pairs={{0,3},{1,2},{2,1},{3,0},{4,7},{5,6},{6,5},{7,4},{8,11},{9,10},{10,... | collective-permute-start | bytes 589832 | tf_op jit(solution)/shard_map/ppermute | solution.py:265
  5.6 14.8 %collective-permute-start.3 = (bf16[192,512]{1,0:T(8,128)(2,1)S(1)}, bf16[192,512]{1,0:T(8,128)(2,1)S(1)}, u32[]{:S(2)}, u32[]{:S(2)}) collective-permute-start(bf16[192,512]{1,0:T(8,128)(2,1)S(1)} %get-tuple-element.39), channel_id=1, source_target_pairs={{0,4},{1,5},{2,6},{3,7},{4,0},{5,1},{6,2},{7,3},{8,12},{9,13},{10,... | collective-permute-start | bytes 589832 | tf_op jit(solution)/shard_map/ppermute | solution.py:265
  7.9 25.3 %collective-permute-start.4 = (bf16[192,512]{1,0:T(8,128)(2,1)S(1)}, bf16[192,512]{1,0:T(8,128)(2,1)S(1)}, u32[]{:S(2)}, u32[]{:S(2)}) collective-permute-start(bf16[192,512]{1,0:T(8,128)(2,1)S(1)} %get-tuple-element.40), channel_id=1, source_target_pairs={{0,5},{1,4},{2,7},{3,6},{4,1},{5,0},{6,3},{7,2},{8,13},{9,12},{10,... | collective-permute-start | bytes 589832 | tf_op jit(solution)/shard_map/ppermute | solution.py:265
  8.3 29.1 %collective-permute-start.5 = (bf16[192,512]{1,0:T(8,128)(2,1)S(1)}, bf16[192,512]{1,0:T(8,128)(2,1)S(1)}, u32[]{:S(2)}, u32[]{:S(2)}) collective-permute-start(bf16[192,512]{1,0:T(8,128)(2,1)S(1)} %get-tuple-element.41), channel_id=1, source_target_pairs={{0,6},{1,7},{2,4},{3,5},{4,2},{5,3},{6,0},{7,1},{8,14},{9,15},{10,... | collective-permute-start | bytes 589832 | tf_op jit(solution)/shard_map/ppermute | solution.py:265
  16.1 25.6 %collective-permute-start.6 = (bf16[192,512]{1,0:T(8,128)(2,1)S(1)}, bf16[192,512]{1,0:T(8,128)(2,1)S(1)}, u32[]{:S(2)}, u32[]{:S(2)}) collective-permute-start(bf16[192,512]{1,0:T(8,128)(2,1)S(1)} %get-tuple-element.42), channel_id=1, source_target_pairs={{0,7},{1,6},{2,5},{3,4},{4,3},{5,2},{6,1},{7,0},{8,15},{9,14},{10,... | collective-permute-start | bytes 589832 | tf_op jit(solution)/shard_map/ppermute | solution.py:265
  44.6 46.5 %collective-permute-start.7 = (bf16[1024,512]{1,0:T(8,128)(2,1)}, bf16[1024,512]{1,0:T(8,128)(2,1)}, u32[]{:S(2)}, u32[]{:S(2)}) collective-permute-start(bf16[1024,512]{1,0:T(8,128)(2,1)} %get-tuple-element.43), channel_id=1, source_target_pairs={{0,8},{8,16},{16,24},{1,9},{9,17},{17,25},{2,10},{10,18},{18,26},{... | collective-permute-start | bytes 3145736 | tf_op jit(solution)/shard_map/ppermute | solution.py:29
  51.8 15.2 %collective-permute-start.10 = (bf16[192,512]{1,0:T(8,128)(2,1)S(1)}, bf16[192,512]{1,0:T(8,128)(2,1)S(1)}, u32[]{:S(2)}, u32[]{:S(2)}) collective-permute-start(bf16[192,512]{1,0:T(8,128)(2,1)S(1)} %packed.21), channel_id=1, source_target_pairs={{0,3},{1,2},{2,1},{3,0},{4,7},{5,6},{6,5},{7,4},{8,11},{9,10},{10,... | collective-permute-start | bytes 589832 | tf_op jit(solution)/shard_map/ppermute | solution.py:265
  54.3 14.7 %collective-permute-start.11 = (bf16[192,512]{1,0:T(8,128)(2,1)S(1)}, bf16[192,512]{1,0:T(8,128)(2,1)S(1)}, u32[]{:S(2)}, u32[]{:S(2)}) collective-permute-start(bf16[192,512]{1,0:T(8,128)(2,1)S(1)} %packed.22), channel_id=1, source_target_pairs={{0,4},{1,5},{2,6},{3,7},{4,0},{5,1},{6,2},{7,3},{8,12},{9,13},{10,... | collective-permute-start | bytes 589832 | tf_op jit(solution)/shard_map/ppermute | solution.py:265
  56.6 24.0 %collective-permute-start.12 = (bf16[192,512]{1,0:T(8,128)(2,1)S(1)}, bf16[192,512]{1,0:T(8,128)(2,1)S(1)}, u32[]{:S(2)}, u32[]{:S(2)}) collective-permute-start(bf16[192,512]{1,0:T(8,128)(2,1)S(1)} %packed.23), channel_id=1, source_target_pairs={{0,5},{1,4},{2,7},{3,6},{4,1},{5,0},{6,3},{7,2},{8,13},{9,12},{10,... | collective-permute-start | bytes 589832 | tf_op jit(solution)/shard_map/ppermute | solution.py:265
  57.7 29.0 %collective-permute-start.13 = (bf16[192,512]{1,0:T(8,128)(2,1)S(1)}, bf16[192,512]{1,0:T(8,128)(2,1)S(1)}, u32[]{:S(2)}, u32[]{:S(2)}) collective-permute-start(bf16[192,512]{1,0:T(8,128)(2,1)S(1)} %packed.24), channel_id=1, source_target_pairs={{0,6},{1,7},{2,4},{3,5},{4,2},{5,3},{6,0},{7,1},{8,14},{9,15},{10,... | collective-permute-start | bytes 589832 | tf_op jit(solution)/shard_map/ppermute | solution.py:265
  67.0 24.0 %collective-permute-start.14 = (bf16[192,512]{1,0:T(8,128)(2,1)S(1)}, bf16[192,512]{1,0:T(8,128)(2,1)S(1)}, u32[]{:S(2)}, u32[]{:S(2)}) collective-permute-start(bf16[192,512]{1,0:T(8,128)(2,1)S(1)} %packed.25), channel_id=1, source_target_pairs={{0,7},{1,6},{2,5},{3,4},{4,3},{5,2},{6,1},{7,0},{8,15},{9,14},{10,... | collective-permute-start | bytes 589832 | tf_op jit(solution)/shard_map/ppermute | solution.py:265
  69.0 35.6 %collective-permute-start.21 = (bf16[192,512]{1,0:T(8,128)(2,1)S(1)}, bf16[192,512]{1,0:T(8,128)(2,1)S(1)}, u32[]{:S(2)}, u32[]{:S(2)}) collective-permute-start(bf16[192,512]{1,0:T(8,128)(2,1)S(1)} %packed.27), channel_id=1, source_target_pairs={{0,1},{1,0},{2,3},{3,2},{4,5},{5,4},{6,7},{7,6},{8,9},{9,8},{10,11... | collective-permute-start | bytes 589832 | tf_op jit(solution)/shard_map/ppermute | solution.py:265
  80.5 24.4 %collective-permute-start.22 = (bf16[192,512]{1,0:T(8,128)(2,1)S(1)}, bf16[192,512]{1,0:T(8,128)(2,1)S(1)}, u32[]{:S(2)}, u32[]{:S(2)}) collective-permute-start(bf16[192,512]{1,0:T(8,128)(2,1)S(1)} %packed.28), channel_id=1, source_target_pairs={{0,2},{1,3},{2,0},{3,1},{4,6},{5,7},{6,4},{7,5},{8,10},{9,11},{10,... | collective-permute-start | bytes 589832 | tf_op jit(solution)/shard_map/ppermute | solution.py:265
  86.7 19.6 %collective-permute-start.23 = (bf16[192,512]{1,0:T(8,128)(2,1)S(1)}, bf16[192,512]{1,0:T(8,128)(2,1)S(1)}, u32[]{:S(2)}, u32[]{:S(2)}) collective-permute-start(bf16[192,512]{1,0:T(8,128)(2,1)S(1)} %packed.29), channel_id=1, source_target_pairs={{0,3},{1,2},{2,1},{3,0},{4,7},{5,6},{6,5},{7,4},{8,11},{9,10},{10,... | collective-permute-start | bytes 589832 | tf_op jit(solution)/shard_map/ppermute | solution.py:265
  91.1 20.7 %collective-permute-start.24 = (bf16[192,512]{1,0:T(8,128)(2,1)S(1)}, bf16[192,512]{1,0:T(8,128)(2,1)S(1)}, u32[]{:S(2)}, u32[]{:S(2)}) collective-permute-start(bf16[192,512]{1,0:T(8,128)(2,1)S(1)} %packed.30), channel_id=1, source_target_pairs={{0,4},{1,5},{2,6},{3,7},{4,0},{5,1},{6,2},{7,3},{8,12},{9,13},{10,... | collective-permute-start | bytes 589832 | tf_op jit(solution)/shard_map/ppermute | solution.py:265
  91.1 25.4 %collective-permute-start.25 = (bf16[192,512]{1,0:T(8,128)(2,1)S(1)}, bf16[192,512]{1,0:T(8,128)(2,1)S(1)}, u32[]{:S(2)}, u32[]{:S(2)}) collective-permute-start(bf16[192,512]{1,0:T(8,128)(2,1)S(1)} %packed.31), channel_id=1, source_target_pairs={{0,5},{1,4},{2,7},{3,6},{4,1},{5,0},{6,3},{7,2},{8,13},{9,12},{10,... | collective-permute-start | bytes 589832 | tf_op jit(solution)/shard_map/ppermute | solution.py:265
  104.6 18.2 %collective-permute-start.26 = (bf16[192,512]{1,0:T(8,128)(2,1)S(1)}, bf16[192,512]{1,0:T(8,128)(2,1)S(1)}, u32[]{:S(2)}, u32[]{:S(2)}) collective-permute-start(bf16[192,512]{1,0:T(8,128)(2,1)S(1)} %packed.32), channel_id=1, source_target_pairs={{0,6},{1,7},{2,4},{3,5},{4,2},{5,3},{6,0},{7,1},{8,14},{9,15},{10,... | collective-permute-start | bytes 589832 | tf_op jit(solution)/shard_map/ppermute | solution.py:265
  104.9 21.6 %collective-permute-start.27 = (bf16[192,512]{1,0:T(8,128)(2,1)S(1)}, bf16[192,512]{1,0:T(8,128)(2,1)S(1)}, u32[]{:S(2)}, u32[]{:S(2)}) collective-permute-start(bf16[192,512]{1,0:T(8,128)(2,1)S(1)} %packed.33), channel_id=1, source_target_pairs={{0,7},{1,6},{2,5},{3,4},{4,3},{5,2},{6,1},{7,0},{8,15},{9,14},{10,... | collective-permute-start | bytes 589832 | tf_op jit(solution)/shard_map/ppermute | solution.py:265
  106.3 36.0 %collective-permute-start.15 = (bf16[1024,256]{1,0:T(8,128)(2,1)S(1)}, bf16[1024,256]{1,0:T(8,128)(2,1)S(1)}, u32[]{:S(2)}, u32[]{:S(2)}) collective-permute-start(bf16[1024,256]{1,0:T(8,128)(2,1)S(1)} %get-tuple-element.47), channel_id=1, source_target_pairs={{8,0},{16,8},{24,16},{9,1},{17,9},{25,17},{10,2},{18,10},{26,18},{... | collective-permute-start | bytes 1572872 | tf_op jit(solution)/shard_map/ppermute | solution.py:29
  137.1 19.3 %collective-permute-start.30 = (bf16[1024,256]{1,0:T(8,128)(2,1)S(1)}, bf16[1024,256]{1,0:T(8,128)(2,1)S(1)}, u32[]{:S(2)}, u32[]{:S(2)}) collective-permute-start(bf16[1024,256]{1,0:T(8,128)(2,1)S(1)} %get-tuple-element.58), channel_id=1, source_target_pairs={{8,0},{16,8},{24,16},{9,1},{17,9},{25,17},{10,2},{18,10},{26,18},{... | collective-permute-start | bytes 1572872 | tf_op jit(solution)/shard_map/ppermute | solution.py:29
  142.6 14.2 %collective-permute-start.28 = (bf16[192,512]{1,0:T(8,128)(2,1)S(1)}, bf16[192,512]{1,0:T(8,128)(2,1)S(1)}, u32[]{:S(2)}, u32[]{:S(2)}) collective-permute-start(bf16[192,512]{1,0:T(8,128)(2,1)S(1)} %get-tuple-element.55), channel_id=1, source_target_pairs={{0,6},{1,7},{2,4},{3,5},{4,2},{5,3},{6,0},{7,1},{8,14},{9,15},{10,... | collective-permute-start | bytes 589832 | tf_op jit(solution)/shard_map/ppermute | solution.py:265
  143.4 15.5 %collective-permute-start.29 = (bf16[192,512]{1,0:T(8,128)(2,1)S(1)}, bf16[192,512]{1,0:T(8,128)(2,1)S(1)}, u32[]{:S(2)}, u32[]{:S(2)}) collective-permute-start(bf16[192,512]{1,0:T(8,128)(2,1)S(1)} %get-tuple-element.56), channel_id=1, source_target_pairs={{0,7},{1,6},{2,5},{3,4},{4,3},{5,2},{6,1},{7,0},{8,15},{9,14},{10,... | collective-permute-start | bytes 589832 | tf_op jit(solution)/shard_map/ppermute | solution.py:265
  145.5 14.8 %collective-permute-start.16 = (bf16[192,512]{1,0:T(8,128)(2,1)S(1)}, bf16[192,512]{1,0:T(8,128)(2,1)S(1)}, u32[]{:S(2)}, u32[]{:S(2)}) collective-permute-start(bf16[192,512]{1,0:T(8,128)(2,1)S(1)} %get-tuple-element.49), channel_id=1, source_target_pairs={{0,1},{1,0},{2,3},{3,2},{4,5},{5,4},{6,7},{7,6},{8,9},{9,8},{10,11... | collective-permute-start | bytes 589832 | tf_op jit(solution)/shard_map/ppermute | solution.py:265
  145.6 14.7 %collective-permute-start.17 = (bf16[192,512]{1,0:T(8,128)(2,1)S(1)}, bf16[192,512]{1,0:T(8,128)(2,1)S(1)}, u32[]{:S(2)}, u32[]{:S(2)}) collective-permute-start(bf16[192,512]{1,0:T(8,128)(2,1)S(1)} %get-tuple-element.50), channel_id=1, source_target_pairs={{0,2},{1,3},{2,0},{3,1},{4,6},{5,7},{6,4},{7,5},{8,10},{9,11},{10,... | collective-permute-start | bytes 589832 | tf_op jit(solution)/shard_map/ppermute | solution.py:265
  156.8 15.0 %collective-permute-start.19 = (bf16[192,512]{1,0:T(8,128)(2,1)S(1)}, bf16[192,512]{1,0:T(8,128)(2,1)S(1)}, u32[]{:S(2)}, u32[]{:S(2)}) collective-permute-start(bf16[192,512]{1,0:T(8,128)(2,1)S(1)} %get-tuple-element.52), channel_id=1, source_target_pairs={{0,4},{1,5},{2,6},{3,7},{4,0},{5,1},{6,2},{7,3},{8,12},{9,13},{10,... | collective-permute-start | bytes 589832 | tf_op jit(solution)/shard_map/ppermute | solution.py:265
  159.0 17.2 %collective-permute-start.20 = (bf16[192,512]{1,0:T(8,128)(2,1)S(1)}, bf16[192,512]{1,0:T(8,128)(2,1)S(1)}, u32[]{:S(2)}, u32[]{:S(2)}) collective-permute-start(bf16[192,512]{1,0:T(8,128)(2,1)S(1)} %get-tuple-element.53), channel_id=1, source_target_pairs={{0,5},{1,4},{2,7},{3,6},{4,1},{5,0},{6,3},{7,2},{8,13},{9,12},{10,... | collective-permute-start | bytes 589832 | tf_op jit(solution)/shard_map/ppermute | solution.py:265
  160.3 19.3 %collective-permute-start.31 = (bf16[192,512]{1,0:T(8,128)(2,1)S(1)}, bf16[192,512]{1,0:T(8,128)(2,1)S(1)}, u32[]{:S(2)}, u32[]{:S(2)}) collective-permute-start(bf16[192,512]{1,0:T(8,128)(2,1)S(1)} %get-tuple-element.60), channel_id=1, source_target_pairs={{0,1},{1,0},{2,3},{3,2},{4,5},{5,4},{6,7},{7,6},{8,9},{9,8},{10,11... | collective-permute-start | bytes 589832 | tf_op jit(solution)/shard_map/ppermute | solution.py:265
  160.3 20.8 %collective-permute-start.32 = (bf16[192,512]{1,0:T(8,128)(2,1)S(1)}, bf16[192,512]{1,0:T(8,128)(2,1)S(1)}, u32[]{:S(2)}, u32[]{:S(2)}) collective-permute-start(bf16[192,512]{1,0:T(8,128)(2,1)S(1)} %get-tuple-element.61), channel_id=1, source_target_pairs={{0,2},{1,3},{2,0},{3,1},{4,6},{5,7},{6,4},{7,5},{8,10},{9,11},{10,... | collective-permute-start | bytes 589832 | tf_op jit(solution)/shard_map/ppermute | solution.py:265
  163.7 17.8 %collective-permute-start.33 = (bf16[192,512]{1,0:T(8,128)(2,1)S(1)}, bf16[192,512]{1,0:T(8,128)(2,1)S(1)}, u32[]{:S(2)}, u32[]{:S(2)}) collective-permute-start(bf16[192,512]{1,0:T(8,128)(2,1)S(1)} %get-tuple-element.62), channel_id=1, source_target_pairs={{0,3},{1,2},{2,1},{3,0},{4,7},{5,6},{6,5},{7,4},{8,11},{9,10},{10,... | collective-permute-start | bytes 589832 | tf_op jit(solution)/shard_map/ppermute | solution.py:265
  176.2 24.9 %collective-permute-start.35 = (bf16[192,512]{1,0:T(8,128)(2,1)S(1)}, bf16[192,512]{1,0:T(8,128)(2,1)S(1)}, u32[]{:S(2)}, u32[]{:S(2)}) collective-permute-start(bf16[192,512]{1,0:T(8,128)(2,1)S(1)} %get-tuple-element.64), channel_id=1, source_target_pairs={{0,5},{1,4},{2,7},{3,6},{4,1},{5,0},{6,3},{7,2},{8,13},{9,12},{10,... | collective-permute-start | bytes 589832 | tf_op jit(solution)/shard_map/ppermute | solution.py:265
  179.6 27.9 %collective-permute-start.36 = (bf16[192,512]{1,0:T(8,128)(2,1)S(1)}, bf16[192,512]{1,0:T(8,128)(2,1)S(1)}, u32[]{:S(2)}, u32[]{:S(2)}) collective-permute-start(bf16[192,512]{1,0:T(8,128)(2,1)S(1)} %get-tuple-element.65), channel_id=1, source_target_pairs={{0,6},{1,7},{2,4},{3,5},{4,2},{5,3},{6,0},{7,1},{8,14},{9,15},{10,... | collective-permute-start | bytes 589832 | tf_op jit(solution)/shard_map/ppermute | solution.py:265
  181.1 30.8 %collective-permute-start.37 = (bf16[192,512]{1,0:T(8,128)(2,1)S(1)}, bf16[192,512]{1,0:T(8,128)(2,1)S(1)}, u32[]{:S(2)}, u32[]{:S(2)}) collective-permute-start(bf16[192,512]{1,0:T(8,128)(2,1)S(1)} %get-tuple-element.66), channel_id=1, source_target_pairs={{0,7},{1,6},{2,5},{3,4},{4,3},{5,2},{6,1},{7,0},{8,15},{9,14},{10,... | collective-permute-start | bytes 589832 | tf_op jit(solution)/shard_map/ppermute | solution.py:265
  (24 other events, 324.1 us)

commit v5 on v4

--- a/solution.py
+++ b/solution.py
@@ -41,17 +41,17 @@
     return pl.ds(pl.multiple_of((me_ref[0] ^ k) * tokens, tokens), tokens)
 
 
-def gather_rows(me_ref, blocks, out_ref):
-    for k, block in enumerate(blocks):
+def gather_rows(me_ref, blocks, places, out_ref):
+    for k, block in zip(places, blocks):
         out_ref[partner_rows(me_ref, k, block.shape[0]), :] = block[...]
 
 
 def attend_kernel(
-    per_group, ways, chunk, kv_local, me_ref, first_tile, low_ref, halo_ref, kv_ref, *refs
+    per_group, places, chunk, kv_local, me_ref, docs_ref, halo_ref, kv_ref, *refs
 ):
-    blocks, refs = refs[:ways], refs[ways:]
+    blocks, refs = refs[: len(places)], refs[-11:]
     dq_ref, own_ref, rim_ref, qd_ref, k_ext, v_ext, k_t, dk_ext, dv_ext, s_buf, dp_buf = refs
-    gather_rows(me_ref, blocks, qd_ref)
+    gather_rows(me_ref, blocks, places, qd_ref)
     group = qd_ref.shape[0]
     reach = WINDOW // TK
     for ref, at in ((k_ext, chunk * HD), (v_ext, (kv_local + chunk) * HD)):
@@ -71,7 +71,7 @@
     query_iota = lax.broadcasted_iota(jnp.int32, (1, TQ), 1)
     diagonal = jnp.concatenate([query_iota] * per_group, axis=1)
 
-    def q_block(b, tiles):
+    def q_block(b, low, tiles):
         q_rows = pl.ds(pl.multiple_of(b * TQ, TQ), TQ)
         first = b + reach + 1 - tiles
         q = jnp.concatenate(
@@ -81,7 +81,7 @@
             [qd_ref[q_rows, i * HD : (i + 1) * HD] for i in range(per_group, 2 * per_group)],
             axis=0,
         )
-        low = jnp.concatenate([low_ref[:, q_rows]] * per_group, axis=1) - first * TK
+        low = jnp.concatenate([low] * per_group, axis=1) - first * TK
         key_rows = [pl.ds(pl.multiple_of((first + t) * TK, TK), TK) for t in range(tiles)]
         slots = [slice(t * TK, (t + 1) * TK) for t in range(tiles)]
 
@@ -119,10 +119,19 @@
         for i in range(per_group):
             dq_ref[q_rows, i * HD : (i + 1) * HD] = dq[i * TQ : (i + 1) * TQ, :]
 
+    def first_allowed(position):
+        start, end = 0, 0
+        for d in range(docs_ref.shape[0]):
+            end = end + docs_ref[d]
+            start = jnp.where(position >= end, end, start)
+        return jnp.maximum(start, position - (WINDOW - 1)) - (me_ref[1] - WINDOW)
+
     def any_block(b, carry):
-        tiles = b + reach + 1 - first_tile[b]
+        position = me_ref[1] + b * TQ
+        tiles = b + reach + 1 - lax.div(first_allowed(position), TK)
+        low = first_allowed(position + query_iota)
         for count in range(1, reach + 2):
-            pl.when(tiles == count)(functools.partial(q_block, b, count))
+            pl.when(tiles == count)(functools.partial(q_block, b, low, count))
         return carry
 
     lax.fori_loop(0, group // TQ, any_block, 0)
@@ -132,10 +141,9 @@
     own_ref[:, HD:] = dv_ext[WINDOW:, :]
 
 
-def attend(me, qd_blocks, halo, own, chunk, kv_local, low, first_tile):
+def attend(me, docs, qd_blocks, places, halo, own, chunk, kv_local, earlier):
     group = own.shape[0]
-    tokens, qd_lanes = qd_blocks[0].shape
-    ways = len(qd_blocks)
+    qd_lanes = qd_blocks[0].shape[1]
     per_group = qd_lanes // (2 * HD)
     ext = group + WINDOW
     wide = per_group * TQ
@@ -157,11 +165,11 @@
         jax.ShapeDtypeStruct((span, wide), jnp.float32),
         jax.ShapeDtypeStruct((span, wide), jnp.float32),
     ]
-    needed = array_bytes([low, halo, own, *qd_blocks, *outs, *scratch])
+    needed = array_bytes([halo, own, *qd_blocks, *earlier, *outs, *scratch])
     return pl.pallas_call(
-        functools.partial(attend_kernel, per_group, ways, chunk, kv_local),
+        functools.partial(attend_kernel, per_group, places, chunk, kv_local),
         out_shape=tuple(outs),
-        in_specs=[SMEM, SMEM] + [VMEM] * (3 + ways),
+        in_specs=[SMEM, SMEM] + [VMEM] * (2 + len(qd_blocks) + len(earlier)),
         out_specs=(VMEM,) * 3,
         scratch_shapes=[pltpu.VMEM(s.shape, s.dtype) for s in scratch],
         compiler_params=pltpu.CompilerParams(vmem_limit_bytes=needed + SPARE),
@@ -169,7 +177,7 @@
             flops=area * HD * 2 * 5, bytes_accessed=group * HD * 24, transcendentals=area
         ),
         name="attend",
-    )(me, first_tile, low, halo, own, *qd_blocks)
+    )(me, docs, halo, own, *qd_blocks, *earlier)
 
 
 def on_chip(kernel, me, arrays, shapes, name, scratch=(), earlier=()):
@@ -208,33 +216,32 @@
     return on_chip(kernel, me, arrays, shapes, "packed", earlier=earlier)
 
 
-def unpacked(me, grads, q_lanes):
-    chunks, ways = len(grads), len(grads[0])
+def unpacked(me, grads, places, q_lanes):
+    chunks, ways = len(grads), len(places)
     tokens = grads[0][0].shape[0]
     lanes = (q_lanes, HD, HD)
 
     def kernel(me_ref, *refs):
         ins, outs = refs[: chunks * ways], refs[chunks * ways :]
         for c in range(chunks):
-            for k in range(ways):
+            for k, block in zip(places, ins[c * ways : (c + 1) * ways]):
                 first = 0
                 for out, width in zip(outs, lanes):
                     at = pl.multiple_of(((me_ref[0] ^ k) * chunks + c) * width, width)
-                    out[:, pl.ds(at, width)] = ins[c * ways + k][:, first : first + width]
+                    out[:, pl.ds(at, width)] = block[:, first : first + width]
                     first += width
 
     shapes = [(tokens, ways * chunks * width) for width in lanes]
     return on_chip(kernel, me, [g for blocks in grads for g in blocks], shapes, "unpacked")
 
 
-def gathered(me, blocks):
+def gathered(me, blocks, places):
     tokens, lanes = blocks[0].shape
-    ways = len(blocks)
-    group = ways * tokens
+    group = len(places) * tokens
 
     def kernel(me_ref, *refs):
-        all_ref, tail_ref = refs[ways:]
-        gather_rows(me_ref, refs[:ways], all_ref)
+        all_ref, tail_ref = refs[len(places) :]
+        gather_rows(me_ref, refs[: len(places)], places, all_ref)
         tail_ref[...] = all_ref[group - WINDOW :, :]
 
     return on_chip(kernel, me, blocks, [(group, lanes), (WINDOW, lanes)], "gathered")
@@ -259,10 +266,11 @@
     return on_chip(kernel, me, (dq, own, returned), shapes, "settled", scratch, earlier)
 
 
-def exchanged(blocks):
-    ways = len(blocks)
-    return [blocks[0]] + [
-        lax.ppermute(blocks[k], "head", [(i, i ^ k) for i in range(ways)]) for k in range(1, ways)
+def exchanged(blocks, places):
+    ways = lax.axis_size("head")
+    return [
+        lax.ppermute(block, "head", [(i, i ^ k) for i in range(ways)]) if k else block
+        for k, block in zip(places, blocks)
     ]
 
 
@@ -274,45 +282,39 @@
     per_group = queries.shape[1] // keys.shape[1]
     q_lanes = per_group * HD
     group_first = lax.axis_index("seq") * group
-    me = lax.axis_index("head").astype(jnp.int32).reshape(1)
-    places = list(range(ways))
-    early = places[: ways - ways // 4]
-    late = places[ways - ways // 4 :]
-
-    position = group_first + jnp.arange(group, dtype=jnp.int32)
-    ends = jnp.cumsum(doc_lengths)
-    doc_start = jnp.sum(
-        jnp.where(position[:, None] >= ends[None, :], doc_lengths[None, :], 0), axis=1
-    )
-    low = jnp.maximum(doc_start, position - (WINDOW - 1)) - (group_first - WINDOW)
-    low = low.astype(jnp.int32)
-    first_tile = low[::TQ] // TK
-
-    came = exchanged(packed(me, (keys, values), ways, places))
-    kv, tail = gathered(me, came)
+    me = jnp.stack([lax.axis_index("head"), group_first]).astype(jnp.int32)
+    half, quarter = ways // 2, ways // 4
+    early = [*range(half, half + quarter), *range(quarter, half, 2)]
+    late = [k for k in [*range(ways - 1, 0, -1), 0] if k not in early]
+    places = early + late
+
+    came = exchanged(packed(me, (keys, values), ways, places), places)
+    kv, tail = gathered(me, came, places)
     halo = passed_along(tail, "seq", 1)
 
-    parts, returned = [], []
+    parts, returned, firsts = [], [], []
     for c in range(kv_local):
         sent = []
-        for k in places:
-            earlier = [parts[-1][0]] if parts and k in late else [came[k]] if k else []
+        for k, before in zip(places, came):
+            earlier = [parts[-1][0]] if parts and k in late else [before] if k else []
             sent += packed(me, (queries, grad_out), ways, [k], c, kv_local, earlier)
-        came = exchanged(sent)
-        parts.append(attend(me, came, halo, kv, c, kv_local, low.reshape(1, group), first_tile))
+        came = exchanged(sent, places)
+        if parts:
+            dq, own, _ = parts[-1]
+            firsts.append(settled(me, dq, own, returned[-1], ways, early))
+        earlier = [firsts[-1][0]] if firsts else []
+        parts.append(attend(me, doc_lengths, came, places, halo, kv, c, kv_local, earlier))
         returned.append(passed_along(parts[-1][2], "seq", -1))
 
     grads = []
     for c, (dq, own, _) in enumerate(parts):
         if c < kv_local - 1:
-            sent = [
-                *settled(me, dq, own, returned[c], ways, early),
-                *settled(me, dq, own, returned[c], ways, late, [parts[c + 1][0]]),
-            ]
+            rest = settled(me, dq, own, returned[c], ways, late, [parts[c + 1][0]])
+            sent = [*firsts[c], *rest]
         else:
             sent = settled(me, dq, own, returned[c], ways, places)
-        grads.append(exchanged(sent))
-    return unpacked(me, grads, q_lanes)
+        grads.append(exchanged(sent, places))
+    return unpacked(me, grads, places, q_lanes)
 
 
 def solution(mesh):

time: 213 us -> 223 us (1.047); the launches traced: 214 us -> 221 us
  waiting for transfers between devices: 120 us -> 96.2 us
  starting transfers between devices: 59.8 us -> 77.8 us
  Pallas kernels: 26.2 us -> 43.4 us
  local copies, waits for them, and re-layouts: 6.59 us -> 2.28 us
    ppermute x35, starting transfers between devices: 46.1 us -> 70.7 us  [exchanged(): lax.ppermute(block, 'head', [(i, i ^ k) for i in range(ways)])]
    ppermute x35, waiting for transfers between devices: 109 us -> 95.2 us  [exchanged(): lax.ppermute(block, 'head', [(i, i ^ k) for i in range(ways)])]
    pallas_call x22, Pallas kernels: 4.97 us -> 15.9 us  [on_chip(): pl.pallas_call(body, out_shape=outs, in_specs=[SMEM] + [VMEM] * (len(earl...]
    ppermute x3, waiting for transfers between devices: 10.8 us -> 0.96 us  [passed_along(): return lax.ppermute(shard, axis, pairs)]
    ppermute x3, starting transfers between devices: 13.7 us -> 7.14 us  [passed_along(): return lax.ppermute(shard, axis, pairs)]
    pallas_call x2, Pallas kernels: 21.3 us -> 27.5 us  [attend(): pl.pallas_call(functools.partial(attend_kernel, per_group, places, chunk,...]
    unnamed x36 -> x10, local copies, waits for them, and re-layouts: 5.9 us -> 2.28 us
  transfers between devices with their start and end apart: 38 -> 38, of which waited for: 20 -> 18; matrix products, arithmetic and copies ran while one was open for 1% -> 0% of each run, Pallas kernels for 11% -> 5%
where the time goes in v5:
time: 223 us; the launch traced here: 221 us
  waiting for transfers between devices  96.2 us (43%)
  starting transfers between devices  77.8 us (35%)
  Pallas kernels  43.4 us (19%)
  local copies, waits for them, and re-layouts  2.28 us (1%)
    ppermute x35, waiting for transfers between devices, exchanged(): lax.ppermute(block, 'head', [(i, i ^ k) for i in range(ways)])  95.2 us
    ppermute x35, starting transfers between devices, exchanged(): lax.ppermute(block, 'head', [(i, i ^ k) for i in range(ways)])  70.7 us
    pallas_call x2, Pallas kernels, attend(): pl.pallas_call(functools.partial(attend_kernel, per_group, places, chunk,...  27.5 us
    pallas_call x22, Pallas kernels, on_chip(): pl.pallas_call(body, out_shape=outs, in_specs=[SMEM] + [VMEM] * (len(earl...  15.9 us
    ppermute x3, starting transfers between devices, passed_along(): return lax.ppermute(shard, axis, pairs)  7.14 us
  transfers between devices with their start and end apart: 38, of which 18 were waited for; matrix products, arithmetic and copies ran while one was open for 0% of the time, Pallas kernels for 5%

profile of v5, /device:TPU:13, one launch (start us, length us, event | category | flops | bytes accessed | tf_op | source)
XLA Modules:
  0.0 220.7 jit_solution(1933382641093881885)
XLA Ops:
  3.7 2.4 %collective-permute-start = (bf16[192,512]{1,0:T(8,128)(2,1)S(1)}, bf16[192,512]{1,0:T(8,128)(2,1)S(1)}, u32[]{:S(2)}, u32[]{:S(2)}) collective-permute-start(bf16[192,512]{1,0:T(8,128)(2,1)S(1)} %get-tuple-element.35), channel_id=1, source_target_pairs={{0,4},{1,5},{2,6},{3,7},{4,0},{5,1},{6,2},{7,3},{8,12},{9,13},{10,... | collective-permute-start | bytes 589832 | tf_op jit(solution)/shard_map/ppermute | solution.py:272
  7.2 2.1 collective-permute-start.3
  9.6 9.9 %collective-permute-done.refs_0_ = bf16[192,512]{1,0:T(8,128)(2,1)S(1)} collective-permute-done((bf16[192,512]{1,0:T(8,128)(2,1)S(1)}, bf16[192,512]{1,0:T(8,128)(2,1)S(1)}, u32[]{:S(2)}, u32[]{:S(2)}) %collective-permute-start) | collective-permute-done | bytes 196640 | tf_op jit(solution)/shard_map/ppermute | solution.py:272
  19.6 3.2 %collective-permute-start.5 = (bf16[192,512]{1,0:T(8,128)(2,1)S(1)}, bf16[192,512]{1,0:T(8,128)(2,1)S(1)}, u32[]{:S(2)}, u32[]{:S(2)}) collective-permute-start(bf16[192,512]{1,0:T(8,128)(2,1)S(1)} %get-tuple-element.40), channel_id=1, source_target_pairs={{0,3},{1,2},{2,1},{3,0},{4,7},{5,6},{6,5},{7,4},{8,11},{9,10},{10,... | collective-permute-start | bytes 589832 | tf_op jit(solution)/shard_map/ppermute | solution.py:272
  22.7 9.0 %collective-permute-done.1.refs_1_.refs_0_ = bf16[192,512]{1,0:T(8,128)(2,1)S(1)} collective-permute-done((bf16[192,512]{1,0:T(8,128)(2,1)S(1)}, bf16[192,512]{1,0:T(8,128)(2,1)S(1)}, u32[]{:S(2)}, u32[]{:S(2)}) %collective-permute-start.1) | collective-permute-done | bytes 196640 | tf_op jit(solution)/shard_map/ppermute | solution.py:272
  32.3 4.4 %collective-permute-done.3.refs_3_.refs_0_ = bf16[192,512]{1,0:T(8,128)(2,1)S(1)} collective-permute-done((bf16[192,512]{1,0:T(8,128)(2,1)S(1)}, bf16[192,512]{1,0:T(8,128)(2,1)S(1)}, u32[]{:S(2)}, u32[]{:S(2)}) %collective-permute-start.3) | collective-permute-done | bytes 196640 | tf_op jit(solution)/shard_map/ppermute | solution.py:272
  36.8 3.4 %collective-permute-done.4.refs_4_.refs_0_ = bf16[192,512]{1,0:T(8,128)(2,1)S(1)} collective-permute-done((bf16[192,512]{1,0:T(8,128)(2,1)S(1)}, bf16[192,512]{1,0:T(8,128)(2,1)S(1)}, u32[]{:S(2)}, u32[]{:S(2)}) %collective-permute-start.4) | collective-permute-done | bytes 196640 | tf_op jit(solution)/shard_map/ppermute | solution.py:272
  40.9 3.1 %collective-permute-start.7 = (bf16[1024,512]{1,0:T(8,128)(2,1)S(1)}, bf16[1024,512]{1,0:T(8,128)(2,1)S(1)}, u32[]{:S(2)}, u32[]{:S(2)}) collective-permute-start(bf16[1024,512]{1,0:T(8,128)(2,1)S(1)} %get-tuple-element.43), channel_id=1, source_target_pairs={{0,8},{8,16},{16,24},{1,9},{9,17},{17,25},{2,10},{10,18},{18,26},{... | collective-permute-start | bytes 3145736 | tf_op jit(solution)/shard_map/ppermute | solution.py:29
  45.3 3.4 %collective-permute-start.9 = (bf16[192,512]{1,0:T(8,128)(2,1)S(1)}, bf16[192,512]{1,0:T(8,128)(2,1)S(1)}, u32[]{:S(2)}, u32[]{:S(2)}) collective-permute-start(bf16[192,512]{1,0:T(8,128)(2,1)S(1)} %packed.19), channel_id=1, source_target_pairs={{0,5},{1,4},{2,7},{3,6},{4,1},{5,0},{6,3},{7,2},{8,13},{9,12},{10,... | collective-permute-start | bytes 589832 | tf_op jit(solution)/shard_map/ppermute | solution.py:272
  53.3 6.8 %collective-permute-start.12 = (bf16[192,512]{1,0:T(8,128)(2,1)S(1)}, bf16[192,512]{1,0:T(8,128)(2,1)S(1)}, u32[]{:S(2)}, u32[]{:S(2)}) collective-permute-start(bf16[192,512]{1,0:T(8,128)(2,1)S(1)} %packed.22), channel_id=1, source_target_pairs={{0,6},{1,7},{2,4},{3,5},{4,2},{5,3},{6,0},{7,1},{8,14},{9,15},{10,... | collective-permute-start | bytes 589832 | tf_op jit(solution)/shard_map/ppermute | solution.py:272
  62.0 12.7 %collective-permute-start.13 = (bf16[192,512]{1,0:T(8,128)(2,1)S(1)}, bf16[192,512]{1,0:T(8,128)(2,1)S(1)}, u32[]{:S(2)}, u32[]{:S(2)}) collective-permute-start(bf16[192,512]{1,0:T(8,128)(2,1)S(1)} %packed.23), channel_id=1, source_target_pairs={{0,3},{1,2},{2,1},{3,0},{4,7},{5,6},{6,5},{7,4},{8,11},{9,10},{10,... | collective-permute-start | bytes 589832 | tf_op jit(solution)/shard_map/ppermute | solution.py:272
  75.5 2.3 %collective-permute-done.11.refs_3_ = bf16[192,512]{1,0:T(8,128)(2,1)S(1)} collective-permute-done((bf16[192,512]{1,0:T(8,128)(2,1)S(1)}, bf16[192,512]{1,0:T(8,128)(2,1)S(1)}, u32[]{:S(2)}, u32[]{:S(2)}) %collective-permute-start.11) | collective-permute-done | bytes 196640 | tf_op jit(solution)/shard_map/ppermute | solution.py:272
  77.9 3.7 %collective-permute-done.12.refs_4_ = bf16[192,512]{1,0:T(8,128)(2,1)S(1)} collective-permute-done((bf16[192,512]{1,0:T(8,128)(2,1)S(1)}, bf16[192,512]{1,0:T(8,128)(2,1)S(1)}, u32[]{:S(2)}, u32[]{:S(2)}) %collective-permute-start.12) | collective-permute-done | bytes 196640 | tf_op jit(solution)/shard_map/ppermute | solution.py:272
  81.6 13.7 %attend.2 = (bf16[1536,256]{1,0:T(8,128)(2,1)S(1)}, f32[1536,256]{1,0:T(8,128)S(1)}, bf16[1024,256]{1,0:T(8,128)(2,1)S(1)}) custom-call(s32[2]{0:T(128)S(1)} %pad_add_fusion.me_ref, s32[16]{0:T(128)S(1)} %copy-done.4, bf16[1024,512]{1,0:T(8,128)(2,1)S(1)} %collective-permute-done.7.halo_ref, bf16[1536,512]{1,0:T(8,128)(2,1)S(1)} %get-tuple-element.44.kv_ref, ...), custom_call_target="tpu_custom_call" | custom-call | flops 5033164800 | bytes 4718592 | tf_op jit(solution)/shard_map/attend/pallas_call | solution.py:169
  95.3 2.1 collective-permute-start.15
  98.7 3.2 %collective-permute-start.20 = (bf16[192,512]{1,0:T(8,128)(2,1)S(1)}, bf16[192,512]{1,0:T(8,128)(2,1)S(1)}, u32[]{:S(2)}, u32[]{:S(2)}) collective-permute-start(bf16[192,512]{1,0:T(8,128)(2,1)S(1)} %packed.27), channel_id=1, source_target_pairs={{0,5},{1,4},{2,7},{3,6},{4,1},{5,0},{6,3},{7,2},{8,13},{9,12},{10,... | collective-permute-start | bytes 589832 | tf_op jit(solution)/shard_map/ppermute | solution.py:272
  105.5 5.5 %collective-permute-done.19.refs_0_ = bf16[192,512]{1,0:T(8,128)(2,1)S(1)} collective-permute-done((bf16[192,512]{1,0:T(8,128)(2,1)S(1)}, bf16[192,512]{1,0:T(8,128)(2,1)S(1)}, u32[]{:S(2)}, u32[]{:S(2)}) %collective-permute-start.19) | collective-permute-done | bytes 196640 | tf_op jit(solution)/shard_map/ppermute | solution.py:272
  111.4 12.2 %collective-permute-done.20.refs_1_ = bf16[192,512]{1,0:T(8,128)(2,1)S(1)} collective-permute-done((bf16[192,512]{1,0:T(8,128)(2,1)S(1)}, bf16[192,512]{1,0:T(8,128)(2,1)S(1)}, u32[]{:S(2)}, u32[]{:S(2)}) %collective-permute-start.20) | collective-permute-done | bytes 196640 | tf_op jit(solution)/shard_map/ppermute | solution.py:272
  123.6 2.6 %collective-permute-start.24 = (bf16[192,512]{1,0:T(8,128)(2,1)S(1)}, bf16[192,512]{1,0:T(8,128)(2,1)S(1)}, u32[]{:S(2)}, u32[]{:S(2)}) collective-permute-start(bf16[192,512]{1,0:T(8,128)(2,1)S(1)} %packed.31), channel_id=1, source_target_pairs={{0,3},{1,2},{2,1},{3,0},{4,7},{5,6},{6,5},{7,4},{8,11},{9,10},{10,... | collective-permute-start | bytes 589832 | tf_op jit(solution)/shard_map/ppermute | solution.py:272
  130.3 2.9 %collective-permute-done.23.refs_4_ = bf16[192,512]{1,0:T(8,128)(2,1)S(1)} collective-permute-done((bf16[192,512]{1,0:T(8,128)(2,1)S(1)}, bf16[192,512]{1,0:T(8,128)(2,1)S(1)}, u32[]{:S(2)}, u32[]{:S(2)}) %collective-permute-start.23) | collective-permute-done | bytes 196640 | tf_op jit(solution)/shard_map/ppermute | solution.py:272
  133.2 13.7 %attend.3 = (bf16[1536,256]{1,0:T(8,128)(2,1)S(1)}, f32[1536,256]{1,0:T(8,128)S(1)}, bf16[1024,256]{1,0:T(8,128)(2,1)S(1)}) custom-call(s32[2]{0:T(128)S(1)} %pad_add_fusion.me_ref, s32[16]{0:T(128)S(1)} %copy-done.4, bf16[1024,512]{1,0:T(8,128)(2,1)S(1)} %collective-permute-done.7.halo_ref, bf16[1536,512]{1,0:T(8,128)(2,1)S(1)} %get-tuple-element.44.kv_ref, ...), custom_call_target="tpu_custom_call" | custom-call | flops 5033164800 | bytes 4718592 | tf_op jit(solution)/shard_map/attend/pallas_call | solution.py:169
  149.5 2.3 %collective-permute-start.18 = (bf16[192,512]{1,0:T(8,128)(2,1)S(1)}, bf16[192,512]{1,0:T(8,128)(2,1)S(1)}, u32[]{:S(2)}, u32[]{:S(2)}) collective-permute-start(bf16[192,512]{1,0:T(8,128)(2,1)S(1)} %get-tuple-element.50), channel_id=1, source_target_pairs={{0,2},{1,3},{2,0},{3,1},{4,6},{5,7},{6,4},{7,5},{8,10},{9,11},{10,... | collective-permute-start | bytes 589832 | tf_op jit(solution)/shard_map/ppermute | solution.py:272
  154.1 3.6 %collective-permute-done.17.refs_1_ = bf16[192,512]{1,0:T(8,128)(2,1)S(1)} collective-permute-done((bf16[192,512]{1,0:T(8,128)(2,1)S(1)}, bf16[192,512]{1,0:T(8,128)(2,1)S(1)}, u32[]{:S(2)}, u32[]{:S(2)}) %collective-permute-start.17) | collective-permute-done | bytes 196640 | tf_op jit(solution)/shard_map/ppermute | solution.py:272
  157.7 2.6 %collective-permute-start.28 = (bf16[192,512]{1,0:T(8,128)(2,1)S(1)}, bf16[192,512]{1,0:T(8,128)(2,1)S(1)}, u32[]{:S(2)}, u32[]{:S(2)}) collective-permute-start(bf16[192,512]{1,0:T(8,128)(2,1)S(1)} %get-tuple-element.54), channel_id=1, source_target_pairs={{0,3},{1,2},{2,1},{3,0},{4,7},{5,6},{6,5},{7,4},{8,11},{9,10},{10,... | collective-permute-start | bytes 589832 | tf_op jit(solution)/shard_map/ppermute | solution.py:272
  164.5 8.6 %collective-permute-done.26.refs_3_ = bf16[192,512]{1,0:T(8,128)(2,1)S(1)} collective-permute-done((bf16[192,512]{1,0:T(8,128)(2,1)S(1)}, bf16[192,512]{1,0:T(8,128)(2,1)S(1)}, u32[]{:S(2)}, u32[]{:S(2)}) %collective-permute-start.26) | collective-permute-done | bytes 196640 | tf_op jit(solution)/shard_map/ppermute | solution.py:272
  173.1 11.0 %collective-permute-done.27.refs_4_ = bf16[192,512]{1,0:T(8,128)(2,1)S(1)} collective-permute-done((bf16[192,512]{1,0:T(8,128)(2,1)S(1)}, bf16[192,512]{1,0:T(8,128)(2,1)S(1)}, u32[]{:S(2)}, u32[]{:S(2)}) %collective-permute-start.27) | collective-permute-done | bytes 196640 | tf_op jit(solution)/shard_map/ppermute | solution.py:272
  184.1 4.0 %collective-permute-start.33 = (bf16[192,512]{1,0:T(8,128)(2,1)S(1)}, bf16[192,512]{1,0:T(8,128)(2,1)S(1)}, u32[]{:S(2)}, u32[]{:S(2)}) collective-permute-start(bf16[192,512]{1,0:T(8,128)(2,1)S(1)} %get-tuple-element.61), channel_id=1, source_target_pairs={{0,2},{1,3},{2,0},{3,1},{4,6},{5,7},{6,4},{7,5},{8,10},{9,11},{10,... | collective-permute-start | bytes 589832 | tf_op jit(solution)/shard_map/ppermute | solution.py:272
  188.8 7.4 %collective-permute-done.31.refs_8_ = bf16[192,512]{1,0:T(8,128)(2,1)S(1)} collective-permute-done((bf16[192,512]{1,0:T(8,128)(2,1)S(1)}, bf16[192,512]{1,0:T(8,128)(2,1)S(1)}, u32[]{:S(2)}, u32[]{:S(2)}) %collective-permute-start.31) | collective-permute-done | bytes 196640 | tf_op jit(solution)/shard_map/ppermute | solution.py:272
  196.2 12.2 %collective-permute-start.36 = (bf16[192,512]{1,0:T(8,128)(2,1)S(1)}, bf16[192,512]{1,0:T(8,128)(2,1)S(1)}, u32[]{:S(2)}, u32[]{:S(2)}) collective-permute-start(bf16[192,512]{1,0:T(8,128)(2,1)S(1)} %get-tuple-element.64), channel_id=1, source_target_pairs={{0,3},{1,2},{2,1},{3,0},{4,7},{5,6},{6,5},{7,4},{8,11},{9,10},{10,... | collective-permute-start | bytes 589832 | tf_op jit(solution)/shard_map/ppermute | solution.py:272
  210.1 4.9 %collective-permute-done.34.refs_11_ = bf16[192,512]{1,0:T(8,128)(2,1)S(1)} collective-permute-done((bf16[192,512]{1,0:T(8,128)(2,1)S(1)}, bf16[192,512]{1,0:T(8,128)(2,1)S(1)}, u32[]{:S(2)}, u32[]{:S(2)}) %collective-permute-start.34) | collective-permute-done | bytes 196640 | tf_op jit(solution)/shard_map/ppermute | solution.py:272
  215.0 2.8 %collective-permute-done.35.refs_12_ = bf16[192,512]{1,0:T(8,128)(2,1)S(1)} collective-permute-done((bf16[192,512]{1,0:T(8,128)(2,1)S(1)}, bf16[192,512]{1,0:T(8,128)(2,1)S(1)}, u32[]{:S(2)}, u32[]{:S(2)}) %collective-permute-start.35) | collective-permute-done | bytes 196640 | tf_op jit(solution)/shard_map/ppermute | solution.py:272
  217.8 2.8 %unpacked.1 = (bf16[192,4096]{1,0:T(8,128)(2,1)}, bf16[192,2048]{1,0:T(8,128)(2,1)}, bf16[192,2048]{1,0:T(8,128)(2,1)}) custom-call(s32[2]{0:T(128)S(1)} %pad_add_fusion.me_ref, bf16[192,512]{1,0:T(8,128)(2,1)S(1)} %collective-permute-done.16.refs_0_, bf16[192,512]{1,0:T(8,128)(2,1)S(1)} %collective-permute-done.17.refs_1_, ...), custom_call_target="tpu_custom_call" | custom-call | bytes 6291456 | tf_op jit(solution)/shard_map/unpacked/pallas_call | solution.py:190
  (79 shorter events, 35.1 us)
Async XLA Ops:
  3.7 15.8 %collective-permute-start = (bf16[192,512]{1,0:T(8,128)(2,1)S(1)}, bf16[192,512]{1,0:T(8,128)(2,1)S(1)}, u32[]{:S(2)}, u32[]{:S(2)}) collective-permute-start(bf16[192,512]{1,0:T(8,128)(2,1)S(1)} %get-tuple-element.35), channel_id=1, source_target_pairs={{0,4},{1,5},{2,6},{3,7},{4,0},{5,1},{6,2},{7,3},{8,12},{9,13},{10,... | collective-permute-start | bytes 589832 | tf_op jit(solution)/shard_map/ppermute | solution.py:272
  6.1 25.6 %collective-permute-start.1 = (bf16[192,512]{1,0:T(8,128)(2,1)S(1)}, bf16[192,512]{1,0:T(8,128)(2,1)S(1)}, u32[]{:S(2)}, u32[]{:S(2)}) collective-permute-start(bf16[192,512]{1,0:T(8,128)(2,1)S(1)} %get-tuple-element.36), channel_id=1, source_target_pairs={{0,5},{1,4},{2,7},{3,6},{4,1},{5,0},{6,3},{7,2},{8,13},{9,12},{10,... | collective-permute-start | bytes 589832 | tf_op jit(solution)/shard_map/ppermute | solution.py:272
  7.0 25.3 %collective-permute-start.2 = (bf16[192,512]{1,0:T(8,128)(2,1)S(1)}, bf16[192,512]{1,0:T(8,128)(2,1)S(1)}, u32[]{:S(2)}, u32[]{:S(2)}) collective-permute-start(bf16[192,512]{1,0:T(8,128)(2,1)S(1)} %get-tuple-element.37), channel_id=1, source_target_pairs={{0,2},{1,3},{2,0},{3,1},{4,6},{5,7},{6,4},{7,5},{8,10},{9,11},{10,... | collective-permute-start | bytes 589832 | tf_op jit(solution)/shard_map/ppermute | solution.py:272
  7.2 29.6 %collective-permute-start.3 = (bf16[192,512]{1,0:T(8,128)(2,1)S(1)}, bf16[192,512]{1,0:T(8,128)(2,1)S(1)}, u32[]{:S(2)}, u32[]{:S(2)}) collective-permute-start(bf16[192,512]{1,0:T(8,128)(2,1)S(1)} %get-tuple-element.38), channel_id=1, source_target_pairs={{0,7},{1,6},{2,5},{3,4},{4,3},{5,2},{6,1},{7,0},{8,15},{9,14},{10,... | collective-permute-start | bytes 589832 | tf_op jit(solution)/shard_map/ppermute | solution.py:272
  9.3 30.8 %collective-permute-start.4 = (bf16[192,512]{1,0:T(8,128)(2,1)S(1)}, bf16[192,512]{1,0:T(8,128)(2,1)S(1)}, u32[]{:S(2)}, u32[]{:S(2)}) collective-permute-start(bf16[192,512]{1,0:T(8,128)(2,1)S(1)} %get-tuple-element.39), channel_id=1, source_target_pairs={{0,6},{1,7},{2,4},{3,5},{4,2},{5,3},{6,0},{7,1},{8,14},{9,15},{10,... | collective-permute-start | bytes 589832 | tf_op jit(solution)/shard_map/ppermute | solution.py:272
  19.6 20.6 %collective-permute-start.5 = (bf16[192,512]{1,0:T(8,128)(2,1)S(1)}, bf16[192,512]{1,0:T(8,128)(2,1)S(1)}, u32[]{:S(2)}, u32[]{:S(2)}) collective-permute-start(bf16[192,512]{1,0:T(8,128)(2,1)S(1)} %get-tuple-element.40), channel_id=1, source_target_pairs={{0,3},{1,2},{2,1},{3,0},{4,7},{5,6},{6,5},{7,4},{8,11},{9,10},{10,... | collective-permute-start | bytes 589832 | tf_op jit(solution)/shard_map/ppermute | solution.py:272
  40.9 40.7 %collective-permute-start.7 = (bf16[1024,512]{1,0:T(8,128)(2,1)S(1)}, bf16[1024,512]{1,0:T(8,128)(2,1)S(1)}, u32[]{:S(2)}, u32[]{:S(2)}) collective-permute-start(bf16[1024,512]{1,0:T(8,128)(2,1)S(1)} %get-tuple-element.43), channel_id=1, source_target_pairs={{0,8},{8,16},{16,24},{1,9},{9,17},{17,25},{2,10},{10,18},{18,26},{... | collective-permute-start | bytes 3145736 | tf_op jit(solution)/shard_map/ppermute | solution.py:29
  45.3 16.7 %collective-permute-start.9 = (bf16[192,512]{1,0:T(8,128)(2,1)S(1)}, bf16[192,512]{1,0:T(8,128)(2,1)S(1)}, u32[]{:S(2)}, u32[]{:S(2)}) collective-permute-start(bf16[192,512]{1,0:T(8,128)(2,1)S(1)} %packed.19), channel_id=1, source_target_pairs={{0,5},{1,4},{2,7},{3,6},{4,1},{5,0},{6,3},{7,2},{8,13},{9,12},{10,... | collective-permute-start | bytes 589832 | tf_op jit(solution)/shard_map/ppermute | solution.py:272
  49.2 25.4 %collective-permute-start.10 = (bf16[192,512]{1,0:T(8,128)(2,1)S(1)}, bf16[192,512]{1,0:T(8,128)(2,1)S(1)}, u32[]{:S(2)}, u32[]{:S(2)}) collective-permute-start(bf16[192,512]{1,0:T(8,128)(2,1)S(1)} %packed.20), channel_id=1, source_target_pairs={{0,2},{1,3},{2,0},{3,1},{4,6},{5,7},{6,4},{7,5},{8,10},{9,11},{10,... | collective-permute-start | bytes 589832 | tf_op jit(solution)/shard_map/ppermute | solution.py:272
  50.6 27.3 %collective-permute-start.11 = (bf16[192,512]{1,0:T(8,128)(2,1)S(1)}, bf16[192,512]{1,0:T(8,128)(2,1)S(1)}, u32[]{:S(2)}, u32[]{:S(2)}) collective-permute-start(bf16[192,512]{1,0:T(8,128)(2,1)S(1)} %packed.21), channel_id=1, source_target_pairs={{0,7},{1,6},{2,5},{3,4},{4,3},{5,2},{6,1},{7,0},{8,15},{9,14},{10,... | collective-permute-start | bytes 589832 | tf_op jit(solution)/shard_map/ppermute | solution.py:272
  53.3 28.3 %collective-permute-start.12 = (bf16[192,512]{1,0:T(8,128)(2,1)S(1)}, bf16[192,512]{1,0:T(8,128)(2,1)S(1)}, u32[]{:S(2)}, u32[]{:S(2)}) collective-permute-start(bf16[192,512]{1,0:T(8,128)(2,1)S(1)} %packed.22), channel_id=1, source_target_pairs={{0,6},{1,7},{2,4},{3,5},{4,2},{5,3},{6,0},{7,1},{8,14},{9,15},{10,... | collective-permute-start | bytes 589832 | tf_op jit(solution)/shard_map/ppermute | solution.py:272
  62.0 19.6 %collective-permute-start.13 = (bf16[192,512]{1,0:T(8,128)(2,1)S(1)}, bf16[192,512]{1,0:T(8,128)(2,1)S(1)}, u32[]{:S(2)}, u32[]{:S(2)}) collective-permute-start(bf16[192,512]{1,0:T(8,128)(2,1)S(1)} %packed.23), channel_id=1, source_target_pairs={{0,3},{1,2},{2,1},{3,0},{4,7},{5,6},{6,5},{7,4},{8,11},{9,10},{10,... | collective-permute-start | bytes 589832 | tf_op jit(solution)/shard_map/ppermute | solution.py:272
  95.3 30.9 %collective-permute-start.15 = (bf16[1024,256]{1,0:T(8,128)(2,1)S(1)}, bf16[1024,256]{1,0:T(8,128)(2,1)S(1)}, u32[]{:S(2)}, u32[]{:S(2)}) collective-permute-start(bf16[1024,256]{1,0:T(8,128)(2,1)S(1)} %get-tuple-element.47), channel_id=1, source_target_pairs={{8,0},{16,8},{24,16},{9,1},{17,9},{25,17},{10,2},{18,10},{26,18},{... | collective-permute-start | bytes 1572872 | tf_op jit(solution)/shard_map/ppermute | solution.py:29
  98.0 13.0 %collective-permute-start.19 = (bf16[192,512]{1,0:T(8,128)(2,1)S(1)}, bf16[192,512]{1,0:T(8,128)(2,1)S(1)}, u32[]{:S(2)}, u32[]{:S(2)}) collective-permute-start(bf16[192,512]{1,0:T(8,128)(2,1)S(1)} %packed.26), channel_id=1, source_target_pairs={{0,4},{1,5},{2,6},{3,7},{4,0},{5,1},{6,2},{7,3},{8,12},{9,13},{10,... | collective-permute-start | bytes 589832 | tf_op jit(solution)/shard_map/ppermute | solution.py:272
  98.7 24.9 %collective-permute-start.20 = (bf16[192,512]{1,0:T(8,128)(2,1)S(1)}, bf16[192,512]{1,0:T(8,128)(2,1)S(1)}, u32[]{:S(2)}, u32[]{:S(2)}) collective-permute-start(bf16[192,512]{1,0:T(8,128)(2,1)S(1)} %packed.27), channel_id=1, source_target_pairs={{0,5},{1,4},{2,7},{3,6},{4,1},{5,0},{6,3},{7,2},{8,13},{9,12},{10,... | collective-permute-start | bytes 589832 | tf_op jit(solution)/shard_map/ppermute | solution.py:272
  102.5 26.3 %collective-permute-start.21 = (bf16[192,512]{1,0:T(8,128)(2,1)S(1)}, bf16[192,512]{1,0:T(8,128)(2,1)S(1)}, u32[]{:S(2)}, u32[]{:S(2)}) collective-permute-start(bf16[192,512]{1,0:T(8,128)(2,1)S(1)} %packed.28), channel_id=1, source_target_pairs={{0,2},{1,3},{2,0},{3,1},{4,6},{5,7},{6,4},{7,5},{8,10},{9,11},{10,... | collective-permute-start | bytes 589832 | tf_op jit(solution)/shard_map/ppermute | solution.py:272
  104.9 25.4 %collective-permute-start.22 = (bf16[192,512]{1,0:T(8,128)(2,1)S(1)}, bf16[192,512]{1,0:T(8,128)(2,1)S(1)}, u32[]{:S(2)}, u32[]{:S(2)}) collective-permute-start(bf16[192,512]{1,0:T(8,128)(2,1)S(1)} %packed.29), channel_id=1, source_target_pairs={{0,7},{1,6},{2,5},{3,4},{4,3},{5,2},{6,1},{7,0},{8,15},{9,14},{10,... | collective-permute-start | bytes 589832 | tf_op jit(solution)/shard_map/ppermute | solution.py:272
  111.1 22.1 %collective-permute-start.23 = (bf16[192,512]{1,0:T(8,128)(2,1)S(1)}, bf16[192,512]{1,0:T(8,128)(2,1)S(1)}, u32[]{:S(2)}, u32[]{:S(2)}) collective-permute-start(bf16[192,512]{1,0:T(8,128)(2,1)S(1)} %packed.30), channel_id=1, source_target_pairs={{0,6},{1,7},{2,4},{3,5},{4,2},{5,3},{6,0},{7,1},{8,14},{9,15},{10,... | collective-permute-start | bytes 589832 | tf_op jit(solution)/shard_map/ppermute | solution.py:272
  123.6 9.6 %collective-permute-start.24 = (bf16[192,512]{1,0:T(8,128)(2,1)S(1)}, bf16[192,512]{1,0:T(8,128)(2,1)S(1)}, u32[]{:S(2)}, u32[]{:S(2)}) collective-permute-start(bf16[192,512]{1,0:T(8,128)(2,1)S(1)} %packed.31), channel_id=1, source_target_pairs={{0,3},{1,2},{2,1},{3,0},{4,7},{5,6},{6,5},{7,4},{8,11},{9,10},{10,... | collective-permute-start | bytes 589832 | tf_op jit(solution)/shard_map/ppermute | solution.py:272
  147.0 14.3 %collective-permute-start.30 = (bf16[1024,256]{1,0:T(8,128)(2,1)S(1)}, bf16[1024,256]{1,0:T(8,128)(2,1)S(1)}, u32[]{:S(2)}, u32[]{:S(2)}) collective-permute-start(bf16[1024,256]{1,0:T(8,128)(2,1)S(1)} %get-tuple-element.58), channel_id=1, source_target_pairs={{8,0},{16,8},{24,16},{9,1},{17,9},{25,17},{10,2},{18,10},{26,18},{... | collective-permute-start | bytes 1572872 | tf_op jit(solution)/shard_map/ppermute | solution.py:29
  149.5 14.6 %collective-permute-start.18 = (bf16[192,512]{1,0:T(8,128)(2,1)S(1)}, bf16[192,512]{1,0:T(8,128)(2,1)S(1)}, u32[]{:S(2)}, u32[]{:S(2)}) collective-permute-start(bf16[192,512]{1,0:T(8,128)(2,1)S(1)} %get-tuple-element.50), channel_id=1, source_target_pairs={{0,2},{1,3},{2,0},{3,1},{4,6},{5,7},{6,4},{7,5},{8,10},{9,11},{10,... | collective-permute-start | bytes 589832 | tf_op jit(solution)/shard_map/ppermute | solution.py:272
  152.5 20.6 %collective-permute-start.26 = (bf16[192,512]{1,0:T(8,128)(2,1)S(1)}, bf16[192,512]{1,0:T(8,128)(2,1)S(1)}, u32[]{:S(2)}, u32[]{:S(2)}) collective-permute-start(bf16[192,512]{1,0:T(8,128)(2,1)S(1)} %get-tuple-element.52), channel_id=1, source_target_pairs={{0,7},{1,6},{2,5},{3,4},{4,3},{5,2},{6,1},{7,0},{8,15},{9,14},{10,... | collective-permute-start | bytes 589832 | tf_op jit(solution)/shard_map/ppermute | solution.py:272
  153.1 31.0 %collective-permute-start.27 = (bf16[192,512]{1,0:T(8,128)(2,1)S(1)}, bf16[192,512]{1,0:T(8,128)(2,1)S(1)}, u32[]{:S(2)}, u32[]{:S(2)}) collective-permute-start(bf16[192,512]{1,0:T(8,128)(2,1)S(1)} %get-tuple-element.53), channel_id=1, source_target_pairs={{0,6},{1,7},{2,4},{3,5},{4,2},{5,3},{6,0},{7,1},{8,14},{9,15},{10,... | collective-permute-start | bytes 589832 | tf_op jit(solution)/shard_map/ppermute | solution.py:272
  157.7 26.4 %collective-permute-start.28 = (bf16[192,512]{1,0:T(8,128)(2,1)S(1)}, bf16[192,512]{1,0:T(8,128)(2,1)S(1)}, u32[]{:S(2)}, u32[]{:S(2)}) collective-permute-start(bf16[192,512]{1,0:T(8,128)(2,1)S(1)} %get-tuple-element.54), channel_id=1, source_target_pairs={{0,3},{1,2},{2,1},{3,0},{4,7},{5,6},{6,5},{7,4},{8,11},{9,10},{10,... | collective-permute-start | bytes 589832 | tf_op jit(solution)/shard_map/ppermute | solution.py:272
  161.2 26.8 %collective-permute-start.29 = (bf16[192,512]{1,0:T(8,128)(2,1)S(1)}, bf16[192,512]{1,0:T(8,128)(2,1)S(1)}, u32[]{:S(2)}, u32[]{:S(2)}) collective-permute-start(bf16[192,512]{1,0:T(8,128)(2,1)S(1)} %get-tuple-element.55), channel_id=1, source_target_pairs={{0,1},{1,0},{2,3},{3,2},{4,5},{5,4},{6,7},{7,6},{8,9},{9,8},{10,11... | collective-permute-start | bytes 589832 | tf_op jit(solution)/shard_map/ppermute | solution.py:272
  164.1 24.0 %collective-permute-start.16 = (bf16[192,512]{1,0:T(8,128)(2,1)S(1)}, bf16[192,512]{1,0:T(8,128)(2,1)S(1)}, u32[]{:S(2)}, u32[]{:S(2)}) collective-permute-start(bf16[192,512]{1,0:T(8,128)(2,1)S(1)} %get-tuple-element.48.refs_8_), channel_id=1, source_target_pairs={{0,4},{1,5},{2,6},{3,7},{4,0},{5,1},{6,2},{7,3},{8,12},{9,13},{10,... | collective-permute-start | bytes 589832 | tf_op jit(solution)/shard_map/ppermute | solution.py:272
  173.1 23.1 %collective-permute-start.31 = (bf16[192,512]{1,0:T(8,128)(2,1)S(1)}, bf16[192,512]{1,0:T(8,128)(2,1)S(1)}, u32[]{:S(2)}, u32[]{:S(2)}) collective-permute-start(bf16[192,512]{1,0:T(8,128)(2,1)S(1)} %get-tuple-element.59), channel_id=1, source_target_pairs={{0,4},{1,5},{2,6},{3,7},{4,0},{5,1},{6,2},{7,3},{8,12},{9,13},{10,... | collective-permute-start | bytes 589832 | tf_op jit(solution)/shard_map/ppermute | solution.py:272
  184.1 24.3 %collective-permute-start.32 = (bf16[192,512]{1,0:T(8,128)(2,1)S(1)}, bf16[192,512]{1,0:T(8,128)(2,1)S(1)}, u32[]{:S(2)}, u32[]{:S(2)}) collective-permute-start(bf16[192,512]{1,0:T(8,128)(2,1)S(1)} %get-tuple-element.60), channel_id=1, source_target_pairs={{0,5},{1,4},{2,7},{3,6},{4,1},{5,0},{6,3},{7,2},{8,13},{9,12},{10,... | collective-permute-start | bytes 589832 | tf_op jit(solution)/shard_map/ppermute | solution.py:272
  184.1 26.0 %collective-permute-start.33 = (bf16[192,512]{1,0:T(8,128)(2,1)S(1)}, bf16[192,512]{1,0:T(8,128)(2,1)S(1)}, u32[]{:S(2)}, u32[]{:S(2)}) collective-permute-start(bf16[192,512]{1,0:T(8,128)(2,1)S(1)} %get-tuple-element.61), channel_id=1, source_target_pairs={{0,2},{1,3},{2,0},{3,1},{4,6},{5,7},{6,4},{7,5},{8,10},{9,11},{10,... | collective-permute-start | bytes 589832 | tf_op jit(solution)/shard_map/ppermute | solution.py:272
  188.0 27.0 %collective-permute-start.34 = (bf16[192,512]{1,0:T(8,128)(2,1)S(1)}, bf16[192,512]{1,0:T(8,128)(2,1)S(1)}, u32[]{:S(2)}, u32[]{:S(2)}) collective-permute-start(bf16[192,512]{1,0:T(8,128)(2,1)S(1)} %get-tuple-element.62), channel_id=1, source_target_pairs={{0,7},{1,6},{2,5},{3,4},{4,3},{5,2},{6,1},{7,0},{8,15},{9,14},{10,... | collective-permute-start | bytes 589832 | tf_op jit(solution)/shard_map/ppermute | solution.py:272
  188.1 29.8 %collective-permute-start.35 = (bf16[192,512]{1,0:T(8,128)(2,1)S(1)}, bf16[192,512]{1,0:T(8,128)(2,1)S(1)}, u32[]{:S(2)}, u32[]{:S(2)}) collective-permute-start(bf16[192,512]{1,0:T(8,128)(2,1)S(1)} %get-tuple-element.63), channel_id=1, source_target_pairs={{0,6},{1,7},{2,4},{3,5},{4,2},{5,3},{6,0},{7,1},{8,14},{9,15},{10,... | collective-permute-start | bytes 589832 | tf_op jit(solution)/shard_map/ppermute | solution.py:272
  196.2 21.7 %collective-permute-start.36 = (bf16[192,512]{1,0:T(8,128)(2,1)S(1)}, bf16[192,512]{1,0:T(8,128)(2,1)S(1)}, u32[]{:S(2)}, u32[]{:S(2)}) collective-permute-start(bf16[192,512]{1,0:T(8,128)(2,1)S(1)} %get-tuple-element.64), channel_id=1, source_target_pairs={{0,3},{1,2},{2,1},{3,0},{4,7},{5,6},{6,5},{7,4},{8,11},{9,10},{10,... | collective-permute-start | bytes 589832 | tf_op jit(solution)/shard_map/ppermute | solution.py:272
  (11 other events, 162.0 us)

commit v6 on v5

--- a/solution.py
+++ b/solution.py
@@ -218,16 +218,21 @@
 
 def unpacked(me, grads, places, q_lanes):
     chunks, ways = len(grads), len(places)
-    tokens = grads[0][0].shape[0]
+    tokens = grads[0][0].shape[-2]
     lanes = (q_lanes, HD, HD)
+    counts = [len(blocks) for blocks in grads]
 
     def kernel(me_ref, *refs):
-        ins, outs = refs[: chunks * ways], refs[chunks * ways :]
+        outs = refs[sum(counts) :]
         for c in range(chunks):
-            for k, block in zip(places, ins[c * ways : (c + 1) * ways]):
+            ins = refs[sum(counts[:c]) : sum(counts[: c + 1])]
+            for n in range(ways):
+                block = ins[n] if len(ins) > 1 else ins[0].at[n]
+                place = me_ref[0] ^ places[n] if len(ins) > 1 else n
                 first = 0
                 for out, width in zip(outs, lanes):
-                    at = pl.multiple_of(((me_ref[0] ^ k) * chunks + c) * width, width)
+                    at = (place * chunks + c) * width
+                    at = at if isinstance(at, int) else pl.multiple_of(at, width)
                     out[:, pl.ds(at, width)] = block[:, first : first + width]
                     first += width
 
@@ -247,23 +252,27 @@
     return on_chip(kernel, me, blocks, [(group, lanes), (WINDOW, lanes)], "gathered")
 
 
-def settled(me, dq, own, returned, ways, places, earlier=()):
+def settled(me, dq, own, returned, ways, places=None):
     group, q_lanes = dq.shape
     tokens = group // ways
+    total_lanes = q_lanes + 2 * HD
 
     def kernel(me_ref, dq_ref, own_ref, back_ref, *refs):
-        outs, total = refs[:-1], refs[-1]
         cut = group - WINDOW
+        total = refs[-1] if places else refs[0].at[:, q_lanes:]
         total[:cut, :] = own_ref[:cut, :].astype(jnp.bfloat16)
         total[cut:, :] = (own_ref[cut:, :] + back_ref[...].astype(jnp.float32)).astype(jnp.bfloat16)
-        for k, out in zip(places, outs):
+        if not places:
+            refs[0][:, :q_lanes] = dq_ref[...]
+            return
+        for k, out in zip(places, refs):
             rows = partner_rows(me_ref, k, tokens)
             out[:, :q_lanes] = dq_ref[rows, :]
             out[:, q_lanes:] = total[rows, :]
 
-    shapes = [(tokens, q_lanes + 2 * HD)] * len(places)
-    scratch = [pltpu.VMEM((group, 2 * HD), jnp.bfloat16)]
-    return on_chip(kernel, me, (dq, own, returned), shapes, "settled", scratch, earlier)
+    shapes = [(tokens, total_lanes)] * ways if places else [(group, total_lanes)]
+    scratch = [pltpu.VMEM((group, 2 * HD), jnp.bfloat16)] if places else []
+    return on_chip(kernel, me, (dq, own, returned), shapes, "settled", scratch)
 
 
 def exchanged(blocks, places):
@@ -283,10 +292,8 @@
     q_lanes = per_group * HD
     group_first = lax.axis_index("seq") * group
     me = jnp.stack([lax.axis_index("head"), group_first]).astype(jnp.int32)
-    half, quarter = ways // 2, ways // 4
-    early = [*range(half, half + quarter), *range(quarter, half, 2)]
-    late = [k for k in [*range(ways - 1, 0, -1), 0] if k not in early]
-    places = early + late
+    places = list(range(ways))
+    late = places[ways - ways // 4 :]
 
     came = exchanged(packed(me, (keys, values), ways, places), places)
     kv, tail = gathered(me, came, places)
@@ -301,19 +308,17 @@
         came = exchanged(sent, places)
         if parts:
             dq, own, _ = parts[-1]
-            firsts.append(settled(me, dq, own, returned[-1], ways, early))
-        earlier = [firsts[-1][0]] if firsts else []
+            firsts += settled(me, dq, own, returned[-1], ways)
+        earlier = firsts[-1:]
         parts.append(attend(me, doc_lengths, came, places, halo, kv, c, kv_local, earlier))
         returned.append(passed_along(parts[-1][2], "seq", -1))
 
     grads = []
-    for c, (dq, own, _) in enumerate(parts):
-        if c < kv_local - 1:
-            rest = settled(me, dq, own, returned[c], ways, late, [parts[c + 1][0]])
-            sent = [*firsts[c], *rest]
-        else:
-            sent = settled(me, dq, own, returned[c], ways, places)
-        grads.append(exchanged(sent, places))
+    for rows in firsts:
+        sent = rows.reshape(ways, tokens, rows.shape[1])
+        grads.append([lax.all_to_all(sent, "head", split_axis=0, concat_axis=0, tiled=True)])
+    dq, own, _ = parts[-1]
+    grads.append(exchanged(settled(me, dq, own, returned[-1], ways, places), places))
     return unpacked(me, grads, places, q_lanes)
 
 

time: 223 us -> 266 us (1.19); the launches traced: 221 us -> 267 us
  waiting for transfers between devices: 96.2 us -> 172 us
  starting transfers between devices: 77.8 us -> 45.3 us
    ppermute x35 -> x28, waiting for transfers between devices: 95.2 us -> 145 us  [exchanged(): lax.ppermute(block, 'head', [(i, i ^ k) for i in range(ways)])]
    ppermute x35 -> x28, starting transfers between devices: 70.7 us -> 33.8 us  [exchanged(): lax.ppermute(block, 'head', [(i, i ^ k) for i in range(ways)])]
    ppermute x3, waiting for transfers between devices: 0.96 us -> 26.6 us  [passed_along(): return lax.ppermute(shard, axis, pairs)]
    all_to_all x0 -> x1, starting transfers between devices: none -> 4.54 us  [local(): lax.all_to_all(sent, 'head', split_axis=0, concat_axis=0, tiled=True)]
    pallas_call x22 -> x21, Pallas kernels: 15.9 us -> 15.9 us  [on_chip(): pl.pallas_call(body, out_shape=outs, in_specs=[SMEM] + [VMEM] * (len(earl...]
  transfers between devices with their start and end apart: 38 -> 32, of which waited for: 18 -> 22; matrix products, arithmetic and copies ran while one was open for 0% -> 0% of each run, Pallas kernels for 5% -> 9%
where the time goes in v6:
time: 266 us; the launch traced here: 267 us
  waiting for transfers between devices  172 us (65%)
  starting transfers between devices  45.3 us (17%)
  Pallas kernels  45.1 us (17%)
  local copies, waits for them, and re-layouts  3.48 us (1%)
    ppermute x28, waiting for transfers between devices, exchanged(): lax.ppermute(block, 'head', [(i, i ^ k) for i in range(ways)])  145 us
    ppermute x28, starting transfers between devices, exchanged(): lax.ppermute(block, 'head', [(i, i ^ k) for i in range(ways)])  33.8 us
    pallas_call x2, Pallas kernels, attend(): pl.pallas_call(functools.partial(attend_kernel, per_group, places, chunk,...  29.2 us
    ppermute x3, waiting for transfers between devices, passed_along(): return lax.ppermute(shard, axis, pairs)  26.6 us
    pallas_call x21, Pallas kernels, on_chip(): pl.pallas_call(body, out_shape=outs, in_specs=[SMEM] + [VMEM] * (len(earl...  15.9 us
    ppermute x3, starting transfers between devices, passed_along(): return lax.ppermute(shard, axis, pairs)  6.96 us
  transfers between devices with their start and end apart: 32, of which 22 were waited for; matrix products, arithmetic and copies ran while one was open for 0% of the time, Pallas kernels for 9%

profile of v6, /device:TPU:13, one launch (start us, length us, event | category | flops | bytes accessed | tf_op | source)
XLA Modules:
  0.0 267.0 jit_solution(4667763866009688198)
XLA Ops:
  6.2 2.3 collective-permute-start.3
  10.2 6.5 %collective-permute-done.1.refs_2_.refs_0_ = bf16[192,512]{1,0:T(8,128)(2,1)S(1)} collective-permute-done((bf16[192,512]{1,0:T(8,128)(2,1)S(1)}, bf16[192,512]{1,0:T(8,128)(2,1)S(1)}, u32[]{:S(2)}, u32[]{:S(2)}) %collective-permute-start.1) | collective-permute-done | bytes 196640 | tf_op jit(solution)/shard_map/ppermute | solution.py:281
  18.2 2.8 %collective-permute-done.2.refs_3_.refs_0_ = bf16[192,512]{1,0:T(8,128)(2,1)S(1)} collective-permute-done((bf16[192,512]{1,0:T(8,128)(2,1)S(1)}, bf16[192,512]{1,0:T(8,128)(2,1)S(1)}, u32[]{:S(2)}, u32[]{:S(2)}) %collective-permute-start.2) | collective-permute-done | bytes 196640 | tf_op jit(solution)/shard_map/ppermute | solution.py:281
  21.0 12.7 %collective-permute-done.4.refs_5_.refs_0_ = bf16[192,512]{1,0:T(8,128)(2,1)S(1)} collective-permute-done((bf16[192,512]{1,0:T(8,128)(2,1)S(1)}, bf16[192,512]{1,0:T(8,128)(2,1)S(1)}, u32[]{:S(2)}, u32[]{:S(2)}) %collective-permute-start.4) | collective-permute-done | bytes 196640 | tf_op jit(solution)/shard_map/ppermute | solution.py:281
  33.8 4.2 %collective-permute-done.5.refs_6_.refs_0_ = bf16[192,512]{1,0:T(8,128)(2,1)S(1)} collective-permute-done((bf16[192,512]{1,0:T(8,128)(2,1)S(1)}, bf16[192,512]{1,0:T(8,128)(2,1)S(1)}, u32[]{:S(2)}, u32[]{:S(2)}) %collective-permute-start.5) | collective-permute-done | bytes 196640 | tf_op jit(solution)/shard_map/ppermute | solution.py:281
  38.0 4.3 %collective-permute-done.6.refs_7_.refs_0_ = bf16[192,512]{1,0:T(8,128)(2,1)S(1)} collective-permute-done((bf16[192,512]{1,0:T(8,128)(2,1)S(1)}, bf16[192,512]{1,0:T(8,128)(2,1)S(1)}, u32[]{:S(2)}, u32[]{:S(2)}) %collective-permute-start.6) | collective-permute-done | bytes 196640 | tf_op jit(solution)/shard_map/ppermute | solution.py:281
  43.0 3.1 %collective-permute-start.7 = (bf16[1024,512]{1,0:T(8,128)(2,1)S(1)}, bf16[1024,512]{1,0:T(8,128)(2,1)S(1)}, u32[]{:S(2)}, u32[]{:S(2)}) collective-permute-start(bf16[1024,512]{1,0:T(8,128)(2,1)S(1)} %get-tuple-element.35), channel_id=1, source_target_pairs={{0,8},{8,16},{16,24},{1,9},{9,17},{17,25},{2,10},{10,18},{18,26},{... | collective-permute-start | bytes 3145736 | tf_op jit(solution)/shard_map/ppermute | solution.py:29
  57.8 6.0 %collective-permute-done.10.refs_3_.refs_0_ = bf16[192,512]{1,0:T(8,128)(2,1)S(1)} collective-permute-done((bf16[192,512]{1,0:T(8,128)(2,1)S(1)}, bf16[192,512]{1,0:T(8,128)(2,1)S(1)}, u32[]{:S(2)}, u32[]{:S(2)}) %collective-permute-start.10) | collective-permute-done | bytes 196640 | tf_op jit(solution)/shard_map/ppermute | solution.py:281
  65.6 12.2 %collective-permute-done.12.refs_5_.refs_0_ = bf16[192,512]{1,0:T(8,128)(2,1)S(1)} collective-permute-done((bf16[192,512]{1,0:T(8,128)(2,1)S(1)}, bf16[192,512]{1,0:T(8,128)(2,1)S(1)}, u32[]{:S(2)}, u32[]{:S(2)}) %collective-permute-start.12) | collective-permute-done | bytes 196640 | tf_op jit(solution)/shard_map/ppermute | solution.py:281
  77.8 6.3 %collective-permute-done.13.refs_6_ = bf16[192,512]{1,0:T(8,128)(2,1)S(1)} collective-permute-done((bf16[192,512]{1,0:T(8,128)(2,1)S(1)}, bf16[192,512]{1,0:T(8,128)(2,1)S(1)}, u32[]{:S(2)}, u32[]{:S(2)}) %collective-permute-start.13) | collective-permute-done | bytes 196640 | tf_op jit(solution)/shard_map/ppermute | solution.py:281
  84.1 4.2 %collective-permute-done.14.refs_7_ = bf16[192,512]{1,0:T(8,128)(2,1)S(1)} collective-permute-done((bf16[192,512]{1,0:T(8,128)(2,1)S(1)}, bf16[192,512]{1,0:T(8,128)(2,1)S(1)}, u32[]{:S(2)}, u32[]{:S(2)}) %collective-permute-start.14) | collective-permute-done | bytes 196640 | tf_op jit(solution)/shard_map/ppermute | solution.py:281
  88.3 14.6 %attend.2 = (bf16[1536,256]{1,0:T(8,128)(2,1)S(1)}, f32[1536,256]{1,0:T(8,128)S(1)}, bf16[1024,256]{1,0:T(8,128)(2,1)S(1)}) custom-call(s32[2]{0:T(128)S(1)} %pad_add_fusion.me_ref, s32[16]{0:T(128)S(1)} %copy-done.18, bf16[1024,512]{1,0:T(8,128)(2,1)S(1)} %collective-permute-done.7.halo_ref, bf16[1536,512]{1,0:T(8,128)(2,1)S(1)} %get-tuple-element.36.kv_ref, ...), custom_call_target="tpu_custom_call" | custom-call | flops 5033164800 | bytes 4718592 | tf_op jit(solution)/shard_map/attend/pallas_call | solution.py:169
  103.0 1.9 collective-permute-start.15
  104.9 13.1 %collective-permute-done.15.refs_2_ = bf16[1024,256]{1,0:T(8,128)(2,1)S(1)} collective-permute-done((bf16[1024,256]{1,0:T(8,128)(2,1)S(1)}, bf16[1024,256]{1,0:T(8,128)(2,1)S(1)}, u32[]{:S(2)}, u32[]{:S(2)}) %collective-permute-start.15) | collective-permute-done | bytes 524320 | tf_op jit(solution)/shard_map/ppermute | solution.py:29
  119.8 4.5 %all-to-all-start = ((bf16[8,192,512]{2,1,0:T(8,128)(2,1)}), bf16[8,192,512]{2,1,0:T(8,128)(2,1)}, u32[]{:S(2)}, u32[]{:S(2)}) async-start(bf16[8,192,512]{2,1,0:T(8,128)(2,1)} %bitcast.3), calls=%async_computation | async-start | bytes 3145728 | tf_op jit(solution)/shard_map/all_to_all | solution.py:319
  135.1 20.3 %collective-permute-done.17.refs_2_ = bf16[192,512]{1,0:T(8,128)(2,1)S(1)} collective-permute-done((bf16[192,512]{1,0:T(8,128)(2,1)S(1)}, bf16[192,512]{1,0:T(8,128)(2,1)S(1)}, u32[]{:S(2)}, u32[]{:S(2)}) %collective-permute-start.17) | collective-permute-done | bytes 196640 | tf_op jit(solution)/shard_map/ppermute | solution.py:281
  155.3 3.2 %collective-permute-start.22 = (bf16[192,512]{1,0:T(8,128)(2,1)S(1)}, bf16[192,512]{1,0:T(8,128)(2,1)S(1)}, u32[]{:S(2)}, u32[]{:S(2)}) collective-permute-start(bf16[192,512]{1,0:T(8,128)(2,1)S(1)} %packed.33), channel_id=1, source_target_pairs={{0,7},{1,6},{2,5},{3,4},{4,3},{5,2},{6,1},{7,0},{8,15},{9,14},{10,... | collective-permute-start | bytes 589832 | tf_op jit(solution)/shard_map/ppermute | solution.py:281
  159.5 20.1 %collective-permute-done.19.refs_4_ = bf16[192,512]{1,0:T(8,128)(2,1)S(1)} collective-permute-done((bf16[192,512]{1,0:T(8,128)(2,1)S(1)}, bf16[192,512]{1,0:T(8,128)(2,1)S(1)}, u32[]{:S(2)}, u32[]{:S(2)}) %collective-permute-start.19) | collective-permute-done | bytes 196640 | tf_op jit(solution)/shard_map/ppermute | solution.py:281
  179.6 4.2 %collective-permute-done.20.refs_5_ = bf16[192,512]{1,0:T(8,128)(2,1)S(1)} collective-permute-done((bf16[192,512]{1,0:T(8,128)(2,1)S(1)}, bf16[192,512]{1,0:T(8,128)(2,1)S(1)}, u32[]{:S(2)}, u32[]{:S(2)}) %collective-permute-start.20) | collective-permute-done | bytes 196640 | tf_op jit(solution)/shard_map/ppermute | solution.py:281
  183.8 5.7 %collective-permute-done.21.refs_6_ = bf16[192,512]{1,0:T(8,128)(2,1)S(1)} collective-permute-done((bf16[192,512]{1,0:T(8,128)(2,1)S(1)}, bf16[192,512]{1,0:T(8,128)(2,1)S(1)}, u32[]{:S(2)}, u32[]{:S(2)}) %collective-permute-start.21) | collective-permute-done | bytes 196640 | tf_op jit(solution)/shard_map/ppermute | solution.py:281
  189.5 4.6 %collective-permute-done.22.refs_7_ = bf16[192,512]{1,0:T(8,128)(2,1)S(1)} collective-permute-done((bf16[192,512]{1,0:T(8,128)(2,1)S(1)}, bf16[192,512]{1,0:T(8,128)(2,1)S(1)}, u32[]{:S(2)}, u32[]{:S(2)}) %collective-permute-start.22) | collective-permute-done | bytes 196640 | tf_op jit(solution)/shard_map/ppermute | solution.py:281
  194.1 14.6 %attend.3 = (bf16[1536,256]{1,0:T(8,128)(2,1)S(1)}, f32[1536,256]{1,0:T(8,128)S(1)}, bf16[1024,256]{1,0:T(8,128)(2,1)S(1)}) custom-call(s32[2]{0:T(128)S(1)} %pad_add_fusion.me_ref, s32[16]{0:T(128)S(1)} %copy-done.18, bf16[1024,512]{1,0:T(8,128)(2,1)S(1)} %copy-done.17, bf16[1536,512]{1,0:T(8,128)(2,1)S(1)} %copy-done.15, ...), custom_call_target="tpu_custom_call" | custom-call | flops 5033164800 | bytes 4718592 | tf_op jit(solution)/shard_map/attend/pallas_call | solution.py:169
  208.7 1.9 collective-permute-start.23
  210.7 13.5 %collective-permute-done.23.refs_2_ = bf16[1024,256]{1,0:T(8,128)(2,1)S(1)} collective-permute-done((bf16[1024,256]{1,0:T(8,128)(2,1)S(1)}, bf16[1024,256]{1,0:T(8,128)(2,1)S(1)}, u32[]{:S(2)}, u32[]{:S(2)}) %collective-permute-start.23) | collective-permute-done | bytes 524320 | tf_op jit(solution)/shard_map/ppermute | solution.py:29
  227.6 2.7 %collective-permute-start.28 = (bf16[192,512]{1,0:T(8,128)(2,1)S(1)}, bf16[192,512]{1,0:T(8,128)(2,1)S(1)}, u32[]{:S(2)}, u32[]{:S(2)}) collective-permute-start(bf16[192,512]{1,0:T(8,128)(2,1)S(1)} %get-tuple-element.48), channel_id=1, source_target_pairs={{0,5},{1,4},{2,7},{3,6},{4,1},{5,0},{6,3},{7,2},{8,13},{9,12},{10,... | collective-permute-start | bytes 589832 | tf_op jit(solution)/shard_map/ppermute | solution.py:281
  230.6 7.0 %collective-permute-done.25.refs_3_ = bf16[192,512]{1,0:T(8,128)(2,1)S(1)} collective-permute-done((bf16[192,512]{1,0:T(8,128)(2,1)S(1)}, bf16[192,512]{1,0:T(8,128)(2,1)S(1)}, u32[]{:S(2)}, u32[]{:S(2)}) %collective-permute-start.25) | collective-permute-done | bytes 196640 | tf_op jit(solution)/shard_map/ppermute | solution.py:281
  237.6 1.7 collective-permute-start.30
  239.4 2.5 collective-permute-done.26.refs_4_
  241.9 3.9 %collective-permute-done.28.refs_6_ = bf16[192,512]{1,0:T(8,128)(2,1)S(1)} collective-permute-done((bf16[192,512]{1,0:T(8,128)(2,1)S(1)}, bf16[192,512]{1,0:T(8,128)(2,1)S(1)}, u32[]{:S(2)}, u32[]{:S(2)}) %collective-permute-start.28) | collective-permute-done | bytes 196640 | tf_op jit(solution)/shard_map/ppermute | solution.py:281
  245.8 12.8 %collective-permute-done.29.refs_7_ = bf16[192,512]{1,0:T(8,128)(2,1)S(1)} collective-permute-done((bf16[192,512]{1,0:T(8,128)(2,1)S(1)}, bf16[192,512]{1,0:T(8,128)(2,1)S(1)}, u32[]{:S(2)}, u32[]{:S(2)}) %collective-permute-start.29) | collective-permute-done | bytes 196640 | tf_op jit(solution)/shard_map/ppermute | solution.py:281
  258.6 4.7 %collective-permute-done.30.refs_8_ = bf16[192,512]{1,0:T(8,128)(2,1)S(1)} collective-permute-done((bf16[192,512]{1,0:T(8,128)(2,1)S(1)}, bf16[192,512]{1,0:T(8,128)(2,1)S(1)}, u32[]{:S(2)}, u32[]{:S(2)}) %collective-permute-start.30) | collective-permute-done | bytes 196640 | tf_op jit(solution)/shard_map/ppermute | solution.py:281
  263.3 3.7 %unpacked.1 = (bf16[192,4096]{1,0:T(8,128)(2,1)}, bf16[192,2048]{1,0:T(8,128)(2,1)}, bf16[192,2048]{1,0:T(8,128)(2,1)}) custom-call(s32[2]{0:T(128)S(1)} %pad_add_fusion.me_ref, bf16[8,192,512]{2,1,0:T(8,128)(2,1)} %all-to-all-done.refs_0_, bf16[192,512]{1,0:T(8,128)(2,1)S(1)} %get-tuple-element.43.refs_1_, ...), custom_call_target="tpu_custom_call" | custom-call | bytes 6291456 | tf_op jit(solution)/shard_map/unpacked/pallas_call | solution.py:190
  (94 shorter events, 40.1 us)
Async XLA Ops:
  3.7 5.2 %collective-permute-start = (bf16[192,512]{1,0:T(8,128)(2,1)S(1)}, bf16[192,512]{1,0:T(8,128)(2,1)S(1)}, u32[]{:S(2)}, u32[]{:S(2)}) collective-permute-start(bf16[192,512]{1,0:T(8,128)(2,1)S(1)} %get-tuple-element.28), channel_id=1, source_target_pairs={{0,1},{1,0},{2,3},{3,2},{4,5},{5,4},{6,7},{7,6},{8,9},{9,8},{10,11... | collective-permute-start | bytes 589832 | tf_op jit(solution)/shard_map/ppermute | solution.py:281
  4.5 12.2 %collective-permute-start.1 = (bf16[192,512]{1,0:T(8,128)(2,1)S(1)}, bf16[192,512]{1,0:T(8,128)(2,1)S(1)}, u32[]{:S(2)}, u32[]{:S(2)}) collective-permute-start(bf16[192,512]{1,0:T(8,128)(2,1)S(1)} %get-tuple-element.29), channel_id=1, source_target_pairs={{0,2},{1,3},{2,0},{3,1},{4,6},{5,7},{6,4},{7,5},{8,10},{9,11},{10,... | collective-permute-start | bytes 589832 | tf_op jit(solution)/shard_map/ppermute | solution.py:281
  4.7 16.4 %collective-permute-start.2 = (bf16[192,512]{1,0:T(8,128)(2,1)S(1)}, bf16[192,512]{1,0:T(8,128)(2,1)S(1)}, u32[]{:S(2)}, u32[]{:S(2)}) collective-permute-start(bf16[192,512]{1,0:T(8,128)(2,1)S(1)} %get-tuple-element.30), channel_id=1, source_target_pairs={{0,3},{1,2},{2,1},{3,0},{4,7},{5,6},{6,5},{7,4},{8,11},{9,10},{10,... | collective-permute-start | bytes 589832 | tf_op jit(solution)/shard_map/ppermute | solution.py:281
  6.2 14.8 %collective-permute-start.3 = (bf16[192,512]{1,0:T(8,128)(2,1)S(1)}, bf16[192,512]{1,0:T(8,128)(2,1)S(1)}, u32[]{:S(2)}, u32[]{:S(2)}) collective-permute-start(bf16[192,512]{1,0:T(8,128)(2,1)S(1)} %get-tuple-element.31), channel_id=1, source_target_pairs={{0,4},{1,5},{2,6},{3,7},{4,0},{5,1},{6,2},{7,3},{8,12},{9,13},{10,... | collective-permute-start | bytes 589832 | tf_op jit(solution)/shard_map/ppermute | solution.py:281
  8.5 25.3 %collective-permute-start.4 = (bf16[192,512]{1,0:T(8,128)(2,1)S(1)}, bf16[192,512]{1,0:T(8,128)(2,1)S(1)}, u32[]{:S(2)}, u32[]{:S(2)}) collective-permute-start(bf16[192,512]{1,0:T(8,128)(2,1)S(1)} %get-tuple-element.32), channel_id=1, source_target_pairs={{0,5},{1,4},{2,7},{3,6},{4,1},{5,0},{6,3},{7,2},{8,13},{9,12},{10,... | collective-permute-start | bytes 589832 | tf_op jit(solution)/shard_map/ppermute | solution.py:281
  8.9 29.1 %collective-permute-start.5 = (bf16[192,512]{1,0:T(8,128)(2,1)S(1)}, bf16[192,512]{1,0:T(8,128)(2,1)S(1)}, u32[]{:S(2)}, u32[]{:S(2)}) collective-permute-start(bf16[192,512]{1,0:T(8,128)(2,1)S(1)} %get-tuple-element.33), channel_id=1, source_target_pairs={{0,6},{1,7},{2,4},{3,5},{4,2},{5,3},{6,0},{7,1},{8,14},{9,15},{10,... | collective-permute-start | bytes 589832 | tf_op jit(solution)/shard_map/ppermute | solution.py:281
  16.7 25.6 %collective-permute-start.6 = (bf16[192,512]{1,0:T(8,128)(2,1)S(1)}, bf16[192,512]{1,0:T(8,128)(2,1)S(1)}, u32[]{:S(2)}, u32[]{:S(2)}) collective-permute-start(bf16[192,512]{1,0:T(8,128)(2,1)S(1)} %get-tuple-element.34), channel_id=1, source_target_pairs={{0,7},{1,6},{2,5},{3,4},{4,3},{5,2},{6,1},{7,0},{8,15},{9,14},{10,... | collective-permute-start | bytes 589832 | tf_op jit(solution)/shard_map/ppermute | solution.py:281
  43.0 45.3 %collective-permute-start.7 = (bf16[1024,512]{1,0:T(8,128)(2,1)S(1)}, bf16[1024,512]{1,0:T(8,128)(2,1)S(1)}, u32[]{:S(2)}, u32[]{:S(2)}) collective-permute-start(bf16[1024,512]{1,0:T(8,128)(2,1)S(1)} %get-tuple-element.35), channel_id=1, source_target_pairs={{0,8},{8,16},{16,24},{1,9},{9,17},{17,25},{2,10},{10,18},{18,26},{... | collective-permute-start | bytes 3145736 | tf_op jit(solution)/shard_map/ppermute | solution.py:29
  46.7 7.8 %collective-permute-start.8 = (bf16[192,512]{1,0:T(8,128)(2,1)S(1)}, bf16[192,512]{1,0:T(8,128)(2,1)S(1)}, u32[]{:S(2)}, u32[]{:S(2)}) collective-permute-start(bf16[192,512]{1,0:T(8,128)(2,1)S(1)} %packed.19), channel_id=1, source_target_pairs={{0,1},{1,0},{2,3},{3,2},{4,5},{5,4},{6,7},{7,6},{8,9},{9,8},{10,11... | collective-permute-start | bytes 589832 | tf_op jit(solution)/shard_map/ppermute | solution.py:281
  48.5 7.6 %collective-permute-start.9 = (bf16[192,512]{1,0:T(8,128)(2,1)S(1)}, bf16[192,512]{1,0:T(8,128)(2,1)S(1)}, u32[]{:S(2)}, u32[]{:S(2)}) collective-permute-start(bf16[192,512]{1,0:T(8,128)(2,1)S(1)} %packed.20), channel_id=1, source_target_pairs={{0,2},{1,3},{2,0},{3,1},{4,6},{5,7},{6,4},{7,5},{8,10},{9,11},{10,... | collective-permute-start | bytes 589832 | tf_op jit(solution)/shard_map/ppermute | solution.py:281
  49.2 14.6 %collective-permute-start.10 = (bf16[192,512]{1,0:T(8,128)(2,1)S(1)}, bf16[192,512]{1,0:T(8,128)(2,1)S(1)}, u32[]{:S(2)}, u32[]{:S(2)}) collective-permute-start(bf16[192,512]{1,0:T(8,128)(2,1)S(1)} %packed.21), channel_id=1, source_target_pairs={{0,3},{1,2},{2,1},{3,0},{4,7},{5,6},{6,5},{7,4},{8,11},{9,10},{10,... | collective-permute-start | bytes 589832 | tf_op jit(solution)/shard_map/ppermute | solution.py:281
  51.5 14.1 %collective-permute-start.11 = (bf16[192,512]{1,0:T(8,128)(2,1)S(1)}, bf16[192,512]{1,0:T(8,128)(2,1)S(1)}, u32[]{:S(2)}, u32[]{:S(2)}) collective-permute-start(bf16[192,512]{1,0:T(8,128)(2,1)S(1)} %packed.22), channel_id=1, source_target_pairs={{0,4},{1,5},{2,6},{3,7},{4,0},{5,1},{6,2},{7,3},{8,12},{9,13},{10,... | collective-permute-start | bytes 589832 | tf_op jit(solution)/shard_map/ppermute | solution.py:281
  54.5 23.2 %collective-permute-start.12 = (bf16[192,512]{1,0:T(8,128)(2,1)S(1)}, bf16[192,512]{1,0:T(8,128)(2,1)S(1)}, u32[]{:S(2)}, u32[]{:S(2)}) collective-permute-start(bf16[192,512]{1,0:T(8,128)(2,1)S(1)} %packed.23), channel_id=1, source_target_pairs={{0,5},{1,4},{2,7},{3,6},{4,1},{5,0},{6,3},{7,2},{8,13},{9,12},{10,... | collective-permute-start | bytes 589832 | tf_op jit(solution)/shard_map/ppermute | solution.py:281
  56.1 27.9 %collective-permute-start.13 = (bf16[192,512]{1,0:T(8,128)(2,1)S(1)}, bf16[192,512]{1,0:T(8,128)(2,1)S(1)}, u32[]{:S(2)}, u32[]{:S(2)}) collective-permute-start(bf16[192,512]{1,0:T(8,128)(2,1)S(1)} %packed.24), channel_id=1, source_target_pairs={{0,6},{1,7},{2,4},{3,5},{4,2},{5,3},{6,0},{7,1},{8,14},{9,15},{10,... | collective-permute-start | bytes 589832 | tf_op jit(solution)/shard_map/ppermute | solution.py:281
  63.8 24.5 %collective-permute-start.14 = (bf16[192,512]{1,0:T(8,128)(2,1)S(1)}, bf16[192,512]{1,0:T(8,128)(2,1)S(1)}, u32[]{:S(2)}, u32[]{:S(2)}) collective-permute-start(bf16[192,512]{1,0:T(8,128)(2,1)S(1)} %packed.25), channel_id=1, source_target_pairs={{0,7},{1,6},{2,5},{3,4},{4,3},{5,2},{6,1},{7,0},{8,15},{9,14},{10,... | collective-permute-start | bytes 589832 | tf_op jit(solution)/shard_map/ppermute | solution.py:281
  103.0 15.0 %collective-permute-start.15 = (bf16[1024,256]{1,0:T(8,128)(2,1)S(1)}, bf16[1024,256]{1,0:T(8,128)(2,1)S(1)}, u32[]{:S(2)}, u32[]{:S(2)}) collective-permute-start(bf16[1024,256]{1,0:T(8,128)(2,1)S(1)} %get-tuple-element.39), channel_id=1, source_target_pairs={{8,0},{16,8},{24,16},{9,1},{17,9},{25,17},{10,2},{18,10},{26,18},{... | collective-permute-start | bytes 1572872 | tf_op jit(solution)/shard_map/ppermute | solution.py:29
  119.8 143.5 %all-to-all-start = ((bf16[8,192,512]{2,1,0:T(8,128)(2,1)}), bf16[8,192,512]{2,1,0:T(8,128)(2,1)}, u32[]{:S(2)}, u32[]{:S(2)}) async-start(bf16[8,192,512]{2,1,0:T(8,128)(2,1)} %bitcast.3), calls=%async_computation | async-start | bytes 3145728 | tf_op jit(solution)/shard_map/all_to_all | solution.py:319
  125.0 9.4 %collective-permute-start.16 = (bf16[192,512]{1,0:T(8,128)(2,1)S(1)}, bf16[192,512]{1,0:T(8,128)(2,1)S(1)}, u32[]{:S(2)}, u32[]{:S(2)}) collective-permute-start(bf16[192,512]{1,0:T(8,128)(2,1)S(1)} %packed.27), channel_id=1, source_target_pairs={{0,1},{1,0},{2,3},{3,2},{4,5},{5,4},{6,7},{7,6},{8,9},{9,8},{10,11... | collective-permute-start | bytes 589832 | tf_op jit(solution)/shard_map/ppermute | solution.py:281
  126.7 28.6 %collective-permute-start.17 = (bf16[192,512]{1,0:T(8,128)(2,1)S(1)}, bf16[192,512]{1,0:T(8,128)(2,1)S(1)}, u32[]{:S(2)}, u32[]{:S(2)}) collective-permute-start(bf16[192,512]{1,0:T(8,128)(2,1)S(1)} %packed.28), channel_id=1, source_target_pairs={{0,2},{1,3},{2,0},{3,1},{4,6},{5,7},{6,4},{7,5},{8,10},{9,11},{10,... | collective-permute-start | bytes 589832 | tf_op jit(solution)/shard_map/ppermute | solution.py:281
  127.4 32.1 %collective-permute-start.18 = (bf16[192,512]{1,0:T(8,128)(2,1)S(1)}, bf16[192,512]{1,0:T(8,128)(2,1)S(1)}, u32[]{:S(2)}, u32[]{:S(2)}) collective-permute-start(bf16[192,512]{1,0:T(8,128)(2,1)S(1)} %packed.29), channel_id=1, source_target_pairs={{0,3},{1,2},{2,1},{3,0},{4,7},{5,6},{6,5},{7,4},{8,11},{9,10},{10,... | collective-permute-start | bytes 589832 | tf_op jit(solution)/shard_map/ppermute | solution.py:281
  129.7 49.9 %collective-permute-start.19 = (bf16[192,512]{1,0:T(8,128)(2,1)S(1)}, bf16[192,512]{1,0:T(8,128)(2,1)S(1)}, u32[]{:S(2)}, u32[]{:S(2)}) collective-permute-start(bf16[192,512]{1,0:T(8,128)(2,1)S(1)} %packed.30), channel_id=1, source_target_pairs={{0,4},{1,5},{2,6},{3,7},{4,0},{5,1},{6,2},{7,3},{8,12},{9,13},{10,... | collective-permute-start | bytes 589832 | tf_op jit(solution)/shard_map/ppermute | solution.py:281
  131.8 52.0 %collective-permute-start.20 = (bf16[192,512]{1,0:T(8,128)(2,1)S(1)}, bf16[192,512]{1,0:T(8,128)(2,1)S(1)}, u32[]{:S(2)}, u32[]{:S(2)}) collective-permute-start(bf16[192,512]{1,0:T(8,128)(2,1)S(1)} %packed.31), channel_id=1, source_target_pairs={{0,5},{1,4},{2,7},{3,6},{4,1},{5,0},{6,3},{7,2},{8,13},{9,12},{10,... | collective-permute-start | bytes 589832 | tf_op jit(solution)/shard_map/ppermute | solution.py:281
  134.4 55.2 %collective-permute-start.21 = (bf16[192,512]{1,0:T(8,128)(2,1)S(1)}, bf16[192,512]{1,0:T(8,128)(2,1)S(1)}, u32[]{:S(2)}, u32[]{:S(2)}) collective-permute-start(bf16[192,512]{1,0:T(8,128)(2,1)S(1)} %packed.32), channel_id=1, source_target_pairs={{0,6},{1,7},{2,4},{3,5},{4,2},{5,3},{6,0},{7,1},{8,14},{9,15},{10,... | collective-permute-start | bytes 589832 | tf_op jit(solution)/shard_map/ppermute | solution.py:281
  155.3 38.8 %collective-permute-start.22 = (bf16[192,512]{1,0:T(8,128)(2,1)S(1)}, bf16[192,512]{1,0:T(8,128)(2,1)S(1)}, u32[]{:S(2)}, u32[]{:S(2)}) collective-permute-start(bf16[192,512]{1,0:T(8,128)(2,1)S(1)} %packed.33), channel_id=1, source_target_pairs={{0,7},{1,6},{2,5},{3,4},{4,3},{5,2},{6,1},{7,0},{8,15},{9,14},{10,... | collective-permute-start | bytes 589832 | tf_op jit(solution)/shard_map/ppermute | solution.py:281
  208.7 15.4 %collective-permute-start.23 = (bf16[1024,256]{1,0:T(8,128)(2,1)S(1)}, bf16[1024,256]{1,0:T(8,128)(2,1)S(1)}, u32[]{:S(2)}, u32[]{:S(2)}) collective-permute-start(bf16[1024,256]{1,0:T(8,128)(2,1)S(1)} %get-tuple-element.42), channel_id=1, source_target_pairs={{8,0},{16,8},{24,16},{9,1},{17,9},{25,17},{10,2},{18,10},{26,18},{... | collective-permute-start | bytes 1572872 | tf_op jit(solution)/shard_map/ppermute | solution.py:29
  225.0 5.3 %collective-permute-start.24 = (bf16[192,512]{1,0:T(8,128)(2,1)S(1)}, bf16[192,512]{1,0:T(8,128)(2,1)S(1)}, u32[]{:S(2)}, u32[]{:S(2)}) collective-permute-start(bf16[192,512]{1,0:T(8,128)(2,1)S(1)} %get-tuple-element.44), channel_id=1, source_target_pairs={{0,1},{1,0},{2,3},{3,2},{4,5},{5,4},{6,7},{7,6},{8,9},{9,8},{10,11... | collective-permute-start | bytes 589832 | tf_op jit(solution)/shard_map/ppermute | solution.py:281
  225.9 11.8 %collective-permute-start.25 = (bf16[192,512]{1,0:T(8,128)(2,1)S(1)}, bf16[192,512]{1,0:T(8,128)(2,1)S(1)}, u32[]{:S(2)}, u32[]{:S(2)}) collective-permute-start(bf16[192,512]{1,0:T(8,128)(2,1)S(1)} %get-tuple-element.45), channel_id=1, source_target_pairs={{0,2},{1,3},{2,0},{3,1},{4,6},{5,7},{6,4},{7,5},{8,10},{9,11},{10,... | collective-permute-start | bytes 589832 | tf_op jit(solution)/shard_map/ppermute | solution.py:281
  225.9 16.0 %collective-permute-start.26 = (bf16[192,512]{1,0:T(8,128)(2,1)S(1)}, bf16[192,512]{1,0:T(8,128)(2,1)S(1)}, u32[]{:S(2)}, u32[]{:S(2)}) collective-permute-start(bf16[192,512]{1,0:T(8,128)(2,1)S(1)} %get-tuple-element.46), channel_id=1, source_target_pairs={{0,3},{1,2},{2,1},{3,0},{4,7},{5,6},{6,5},{7,4},{8,11},{9,10},{10,... | collective-permute-start | bytes 589832 | tf_op jit(solution)/shard_map/ppermute | solution.py:281
  227.6 14.3 %collective-permute-start.27 = (bf16[192,512]{1,0:T(8,128)(2,1)S(1)}, bf16[192,512]{1,0:T(8,128)(2,1)S(1)}, u32[]{:S(2)}, u32[]{:S(2)}) collective-permute-start(bf16[192,512]{1,0:T(8,128)(2,1)S(1)} %get-tuple-element.47), channel_id=1, source_target_pairs={{0,4},{1,5},{2,6},{3,7},{4,0},{5,1},{6,2},{7,3},{8,12},{9,13},{10,... | collective-permute-start | bytes 589832 | tf_op jit(solution)/shard_map/ppermute | solution.py:281
  227.6 18.2 %collective-permute-start.28 = (bf16[192,512]{1,0:T(8,128)(2,1)S(1)}, bf16[192,512]{1,0:T(8,128)(2,1)S(1)}, u32[]{:S(2)}, u32[]{:S(2)}) collective-permute-start(bf16[192,512]{1,0:T(8,128)(2,1)S(1)} %get-tuple-element.48), channel_id=1, source_target_pairs={{0,5},{1,4},{2,7},{3,6},{4,1},{5,0},{6,3},{7,2},{8,13},{9,12},{10,... | collective-permute-start | bytes 589832 | tf_op jit(solution)/shard_map/ppermute | solution.py:281
  230.3 28.3 %collective-permute-start.29 = (bf16[192,512]{1,0:T(8,128)(2,1)S(1)}, bf16[192,512]{1,0:T(8,128)(2,1)S(1)}, u32[]{:S(2)}, u32[]{:S(2)}) collective-permute-start(bf16[192,512]{1,0:T(8,128)(2,1)S(1)} %get-tuple-element.49), channel_id=1, source_target_pairs={{0,6},{1,7},{2,4},{3,5},{4,2},{5,3},{6,0},{7,1},{8,14},{9,15},{10,... | collective-permute-start | bytes 589832 | tf_op jit(solution)/shard_map/ppermute | solution.py:281
  237.6 25.7 %collective-permute-start.30 = (bf16[192,512]{1,0:T(8,128)(2,1)S(1)}, bf16[192,512]{1,0:T(8,128)(2,1)S(1)}, u32[]{:S(2)}, u32[]{:S(2)}) collective-permute-start(bf16[192,512]{1,0:T(8,128)(2,1)S(1)} %get-tuple-element.50), channel_id=1, source_target_pairs={{0,7},{1,6},{2,5},{3,4},{4,3},{5,2},{6,1},{7,0},{8,15},{9,14},{10,... | collective-permute-start | bytes 589832 | tf_op jit(solution)/shard_map/ppermute | solution.py:281
  (19 other events, 477.7 us)

commit v7 on v6

--- a/solution.py
+++ b/solution.py
@@ -47,11 +47,9 @@
 
 
 def attend_kernel(
-    per_group, places, chunk, kv_local, me_ref, docs_ref, halo_ref, kv_ref, *refs
+    per_group, chunk, kv_local, me_ref, docs_ref, halo_ref, kv_ref, qd_ref,
+    dq_ref, own_ref, rim_ref, k_ext, v_ext, k_t, dk_ext, dv_ext, s_buf, dp_buf,
 ):
-    blocks, refs = refs[: len(places)], refs[-11:]
-    dq_ref, own_ref, rim_ref, qd_ref, k_ext, v_ext, k_t, dk_ext, dv_ext, s_buf, dp_buf = refs
-    gather_rows(me_ref, blocks, places, qd_ref)
     group = qd_ref.shape[0]
     reach = WINDOW // TK
     for ref, at in ((k_ext, chunk * HD), (v_ext, (kv_local + chunk) * HD)):
@@ -141,10 +139,9 @@
     own_ref[:, HD:] = dv_ext[WINDOW:, :]
 
 
-def attend(me, docs, qd_blocks, places, halo, own, chunk, kv_local, earlier):
+def attend(me, docs, qd, halo, own, chunk, kv_local):
     group = own.shape[0]
-    qd_lanes = qd_blocks[0].shape[1]
-    per_group = qd_lanes // (2 * HD)
+    per_group = qd.shape[1] // (2 * HD)
     ext = group + WINDOW
     wide = per_group * TQ
     span = WINDOW + TQ
@@ -156,7 +153,6 @@
         jax.ShapeDtypeStruct((WINDOW, 2 * HD), jnp.bfloat16),
     ]
     scratch = [
-        jax.ShapeDtypeStruct((group, qd_lanes), jnp.bfloat16),
         jax.ShapeDtypeStruct((ext, HD), jnp.bfloat16),
         jax.ShapeDtypeStruct((ext, HD), jnp.bfloat16),
         jax.ShapeDtypeStruct((ext // TK, HD, TK), jnp.bfloat16),
@@ -165,11 +161,11 @@
         jax.ShapeDtypeStruct((span, wide), jnp.float32),
         jax.ShapeDtypeStruct((span, wide), jnp.float32),
     ]
-    needed = array_bytes([halo, own, *qd_blocks, *earlier, *outs, *scratch])
+    needed = array_bytes([halo, own, qd, *outs, *scratch])
     return pl.pallas_call(
-        functools.partial(attend_kernel, per_group, places, chunk, kv_local),
+        functools.partial(attend_kernel, per_group, chunk, kv_local),
         out_shape=tuple(outs),
-        in_specs=[SMEM, SMEM] + [VMEM] * (2 + len(qd_blocks) + len(earlier)),
+        in_specs=[SMEM, SMEM] + [VMEM] * 3,
         out_specs=(VMEM,) * 3,
         scratch_shapes=[pltpu.VMEM(s.shape, s.dtype) for s in scratch],
         compiler_params=pltpu.CompilerParams(vmem_limit_bytes=needed + SPARE),
@@ -177,7 +173,7 @@
             flops=area * HD * 2 * 5, bytes_accessed=group * HD * 24, transcendentals=area
         ),
         name="attend",
-    )(me, docs, halo, own, *qd_blocks, *earlier)
+    )(me, docs, halo, own, qd)
 
 
 def on_chip(kernel, me, arrays, shapes, name, scratch=(), earlier=()):
@@ -199,20 +195,24 @@
     )(me, *earlier, *arrays)
 
 
-def packed(me, arrays, ways, places, chunk=0, chunks=1, earlier=()):
+def packed(me, arrays, ways, chunk=0, chunks=1, places=None, earlier=()):
     tokens = arrays[0].shape[0]
     lanes = [a.shape[1] // (ways * chunks) for a in arrays]
+    total = sum(lanes)
 
     def kernel(me_ref, *refs):
         ins, outs = refs[: len(arrays)], refs[len(arrays) :]
-        for k, out in zip(places, outs):
+        for n in range(ways):
+            out = outs[n] if places else outs[0].at[n]
+            place = me_ref[0] ^ places[n] if places else n
             first = 0
             for ref, width in zip(ins, lanes):
-                at = pl.multiple_of(((me_ref[0] ^ k) * chunks + chunk) * width, width)
+                at = (place * chunks + chunk) * width
+                at = pl.multiple_of(at, width) if places else at
                 out[:, first : first + width] = ref[:, pl.ds(at, width)]
                 first += width
 
-    shapes = [(tokens, sum(lanes))] * len(places)
+    shapes = [(tokens, total)] * ways if places else [(ways, tokens, total)]
     return on_chip(kernel, me, arrays, shapes, "packed", earlier=earlier)
 
 
@@ -240,16 +240,18 @@
     return on_chip(kernel, me, [g for blocks in grads for g in blocks], shapes, "unpacked")
 
 
-def gathered(me, blocks, places):
+def gathered(me, blocks, places, tail):
     tokens, lanes = blocks[0].shape
     group = len(places) * tokens
 
     def kernel(me_ref, *refs):
-        all_ref, tail_ref = refs[len(places) :]
-        gather_rows(me_ref, refs[: len(places)], places, all_ref)
-        tail_ref[...] = all_ref[group - WINDOW :, :]
-
-    return on_chip(kernel, me, blocks, [(group, lanes), (WINDOW, lanes)], "gathered")
+        ins, outs = refs[: len(places)], refs[len(places) :]
+        gather_rows(me_ref, ins, places, outs[0])
+        if tail:
+            outs[1][...] = outs[0][group - tail :, :]
+
+    shapes = [(group, lanes)] + ([(tail, lanes)] if tail else [])
+    return on_chip(kernel, me, blocks, shapes, "gathered")
 
 
 def settled(me, dq, own, returned, ways, places=None):
@@ -283,6 +285,10 @@
     ]
 
 
+def exchanged_at_once(sent):
+    return lax.all_to_all(sent, "head", split_axis=0, concat_axis=0, tiled=True)
+
+
 def local(queries, keys, values, grad_out, doc_lengths):
     ways = lax.axis_size("head")
     tokens = queries.shape[0]
@@ -293,32 +299,25 @@
     group_first = lax.axis_index("seq") * group
     me = jnp.stack([lax.axis_index("head"), group_first]).astype(jnp.int32)
     places = list(range(ways))
-    late = places[ways - ways // 4 :]
-
-    came = exchanged(packed(me, (keys, values), ways, places), places)
-    kv, tail = gathered(me, came, places)
+
+    came = exchanged(packed(me, (keys, values), ways, places=places), places)
+    kv, tail = gathered(me, came, places, WINDOW)
     halo = passed_along(tail, "seq", 1)
-
-    parts, returned, firsts = [], [], []
-    for c in range(kv_local):
-        sent = []
-        for k, before in zip(places, came):
-            earlier = [parts[-1][0]] if parts and k in late else [before] if k else []
-            sent += packed(me, (queries, grad_out), ways, [k], c, kv_local, earlier)
-        came = exchanged(sent, places)
-        if parts:
-            dq, own, _ = parts[-1]
-            firsts += settled(me, dq, own, returned[-1], ways)
-        earlier = firsts[-1:]
-        parts.append(attend(me, doc_lengths, came, places, halo, kv, c, kv_local, earlier))
-        returned.append(passed_along(parts[-1][2], "seq", -1))
+    sent = packed(me, (queries, grad_out), ways, 0, kv_local, places, [came[-1]])
+    qds = list(gathered(me, exchanged(sent, places), places, 0))
+    for c in range(1, kv_local):
+        sent = packed(me, (queries, grad_out), ways, c, kv_local, None, [qds[-1], halo])[0]
+        qds.append(exchanged_at_once(sent).reshape(group, 2 * q_lanes))
 
     grads = []
-    for rows in firsts:
-        sent = rows.reshape(ways, tokens, rows.shape[1])
-        grads.append([lax.all_to_all(sent, "head", split_axis=0, concat_axis=0, tiled=True)])
-    dq, own, _ = parts[-1]
-    grads.append(exchanged(settled(me, dq, own, returned[-1], ways, places), places))
+    for c, qd in enumerate(qds):
+        dq, own, rim = attend(me, doc_lengths, qd, halo, kv, c, kv_local)
+        returned = passed_along(rim, "seq", -1)
+        if c < kv_local - 1:
+            rows = settled(me, dq, own, returned, ways)[0]
+            grads.append([exchanged_at_once(rows.reshape(ways, tokens, rows.shape[1]))])
+        else:
+            grads.append(exchanged(settled(me, dq, own, returned, ways, places), places))
     return unpacked(me, grads, places, q_lanes)
 
 

time: 266 us -> 208 us (0.78); the launches traced: 267 us -> 206 us
  waiting for transfers between devices: 172 us -> 119 us
  Pallas kernels: 45.1 us -> 35.8 us
  local copies, waits for them, and re-layouts: 3.48 us -> 8.53 us
  starting transfers between devices: 45.3 us -> 42.3 us
    ppermute x28 -> x21, waiting for transfers between devices: 145 us -> 91.3 us  [exchanged(): lax.ppermute(block, 'head', [(i, i ^ k) for i in range(ways)])]
    ppermute x28 -> x21, starting transfers between devices: 33.8 us -> 22.8 us  [exchanged(): lax.ppermute(block, 'head', [(i, i ^ k) for i in range(ways)])]
    all_to_all x1 -> x2, starting transfers between devices: 4.54 us -> 11.4 us  [exchanged_at_once(): return lax.all_to_all(sent, 'head', split_axis=0, concat_axis=0, tiled=True)]
    unnamed x38 -> x22, local copies, waits for them, and re-layouts: 3.48 us -> 8.53 us
    pallas_call x21 -> x8, Pallas kernels: 15.9 us -> 11 us  [on_chip(): pl.pallas_call(body, out_shape=outs, in_specs=[SMEM] + [VMEM] * (len(earl...]
    pallas_call x2, Pallas kernels: 29.2 us -> 24.8 us  [attend(): pl.pallas_call(functools.partial(attend_kernel, per_group, chunk, kv_loca...]
  transfers between devices with their start and end apart: 32 -> 26, of which waited for: 22 -> 18; matrix products, arithmetic and copies ran while one was open for 0% -> 0% of each run, Pallas kernels for 9% -> 14%
where the time goes in v7:
time: 208 us; the launch traced here: 206 us
  waiting for transfers between devices  119 us (57%)
  starting transfers between devices  42.3 us (20%)
  Pallas kernels  35.8 us (17%)
  local copies, waits for them, and re-layouts  8.53 us (4%)
    ppermute x21, waiting for transfers between devices, exchanged(): lax.ppermute(block, 'head', [(i, i ^ k) for i in range(ways)])  91.3 us
    ppermute x3, waiting for transfers between devices, passed_along(): return lax.ppermute(shard, axis, pairs)  25.1 us
    pallas_call x2, Pallas kernels, attend(): pl.pallas_call(functools.partial(attend_kernel, per_group, chunk, kv_loca...  24.8 us
    ppermute x21, starting transfers between devices, exchanged(): lax.ppermute(block, 'head', [(i, i ^ k) for i in range(ways)])  22.8 us
    all_to_all x2, starting transfers between devices, exchanged_at_once(): return lax.all_to_all(sent, 'head', split_axis=0, concat_axis=0, tiled=True)  11.4 us
    pallas_call x8, Pallas kernels, on_chip(): pl.pallas_call(body, out_shape=outs, in_specs=[SMEM] + [VMEM] * (len(earl...  11 us
    unnamed x22, local copies, waits for them, and re-layouts  8.53 us
    ppermute x3, starting transfers between devices, passed_along(): return lax.ppermute(shard, axis, pairs)  8.08 us
  transfers between devices with their start and end apart: 26, of which 18 were waited for; matrix products, arithmetic and copies ran while one was open for 0% of the time, Pallas kernels for 14%

profile of v7, /device:TPU:13, one launch (start us, length us, event | category | flops | bytes accessed | tf_op | source)
XLA Modules:
  0.0 206.3 jit_solution(11074716977167815607)
XLA Ops:
  3.7 1.9 collective-permute-start.6
  5.7 2.2 %collective-permute-start.1 = (bf16[192,512]{1,0:T(8,128)(2,1)S(1)}, bf16[192,512]{1,0:T(8,128)(2,1)S(1)}, u32[]{:S(2)}, u32[]{:S(2)}) collective-permute-start(bf16[192,512]{1,0:T(8,128)(2,1)S(1)} %get-tuple-element.37), channel_id=1, source_target_pairs={{0,2},{1,3},{2,0},{3,1},{4,6},{5,7},{6,4},{7,5},{8,10},{9,11},{10,... | collective-permute-start | bytes 589832 | tf_op jit(solution)/shard_map/ppermute | solution.py:283
  8.8 6.9 %collective-permute-done.6.refs_7_.refs_0_ = bf16[192,512]{1,0:T(8,128)(2,1)S(1)} collective-permute-done((bf16[192,512]{1,0:T(8,128)(2,1)S(1)}, bf16[192,512]{1,0:T(8,128)(2,1)S(1)}, u32[]{:S(2)}, u32[]{:S(2)}) %collective-permute-start.6) | collective-permute-done | bytes 196640 | tf_op jit(solution)/shard_map/ppermute | solution.py:283
  16.8 3.4 %collective-permute-done.1.refs_2_ = bf16[192,512]{1,0:T(8,128)(2,1)S(1)} collective-permute-done((bf16[192,512]{1,0:T(8,128)(2,1)S(1)}, bf16[192,512]{1,0:T(8,128)(2,1)S(1)}, u32[]{:S(2)}, u32[]{:S(2)}) %collective-permute-start.1) | collective-permute-done | bytes 196640 | tf_op jit(solution)/shard_map/ppermute | solution.py:283
  20.3 4.4 %collective-permute-done.2.refs_3_ = bf16[192,512]{1,0:T(8,128)(2,1)S(1)} collective-permute-done((bf16[192,512]{1,0:T(8,128)(2,1)S(1)}, bf16[192,512]{1,0:T(8,128)(2,1)S(1)}, u32[]{:S(2)}, u32[]{:S(2)}) %collective-permute-start.2) | collective-permute-done | bytes 196640 | tf_op jit(solution)/shard_map/ppermute | solution.py:283
  24.6 11.1 %collective-permute-done.4.refs_5_ = bf16[192,512]{1,0:T(8,128)(2,1)S(1)} collective-permute-done((bf16[192,512]{1,0:T(8,128)(2,1)S(1)}, bf16[192,512]{1,0:T(8,128)(2,1)S(1)}, u32[]{:S(2)}, u32[]{:S(2)}) %collective-permute-start.4) | collective-permute-done | bytes 196640 | tf_op jit(solution)/shard_map/ppermute | solution.py:283
  35.7 5.0 %collective-permute-done.5.refs_6_ = bf16[192,512]{1,0:T(8,128)(2,1)S(1)} collective-permute-done((bf16[192,512]{1,0:T(8,128)(2,1)S(1)}, bf16[192,512]{1,0:T(8,128)(2,1)S(1)}, u32[]{:S(2)}, u32[]{:S(2)}) %collective-permute-start.5) | collective-permute-done | bytes 196640 | tf_op jit(solution)/shard_map/ppermute | solution.py:283
  41.4 3.1 %collective-permute-start.7 = (bf16[1024,512]{1,0:T(8,128)(2,1)S(1)}, bf16[1024,512]{1,0:T(8,128)(2,1)S(1)}, u32[]{:S(2)}, u32[]{:S(2)}) collective-permute-start(bf16[1024,512]{1,0:T(8,128)(2,1)S(1)} %get-tuple-element.43), channel_id=1, source_target_pairs={{0,8},{8,16},{16,24},{1,9},{9,17},{17,25},{2,10},{10,18},{18,26},{... | collective-permute-start | bytes 3145736 | tf_op jit(solution)/shard_map/ppermute | solution.py:29
  45.4 3.2 %collective-permute-start.11 = (bf16[192,512]{1,0:T(8,128)(2,1)S(1)}, bf16[192,512]{1,0:T(8,128)(2,1)S(1)}, u32[]{:S(2)}, u32[]{:S(2)}) collective-permute-start(bf16[192,512]{1,0:T(8,128)(2,1)S(1)} %get-tuple-element.49), channel_id=1, source_target_pairs={{0,4},{1,5},{2,6},{3,7},{4,0},{5,1},{6,2},{7,3},{8,12},{9,13},{10,... | collective-permute-start | bytes 589832 | tf_op jit(solution)/shard_map/ppermute | solution.py:283
  50.1 2.7 %collective-permute-done.10.refs_3_ = bf16[192,512]{1,0:T(8,128)(2,1)S(1)} collective-permute-done((bf16[192,512]{1,0:T(8,128)(2,1)S(1)}, bf16[192,512]{1,0:T(8,128)(2,1)S(1)}, u32[]{:S(2)}, u32[]{:S(2)}) %collective-permute-start.10) | collective-permute-done | bytes 196640 | tf_op jit(solution)/shard_map/ppermute | solution.py:283
  52.8 1.9 collective-permute-start.14
  54.7 15.2 %collective-permute-done.11.refs_4_ = bf16[192,512]{1,0:T(8,128)(2,1)S(1)} collective-permute-done((bf16[192,512]{1,0:T(8,128)(2,1)S(1)}, bf16[192,512]{1,0:T(8,128)(2,1)S(1)}, u32[]{:S(2)}, u32[]{:S(2)}) %collective-permute-start.11) | collective-permute-done | bytes 196640 | tf_op jit(solution)/shard_map/ppermute | solution.py:283
  70.9 3.3 %collective-permute-done.12.refs_5_ = bf16[192,512]{1,0:T(8,128)(2,1)S(1)} collective-permute-done((bf16[192,512]{1,0:T(8,128)(2,1)S(1)}, bf16[192,512]{1,0:T(8,128)(2,1)S(1)}, u32[]{:S(2)}, u32[]{:S(2)}) %collective-permute-start.12) | collective-permute-done | bytes 196640 | tf_op jit(solution)/shard_map/ppermute | solution.py:283
  74.1 2.2 %collective-permute-start.9 = (bf16[192,512]{1,0:T(8,128)(2,1)S(1)}, bf16[192,512]{1,0:T(8,128)(2,1)S(1)}, u32[]{:S(2)}, u32[]{:S(2)}) collective-permute-start(bf16[192,512]{1,0:T(8,128)(2,1)S(1)} %get-tuple-element.47), channel_id=1, source_target_pairs={{0,2},{1,3},{2,0},{3,1},{4,6},{5,7},{6,4},{7,5},{8,10},{9,11},{10,... | collective-permute-start | bytes 589832 | tf_op jit(solution)/shard_map/ppermute | solution.py:283
  76.4 3.0 %collective-permute-done.13.refs_6_ = bf16[192,512]{1,0:T(8,128)(2,1)S(1)} collective-permute-done((bf16[192,512]{1,0:T(8,128)(2,1)S(1)}, bf16[192,512]{1,0:T(8,128)(2,1)S(1)}, u32[]{:S(2)}, u32[]{:S(2)}) %collective-permute-start.13) | collective-permute-done | bytes 196640 | tf_op jit(solution)/shard_map/ppermute | solution.py:283
  79.4 4.2 %collective-permute-done.14.refs_7_ = bf16[192,512]{1,0:T(8,128)(2,1)S(1)} collective-permute-done((bf16[192,512]{1,0:T(8,128)(2,1)S(1)}, bf16[192,512]{1,0:T(8,128)(2,1)S(1)}, u32[]{:S(2)}, u32[]{:S(2)}) %collective-permute-start.14) | collective-permute-done | bytes 196640 | tf_op jit(solution)/shard_map/ppermute | solution.py:283
  87.1 4.4 %all-to-all-start.1 = ((bf16[8,192,512]{2,1,0:T(8,128)(2,1)}), bf16[8,192,512]{2,1,0:T(8,128)(2,1)S(1)}, u32[]{:S(2)}, u32[]{:S(2)}) async-start(bf16[8,192,512]{2,1,0:T(8,128)(2,1)} %packed.5), calls=%async_computation.1 | async-start | bytes 3145728 | tf_op jit(solution)/shard_map/all_to_all | solution.py:289
  94.1 12.4 %attend.2 = (bf16[1536,256]{1,0:T(8,128)(2,1)S(1)}, f32[1536,256]{1,0:T(8,128)S(1)}, bf16[1024,256]{1,0:T(8,128)(2,1)S(1)}) custom-call(s32[2]{0:T(128)S(1)} %pad_add_fusion.me_ref, s32[16]{0:T(128)S(1)} %copy-done.10, bf16[1024,512]{1,0:T(8,128)(2,1)S(1)} %copy-done.3, bf16[1536,512]{1,0:T(8,128)(2,1)S(1)} %copy-done.8, ...), custom_call_target="tpu_custom_call" | custom-call | flops 5033164800 | bytes 4718592 | tf_op jit(solution)/shard_map/attend/pallas_call | solution.py:165
  106.5 2.5 %collective-permute-start.15 = (bf16[1024,256]{1,0:T(8,128)(2,1)S(1)}, bf16[1024,256]{1,0:T(8,128)(2,1)S(1)}, u32[]{:S(2)}, u32[]{:S(2)}) collective-permute-start(bf16[1024,256]{1,0:T(8,128)(2,1)S(1)} %get-tuple-element.55), channel_id=1, source_target_pairs={{8,0},{16,8},{24,16},{9,1},{17,9},{25,17},{10,2},{18,10},{26,18},{... | collective-permute-start | bytes 1572872 | tf_op jit(solution)/shard_map/ppermute | solution.py:29
  109.0 12.5 %collective-permute-done.15.refs_2_ = bf16[1024,256]{1,0:T(8,128)(2,1)S(1)} collective-permute-done((bf16[1024,256]{1,0:T(8,128)(2,1)S(1)}, bf16[1024,256]{1,0:T(8,128)(2,1)S(1)}, u32[]{:S(2)}, u32[]{:S(2)}) %collective-permute-start.15) | collective-permute-done | bytes 524320 | tf_op jit(solution)/shard_map/ppermute | solution.py:29
  123.4 2.3 %all-to-all-done.1 = bf16[8,192,512]{2,1,0:T(8,128)(2,1)S(1)} async-done(((bf16[8,192,512]{2,1,0:T(8,128)(2,1)}), bf16[8,192,512]{2,1,0:T(8,128)(2,1)S(1)}, u32[]{:S(2)}, u32[]{:S(2)}) %all-to-all-start.1) | async-done | bytes 1572896 | tf_op jit(solution)/shard_map/all_to_all | solution.py:289
  125.7 7.0 %all-to-all-start = ((bf16[8,192,512]{2,1,0:T(8,128)(2,1)}), bf16[8,192,512]{2,1,0:T(8,128)(2,1)S(1)}, u32[]{:S(2)}, u32[]{:S(2)}) async-start(bf16[8,192,512]{2,1,0:T(8,128)(2,1)} %bitcast.2), calls=%async_computation | async-start | bytes 3145728 | tf_op jit(solution)/shard_map/all_to_all | solution.py:289
  135.4 12.4 %attend.3 = (bf16[1536,256]{1,0:T(8,128)(2,1)S(1)}, f32[1536,256]{1,0:T(8,128)S(1)}, bf16[1024,256]{1,0:T(8,128)(2,1)S(1)}) custom-call(s32[2]{0:T(128)S(1)} %pad_add_fusion.me_ref, s32[16]{0:T(128)S(1)} %copy-done.10, bf16[1024,512]{1,0:T(8,128)(2,1)S(1)} %copy-done.4, bf16[1536,512]{1,0:T(8,128)(2,1)S(1)} %copy-done.9, bf16[1536,512]{1,0:T(8,128)(2,1)S(1)} %bitcast.4), custom_call_target="tpu_custom_call" | custom-call | flops 5033164800 | bytes 4718592 | tf_op jit(solution)/shard_map/attend/pallas_call | solution.py:165
  147.8 2.5 %collective-permute-start.16 = (bf16[1024,256]{1,0:T(8,128)(2,1)S(1)}, bf16[1024,256]{1,0:T(8,128)(2,1)S(1)}, u32[]{:S(2)}, u32[]{:S(2)}) collective-permute-start(bf16[1024,256]{1,0:T(8,128)(2,1)S(1)} %get-tuple-element.58), channel_id=1, source_target_pairs={{8,0},{16,8},{24,16},{9,1},{17,9},{25,17},{10,2},{18,10},{26,18},{... | collective-permute-start | bytes 1572872 | tf_op jit(solution)/shard_map/ppermute | solution.py:29
  150.3 12.6 %collective-permute-done.16.refs_2_ = bf16[1024,256]{1,0:T(8,128)(2,1)S(1)} collective-permute-done((bf16[1024,256]{1,0:T(8,128)(2,1)S(1)}, bf16[1024,256]{1,0:T(8,128)(2,1)S(1)}, u32[]{:S(2)}, u32[]{:S(2)}) %collective-permute-start.16) | collective-permute-done | bytes 524320 | tf_op jit(solution)/shard_map/ppermute | solution.py:29
  167.3 2.1 %collective-permute-start.20 = (bf16[192,512]{1,0:T(8,128)(2,1)}, bf16[192,512]{1,0:T(8,128)(2,1)S(1)}, u32[]{:S(2)}, u32[]{:S(2)}) collective-permute-start(bf16[192,512]{1,0:T(8,128)(2,1)} %get-tuple-element.63), channel_id=1, source_target_pairs={{0,4},{1,5},{2,6},{3,7},{4,0},{5,1},{6,2},{7,3},{8,12},{9,13},{10,... | collective-permute-start | bytes 589832 | tf_op jit(solution)/shard_map/ppermute | solution.py:283
  171.2 8.8 %collective-permute-done.18.refs_3_ = bf16[192,512]{1,0:T(8,128)(2,1)S(1)} collective-permute-done((bf16[192,512]{1,0:T(8,128)(2,1)S(1)}, bf16[192,512]{1,0:T(8,128)(2,1)S(1)}, u32[]{:S(2)}, u32[]{:S(2)}) %collective-permute-start.18) | collective-permute-done | bytes 196640 | tf_op jit(solution)/shard_map/ppermute | solution.py:283
  180.0 4.3 %collective-permute-done.19.refs_4_ = bf16[192,512]{1,0:T(8,128)(2,1)S(1)} collective-permute-done((bf16[192,512]{1,0:T(8,128)(2,1)}, bf16[192,512]{1,0:T(8,128)(2,1)S(1)}, u32[]{:S(2)}, u32[]{:S(2)}) %collective-permute-start.19) | collective-permute-done | bytes 196640 | tf_op jit(solution)/shard_map/ppermute | solution.py:283
  184.4 10.5 %collective-permute-done.21.refs_6_ = bf16[192,512]{1,0:T(8,128)(2,1)S(1)} collective-permute-done((bf16[192,512]{1,0:T(8,128)(2,1)}, bf16[192,512]{1,0:T(8,128)(2,1)S(1)}, u32[]{:S(2)}, u32[]{:S(2)}) %collective-permute-start.21) | collective-permute-done | bytes 196640 | tf_op jit(solution)/shard_map/ppermute | solution.py:283
  194.9 4.1 %collective-permute-done.22.refs_7_ = bf16[192,512]{1,0:T(8,128)(2,1)S(1)} collective-permute-done((bf16[192,512]{1,0:T(8,128)(2,1)S(1)}, bf16[192,512]{1,0:T(8,128)(2,1)S(1)}, u32[]{:S(2)}, u32[]{:S(2)}) %collective-permute-start.22) | collective-permute-done | bytes 196640 | tf_op jit(solution)/shard_map/ppermute | solution.py:283
  199.0 4.4 %collective-permute-done.23.refs_8_ = bf16[192,512]{1,0:T(8,128)(2,1)S(1)} collective-permute-done((bf16[192,512]{1,0:T(8,128)(2,1)S(1)}, bf16[192,512]{1,0:T(8,128)(2,1)S(1)}, u32[]{:S(2)}, u32[]{:S(2)}) %collective-permute-start.23) | collective-permute-done | bytes 196640 | tf_op jit(solution)/shard_map/ppermute | solution.py:283
  203.4 2.8 %unpacked.1 = (bf16[192,4096]{1,0:T(8,128)(2,1)}, bf16[192,2048]{1,0:T(8,128)(2,1)}, bf16[192,2048]{1,0:T(8,128)(2,1)}) custom-call(s32[2]{0:T(128)S(1)} %pad_add_fusion.me_ref, bf16[8,192,512]{2,1,0:T(8,128)(2,1)S(1)} %all-to-all-done.refs_0_, bf16[192,512]{1,0:T(8,128)(2,1)S(1)} %get-tuple-element.59.refs_1_, ...), custom_call_target="tpu_custom_call" | custom-call | bytes 6291456 | tf_op jit(solution)/shard_map/unpacked/pallas_call | solution.py:186
  (53 shorter events, 26.1 us)
Async XLA Ops:
  3.0 41.6 %copy-start = (bf16[192,4096]{1,0:T(8,128)(2,1)S(1)}, bf16[192,4096]{1,0:T(8,128)(2,1)}, u32[]{:S(2)}) copy-start(bf16[192,4096]{1,0:T(8,128)(2,1)} %refs_2_.3) | copy-start | bytes 4718596
  3.0 41.6 %copy-start.1 = (bf16[192,4096]{1,0:T(8,128)(2,1)S(1)}, bf16[192,4096]{1,0:T(8,128)(2,1)}, u32[]{:S(2)}) copy-start(bf16[192,4096]{1,0:T(8,128)(2,1)} %refs_3_.1) | copy-start | bytes 4718596
  3.7 11.9 %collective-permute-start.6 = (bf16[192,512]{1,0:T(8,128)(2,1)S(1)}, bf16[192,512]{1,0:T(8,128)(2,1)S(1)}, u32[]{:S(2)}, u32[]{:S(2)}) collective-permute-start(bf16[192,512]{1,0:T(8,128)(2,1)S(1)} %get-tuple-element.42), channel_id=1, source_target_pairs={{0,7},{1,6},{2,5},{3,4},{4,3},{5,2},{6,1},{7,0},{8,15},{9,14},{10,... | collective-permute-start | bytes 589832 | tf_op jit(solution)/shard_map/ppermute | solution.py:283
  5.7 10.2 %collective-permute-start = (bf16[192,512]{1,0:T(8,128)(2,1)S(1)}, bf16[192,512]{1,0:T(8,128)(2,1)S(1)}, u32[]{:S(2)}, u32[]{:S(2)}) collective-permute-start(bf16[192,512]{1,0:T(8,128)(2,1)S(1)} %get-tuple-element.36), channel_id=1, source_target_pairs={{0,1},{1,0},{2,3},{3,2},{4,5},{5,4},{6,7},{7,6},{8,9},{9,8},{10,11... | collective-permute-start | bytes 589832 | tf_op jit(solution)/shard_map/ppermute | solution.py:283
  5.7 14.6 %collective-permute-start.1 = (bf16[192,512]{1,0:T(8,128)(2,1)S(1)}, bf16[192,512]{1,0:T(8,128)(2,1)S(1)}, u32[]{:S(2)}, u32[]{:S(2)}) collective-permute-start(bf16[192,512]{1,0:T(8,128)(2,1)S(1)} %get-tuple-element.37), channel_id=1, source_target_pairs={{0,2},{1,3},{2,0},{3,1},{4,6},{5,7},{6,4},{7,5},{8,10},{9,11},{10,... | collective-permute-start | bytes 589832 | tf_op jit(solution)/shard_map/ppermute | solution.py:283
  7.9 16.7 %collective-permute-start.2 = (bf16[192,512]{1,0:T(8,128)(2,1)S(1)}, bf16[192,512]{1,0:T(8,128)(2,1)S(1)}, u32[]{:S(2)}, u32[]{:S(2)}) collective-permute-start(bf16[192,512]{1,0:T(8,128)(2,1)S(1)} %get-tuple-element.38), channel_id=1, source_target_pairs={{0,3},{1,2},{2,1},{3,0},{4,7},{5,6},{6,5},{7,4},{8,11},{9,10},{10,... | collective-permute-start | bytes 589832 | tf_op jit(solution)/shard_map/ppermute | solution.py:283
  8.3 16.3 %collective-permute-start.3 = (bf16[192,512]{1,0:T(8,128)(2,1)S(1)}, bf16[192,512]{1,0:T(8,128)(2,1)S(1)}, u32[]{:S(2)}, u32[]{:S(2)}) collective-permute-start(bf16[192,512]{1,0:T(8,128)(2,1)S(1)} %get-tuple-element.39), channel_id=1, source_target_pairs={{0,4},{1,5},{2,6},{3,7},{4,0},{5,1},{6,2},{7,3},{8,12},{9,13},{10,... | collective-permute-start | bytes 589832 | tf_op jit(solution)/shard_map/ppermute | solution.py:283
  15.6 20.1 %collective-permute-start.4 = (bf16[192,512]{1,0:T(8,128)(2,1)S(1)}, bf16[192,512]{1,0:T(8,128)(2,1)S(1)}, u32[]{:S(2)}, u32[]{:S(2)}) collective-permute-start(bf16[192,512]{1,0:T(8,128)(2,1)S(1)} %get-tuple-element.40), channel_id=1, source_target_pairs={{0,5},{1,4},{2,7},{3,6},{4,1},{5,0},{6,3},{7,2},{8,13},{9,12},{10,... | collective-permute-start | bytes 589832 | tf_op jit(solution)/shard_map/ppermute | solution.py:283
  15.8 24.9 %collective-permute-start.5 = (bf16[192,512]{1,0:T(8,128)(2,1)S(1)}, bf16[192,512]{1,0:T(8,128)(2,1)S(1)}, u32[]{:S(2)}, u32[]{:S(2)}) collective-permute-start(bf16[192,512]{1,0:T(8,128)(2,1)S(1)} %get-tuple-element.41), channel_id=1, source_target_pairs={{0,6},{1,7},{2,4},{3,5},{4,2},{5,3},{6,0},{7,1},{8,14},{9,15},{10,... | collective-permute-start | bytes 589832 | tf_op jit(solution)/shard_map/ppermute | solution.py:283
  41.4 3.9 %copy-start.7 = (bf16[1536,512]{1,0:T(8,128)(2,1)}, bf16[1536,512]{1,0:T(8,128)(2,1)S(1)}, u32[]{:S(2)}) copy-start(bf16[1536,512]{1,0:T(8,128)(2,1)S(1)} %get-tuple-element.44.kv_ref) | copy-start | bytes 4718596
  41.4 42.8 %collective-permute-start.7 = (bf16[1024,512]{1,0:T(8,128)(2,1)S(1)}, bf16[1024,512]{1,0:T(8,128)(2,1)S(1)}, u32[]{:S(2)}, u32[]{:S(2)}) collective-permute-start(bf16[1024,512]{1,0:T(8,128)(2,1)S(1)} %get-tuple-element.43), channel_id=1, source_target_pairs={{0,8},{8,16},{16,24},{1,9},{9,17},{17,25},{2,10},{10,18},{18,26},{... | collective-permute-start | bytes 3145736 | tf_op jit(solution)/shard_map/ppermute | solution.py:29
  45.4 7.4 %collective-permute-start.10 = (bf16[192,512]{1,0:T(8,128)(2,1)S(1)}, bf16[192,512]{1,0:T(8,128)(2,1)S(1)}, u32[]{:S(2)}, u32[]{:S(2)}) collective-permute-start(bf16[192,512]{1,0:T(8,128)(2,1)S(1)} %get-tuple-element.48), channel_id=1, source_target_pairs={{0,3},{1,2},{2,1},{3,0},{4,7},{5,6},{6,5},{7,4},{8,11},{9,10},{10,... | collective-permute-start | bytes 589832 | tf_op jit(solution)/shard_map/ppermute | solution.py:283
  45.4 24.5 %collective-permute-start.11 = (bf16[192,512]{1,0:T(8,128)(2,1)S(1)}, bf16[192,512]{1,0:T(8,128)(2,1)S(1)}, u32[]{:S(2)}, u32[]{:S(2)}) collective-permute-start(bf16[192,512]{1,0:T(8,128)(2,1)S(1)} %get-tuple-element.49), channel_id=1, source_target_pairs={{0,4},{1,5},{2,6},{3,7},{4,0},{5,1},{6,2},{7,3},{8,12},{9,13},{10,... | collective-permute-start | bytes 589832 | tf_op jit(solution)/shard_map/ppermute | solution.py:283
  48.6 25.6 %collective-permute-start.12 = (bf16[192,512]{1,0:T(8,128)(2,1)S(1)}, bf16[192,512]{1,0:T(8,128)(2,1)S(1)}, u32[]{:S(2)}, u32[]{:S(2)}) collective-permute-start(bf16[192,512]{1,0:T(8,128)(2,1)S(1)} %get-tuple-element.50), channel_id=1, source_target_pairs={{0,5},{1,4},{2,7},{3,6},{4,1},{5,0},{6,3},{7,2},{8,13},{9,12},{10,... | collective-permute-start | bytes 589832 | tf_op jit(solution)/shard_map/ppermute | solution.py:283
  48.8 30.5 %collective-permute-start.13 = (bf16[192,512]{1,0:T(8,128)(2,1)S(1)}, bf16[192,512]{1,0:T(8,128)(2,1)S(1)}, u32[]{:S(2)}, u32[]{:S(2)}) collective-permute-start(bf16[192,512]{1,0:T(8,128)(2,1)S(1)} %get-tuple-element.51), channel_id=1, source_target_pairs={{0,6},{1,7},{2,4},{3,5},{4,2},{5,3},{6,0},{7,1},{8,14},{9,15},{10,... | collective-permute-start | bytes 589832 | tf_op jit(solution)/shard_map/ppermute | solution.py:283
  52.8 30.8 %collective-permute-start.14 = (bf16[192,512]{1,0:T(8,128)(2,1)S(1)}, bf16[192,512]{1,0:T(8,128)(2,1)S(1)}, u32[]{:S(2)}, u32[]{:S(2)}) collective-permute-start(bf16[192,512]{1,0:T(8,128)(2,1)S(1)} %get-tuple-element.52), channel_id=1, source_target_pairs={{0,7},{1,6},{2,5},{3,4},{4,3},{5,2},{6,1},{7,0},{8,15},{9,14},{10,... | collective-permute-start | bytes 589832 | tf_op jit(solution)/shard_map/ppermute | solution.py:283
  69.9 13.7 %collective-permute-start.8 = (bf16[192,512]{1,0:T(8,128)(2,1)S(1)}, bf16[192,512]{1,0:T(8,128)(2,1)S(1)}, u32[]{:S(2)}, u32[]{:S(2)}) collective-permute-start(bf16[192,512]{1,0:T(8,128)(2,1)S(1)} %get-tuple-element.46), channel_id=1, source_target_pairs={{0,1},{1,0},{2,3},{3,2},{4,5},{5,4},{6,7},{7,6},{8,9},{9,8},{10,11... | collective-permute-start | bytes 589832 | tf_op jit(solution)/shard_map/ppermute | solution.py:283
  74.1 9.5 %collective-permute-start.9 = (bf16[192,512]{1,0:T(8,128)(2,1)S(1)}, bf16[192,512]{1,0:T(8,128)(2,1)S(1)}, u32[]{:S(2)}, u32[]{:S(2)}) collective-permute-start(bf16[192,512]{1,0:T(8,128)(2,1)S(1)} %get-tuple-element.47), channel_id=1, source_target_pairs={{0,2},{1,3},{2,0},{3,1},{4,6},{5,7},{6,4},{7,5},{8,10},{9,11},{10,... | collective-permute-start | bytes 589832 | tf_op jit(solution)/shard_map/ppermute | solution.py:283
  87.1 4.4 %copy-start.10 = (s32[16]{0:T(128)S(1)}, s32[16]{0:T(128)}, u32[]{:S(2)}) copy-start(s32[16]{0:T(128)} %docs_ref.3) | copy-start | bytes 196
  87.1 38.6 %all-to-all-start.1 = ((bf16[8,192,512]{2,1,0:T(8,128)(2,1)}), bf16[8,192,512]{2,1,0:T(8,128)(2,1)S(1)}, u32[]{:S(2)}, u32[]{:S(2)}) async-start(bf16[8,192,512]{2,1,0:T(8,128)(2,1)} %packed.5), calls=%async_computation.1 | async-start | bytes 3145728 | tf_op jit(solution)/shard_map/all_to_all | solution.py:289
  92.7 1.4 copy-start.8
  106.5 15.0 %collective-permute-start.15 = (bf16[1024,256]{1,0:T(8,128)(2,1)S(1)}, bf16[1024,256]{1,0:T(8,128)(2,1)S(1)}, u32[]{:S(2)}, u32[]{:S(2)}) collective-permute-start(bf16[1024,256]{1,0:T(8,128)(2,1)S(1)} %get-tuple-element.55), channel_id=1, source_target_pairs={{8,0},{16,8},{24,16},{9,1},{17,9},{25,17},{10,2},{18,10},{26,18},{... | collective-permute-start | bytes 1572872 | tf_op jit(solution)/shard_map/ppermute | solution.py:29
  125.7 54.3 %all-to-all-start = ((bf16[8,192,512]{2,1,0:T(8,128)(2,1)}), bf16[8,192,512]{2,1,0:T(8,128)(2,1)S(1)}, u32[]{:S(2)}, u32[]{:S(2)}) async-start(bf16[8,192,512]{2,1,0:T(8,128)(2,1)} %bitcast.2), calls=%async_computation | async-start | bytes 3145728 | tf_op jit(solution)/shard_map/all_to_all | solution.py:289
  134.0 1.4 copy-start.9
  147.8 15.0 %collective-permute-start.16 = (bf16[1024,256]{1,0:T(8,128)(2,1)S(1)}, bf16[1024,256]{1,0:T(8,128)(2,1)S(1)}, u32[]{:S(2)}, u32[]{:S(2)}) collective-permute-start(bf16[1024,256]{1,0:T(8,128)(2,1)S(1)} %get-tuple-element.58), channel_id=1, source_target_pairs={{8,0},{16,8},{24,16},{9,1},{17,9},{25,17},{10,2},{18,10},{26,18},{... | collective-permute-start | bytes 1572872 | tf_op jit(solution)/shard_map/ppermute | solution.py:29
  164.5 5.6 %collective-permute-start.17 = (bf16[192,512]{1,0:T(8,128)(2,1)S(1)}, bf16[192,512]{1,0:T(8,128)(2,1)S(1)}, u32[]{:S(2)}, u32[]{:S(2)}) collective-permute-start(bf16[192,512]{1,0:T(8,128)(2,1)S(1)} %get-tuple-element.60), channel_id=1, source_target_pairs={{0,1},{1,0},{2,3},{3,2},{4,5},{5,4},{6,7},{7,6},{8,9},{9,8},{10,11... | collective-permute-start | bytes 589832 | tf_op jit(solution)/shard_map/ppermute | solution.py:283
  165.7 14.4 %collective-permute-start.18 = (bf16[192,512]{1,0:T(8,128)(2,1)S(1)}, bf16[192,512]{1,0:T(8,128)(2,1)S(1)}, u32[]{:S(2)}, u32[]{:S(2)}) collective-permute-start(bf16[192,512]{1,0:T(8,128)(2,1)S(1)} %get-tuple-element.61), channel_id=1, source_target_pairs={{0,2},{1,3},{2,0},{3,1},{4,6},{5,7},{6,4},{7,5},{8,10},{9,11},{10,... | collective-permute-start | bytes 589832 | tf_op jit(solution)/shard_map/ppermute | solution.py:283
  165.7 18.6 %collective-permute-start.19 = (bf16[192,512]{1,0:T(8,128)(2,1)}, bf16[192,512]{1,0:T(8,128)(2,1)S(1)}, u32[]{:S(2)}, u32[]{:S(2)}) collective-permute-start(bf16[192,512]{1,0:T(8,128)(2,1)} %get-tuple-element.62), channel_id=1, source_target_pairs={{0,3},{1,2},{2,1},{3,0},{4,7},{5,6},{6,5},{7,4},{8,11},{9,10},{10,... | collective-permute-start | bytes 589832 | tf_op jit(solution)/shard_map/ppermute | solution.py:283
  167.3 17.1 %collective-permute-start.20 = (bf16[192,512]{1,0:T(8,128)(2,1)}, bf16[192,512]{1,0:T(8,128)(2,1)S(1)}, u32[]{:S(2)}, u32[]{:S(2)}) collective-permute-start(bf16[192,512]{1,0:T(8,128)(2,1)} %get-tuple-element.63), channel_id=1, source_target_pairs={{0,4},{1,5},{2,6},{3,7},{4,0},{5,1},{6,2},{7,3},{8,12},{9,13},{10,... | collective-permute-start | bytes 589832 | tf_op jit(solution)/shard_map/ppermute | solution.py:283
  169.4 25.5 %collective-permute-start.21 = (bf16[192,512]{1,0:T(8,128)(2,1)}, bf16[192,512]{1,0:T(8,128)(2,1)S(1)}, u32[]{:S(2)}, u32[]{:S(2)}) collective-permute-start(bf16[192,512]{1,0:T(8,128)(2,1)} %get-tuple-element.64), channel_id=1, source_target_pairs={{0,5},{1,4},{2,7},{3,6},{4,1},{5,0},{6,3},{7,2},{8,13},{9,12},{10,... | collective-permute-start | bytes 589832 | tf_op jit(solution)/shard_map/ppermute | solution.py:283
  170.0 29.0 %collective-permute-start.22 = (bf16[192,512]{1,0:T(8,128)(2,1)S(1)}, bf16[192,512]{1,0:T(8,128)(2,1)S(1)}, u32[]{:S(2)}, u32[]{:S(2)}) collective-permute-start(bf16[192,512]{1,0:T(8,128)(2,1)S(1)} %get-tuple-element.65), channel_id=1, source_target_pairs={{0,6},{1,7},{2,4},{3,5},{4,2},{5,3},{6,0},{7,1},{8,14},{9,15},{10,... | collective-permute-start | bytes 589832 | tf_op jit(solution)/shard_map/ppermute | solution.py:283
  180.0 23.4 %collective-permute-start.23 = (bf16[192,512]{1,0:T(8,128)(2,1)S(1)}, bf16[192,512]{1,0:T(8,128)(2,1)S(1)}, u32[]{:S(2)}, u32[]{:S(2)}) collective-permute-start(bf16[192,512]{1,0:T(8,128)(2,1)S(1)} %get-tuple-element.66), channel_id=1, source_target_pairs={{0,7},{1,6},{2,5},{3,4},{4,3},{5,2},{6,1},{7,0},{8,15},{9,14},{10,... | collective-permute-start | bytes 589832 | tf_op jit(solution)/shard_map/ppermute | solution.py:283
  (5 other events, 5.7 us)

commit v8 on v7

--- a/solution.py
+++ b/solution.py
@@ -195,24 +195,20 @@
     )(me, *earlier, *arrays)
 
 
-def packed(me, arrays, ways, chunk=0, chunks=1, places=None, earlier=()):
+def packed(me, arrays, ways, places, chunk=0, chunks=1, earlier=()):
     tokens = arrays[0].shape[0]
     lanes = [a.shape[1] // (ways * chunks) for a in arrays]
-    total = sum(lanes)
 
     def kernel(me_ref, *refs):
         ins, outs = refs[: len(arrays)], refs[len(arrays) :]
-        for n in range(ways):
-            out = outs[n] if places else outs[0].at[n]
-            place = me_ref[0] ^ places[n] if places else n
+        for k, out in zip(places, outs):
             first = 0
             for ref, width in zip(ins, lanes):
-                at = (place * chunks + chunk) * width
-                at = pl.multiple_of(at, width) if places else at
+                at = pl.multiple_of(((me_ref[0] ^ k) * chunks + chunk) * width, width)
                 out[:, first : first + width] = ref[:, pl.ds(at, width)]
                 first += width
 
-    shapes = [(tokens, total)] * ways if places else [(ways, tokens, total)]
+    shapes = [(tokens, sum(lanes))] * len(places)
     return on_chip(kernel, me, arrays, shapes, "packed", earlier=earlier)
 
 
@@ -254,7 +250,7 @@
     return on_chip(kernel, me, blocks, shapes, "gathered")
 
 
-def settled(me, dq, own, returned, ways, places=None):
+def settled(me, dq, own, returned, ways, places=None, earlier=()):
     group, q_lanes = dq.shape
     tokens = group // ways
     total_lanes = q_lanes + 2 * HD
@@ -274,7 +270,7 @@
 
     shapes = [(tokens, total_lanes)] * ways if places else [(group, total_lanes)]
     scratch = [pltpu.VMEM((group, 2 * HD), jnp.bfloat16)] if places else []
-    return on_chip(kernel, me, (dq, own, returned), shapes, "settled", scratch)
+    return on_chip(kernel, me, (dq, own, returned), shapes, "settled", scratch, earlier)
 
 
 def exchanged(blocks, places):
@@ -300,24 +296,28 @@
     me = jnp.stack([lax.axis_index("head"), group_first]).astype(jnp.int32)
     places = list(range(ways))
 
-    came = exchanged(packed(me, (keys, values), ways, places=places), places)
+    late = places[ways - ways // 4 :]
+    came = exchanged(packed(me, (keys, values), ways, places), places)
     kv, tail = gathered(me, came, places, WINDOW)
     halo = passed_along(tail, "seq", 1)
-    sent = packed(me, (queries, grad_out), ways, 0, kv_local, places, [came[-1]])
-    qds = list(gathered(me, exchanged(sent, places), places, 0))
-    for c in range(1, kv_local):
-        sent = packed(me, (queries, grad_out), ways, c, kv_local, None, [qds[-1], halo])[0]
-        qds.append(exchanged_at_once(sent).reshape(group, 2 * q_lanes))
-
-    grads = []
-    for c, qd in enumerate(qds):
-        dq, own, rim = attend(me, doc_lengths, qd, halo, kv, c, kv_local)
-        returned = passed_along(rim, "seq", -1)
-        if c < kv_local - 1:
-            rows = settled(me, dq, own, returned, ways)[0]
+
+    parts, returned, grads = [], [], []
+    for c in range(kv_local):
+        sent = []
+        for k, before in zip(places, came):
+            earlier = [parts[-1][0]] if parts and k in late else [before] if k else []
+            sent += packed(me, (queries, grad_out), ways, [k], c, kv_local, earlier)
+        came = exchanged(sent, places)
+        qd = gathered(me, came, places, 0)[0]
+        if parts:
+            dq, own, _ = parts[-1]
+            rows = settled(me, dq, own, returned[-1], ways, None, [qd])[0]
             grads.append([exchanged_at_once(rows.reshape(ways, tokens, rows.shape[1]))])
-        else:
-            grads.append(exchanged(settled(me, dq, own, returned, ways, places), places))
+        parts.append(attend(me, doc_lengths, qd, halo, kv, c, kv_local))
+        returned.append(passed_along(parts[-1][2], "seq", -1))
+
+    dq, own, _ = parts[-1]
+    grads.append(exchanged(settled(me, dq, own, returned[-1], ways, places), places))
     return unpacked(me, grads, places, q_lanes)
 
 

time: 208 us -> 224 us (1.077)
  waiting for transfers between devices: 119 us -> 133 us
  local copies, waits for them, and re-layouts: 8.53 us -> 4.92 us
  starting transfers between devices: 42.3 us -> 45.4 us
    ppermute x21 -> x28, waiting for transfers between devices: 91.3 us -> 122 us  [exchanged(): lax.ppermute(block, 'head', [(i, i ^ k) for i in range(ways)])]
    ppermute x3, waiting for transfers between devices: 25.1 us -> 10.9 us  [passed_along(): return lax.ppermute(shard, axis, pairs)]
    all_to_all x2 -> x1, starting transfers between devices: 11.4 us -> 3.9 us  [exchanged_at_once(): return lax.all_to_all(sent, 'head', split_axis=0, concat_axis=0, tiled=True)]
    ppermute x21 -> x28, starting transfers between devices: 22.8 us -> 30.3 us  [exchanged(): lax.ppermute(block, 'head', [(i, i ^ k) for i in range(ways)])]
    pallas_call x8 -> x23, Pallas kernels: 11 us -> 17.5 us  [on_chip(): pl.pallas_call(body, out_shape=outs, in_specs=[SMEM] + [VMEM] * (len(earl...]
    pallas_call x2, Pallas kernels: 24.8 us -> 19.7 us  [attend(): pl.pallas_call(functools.partial(attend_kernel, per_group, chunk, kv_loca...]
    unnamed x22 -> x18, local copies, waits for them, and re-layouts: 8.53 us -> 4.92 us
    ppermute x3, starting transfers between devices: 8.08 us -> 11.2 us  [passed_along(): return lax.ppermute(shard, axis, pairs)]
  transfers between devices with their start and end apart: 26 -> 32, of which waited for: 18 -> 19; matrix products, arithmetic and copies ran while one was open for 0% -> 0% of each run, Pallas kernels for 14% -> 10%
where the time goes in v8:
time: 224 us; the launch traced here: 221 us
  waiting for transfers between devices  133 us (59%)
  starting transfers between devices  45.4 us (20%)
  Pallas kernels  37.2 us (17%)
  local copies, waits for them, and re-layouts  4.92 us (2%)
    ppermute x28, waiting for transfers between devices, exchanged(): lax.ppermute(block, 'head', [(i, i ^ k) for i in range(ways)])  122 us
    ppermute x28, starting transfers between devices, exchanged(): lax.ppermute(block, 'head', [(i, i ^ k) for i in range(ways)])  30.3 us
    pallas_call x2, Pallas kernels, attend(): pl.pallas_call(functools.partial(attend_kernel, per_group, chunk, kv_loca...  19.7 us
    pallas_call x23, Pallas kernels, on_chip(): pl.pallas_call(body, out_shape=outs, in_specs=[SMEM] + [VMEM] * (len(earl...  17.5 us
    ppermute x3, starting transfers between devices, passed_along(): return lax.ppermute(shard, axis, pairs)  11.2 us
    ppermute x3, waiting for transfers between devices, passed_along(): return lax.ppermute(shard, axis, pairs)  10.9 us
    unnamed x18, local copies, waits for them, and re-layouts  4.92 us
  transfers between devices with their start and end apart: 32, of which 19 were waited for; matrix products, arithmetic and copies ran while one was open for 0% of the time, Pallas kernels for 10%

profile of v8, /device:TPU:13, one launch (start us, length us, event | category | flops | bytes accessed | tf_op | source)
XLA Modules:
  0.0 221.3 jit_solution(8389920277445327232)
XLA Ops:
  6.2 2.3 %collective-permute-start.9 = (bf16[192,512]{1,0:T(8,128)(2,1)S(1)}, bf16[192,512]{1,0:T(8,128)(2,1)S(1)}, u32[]{:S(2)}, u32[]{:S(2)}) collective-permute-start(bf16[192,512]{1,0:T(8,128)(2,1)S(1)} %get-tuple-element.30), channel_id=1, source_target_pairs={{0,4},{1,5},{2,6},{3,7},{4,0},{5,1},{6,2},{7,3},{8,12},{9,13},{10,... | collective-permute-start | bytes 589832 | tf_op jit(solution)/shard_map/ppermute | solution.py:279
  10.2 6.5 %collective-permute-done.3.refs_0_.refs_2_ = bf16[192,512]{1,0:T(8,128)(2,1)S(1)} collective-permute-done((bf16[192,512]{1,0:T(8,128)(2,1)S(1)}, bf16[192,512]{1,0:T(8,128)(2,1)S(1)}, u32[]{:S(2)}, u32[]{:S(2)}) %collective-permute-start.3) | collective-permute-done | bytes 196640 | tf_op jit(solution)/shard_map/ppermute | solution.py:279
  18.2 2.8 %collective-permute-done.6.refs_0_.refs_3_ = bf16[192,512]{1,0:T(8,128)(2,1)S(1)} collective-permute-done((bf16[192,512]{1,0:T(8,128)(2,1)S(1)}, bf16[192,512]{1,0:T(8,128)(2,1)S(1)}, u32[]{:S(2)}, u32[]{:S(2)}) %collective-permute-start.6) | collective-permute-done | bytes 196640 | tf_op jit(solution)/shard_map/ppermute | solution.py:279
  21.0 12.7 %collective-permute-done.12.refs_0_.refs_5_ = bf16[192,512]{1,0:T(8,128)(2,1)S(1)} collective-permute-done((bf16[192,512]{1,0:T(8,128)(2,1)S(1)}, bf16[192,512]{1,0:T(8,128)(2,1)S(1)}, u32[]{:S(2)}, u32[]{:S(2)}) %collective-permute-start.12) | collective-permute-done | bytes 196640 | tf_op jit(solution)/shard_map/ppermute | solution.py:279
  33.8 4.2 %collective-permute-done.15.refs_6_.refs_0_ = bf16[192,512]{1,0:T(8,128)(2,1)S(1)} collective-permute-done((bf16[192,512]{1,0:T(8,128)(2,1)S(1)}, bf16[192,512]{1,0:T(8,128)(2,1)S(1)}, u32[]{:S(2)}, u32[]{:S(2)}) %collective-permute-start.15) | collective-permute-done | bytes 196640 | tf_op jit(solution)/shard_map/ppermute | solution.py:279
  38.0 4.3 %collective-permute-done.16.refs_7_.refs_0_ = bf16[192,512]{1,0:T(8,128)(2,1)S(1)} collective-permute-done((bf16[192,512]{1,0:T(8,128)(2,1)S(1)}, bf16[192,512]{1,0:T(8,128)(2,1)S(1)}, u32[]{:S(2)}, u32[]{:S(2)}) %collective-permute-start.16) | collective-permute-done | bytes 196640 | tf_op jit(solution)/shard_map/ppermute | solution.py:279
  43.0 3.1 %collective-permute-start.17 = (bf16[1024,512]{1,0:T(8,128)(2,1)S(1)}, bf16[1024,512]{1,0:T(8,128)(2,1)S(1)}, u32[]{:S(2)}, u32[]{:S(2)}) collective-permute-start(bf16[1024,512]{1,0:T(8,128)(2,1)S(1)} %get-tuple-element.35), channel_id=1, source_target_pairs={{0,8},{8,16},{16,24},{1,9},{9,17},{17,25},{2,10},{10,18},{18,26},{... | collective-permute-start | bytes 3145736 | tf_op jit(solution)/shard_map/ppermute | solution.py:29
  49.2 1.7 collective-permute-start.7
  57.8 6.0 %collective-permute-done.7.refs_0_.refs_3_ = bf16[192,512]{1,0:T(8,128)(2,1)S(1)} collective-permute-done((bf16[192,512]{1,0:T(8,128)(2,1)S(1)}, bf16[192,512]{1,0:T(8,128)(2,1)S(1)}, u32[]{:S(2)}, u32[]{:S(2)}) %collective-permute-start.7) | collective-permute-done | bytes 196640 | tf_op jit(solution)/shard_map/ppermute | solution.py:279
  65.6 12.2 %collective-permute-done.13.refs_0_.refs_5_ = bf16[192,512]{1,0:T(8,128)(2,1)S(1)} collective-permute-done((bf16[192,512]{1,0:T(8,128)(2,1)S(1)}, bf16[192,512]{1,0:T(8,128)(2,1)S(1)}, u32[]{:S(2)}, u32[]{:S(2)}) %collective-permute-start.13) | collective-permute-done | bytes 196640 | tf_op jit(solution)/shard_map/ppermute | solution.py:279
  77.8 6.3 %collective-permute-done.18.refs_6_ = bf16[192,512]{1,0:T(8,128)(2,1)S(1)} collective-permute-done((bf16[192,512]{1,0:T(8,128)(2,1)S(1)}, bf16[192,512]{1,0:T(8,128)(2,1)S(1)}, u32[]{:S(2)}, u32[]{:S(2)}) %collective-permute-start.18) | collective-permute-done | bytes 196640 | tf_op jit(solution)/shard_map/ppermute | solution.py:279
  84.1 4.2 %collective-permute-done.19.refs_7_ = bf16[192,512]{1,0:T(8,128)(2,1)S(1)} collective-permute-done((bf16[192,512]{1,0:T(8,128)(2,1)S(1)}, bf16[192,512]{1,0:T(8,128)(2,1)S(1)}, u32[]{:S(2)}, u32[]{:S(2)}) %collective-permute-start.19) | collective-permute-done | bytes 196640 | tf_op jit(solution)/shard_map/ppermute | solution.py:279
  89.0 10.0 %attend.2 = (bf16[1536,256]{1,0:T(8,128)(2,1)S(1)}, f32[1536,256]{1,0:T(8,128)S(1)}, bf16[1024,256]{1,0:T(8,128)(2,1)S(1)}) custom-call(s32[2]{0:T(128)S(1)} %pad_add_fusion.me_ref, s32[16]{0:T(128)S(1)} %copy-done.8, bf16[1024,512]{1,0:T(8,128)(2,1)S(1)} %collective-permute-done.17.halo_ref, bf16[1536,512]{1,0:T(8,128)(2,1)S(1)} %get-tuple-element.36.kv_ref, ...), custom_call_target="tpu_custom_call" | custom-call | flops 5033164800 | bytes 4718592 | tf_op jit(solution)/shard_map/attend/pallas_call | solution.py:165
  98.9 2.7 %collective-permute-start.22 = (bf16[1024,256]{1,0:T(8,128)(2,1)S(1)}, bf16[1024,256]{1,0:T(8,128)(2,1)S(1)}, u32[]{:S(2)}, u32[]{:S(2)}) collective-permute-start(bf16[1024,256]{1,0:T(8,128)(2,1)S(1)} %get-tuple-element.39), channel_id=1, source_target_pairs={{8,0},{16,8},{24,16},{9,1},{17,9},{25,17},{10,2},{18,10},{26,18},{... | collective-permute-start | bytes 1572872 | tf_op jit(solution)/shard_map/ppermute | solution.py:29
  104.2 1.7 collective-permute-start.8
  108.3 2.8 %collective-permute-start.14 = (bf16[192,512]{1,0:T(8,128)(2,1)S(1)}, bf16[192,512]{1,0:T(8,128)(2,1)S(1)}, u32[]{:S(2)}, u32[]{:S(2)}) collective-permute-start(bf16[192,512]{1,0:T(8,128)(2,1)S(1)} %packed.28), channel_id=1, source_target_pairs={{0,5},{1,4},{2,7},{3,6},{4,1},{5,0},{6,3},{7,2},{8,13},{9,12},{10,... | collective-permute-start | bytes 589832 | tf_op jit(solution)/shard_map/ppermute | solution.py:279
  111.2 6.9 %collective-permute-done.8.refs_3_ = bf16[192,512]{1,0:T(8,128)(2,1)S(1)} collective-permute-done((bf16[192,512]{1,0:T(8,128)(2,1)S(1)}, bf16[192,512]{1,0:T(8,128)(2,1)S(1)}, u32[]{:S(2)}, u32[]{:S(2)}) %collective-permute-start.8) | collective-permute-done | bytes 196640 | tf_op jit(solution)/shard_map/ppermute | solution.py:279
  119.9 12.5 %collective-permute-done.14.refs_5_ = bf16[192,512]{1,0:T(8,128)(2,1)S(1)} collective-permute-done((bf16[192,512]{1,0:T(8,128)(2,1)S(1)}, bf16[192,512]{1,0:T(8,128)(2,1)S(1)}, u32[]{:S(2)}, u32[]{:S(2)}) %collective-permute-start.14) | collective-permute-done | bytes 196640 | tf_op jit(solution)/shard_map/ppermute | solution.py:279
  132.5 5.4 %collective-permute-done.20.refs_6_ = bf16[192,512]{1,0:T(8,128)(2,1)S(1)} collective-permute-done((bf16[192,512]{1,0:T(8,128)(2,1)S(1)}, bf16[192,512]{1,0:T(8,128)(2,1)S(1)}, u32[]{:S(2)}, u32[]{:S(2)}) %collective-permute-start.20) | collective-permute-done | bytes 196640 | tf_op jit(solution)/shard_map/ppermute | solution.py:279
  137.8 4.4 %collective-permute-done.21.refs_7_ = bf16[192,512]{1,0:T(8,128)(2,1)S(1)} collective-permute-done((bf16[192,512]{1,0:T(8,128)(2,1)S(1)}, bf16[192,512]{1,0:T(8,128)(2,1)S(1)}, u32[]{:S(2)}, u32[]{:S(2)}) %collective-permute-start.21) | collective-permute-done | bytes 196640 | tf_op jit(solution)/shard_map/ppermute | solution.py:279
  142.9 1.9 settled.2
  144.8 3.9 %all-to-all-start = ((bf16[8,192,512]{2,1,0:T(8,128)(2,1)}), bf16[8,192,512]{2,1,0:T(8,128)(2,1)S(1)}, u32[]{:S(2)}, u32[]{:S(2)}) async-start(bf16[8,192,512]{2,1,0:T(8,128)(2,1)} %bitcast.2), calls=%async_computation | async-start | bytes 3145728 | tf_op jit(solution)/shard_map/all_to_all | solution.py:285
  151.3 9.7 %attend.3 = (bf16[1536,256]{1,0:T(8,128)(2,1)S(1)}, f32[1536,256]{1,0:T(8,128)S(1)}, bf16[1024,256]{1,0:T(8,128)(2,1)S(1)}) custom-call(s32[2]{0:T(128)S(1)} %pad_add_fusion.me_ref, s32[16]{0:T(128)S(1)} %copy-done.8, bf16[1024,512]{1,0:T(8,128)(2,1)S(1)} %copy-done.7, bf16[1536,512]{1,0:T(8,128)(2,1)S(1)} %copy-done.5, ...), custom_call_target="tpu_custom_call" | custom-call | flops 5033164800 | bytes 4718592 | tf_op jit(solution)/shard_map/attend/pallas_call | solution.py:165
  161.0 5.4 %collective-permute-start.23 = (bf16[1024,256]{1,0:T(8,128)(2,1)S(1)}, bf16[1024,256]{1,0:T(8,128)(2,1)S(1)}, u32[]{:S(2)}, u32[]{:S(2)}) collective-permute-start(bf16[1024,256]{1,0:T(8,128)(2,1)S(1)} %get-tuple-element.42), channel_id=1, source_target_pairs={{8,0},{16,8},{24,16},{9,1},{17,9},{25,17},{10,2},{18,10},{26,18},{... | collective-permute-start | bytes 1572872 | tf_op jit(solution)/shard_map/ppermute | solution.py:29
  166.5 10.9 %collective-permute-done.23.refs_2_ = bf16[1024,256]{1,0:T(8,128)(2,1)S(1)} collective-permute-done((bf16[1024,256]{1,0:T(8,128)(2,1)S(1)}, bf16[1024,256]{1,0:T(8,128)(2,1)S(1)}, u32[]{:S(2)}, u32[]{:S(2)}) %collective-permute-start.23) | collective-permute-done | bytes 524320 | tf_op jit(solution)/shard_map/ppermute | solution.py:29
  181.2 2.1 collective-permute-start.27
  185.1 9.7 %collective-permute-done.25.refs_3_ = bf16[192,512]{1,0:T(8,128)(2,1)S(1)} collective-permute-done((bf16[192,512]{1,0:T(8,128)(2,1)S(1)}, bf16[192,512]{1,0:T(8,128)(2,1)S(1)}, u32[]{:S(2)}, u32[]{:S(2)}) %collective-permute-start.25) | collective-permute-done | bytes 196640 | tf_op jit(solution)/shard_map/ppermute | solution.py:279
  194.8 4.1 %collective-permute-done.26.refs_4_ = bf16[192,512]{1,0:T(8,128)(2,1)S(1)} collective-permute-done((bf16[192,512]{1,0:T(8,128)(2,1)S(1)}, bf16[192,512]{1,0:T(8,128)(2,1)S(1)}, u32[]{:S(2)}, u32[]{:S(2)}) %collective-permute-start.26) | collective-permute-done | bytes 196640 | tf_op jit(solution)/shard_map/ppermute | solution.py:279
  198.8 9.7 %collective-permute-done.28.refs_6_ = bf16[192,512]{1,0:T(8,128)(2,1)S(1)} collective-permute-done((bf16[192,512]{1,0:T(8,128)(2,1)S(1)}, bf16[192,512]{1,0:T(8,128)(2,1)S(1)}, u32[]{:S(2)}, u32[]{:S(2)}) %collective-permute-start.28) | collective-permute-done | bytes 196640 | tf_op jit(solution)/shard_map/ppermute | solution.py:279
  208.6 5.5 %collective-permute-done.29.refs_7_ = bf16[192,512]{1,0:T(8,128)(2,1)S(1)} collective-permute-done((bf16[192,512]{1,0:T(8,128)(2,1)S(1)}, bf16[192,512]{1,0:T(8,128)(2,1)S(1)}, u32[]{:S(2)}, u32[]{:S(2)}) %collective-permute-start.29) | collective-permute-done | bytes 196640 | tf_op jit(solution)/shard_map/ppermute | solution.py:279
  214.1 4.4 %collective-permute-done.30.refs_8_ = bf16[192,512]{1,0:T(8,128)(2,1)S(1)} collective-permute-done((bf16[192,512]{1,0:T(8,128)(2,1)S(1)}, bf16[192,512]{1,0:T(8,128)(2,1)S(1)}, u32[]{:S(2)}, u32[]{:S(2)}) %collective-permute-start.30) | collective-permute-done | bytes 196640 | tf_op jit(solution)/shard_map/ppermute | solution.py:279
  218.5 2.8 %unpacked.1 = (bf16[192,4096]{1,0:T(8,128)(2,1)}, bf16[192,2048]{1,0:T(8,128)(2,1)}, bf16[192,2048]{1,0:T(8,128)(2,1)}) custom-call(s32[2]{0:T(128)S(1)} %pad_add_fusion.me_ref, bf16[8,192,512]{2,1,0:T(8,128)(2,1)S(1)} %all-to-all-done.refs_0_, bf16[192,512]{1,0:T(8,128)(2,1)S(1)} %get-tuple-element.43.refs_1_, ...), custom_call_target="tpu_custom_call" | custom-call | bytes 6291456 | tf_op jit(solution)/shard_map/unpacked/pallas_call | solution.py:186
  (76 shorter events, 37.5 us)
Async XLA Ops:
  3.7 5.2 %collective-permute-start = (bf16[192,512]{1,0:T(8,128)(2,1)S(1)}, bf16[192,512]{1,0:T(8,128)(2,1)S(1)}, u32[]{:S(2)}, u32[]{:S(2)}) collective-permute-start(bf16[192,512]{1,0:T(8,128)(2,1)S(1)} %get-tuple-element.27), channel_id=1, source_target_pairs={{0,1},{1,0},{2,3},{3,2},{4,5},{5,4},{6,7},{7,6},{8,9},{9,8},{10,11... | collective-permute-start | bytes 589832 | tf_op jit(solution)/shard_map/ppermute | solution.py:279
  4.5 12.2 %collective-permute-start.3 = (bf16[192,512]{1,0:T(8,128)(2,1)S(1)}, bf16[192,512]{1,0:T(8,128)(2,1)S(1)}, u32[]{:S(2)}, u32[]{:S(2)}) collective-permute-start(bf16[192,512]{1,0:T(8,128)(2,1)S(1)} %get-tuple-element.28), channel_id=1, source_target_pairs={{0,2},{1,3},{2,0},{3,1},{4,6},{5,7},{6,4},{7,5},{8,10},{9,11},{10,... | collective-permute-start | bytes 589832 | tf_op jit(solution)/shard_map/ppermute | solution.py:279
  4.7 16.4 %collective-permute-start.6 = (bf16[192,512]{1,0:T(8,128)(2,1)S(1)}, bf16[192,512]{1,0:T(8,128)(2,1)S(1)}, u32[]{:S(2)}, u32[]{:S(2)}) collective-permute-start(bf16[192,512]{1,0:T(8,128)(2,1)S(1)} %get-tuple-element.29), channel_id=1, source_target_pairs={{0,3},{1,2},{2,1},{3,0},{4,7},{5,6},{6,5},{7,4},{8,11},{9,10},{10,... | collective-permute-start | bytes 589832 | tf_op jit(solution)/shard_map/ppermute | solution.py:279
  6.2 14.8 %collective-permute-start.9 = (bf16[192,512]{1,0:T(8,128)(2,1)S(1)}, bf16[192,512]{1,0:T(8,128)(2,1)S(1)}, u32[]{:S(2)}, u32[]{:S(2)}) collective-permute-start(bf16[192,512]{1,0:T(8,128)(2,1)S(1)} %get-tuple-element.30), channel_id=1, source_target_pairs={{0,4},{1,5},{2,6},{3,7},{4,0},{5,1},{6,2},{7,3},{8,12},{9,13},{10,... | collective-permute-start | bytes 589832 | tf_op jit(solution)/shard_map/ppermute | solution.py:279
  8.5 25.3 %collective-permute-start.12 = (bf16[192,512]{1,0:T(8,128)(2,1)S(1)}, bf16[192,512]{1,0:T(8,128)(2,1)S(1)}, u32[]{:S(2)}, u32[]{:S(2)}) collective-permute-start(bf16[192,512]{1,0:T(8,128)(2,1)S(1)} %get-tuple-element.31), channel_id=1, source_target_pairs={{0,5},{1,4},{2,7},{3,6},{4,1},{5,0},{6,3},{7,2},{8,13},{9,12},{10,... | collective-permute-start | bytes 589832 | tf_op jit(solution)/shard_map/ppermute | solution.py:279
  8.9 29.1 %collective-permute-start.15 = (bf16[192,512]{1,0:T(8,128)(2,1)S(1)}, bf16[192,512]{1,0:T(8,128)(2,1)S(1)}, u32[]{:S(2)}, u32[]{:S(2)}) collective-permute-start(bf16[192,512]{1,0:T(8,128)(2,1)S(1)} %get-tuple-element.33), channel_id=1, source_target_pairs={{0,6},{1,7},{2,4},{3,5},{4,2},{5,3},{6,0},{7,1},{8,14},{9,15},{10,... | collective-permute-start | bytes 589832 | tf_op jit(solution)/shard_map/ppermute | solution.py:279
  16.7 25.6 %collective-permute-start.16 = (bf16[192,512]{1,0:T(8,128)(2,1)S(1)}, bf16[192,512]{1,0:T(8,128)(2,1)S(1)}, u32[]{:S(2)}, u32[]{:S(2)}) collective-permute-start(bf16[192,512]{1,0:T(8,128)(2,1)S(1)} %get-tuple-element.34), channel_id=1, source_target_pairs={{0,7},{1,6},{2,5},{3,4},{4,3},{5,2},{6,1},{7,0},{8,15},{9,14},{10,... | collective-permute-start | bytes 589832 | tf_op jit(solution)/shard_map/ppermute | solution.py:279
  43.0 45.9 %collective-permute-start.17 = (bf16[1024,512]{1,0:T(8,128)(2,1)S(1)}, bf16[1024,512]{1,0:T(8,128)(2,1)S(1)}, u32[]{:S(2)}, u32[]{:S(2)}) collective-permute-start(bf16[1024,512]{1,0:T(8,128)(2,1)S(1)} %get-tuple-element.35), channel_id=1, source_target_pairs={{0,8},{8,16},{16,24},{1,9},{9,17},{17,25},{2,10},{10,18},{18,26},{... | collective-permute-start | bytes 3145736 | tf_op jit(solution)/shard_map/ppermute | solution.py:29
  46.7 7.8 %collective-permute-start.1 = (bf16[192,512]{1,0:T(8,128)(2,1)S(1)}, bf16[192,512]{1,0:T(8,128)(2,1)S(1)}, u32[]{:S(2)}, u32[]{:S(2)}) collective-permute-start(bf16[192,512]{1,0:T(8,128)(2,1)S(1)} %packed.19), channel_id=1, source_target_pairs={{0,1},{1,0},{2,3},{3,2},{4,5},{5,4},{6,7},{7,6},{8,9},{9,8},{10,11... | collective-permute-start | bytes 589832 | tf_op jit(solution)/shard_map/ppermute | solution.py:279
  48.5 7.6 %collective-permute-start.4 = (bf16[192,512]{1,0:T(8,128)(2,1)S(1)}, bf16[192,512]{1,0:T(8,128)(2,1)S(1)}, u32[]{:S(2)}, u32[]{:S(2)}) collective-permute-start(bf16[192,512]{1,0:T(8,128)(2,1)S(1)} %packed.21), channel_id=1, source_target_pairs={{0,2},{1,3},{2,0},{3,1},{4,6},{5,7},{6,4},{7,5},{8,10},{9,11},{10,... | collective-permute-start | bytes 589832 | tf_op jit(solution)/shard_map/ppermute | solution.py:279
  49.2 14.6 %collective-permute-start.7 = (bf16[192,512]{1,0:T(8,128)(2,1)S(1)}, bf16[192,512]{1,0:T(8,128)(2,1)S(1)}, u32[]{:S(2)}, u32[]{:S(2)}) collective-permute-start(bf16[192,512]{1,0:T(8,128)(2,1)S(1)} %packed.23), channel_id=1, source_target_pairs={{0,3},{1,2},{2,1},{3,0},{4,7},{5,6},{6,5},{7,4},{8,11},{9,10},{10,... | collective-permute-start | bytes 589832 | tf_op jit(solution)/shard_map/ppermute | solution.py:279
  51.5 14.1 %collective-permute-start.10 = (bf16[192,512]{1,0:T(8,128)(2,1)S(1)}, bf16[192,512]{1,0:T(8,128)(2,1)S(1)}, u32[]{:S(2)}, u32[]{:S(2)}) collective-permute-start(bf16[192,512]{1,0:T(8,128)(2,1)S(1)} %packed.25), channel_id=1, source_target_pairs={{0,4},{1,5},{2,6},{3,7},{4,0},{5,1},{6,2},{7,3},{8,12},{9,13},{10,... | collective-permute-start | bytes 589832 | tf_op jit(solution)/shard_map/ppermute | solution.py:279
  54.5 23.2 %collective-permute-start.13 = (bf16[192,512]{1,0:T(8,128)(2,1)S(1)}, bf16[192,512]{1,0:T(8,128)(2,1)S(1)}, u32[]{:S(2)}, u32[]{:S(2)}) collective-permute-start(bf16[192,512]{1,0:T(8,128)(2,1)S(1)} %packed.27), channel_id=1, source_target_pairs={{0,5},{1,4},{2,7},{3,6},{4,1},{5,0},{6,3},{7,2},{8,13},{9,12},{10,... | collective-permute-start | bytes 589832 | tf_op jit(solution)/shard_map/ppermute | solution.py:279
  56.1 27.9 %collective-permute-start.18 = (bf16[192,512]{1,0:T(8,128)(2,1)S(1)}, bf16[192,512]{1,0:T(8,128)(2,1)S(1)}, u32[]{:S(2)}, u32[]{:S(2)}) collective-permute-start(bf16[192,512]{1,0:T(8,128)(2,1)S(1)} %packed.30), channel_id=1, source_target_pairs={{0,6},{1,7},{2,4},{3,5},{4,2},{5,3},{6,0},{7,1},{8,14},{9,15},{10,... | collective-permute-start | bytes 589832 | tf_op jit(solution)/shard_map/ppermute | solution.py:279
  63.8 24.5 %collective-permute-start.19 = (bf16[192,512]{1,0:T(8,128)(2,1)S(1)}, bf16[192,512]{1,0:T(8,128)(2,1)S(1)}, u32[]{:S(2)}, u32[]{:S(2)}) collective-permute-start(bf16[192,512]{1,0:T(8,128)(2,1)S(1)} %packed.31), channel_id=1, source_target_pairs={{0,7},{1,6},{2,5},{3,4},{4,3},{5,2},{6,1},{7,0},{8,15},{9,14},{10,... | collective-permute-start | bytes 589832 | tf_op jit(solution)/shard_map/ppermute | solution.py:279
  98.9 44.0 %collective-permute-start.22 = (bf16[1024,256]{1,0:T(8,128)(2,1)S(1)}, bf16[1024,256]{1,0:T(8,128)(2,1)S(1)}, u32[]{:S(2)}, u32[]{:S(2)}) collective-permute-start(bf16[1024,256]{1,0:T(8,128)(2,1)S(1)} %get-tuple-element.39), channel_id=1, source_target_pairs={{8,0},{16,8},{24,16},{9,1},{17,9},{25,17},{10,2},{18,10},{26,18},{... | collective-permute-start | bytes 1572872 | tf_op jit(solution)/shard_map/ppermute | solution.py:29
  102.2 6.1 %collective-permute-start.2 = (bf16[192,512]{1,0:T(8,128)(2,1)S(1)}, bf16[192,512]{1,0:T(8,128)(2,1)S(1)}, u32[]{:S(2)}, u32[]{:S(2)}) collective-permute-start(bf16[192,512]{1,0:T(8,128)(2,1)S(1)} %packed.20), channel_id=1, source_target_pairs={{0,1},{1,0},{2,3},{3,2},{4,5},{5,4},{6,7},{7,6},{8,9},{9,8},{10,11... | collective-permute-start | bytes 589832 | tf_op jit(solution)/shard_map/ppermute | solution.py:279
  103.5 7.6 %collective-permute-start.5 = (bf16[192,512]{1,0:T(8,128)(2,1)S(1)}, bf16[192,512]{1,0:T(8,128)(2,1)S(1)}, u32[]{:S(2)}, u32[]{:S(2)}) collective-permute-start(bf16[192,512]{1,0:T(8,128)(2,1)S(1)} %packed.22), channel_id=1, source_target_pairs={{0,2},{1,3},{2,0},{3,1},{4,6},{5,7},{6,4},{7,5},{8,10},{9,11},{10,... | collective-permute-start | bytes 589832 | tf_op jit(solution)/shard_map/ppermute | solution.py:279
  104.2 14.0 %collective-permute-start.8 = (bf16[192,512]{1,0:T(8,128)(2,1)S(1)}, bf16[192,512]{1,0:T(8,128)(2,1)S(1)}, u32[]{:S(2)}, u32[]{:S(2)}) collective-permute-start(bf16[192,512]{1,0:T(8,128)(2,1)S(1)} %packed.24), channel_id=1, source_target_pairs={{0,3},{1,2},{2,1},{3,0},{4,7},{5,6},{6,5},{7,4},{8,11},{9,10},{10,... | collective-permute-start | bytes 589832 | tf_op jit(solution)/shard_map/ppermute | solution.py:279
  106.4 13.5 %collective-permute-start.11 = (bf16[192,512]{1,0:T(8,128)(2,1)S(1)}, bf16[192,512]{1,0:T(8,128)(2,1)S(1)}, u32[]{:S(2)}, u32[]{:S(2)}) collective-permute-start(bf16[192,512]{1,0:T(8,128)(2,1)S(1)} %packed.26), channel_id=1, source_target_pairs={{0,4},{1,5},{2,6},{3,7},{4,0},{5,1},{6,2},{7,3},{8,12},{9,13},{10,... | collective-permute-start | bytes 589832 | tf_op jit(solution)/shard_map/ppermute | solution.py:279
  108.3 24.2 %collective-permute-start.14 = (bf16[192,512]{1,0:T(8,128)(2,1)S(1)}, bf16[192,512]{1,0:T(8,128)(2,1)S(1)}, u32[]{:S(2)}, u32[]{:S(2)}) collective-permute-start(bf16[192,512]{1,0:T(8,128)(2,1)S(1)} %packed.28), channel_id=1, source_target_pairs={{0,5},{1,4},{2,7},{3,6},{4,1},{5,0},{6,3},{7,2},{8,13},{9,12},{10,... | collective-permute-start | bytes 589832 | tf_op jit(solution)/shard_map/ppermute | solution.py:279
  111.1 26.7 %collective-permute-start.20 = (bf16[192,512]{1,0:T(8,128)(2,1)S(1)}, bf16[192,512]{1,0:T(8,128)(2,1)S(1)}, u32[]{:S(2)}, u32[]{:S(2)}) collective-permute-start(bf16[192,512]{1,0:T(8,128)(2,1)S(1)} %packed.32), channel_id=1, source_target_pairs={{0,6},{1,7},{2,4},{3,5},{4,2},{5,3},{6,0},{7,1},{8,14},{9,15},{10,... | collective-permute-start | bytes 589832 | tf_op jit(solution)/shard_map/ppermute | solution.py:279
  118.2 24.1 %collective-permute-start.21 = (bf16[192,512]{1,0:T(8,128)(2,1)S(1)}, bf16[192,512]{1,0:T(8,128)(2,1)S(1)}, u32[]{:S(2)}, u32[]{:S(2)}) collective-permute-start(bf16[192,512]{1,0:T(8,128)(2,1)S(1)} %packed.33), channel_id=1, source_target_pairs={{0,7},{1,6},{2,5},{3,4},{4,3},{5,2},{6,1},{7,0},{8,15},{9,14},{10,... | collective-permute-start | bytes 589832 | tf_op jit(solution)/shard_map/ppermute | solution.py:279
  144.8 73.7 %all-to-all-start = ((bf16[8,192,512]{2,1,0:T(8,128)(2,1)}), bf16[8,192,512]{2,1,0:T(8,128)(2,1)S(1)}, u32[]{:S(2)}, u32[]{:S(2)}) async-start(bf16[8,192,512]{2,1,0:T(8,128)(2,1)} %bitcast.2), calls=%async_computation | async-start | bytes 3145728 | tf_op jit(solution)/shard_map/all_to_all | solution.py:285
  161.0 16.4 %collective-permute-start.23 = (bf16[1024,256]{1,0:T(8,128)(2,1)S(1)}, bf16[1024,256]{1,0:T(8,128)(2,1)S(1)}, u32[]{:S(2)}, u32[]{:S(2)}) collective-permute-start(bf16[1024,256]{1,0:T(8,128)(2,1)S(1)} %get-tuple-element.42), channel_id=1, source_target_pairs={{8,0},{16,8},{24,16},{9,1},{17,9},{25,17},{10,2},{18,10},{26,18},{... | collective-permute-start | bytes 1572872 | tf_op jit(solution)/shard_map/ppermute | solution.py:29
  178.3 5.7 %collective-permute-start.24 = (bf16[192,512]{1,0:T(8,128)(2,1)S(1)}, bf16[192,512]{1,0:T(8,128)(2,1)S(1)}, u32[]{:S(2)}, u32[]{:S(2)}) collective-permute-start(bf16[192,512]{1,0:T(8,128)(2,1)S(1)} %get-tuple-element.44), channel_id=1, source_target_pairs={{0,1},{1,0},{2,3},{3,2},{4,5},{5,4},{6,7},{7,6},{8,9},{9,8},{10,11... | collective-permute-start | bytes 589832 | tf_op jit(solution)/shard_map/ppermute | solution.py:279
  179.5 15.2 %collective-permute-start.25 = (bf16[192,512]{1,0:T(8,128)(2,1)S(1)}, bf16[192,512]{1,0:T(8,128)(2,1)S(1)}, u32[]{:S(2)}, u32[]{:S(2)}) collective-permute-start(bf16[192,512]{1,0:T(8,128)(2,1)S(1)} %get-tuple-element.45), channel_id=1, source_target_pairs={{0,2},{1,3},{2,0},{3,1},{4,6},{5,7},{6,4},{7,5},{8,10},{9,11},{10,... | collective-permute-start | bytes 589832 | tf_op jit(solution)/shard_map/ppermute | solution.py:279
  179.6 19.2 %collective-permute-start.26 = (bf16[192,512]{1,0:T(8,128)(2,1)S(1)}, bf16[192,512]{1,0:T(8,128)(2,1)S(1)}, u32[]{:S(2)}, u32[]{:S(2)}) collective-permute-start(bf16[192,512]{1,0:T(8,128)(2,1)S(1)} %get-tuple-element.46), channel_id=1, source_target_pairs={{0,3},{1,2},{2,1},{3,0},{4,7},{5,6},{6,5},{7,4},{8,11},{9,10},{10,... | collective-permute-start | bytes 589832 | tf_op jit(solution)/shard_map/ppermute | solution.py:279
  181.2 17.6 %collective-permute-start.27 = (bf16[192,512]{1,0:T(8,128)(2,1)S(1)}, bf16[192,512]{1,0:T(8,128)(2,1)S(1)}, u32[]{:S(2)}, u32[]{:S(2)}) collective-permute-start(bf16[192,512]{1,0:T(8,128)(2,1)S(1)} %get-tuple-element.47), channel_id=1, source_target_pairs={{0,4},{1,5},{2,6},{3,7},{4,0},{5,1},{6,2},{7,3},{8,12},{9,13},{10,... | collective-permute-start | bytes 589832 | tf_op jit(solution)/shard_map/ppermute | solution.py:279
  183.3 25.3 %collective-permute-start.28 = (bf16[192,512]{1,0:T(8,128)(2,1)S(1)}, bf16[192,512]{1,0:T(8,128)(2,1)S(1)}, u32[]{:S(2)}, u32[]{:S(2)}) collective-permute-start(bf16[192,512]{1,0:T(8,128)(2,1)S(1)} %get-tuple-element.48), channel_id=1, source_target_pairs={{0,5},{1,4},{2,7},{3,6},{4,1},{5,0},{6,3},{7,2},{8,13},{9,12},{10,... | collective-permute-start | bytes 589832 | tf_op jit(solution)/shard_map/ppermute | solution.py:279
  183.9 30.2 %collective-permute-start.29 = (bf16[192,512]{1,0:T(8,128)(2,1)S(1)}, bf16[192,512]{1,0:T(8,128)(2,1)S(1)}, u32[]{:S(2)}, u32[]{:S(2)}) collective-permute-start(bf16[192,512]{1,0:T(8,128)(2,1)S(1)} %get-tuple-element.49), channel_id=1, source_target_pairs={{0,6},{1,7},{2,4},{3,5},{4,2},{5,3},{6,0},{7,1},{8,14},{9,15},{10,... | collective-permute-start | bytes 589832 | tf_op jit(solution)/shard_map/ppermute | solution.py:279
  194.8 23.7 %collective-permute-start.30 = (bf16[192,512]{1,0:T(8,128)(2,1)S(1)}, bf16[192,512]{1,0:T(8,128)(2,1)S(1)}, u32[]{:S(2)}, u32[]{:S(2)}) collective-permute-start(bf16[192,512]{1,0:T(8,128)(2,1)S(1)} %get-tuple-element.50), channel_id=1, source_target_pairs={{0,7},{1,6},{2,5},{3,4},{4,3},{5,2},{6,1},{7,0},{8,15},{9,14},{10,... | collective-permute-start | bytes 589832 | tf_op jit(solution)/shard_map/ppermute | solution.py:279
  (9 other events, 170.5 us)

commit v9 on v7

--- a/solution.py
+++ b/solution.py
@@ -303,7 +303,7 @@
     came = exchanged(packed(me, (keys, values), ways, places=places), places)
     kv, tail = gathered(me, came, places, WINDOW)
     halo = passed_along(tail, "seq", 1)
-    sent = packed(me, (queries, grad_out), ways, 0, kv_local, places, [came[-1]])
+    sent = packed(me, (queries, grad_out), ways, 0, kv_local, places, [came[1]])
     qds = list(gathered(me, exchanged(sent, places), places, 0))
     for c in range(1, kv_local):
         sent = packed(me, (queries, grad_out), ways, c, kv_local, None, [qds[-1], halo])[0]

time: 208 us -> 212 us (1.019)
  starting transfers between devices: 42.3 us -> 54.6 us
  waiting for transfers between devices: 119 us -> 114 us
  Pallas kernels: 35.8 us -> 31.4 us
    ppermute x3, starting transfers between devices: 8.08 us -> 16.8 us  [passed_along(): return lax.ppermute(shard, axis, pairs)]
    pallas_call x2, Pallas kernels: 24.8 us -> 20.4 us  [attend(): pl.pallas_call(functools.partial(attend_kernel, per_group, chunk, kv_loca...]
    ppermute x3, waiting for transfers between devices: 25.1 us -> 21.9 us  [passed_along(): return lax.ppermute(shard, axis, pairs)]
    ppermute x21, starting transfers between devices: 22.8 us -> 25.9 us  [exchanged(): lax.ppermute(block, 'head', [(i, i ^ k) for i in range(ways)])]
  transfers between devices with their start and end apart: 26 -> 26, of which waited for: 18 -> 18; matrix products, arithmetic and copies ran while one was open for 0% -> 0% of each run, Pallas kernels for 14% -> 12%
where the time goes in v9:
time: 212 us; the launch traced here: 209 us
  waiting for transfers between devices  114 us (54%)
  starting transfers between devices  54.6 us (26%)
  Pallas kernels  31.4 us (15%)
  local copies, waits for them, and re-layouts  8.53 us (4%)
    ppermute x21, waiting for transfers between devices, exchanged(): lax.ppermute(block, 'head', [(i, i ^ k) for i in range(ways)])  89.9 us
    ppermute x21, starting transfers between devices, exchanged(): lax.ppermute(block, 'head', [(i, i ^ k) for i in range(ways)])  25.9 us
    ppermute x3, waiting for transfers between devices, passed_along(): return lax.ppermute(shard, axis, pairs)  21.9 us
    pallas_call x2, Pallas kernels, attend(): pl.pallas_call(functools.partial(attend_kernel, per_group, chunk, kv_loca...  20.4 us
    ppermute x3, starting transfers between devices, passed_along(): return lax.ppermute(shard, axis, pairs)  16.8 us
    all_to_all x2, starting transfers between devices, exchanged_at_once(): return lax.all_to_all(sent, 'head', split_axis=0, concat_axis=0, tiled=True)  11.9 us
    pallas_call x8, Pallas kernels, on_chip(): pl.pallas_call(body, out_shape=outs, in_specs=[SMEM] + [VMEM] * (len(earl...  11 us
    unnamed x22, local copies, waits for them, and re-layouts  8.53 us
  transfers between devices with their start and end apart: 26, of which 18 were waited for; matrix products, arithmetic and copies ran while one was open for 0% of the time, Pallas kernels for 12%

profile of v9, /device:TPU:13, one launch (start us, length us, event | category | flops | bytes accessed | tf_op | source)
XLA Modules:
  0.0 209.0 jit_solution(18287987498284324405)
XLA Ops:
  6.2 2.3 %collective-permute-start.3 = (bf16[192,512]{1,0:T(8,128)(2,1)S(1)}, bf16[192,512]{1,0:T(8,128)(2,1)S(1)}, u32[]{:S(2)}, u32[]{:S(2)}) collective-permute-start(bf16[192,512]{1,0:T(8,128)(2,1)S(1)} %get-tuple-element.39), channel_id=1, source_target_pairs={{0,4},{1,5},{2,6},{3,7},{4,0},{5,1},{6,2},{7,3},{8,12},{9,13},{10,... | collective-permute-start | bytes 589832 | tf_op jit(solution)/shard_map/ppermute | solution.py:283
  10.2 6.5 %collective-permute-done.1.refs_2_ = bf16[192,512]{1,0:T(8,128)(2,1)S(1)} collective-permute-done((bf16[192,512]{1,0:T(8,128)(2,1)S(1)}, bf16[192,512]{1,0:T(8,128)(2,1)S(1)}, u32[]{:S(2)}, u32[]{:S(2)}) %collective-permute-start.1) | collective-permute-done | bytes 196640 | tf_op jit(solution)/shard_map/ppermute | solution.py:283
  18.2 2.8 %collective-permute-done.2.refs_3_ = bf16[192,512]{1,0:T(8,128)(2,1)S(1)} collective-permute-done((bf16[192,512]{1,0:T(8,128)(2,1)S(1)}, bf16[192,512]{1,0:T(8,128)(2,1)S(1)}, u32[]{:S(2)}, u32[]{:S(2)}) %collective-permute-start.2) | collective-permute-done | bytes 196640 | tf_op jit(solution)/shard_map/ppermute | solution.py:283
  21.0 12.7 %collective-permute-done.4.refs_5_ = bf16[192,512]{1,0:T(8,128)(2,1)S(1)} collective-permute-done((bf16[192,512]{1,0:T(8,128)(2,1)S(1)}, bf16[192,512]{1,0:T(8,128)(2,1)S(1)}, u32[]{:S(2)}, u32[]{:S(2)}) %collective-permute-start.4) | collective-permute-done | bytes 196640 | tf_op jit(solution)/shard_map/ppermute | solution.py:283
  33.8 4.2 %collective-permute-done.5.refs_6_ = bf16[192,512]{1,0:T(8,128)(2,1)S(1)} collective-permute-done((bf16[192,512]{1,0:T(8,128)(2,1)S(1)}, bf16[192,512]{1,0:T(8,128)(2,1)S(1)}, u32[]{:S(2)}, u32[]{:S(2)}) %collective-permute-start.5) | collective-permute-done | bytes 196640 | tf_op jit(solution)/shard_map/ppermute | solution.py:283
  38.0 4.3 %collective-permute-done.6.refs_7_ = bf16[192,512]{1,0:T(8,128)(2,1)S(1)} collective-permute-done((bf16[192,512]{1,0:T(8,128)(2,1)S(1)}, bf16[192,512]{1,0:T(8,128)(2,1)S(1)}, u32[]{:S(2)}, u32[]{:S(2)}) %collective-permute-start.6) | collective-permute-done | bytes 196640 | tf_op jit(solution)/shard_map/ppermute | solution.py:283
  43.0 3.1 %collective-permute-start.7 = (bf16[1024,512]{1,0:T(8,128)(2,1)S(1)}, bf16[1024,512]{1,0:T(8,128)(2,1)S(1)}, u32[]{:S(2)}, u32[]{:S(2)}) collective-permute-start(bf16[1024,512]{1,0:T(8,128)(2,1)S(1)} %get-tuple-element.43), channel_id=1, source_target_pairs={{0,8},{8,16},{16,24},{1,9},{9,17},{17,25},{2,10},{10,18},{18,26},{... | collective-permute-start | bytes 3145736 | tf_op jit(solution)/shard_map/ppermute | solution.py:29
  47.0 3.9 %collective-permute-start.11 = (bf16[192,512]{1,0:T(8,128)(2,1)S(1)}, bf16[192,512]{1,0:T(8,128)(2,1)S(1)}, u32[]{:S(2)}, u32[]{:S(2)}) collective-permute-start(bf16[192,512]{1,0:T(8,128)(2,1)S(1)} %get-tuple-element.49), channel_id=1, source_target_pairs={{0,4},{1,5},{2,6},{3,7},{4,0},{5,1},{6,2},{7,3},{8,12},{9,13},{10,... | collective-permute-start | bytes 589832 | tf_op jit(solution)/shard_map/ppermute | solution.py:283
  54.0 2.6 %collective-permute-start.14 = (bf16[192,512]{1,0:T(8,128)(2,1)S(1)}, bf16[192,512]{1,0:T(8,128)(2,1)S(1)}, u32[]{:S(2)}, u32[]{:S(2)}) collective-permute-start(bf16[192,512]{1,0:T(8,128)(2,1)S(1)} %get-tuple-element.52), channel_id=1, source_target_pairs={{0,7},{1,6},{2,5},{3,4},{4,3},{5,2},{6,1},{7,0},{8,15},{9,14},{10,... | collective-permute-start | bytes 589832 | tf_op jit(solution)/shard_map/ppermute | solution.py:283
  56.6 15.4 %collective-permute-done.11.refs_4_ = bf16[192,512]{1,0:T(8,128)(2,1)S(1)} collective-permute-done((bf16[192,512]{1,0:T(8,128)(2,1)S(1)}, bf16[192,512]{1,0:T(8,128)(2,1)S(1)}, u32[]{:S(2)}, u32[]{:S(2)}) %collective-permute-start.11) | collective-permute-done | bytes 196640 | tf_op jit(solution)/shard_map/ppermute | solution.py:283
  73.4 2.9 %collective-permute-done.12.refs_5_ = bf16[192,512]{1,0:T(8,128)(2,1)S(1)} collective-permute-done((bf16[192,512]{1,0:T(8,128)(2,1)S(1)}, bf16[192,512]{1,0:T(8,128)(2,1)S(1)}, u32[]{:S(2)}, u32[]{:S(2)}) %collective-permute-start.12) | collective-permute-done | bytes 196640 | tf_op jit(solution)/shard_map/ppermute | solution.py:283
  76.3 1.7 collective-permute-start.9
  78.0 3.5 %collective-permute-done.13.refs_6_ = bf16[192,512]{1,0:T(8,128)(2,1)S(1)} collective-permute-done((bf16[192,512]{1,0:T(8,128)(2,1)S(1)}, bf16[192,512]{1,0:T(8,128)(2,1)S(1)}, u32[]{:S(2)}, u32[]{:S(2)}) %collective-permute-start.13) | collective-permute-done | bytes 196640 | tf_op jit(solution)/shard_map/ppermute | solution.py:283
  81.5 3.8 %collective-permute-done.14.refs_7_ = bf16[192,512]{1,0:T(8,128)(2,1)S(1)} collective-permute-done((bf16[192,512]{1,0:T(8,128)(2,1)S(1)}, bf16[192,512]{1,0:T(8,128)(2,1)S(1)}, u32[]{:S(2)}, u32[]{:S(2)}) %collective-permute-start.14) | collective-permute-done | bytes 196640 | tf_op jit(solution)/shard_map/ppermute | solution.py:283
  85.9 1.8 packed.5
  88.7 4.8 %all-to-all-start.1 = ((bf16[8,192,512]{2,1,0:T(8,128)(2,1)}), bf16[8,192,512]{2,1,0:T(8,128)(2,1)S(1)}, u32[]{:S(2)}, u32[]{:S(2)}) async-start(bf16[8,192,512]{2,1,0:T(8,128)(2,1)} %packed.5), calls=%async_computation.1 | async-start | bytes 3145728 | tf_op jit(solution)/shard_map/all_to_all | solution.py:289
  96.2 10.2 %attend.2 = (bf16[1536,256]{1,0:T(8,128)(2,1)S(1)}, f32[1536,256]{1,0:T(8,128)S(1)}, bf16[1024,256]{1,0:T(8,128)(2,1)S(1)}) custom-call(s32[2]{0:T(128)S(1)} %pad_add_fusion.me_ref, s32[16]{0:T(128)S(1)} %copy-done.10, bf16[1024,512]{1,0:T(8,128)(2,1)S(1)} %copy-done.3, bf16[1536,512]{1,0:T(8,128)(2,1)S(1)} %copy-done.8, ...), custom_call_target="tpu_custom_call" | custom-call | flops 5033164800 | bytes 4718592 | tf_op jit(solution)/shard_map/attend/pallas_call | solution.py:165
  106.4 6.8 %collective-permute-start.15 = (bf16[1024,256]{1,0:T(8,128)(2,1)S(1)}, bf16[1024,256]{1,0:T(8,128)(2,1)S(1)}, u32[]{:S(2)}, u32[]{:S(2)}) collective-permute-start(bf16[1024,256]{1,0:T(8,128)(2,1)S(1)} %get-tuple-element.55), channel_id=1, source_target_pairs={{8,0},{16,8},{24,16},{9,1},{17,9},{25,17},{10,2},{18,10},{26,18},{... | collective-permute-start | bytes 1572872 | tf_op jit(solution)/shard_map/ppermute | solution.py:29
  113.3 10.9 %collective-permute-done.15.refs_2_ = bf16[1024,256]{1,0:T(8,128)(2,1)S(1)} collective-permute-done((bf16[1024,256]{1,0:T(8,128)(2,1)S(1)}, bf16[1024,256]{1,0:T(8,128)(2,1)S(1)}, u32[]{:S(2)}, u32[]{:S(2)}) %collective-permute-start.15) | collective-permute-done | bytes 524320 | tf_op jit(solution)/shard_map/ppermute | solution.py:29
  124.2 1.9 settled.2
  126.1 1.8 all-to-all-done.1
  127.9 7.0 %all-to-all-start = ((bf16[8,192,512]{2,1,0:T(8,128)(2,1)}), bf16[8,192,512]{2,1,0:T(8,128)(2,1)S(1)}, u32[]{:S(2)}, u32[]{:S(2)}) async-start(bf16[8,192,512]{2,1,0:T(8,128)(2,1)} %bitcast.2), calls=%async_computation | async-start | bytes 3145728 | tf_op jit(solution)/shard_map/all_to_all | solution.py:289
  137.5 10.2 %attend.3 = (bf16[1536,256]{1,0:T(8,128)(2,1)S(1)}, f32[1536,256]{1,0:T(8,128)S(1)}, bf16[1024,256]{1,0:T(8,128)(2,1)S(1)}) custom-call(s32[2]{0:T(128)S(1)} %pad_add_fusion.me_ref, s32[16]{0:T(128)S(1)} %copy-done.10, bf16[1024,512]{1,0:T(8,128)(2,1)S(1)} %copy-done.4, bf16[1536,512]{1,0:T(8,128)(2,1)S(1)} %copy-done.9, bf16[1536,512]{1,0:T(8,128)(2,1)S(1)} %bitcast.4), custom_call_target="tpu_custom_call" | custom-call | flops 5033164800 | bytes 4718592 | tf_op jit(solution)/shard_map/attend/pallas_call | solution.py:165
  147.8 6.8 %collective-permute-start.16 = (bf16[1024,256]{1,0:T(8,128)(2,1)S(1)}, bf16[1024,256]{1,0:T(8,128)(2,1)S(1)}, u32[]{:S(2)}, u32[]{:S(2)}) collective-permute-start(bf16[1024,256]{1,0:T(8,128)(2,1)S(1)} %get-tuple-element.58), channel_id=1, source_target_pairs={{8,0},{16,8},{24,16},{9,1},{17,9},{25,17},{10,2},{18,10},{26,18},{... | collective-permute-start | bytes 1572872 | tf_op jit(solution)/shard_map/ppermute | solution.py:29
  154.6 10.9 %collective-permute-done.16.refs_2_ = bf16[1024,256]{1,0:T(8,128)(2,1)S(1)} collective-permute-done((bf16[1024,256]{1,0:T(8,128)(2,1)S(1)}, bf16[1024,256]{1,0:T(8,128)(2,1)S(1)}, u32[]{:S(2)}, u32[]{:S(2)}) %collective-permute-start.16) | collective-permute-done | bytes 524320 | tf_op jit(solution)/shard_map/ppermute | solution.py:29
  170.0 2.1 %collective-permute-start.20 = (bf16[192,512]{1,0:T(8,128)(2,1)}, bf16[192,512]{1,0:T(8,128)(2,1)S(1)}, u32[]{:S(2)}, u32[]{:S(2)}) collective-permute-start(bf16[192,512]{1,0:T(8,128)(2,1)} %get-tuple-element.63), channel_id=1, source_target_pairs={{0,4},{1,5},{2,6},{3,7},{4,0},{5,1},{6,2},{7,3},{8,12},{9,13},{10,... | collective-permute-start | bytes 589832 | tf_op jit(solution)/shard_map/ppermute | solution.py:283
  173.9 8.2 %collective-permute-done.18.refs_3_ = bf16[192,512]{1,0:T(8,128)(2,1)S(1)} collective-permute-done((bf16[192,512]{1,0:T(8,128)(2,1)S(1)}, bf16[192,512]{1,0:T(8,128)(2,1)S(1)}, u32[]{:S(2)}, u32[]{:S(2)}) %collective-permute-start.18) | collective-permute-done | bytes 196640 | tf_op jit(solution)/shard_map/ppermute | solution.py:283
  182.2 4.3 %collective-permute-done.19.refs_4_ = bf16[192,512]{1,0:T(8,128)(2,1)S(1)} collective-permute-done((bf16[192,512]{1,0:T(8,128)(2,1)}, bf16[192,512]{1,0:T(8,128)(2,1)S(1)}, u32[]{:S(2)}, u32[]{:S(2)}) %collective-permute-start.19) | collective-permute-done | bytes 196640 | tf_op jit(solution)/shard_map/ppermute | solution.py:283
  186.5 11.1 %collective-permute-done.21.refs_6_ = bf16[192,512]{1,0:T(8,128)(2,1)S(1)} collective-permute-done((bf16[192,512]{1,0:T(8,128)(2,1)}, bf16[192,512]{1,0:T(8,128)(2,1)S(1)}, u32[]{:S(2)}, u32[]{:S(2)}) %collective-permute-start.21) | collective-permute-done | bytes 196640 | tf_op jit(solution)/shard_map/ppermute | solution.py:283
  197.6 4.1 %collective-permute-done.22.refs_7_ = bf16[192,512]{1,0:T(8,128)(2,1)S(1)} collective-permute-done((bf16[192,512]{1,0:T(8,128)(2,1)S(1)}, bf16[192,512]{1,0:T(8,128)(2,1)S(1)}, u32[]{:S(2)}, u32[]{:S(2)}) %collective-permute-start.22) | collective-permute-done | bytes 196640 | tf_op jit(solution)/shard_map/ppermute | solution.py:283
  201.7 4.4 %collective-permute-done.23.refs_8_ = bf16[192,512]{1,0:T(8,128)(2,1)S(1)} collective-permute-done((bf16[192,512]{1,0:T(8,128)(2,1)S(1)}, bf16[192,512]{1,0:T(8,128)(2,1)S(1)}, u32[]{:S(2)}, u32[]{:S(2)}) %collective-permute-start.23) | collective-permute-done | bytes 196640 | tf_op jit(solution)/shard_map/ppermute | solution.py:283
  206.2 2.8 %unpacked.1 = (bf16[192,4096]{1,0:T(8,128)(2,1)}, bf16[192,2048]{1,0:T(8,128)(2,1)}, bf16[192,2048]{1,0:T(8,128)(2,1)}) custom-call(s32[2]{0:T(128)S(1)} %pad_add_fusion.me_ref, bf16[8,192,512]{2,1,0:T(8,128)(2,1)S(1)} %all-to-all-done.refs_0_, bf16[192,512]{1,0:T(8,128)(2,1)S(1)} %get-tuple-element.59.refs_1_, ...), custom_call_target="tpu_custom_call" | custom-call | bytes 6291456 | tf_op jit(solution)/shard_map/unpacked/pallas_call | solution.py:186
  (53 shorter events, 27.9 us)
Async XLA Ops:
  3.0 43.1 %copy-start = (bf16[192,4096]{1,0:T(8,128)(2,1)S(1)}, bf16[192,4096]{1,0:T(8,128)(2,1)}, u32[]{:S(2)}) copy-start(bf16[192,4096]{1,0:T(8,128)(2,1)} %refs_2_.3) | copy-start | bytes 4718596
  3.0 43.1 %copy-start.1 = (bf16[192,4096]{1,0:T(8,128)(2,1)S(1)}, bf16[192,4096]{1,0:T(8,128)(2,1)}, u32[]{:S(2)}) copy-start(bf16[192,4096]{1,0:T(8,128)(2,1)} %refs_3_.1) | copy-start | bytes 4718596
  3.7 5.2 %collective-permute-start = (bf16[192,512]{1,0:T(8,128)(2,1)S(1)}, bf16[192,512]{1,0:T(8,128)(2,1)S(1)}, u32[]{:S(2)}, u32[]{:S(2)}) collective-permute-start(bf16[192,512]{1,0:T(8,128)(2,1)S(1)} %get-tuple-element.36), channel_id=1, source_target_pairs={{0,1},{1,0},{2,3},{3,2},{4,5},{5,4},{6,7},{7,6},{8,9},{9,8},{10,11... | collective-permute-start | bytes 589832 | tf_op jit(solution)/shard_map/ppermute | solution.py:283
  4.5 12.2 %collective-permute-start.1 = (bf16[192,512]{1,0:T(8,128)(2,1)S(1)}, bf16[192,512]{1,0:T(8,128)(2,1)S(1)}, u32[]{:S(2)}, u32[]{:S(2)}) collective-permute-start(bf16[192,512]{1,0:T(8,128)(2,1)S(1)} %get-tuple-element.37), channel_id=1, source_target_pairs={{0,2},{1,3},{2,0},{3,1},{4,6},{5,7},{6,4},{7,5},{8,10},{9,11},{10,... | collective-permute-start | bytes 589832 | tf_op jit(solution)/shard_map/ppermute | solution.py:283
  4.7 16.4 %collective-permute-start.2 = (bf16[192,512]{1,0:T(8,128)(2,1)S(1)}, bf16[192,512]{1,0:T(8,128)(2,1)S(1)}, u32[]{:S(2)}, u32[]{:S(2)}) collective-permute-start(bf16[192,512]{1,0:T(8,128)(2,1)S(1)} %get-tuple-element.38), channel_id=1, source_target_pairs={{0,3},{1,2},{2,1},{3,0},{4,7},{5,6},{6,5},{7,4},{8,11},{9,10},{10,... | collective-permute-start | bytes 589832 | tf_op jit(solution)/shard_map/ppermute | solution.py:283
  6.2 14.8 %collective-permute-start.3 = (bf16[192,512]{1,0:T(8,128)(2,1)S(1)}, bf16[192,512]{1,0:T(8,128)(2,1)S(1)}, u32[]{:S(2)}, u32[]{:S(2)}) collective-permute-start(bf16[192,512]{1,0:T(8,128)(2,1)S(1)} %get-tuple-element.39), channel_id=1, source_target_pairs={{0,4},{1,5},{2,6},{3,7},{4,0},{5,1},{6,2},{7,3},{8,12},{9,13},{10,... | collective-permute-start | bytes 589832 | tf_op jit(solution)/shard_map/ppermute | solution.py:283
  8.5 25.3 %collective-permute-start.4 = (bf16[192,512]{1,0:T(8,128)(2,1)S(1)}, bf16[192,512]{1,0:T(8,128)(2,1)S(1)}, u32[]{:S(2)}, u32[]{:S(2)}) collective-permute-start(bf16[192,512]{1,0:T(8,128)(2,1)S(1)} %get-tuple-element.40), channel_id=1, source_target_pairs={{0,5},{1,4},{2,7},{3,6},{4,1},{5,0},{6,3},{7,2},{8,13},{9,12},{10,... | collective-permute-start | bytes 589832 | tf_op jit(solution)/shard_map/ppermute | solution.py:283
  8.9 29.1 %collective-permute-start.5 = (bf16[192,512]{1,0:T(8,128)(2,1)S(1)}, bf16[192,512]{1,0:T(8,128)(2,1)S(1)}, u32[]{:S(2)}, u32[]{:S(2)}) collective-permute-start(bf16[192,512]{1,0:T(8,128)(2,1)S(1)} %get-tuple-element.41), channel_id=1, source_target_pairs={{0,6},{1,7},{2,4},{3,5},{4,2},{5,3},{6,0},{7,1},{8,14},{9,15},{10,... | collective-permute-start | bytes 589832 | tf_op jit(solution)/shard_map/ppermute | solution.py:283
  16.7 25.6 %collective-permute-start.6 = (bf16[192,512]{1,0:T(8,128)(2,1)S(1)}, bf16[192,512]{1,0:T(8,128)(2,1)S(1)}, u32[]{:S(2)}, u32[]{:S(2)}) collective-permute-start(bf16[192,512]{1,0:T(8,128)(2,1)S(1)} %get-tuple-element.42), channel_id=1, source_target_pairs={{0,7},{1,6},{2,5},{3,4},{4,3},{5,2},{6,1},{7,0},{8,15},{9,14},{10,... | collective-permute-start | bytes 589832 | tf_op jit(solution)/shard_map/ppermute | solution.py:283
  43.0 3.9 %copy-start.7 = (bf16[1536,512]{1,0:T(8,128)(2,1)}, bf16[1536,512]{1,0:T(8,128)(2,1)S(1)}, u32[]{:S(2)}) copy-start(bf16[1536,512]{1,0:T(8,128)(2,1)S(1)} %get-tuple-element.44.kv_ref) | copy-start | bytes 4718596
  43.0 42.9 %collective-permute-start.7 = (bf16[1024,512]{1,0:T(8,128)(2,1)S(1)}, bf16[1024,512]{1,0:T(8,128)(2,1)S(1)}, u32[]{:S(2)}, u32[]{:S(2)}) collective-permute-start(bf16[1024,512]{1,0:T(8,128)(2,1)S(1)} %get-tuple-element.43), channel_id=1, source_target_pairs={{0,8},{8,16},{16,24},{1,9},{9,17},{17,25},{2,10},{10,18},{18,26},{... | collective-permute-start | bytes 3145736 | tf_op jit(solution)/shard_map/ppermute | solution.py:29
  46.9 7.1 %collective-permute-start.10 = (bf16[192,512]{1,0:T(8,128)(2,1)S(1)}, bf16[192,512]{1,0:T(8,128)(2,1)S(1)}, u32[]{:S(2)}, u32[]{:S(2)}) collective-permute-start(bf16[192,512]{1,0:T(8,128)(2,1)S(1)} %get-tuple-element.48), channel_id=1, source_target_pairs={{0,3},{1,2},{2,1},{3,0},{4,7},{5,6},{6,5},{7,4},{8,11},{9,10},{10,... | collective-permute-start | bytes 589832 | tf_op jit(solution)/shard_map/ppermute | solution.py:283
  47.0 25.1 %collective-permute-start.11 = (bf16[192,512]{1,0:T(8,128)(2,1)S(1)}, bf16[192,512]{1,0:T(8,128)(2,1)S(1)}, u32[]{:S(2)}, u32[]{:S(2)}) collective-permute-start(bf16[192,512]{1,0:T(8,128)(2,1)S(1)} %get-tuple-element.49), channel_id=1, source_target_pairs={{0,4},{1,5},{2,6},{3,7},{4,0},{5,1},{6,2},{7,3},{8,12},{9,13},{10,... | collective-permute-start | bytes 589832 | tf_op jit(solution)/shard_map/ppermute | solution.py:283
  50.9 25.4 %collective-permute-start.12 = (bf16[192,512]{1,0:T(8,128)(2,1)S(1)}, bf16[192,512]{1,0:T(8,128)(2,1)S(1)}, u32[]{:S(2)}, u32[]{:S(2)}) collective-permute-start(bf16[192,512]{1,0:T(8,128)(2,1)S(1)} %get-tuple-element.50), channel_id=1, source_target_pairs={{0,5},{1,4},{2,7},{3,6},{4,1},{5,0},{6,3},{7,2},{8,13},{9,12},{10,... | collective-permute-start | bytes 589832 | tf_op jit(solution)/shard_map/ppermute | solution.py:283
  50.9 30.6 %collective-permute-start.13 = (bf16[192,512]{1,0:T(8,128)(2,1)S(1)}, bf16[192,512]{1,0:T(8,128)(2,1)S(1)}, u32[]{:S(2)}, u32[]{:S(2)}) collective-permute-start(bf16[192,512]{1,0:T(8,128)(2,1)S(1)} %get-tuple-element.51), channel_id=1, source_target_pairs={{0,6},{1,7},{2,4},{3,5},{4,2},{5,3},{6,0},{7,1},{8,14},{9,15},{10,... | collective-permute-start | bytes 589832 | tf_op jit(solution)/shard_map/ppermute | solution.py:283
  54.0 31.2 %collective-permute-start.14 = (bf16[192,512]{1,0:T(8,128)(2,1)S(1)}, bf16[192,512]{1,0:T(8,128)(2,1)S(1)}, u32[]{:S(2)}, u32[]{:S(2)}) collective-permute-start(bf16[192,512]{1,0:T(8,128)(2,1)S(1)} %get-tuple-element.52), channel_id=1, source_target_pairs={{0,7},{1,6},{2,5},{3,4},{4,3},{5,2},{6,1},{7,0},{8,15},{9,14},{10,... | collective-permute-start | bytes 589832 | tf_op jit(solution)/shard_map/ppermute | solution.py:283
  72.1 13.2 %collective-permute-start.8 = (bf16[192,512]{1,0:T(8,128)(2,1)S(1)}, bf16[192,512]{1,0:T(8,128)(2,1)S(1)}, u32[]{:S(2)}, u32[]{:S(2)}) collective-permute-start(bf16[192,512]{1,0:T(8,128)(2,1)S(1)} %get-tuple-element.46), channel_id=1, source_target_pairs={{0,1},{1,0},{2,3},{3,2},{4,5},{5,4},{6,7},{7,6},{8,9},{9,8},{10,11... | collective-permute-start | bytes 589832 | tf_op jit(solution)/shard_map/ppermute | solution.py:283
  76.3 9.0 %collective-permute-start.9 = (bf16[192,512]{1,0:T(8,128)(2,1)S(1)}, bf16[192,512]{1,0:T(8,128)(2,1)S(1)}, u32[]{:S(2)}, u32[]{:S(2)}) collective-permute-start(bf16[192,512]{1,0:T(8,128)(2,1)S(1)} %get-tuple-element.47), channel_id=1, source_target_pairs={{0,2},{1,3},{2,0},{3,1},{4,6},{5,7},{6,4},{7,5},{8,10},{9,11},{10,... | collective-permute-start | bytes 589832 | tf_op jit(solution)/shard_map/ppermute | solution.py:283
  88.7 4.9 %copy-start.10 = (s32[16]{0:T(128)S(1)}, s32[16]{0:T(128)}, u32[]{:S(2)}) copy-start(s32[16]{0:T(128)} %docs_ref.3) | copy-start | bytes 196
  88.7 39.1 %all-to-all-start.1 = ((bf16[8,192,512]{2,1,0:T(8,128)(2,1)}), bf16[8,192,512]{2,1,0:T(8,128)(2,1)S(1)}, u32[]{:S(2)}, u32[]{:S(2)}) async-start(bf16[8,192,512]{2,1,0:T(8,128)(2,1)} %packed.5), calls=%async_computation.1 | async-start | bytes 3145728 | tf_op jit(solution)/shard_map/all_to_all | solution.py:289
  94.8 1.4 copy-start.8
  106.4 17.8 %collective-permute-start.15 = (bf16[1024,256]{1,0:T(8,128)(2,1)S(1)}, bf16[1024,256]{1,0:T(8,128)(2,1)S(1)}, u32[]{:S(2)}, u32[]{:S(2)}) collective-permute-start(bf16[1024,256]{1,0:T(8,128)(2,1)S(1)} %get-tuple-element.55), channel_id=1, source_target_pairs={{8,0},{16,8},{24,16},{9,1},{17,9},{25,17},{10,2},{18,10},{26,18},{... | collective-permute-start | bytes 1572872 | tf_op jit(solution)/shard_map/ppermute | solution.py:29
  127.9 54.3 %all-to-all-start = ((bf16[8,192,512]{2,1,0:T(8,128)(2,1)}), bf16[8,192,512]{2,1,0:T(8,128)(2,1)S(1)}, u32[]{:S(2)}, u32[]{:S(2)}) async-start(bf16[8,192,512]{2,1,0:T(8,128)(2,1)} %bitcast.2), calls=%async_computation | async-start | bytes 3145728 | tf_op jit(solution)/shard_map/all_to_all | solution.py:289
  136.1 1.4 copy-start.9
  147.8 17.8 %collective-permute-start.16 = (bf16[1024,256]{1,0:T(8,128)(2,1)S(1)}, bf16[1024,256]{1,0:T(8,128)(2,1)S(1)}, u32[]{:S(2)}, u32[]{:S(2)}) collective-permute-start(bf16[1024,256]{1,0:T(8,128)(2,1)S(1)} %get-tuple-element.58), channel_id=1, source_target_pairs={{8,0},{16,8},{24,16},{9,1},{17,9},{25,17},{10,2},{18,10},{26,18},{... | collective-permute-start | bytes 1572872 | tf_op jit(solution)/shard_map/ppermute | solution.py:29
  167.2 5.6 %collective-permute-start.17 = (bf16[192,512]{1,0:T(8,128)(2,1)S(1)}, bf16[192,512]{1,0:T(8,128)(2,1)S(1)}, u32[]{:S(2)}, u32[]{:S(2)}) collective-permute-start(bf16[192,512]{1,0:T(8,128)(2,1)S(1)} %get-tuple-element.60), channel_id=1, source_target_pairs={{0,1},{1,0},{2,3},{3,2},{4,5},{5,4},{6,7},{7,6},{8,9},{9,8},{10,11... | collective-permute-start | bytes 589832 | tf_op jit(solution)/shard_map/ppermute | solution.py:283
  168.3 13.8 %collective-permute-start.18 = (bf16[192,512]{1,0:T(8,128)(2,1)S(1)}, bf16[192,512]{1,0:T(8,128)(2,1)S(1)}, u32[]{:S(2)}, u32[]{:S(2)}) collective-permute-start(bf16[192,512]{1,0:T(8,128)(2,1)S(1)} %get-tuple-element.61), channel_id=1, source_target_pairs={{0,2},{1,3},{2,0},{3,1},{4,6},{5,7},{6,4},{7,5},{8,10},{9,11},{10,... | collective-permute-start | bytes 589832 | tf_op jit(solution)/shard_map/ppermute | solution.py:283
  168.4 18.1 %collective-permute-start.19 = (bf16[192,512]{1,0:T(8,128)(2,1)}, bf16[192,512]{1,0:T(8,128)(2,1)S(1)}, u32[]{:S(2)}, u32[]{:S(2)}) collective-permute-start(bf16[192,512]{1,0:T(8,128)(2,1)} %get-tuple-element.62), channel_id=1, source_target_pairs={{0,3},{1,2},{2,1},{3,0},{4,7},{5,6},{6,5},{7,4},{8,11},{9,10},{10,... | collective-permute-start | bytes 589832 | tf_op jit(solution)/shard_map/ppermute | solution.py:283
  170.0 16.5 %collective-permute-start.20 = (bf16[192,512]{1,0:T(8,128)(2,1)}, bf16[192,512]{1,0:T(8,128)(2,1)S(1)}, u32[]{:S(2)}, u32[]{:S(2)}) collective-permute-start(bf16[192,512]{1,0:T(8,128)(2,1)} %get-tuple-element.63), channel_id=1, source_target_pairs={{0,4},{1,5},{2,6},{3,7},{4,0},{5,1},{6,2},{7,3},{8,12},{9,13},{10,... | collective-permute-start | bytes 589832 | tf_op jit(solution)/shard_map/ppermute | solution.py:283
  172.1 25.5 %collective-permute-start.21 = (bf16[192,512]{1,0:T(8,128)(2,1)}, bf16[192,512]{1,0:T(8,128)(2,1)S(1)}, u32[]{:S(2)}, u32[]{:S(2)}) collective-permute-start(bf16[192,512]{1,0:T(8,128)(2,1)} %get-tuple-element.64), channel_id=1, source_target_pairs={{0,5},{1,4},{2,7},{3,6},{4,1},{5,0},{6,3},{7,2},{8,13},{9,12},{10,... | collective-permute-start | bytes 589832 | tf_op jit(solution)/shard_map/ppermute | solution.py:283
  172.7 29.0 %collective-permute-start.22 = (bf16[192,512]{1,0:T(8,128)(2,1)S(1)}, bf16[192,512]{1,0:T(8,128)(2,1)S(1)}, u32[]{:S(2)}, u32[]{:S(2)}) collective-permute-start(bf16[192,512]{1,0:T(8,128)(2,1)S(1)} %get-tuple-element.65), channel_id=1, source_target_pairs={{0,6},{1,7},{2,4},{3,5},{4,2},{5,3},{6,0},{7,1},{8,14},{9,15},{10,... | collective-permute-start | bytes 589832 | tf_op jit(solution)/shard_map/ppermute | solution.py:283
  182.2 24.0 %collective-permute-start.23 = (bf16[192,512]{1,0:T(8,128)(2,1)S(1)}, bf16[192,512]{1,0:T(8,128)(2,1)S(1)}, u32[]{:S(2)}, u32[]{:S(2)}) collective-permute-start(bf16[192,512]{1,0:T(8,128)(2,1)S(1)} %get-tuple-element.66), channel_id=1, source_target_pairs={{0,7},{1,6},{2,5},{3,4},{4,3},{5,2},{6,1},{7,0},{8,15},{9,14},{10,... | collective-permute-start | bytes 589832 | tf_op jit(solution)/shard_map/ppermute | solution.py:283
  (5 other events, 5.7 us)

commit v10 on v9

--- a/solution.py
+++ b/solution.py
@@ -304,9 +304,10 @@
     kv, tail = gathered(me, came, places, WINDOW)
     halo = passed_along(tail, "seq", 1)
     sent = packed(me, (queries, grad_out), ways, 0, kv_local, places, [came[1]])
-    qds = list(gathered(me, exchanged(sent, places), places, 0))
+    first = exchanged(sent, places)
+    qds = list(gathered(me, first, places, 0))
     for c in range(1, kv_local):
-        sent = packed(me, (queries, grad_out), ways, c, kv_local, None, [qds[-1], halo])[0]
+        sent = packed(me, (queries, grad_out), ways, c, kv_local, None, [*(first[1:] if c == 1 else qds[-1:]), halo])[0]
         qds.append(exchanged_at_once(sent).reshape(group, 2 * q_lanes))
 
     grads = []

time: 212 us -> 213 us (level)
  starting transfers between devices: 54.6 us -> 39.1 us
  waiting for transfers between devices: 114 us -> 121 us
  Pallas kernels: 31.4 us -> 36.1 us
  local copies, waits for them, and re-layouts: 8.53 us -> 12.1 us
    ppermute x3, starting transfers between devices: 16.8 us -> 6.96 us  [passed_along(): return lax.ppermute(shard, axis, pairs)]
    ppermute x21, waiting for transfers between devices: 89.9 us -> 94.9 us  [exchanged(): lax.ppermute(block, 'head', [(i, i ^ k) for i in range(ways)])]
    pallas_call x2, Pallas kernels: 20.4 us -> 25.1 us  [attend(): pl.pallas_call(functools.partial(attend_kernel, per_group, chunk, kv_loca...]
    ppermute x3, waiting for transfers between devices: 21.9 us -> 26.2 us  [passed_along(): return lax.ppermute(shard, axis, pairs)]
    ppermute x21, starting transfers between devices: 25.9 us -> 21.9 us  [exchanged(): lax.ppermute(block, 'head', [(i, i ^ k) for i in range(ways)])]
    unnamed x22 -> x36, local copies, waits for them, and re-layouts: 8.53 us -> 12.1 us
  transfers between devices with their start and end apart: 26 -> 26, of which waited for: 18 -> 17; matrix products, arithmetic and copies ran while one was open for 0% -> 0% of each run, Pallas kernels for 12% -> 14%
where the time goes in v10:
time: 213 us; the launch traced here: 209 us
  waiting for transfers between devices  121 us (57%)
  starting transfers between devices  39.1 us (18%)
  Pallas kernels  36.1 us (17%)
  local copies, waits for them, and re-layouts  12.1 us (6%)
    ppermute x21, waiting for transfers between devices, exchanged(): lax.ppermute(block, 'head', [(i, i ^ k) for i in range(ways)])  94.9 us
    ppermute x3, waiting for transfers between devices, passed_along(): return lax.ppermute(shard, axis, pairs)  26.2 us
    pallas_call x2, Pallas kernels, attend(): pl.pallas_call(functools.partial(attend_kernel, per_group, chunk, kv_loca...  25.1 us
    ppermute x21, starting transfers between devices, exchanged(): lax.ppermute(block, 'head', [(i, i ^ k) for i in range(ways)])  21.9 us
    unnamed x36, local copies, waits for them, and re-layouts  12.1 us
    pallas_call x8, Pallas kernels, on_chip(): pl.pallas_call(body, out_shape=outs, in_specs=[SMEM] + [VMEM] * (len(earl...  11 us
    all_to_all x2, starting transfers between devices, exchanged_at_once(): return lax.all_to_all(sent, 'head', split_axis=0, concat_axis=0, tiled=True)  10.3 us
    ppermute x3, starting transfers between devices, passed_along(): return lax.ppermute(shard, axis, pairs)  6.96 us
  transfers between devices with their start and end apart: 26, of which 17 were waited for; matrix products, arithmetic and copies ran while one was open for 0% of the time, Pallas kernels for 14%

profile of v10, /device:TPU:13, one launch (start us, length us, event | category | flops | bytes accessed | tf_op | source)
XLA Modules:
  0.0 209.3 jit_solution(14102360220783030313)
XLA Ops:
  6.2 2.3 %collective-permute-start.3 = (bf16[192,512]{1,0:T(8,128)(2,1)S(1)}, bf16[192,512]{1,0:T(8,128)(2,1)S(1)}, u32[]{:S(2)}, u32[]{:S(2)}) collective-permute-start(bf16[192,512]{1,0:T(8,128)(2,1)S(1)} %get-tuple-element.39), channel_id=1, source_target_pairs={{0,4},{1,5},{2,6},{3,7},{4,0},{5,1},{6,2},{7,3},{8,12},{9,13},{10,... | collective-permute-start | bytes 589832 | tf_op jit(solution)/shard_map/ppermute | solution.py:283
  10.2 6.5 %collective-permute-done.1.refs_2_ = bf16[192,512]{1,0:T(8,128)(2,1)S(1)} collective-permute-done((bf16[192,512]{1,0:T(8,128)(2,1)S(1)}, bf16[192,512]{1,0:T(8,128)(2,1)S(1)}, u32[]{:S(2)}, u32[]{:S(2)}) %collective-permute-start.1) | collective-permute-done | bytes 196640 | tf_op jit(solution)/shard_map/ppermute | solution.py:283
  18.2 2.8 %collective-permute-done.2.refs_3_ = bf16[192,512]{1,0:T(8,128)(2,1)S(1)} collective-permute-done((bf16[192,512]{1,0:T(8,128)(2,1)S(1)}, bf16[192,512]{1,0:T(8,128)(2,1)S(1)}, u32[]{:S(2)}, u32[]{:S(2)}) %collective-permute-start.2) | collective-permute-done | bytes 196640 | tf_op jit(solution)/shard_map/ppermute | solution.py:283
  21.0 12.7 %collective-permute-done.4.refs_5_ = bf16[192,512]{1,0:T(8,128)(2,1)S(1)} collective-permute-done((bf16[192,512]{1,0:T(8,128)(2,1)S(1)}, bf16[192,512]{1,0:T(8,128)(2,1)S(1)}, u32[]{:S(2)}, u32[]{:S(2)}) %collective-permute-start.4) | collective-permute-done | bytes 196640 | tf_op jit(solution)/shard_map/ppermute | solution.py:283
  33.8 4.2 %collective-permute-done.5.refs_6_ = bf16[192,512]{1,0:T(8,128)(2,1)S(1)} collective-permute-done((bf16[192,512]{1,0:T(8,128)(2,1)S(1)}, bf16[192,512]{1,0:T(8,128)(2,1)S(1)}, u32[]{:S(2)}, u32[]{:S(2)}) %collective-permute-start.5) | collective-permute-done | bytes 196640 | tf_op jit(solution)/shard_map/ppermute | solution.py:283
  38.0 4.3 %collective-permute-done.6.refs_7_ = bf16[192,512]{1,0:T(8,128)(2,1)S(1)} collective-permute-done((bf16[192,512]{1,0:T(8,128)(2,1)S(1)}, bf16[192,512]{1,0:T(8,128)(2,1)S(1)}, u32[]{:S(2)}, u32[]{:S(2)}) %collective-permute-start.6) | collective-permute-done | bytes 196640 | tf_op jit(solution)/shard_map/ppermute | solution.py:283
  43.0 3.1 %collective-permute-start.7 = (bf16[1024,512]{1,0:T(8,128)(2,1)S(1)}, bf16[1024,512]{1,0:T(8,128)(2,1)S(1)}, u32[]{:S(2)}, u32[]{:S(2)}) collective-permute-start(bf16[1024,512]{1,0:T(8,128)(2,1)S(1)} %get-tuple-element.43), channel_id=1, source_target_pairs={{0,8},{8,16},{16,24},{1,9},{9,17},{17,25},{2,10},{10,18},{18,26},{... | collective-permute-start | bytes 3145736 | tf_op jit(solution)/shard_map/ppermute | solution.py:29
  48.8 1.6 collective-permute-start.10
  53.2 8.0 %collective-permute-done.9.refs_2_.refs_1_ = bf16[192,512]{1,0:T(8,128)(2,1)S(1)} collective-permute-done((bf16[192,512]{1,0:T(8,128)(2,1)S(1)}, bf16[192,512]{1,0:T(8,128)(2,1)S(1)}, u32[]{:S(2)}, u32[]{:S(2)}) %collective-permute-start.9) | collective-permute-done | bytes 196640 | tf_op jit(solution)/shard_map/ppermute | solution.py:283
  61.7 3.8 %collective-permute-done.10.refs_3_.refs_2_ = bf16[192,512]{1,0:T(8,128)(2,1)S(1)} collective-permute-done((bf16[192,512]{1,0:T(8,128)(2,1)S(1)}, bf16[192,512]{1,0:T(8,128)(2,1)S(1)}, u32[]{:S(2)}, u32[]{:S(2)}) %collective-permute-start.10) | collective-permute-done | bytes 196640 | tf_op jit(solution)/shard_map/ppermute | solution.py:283
  66.5 10.0 %collective-permute-done.12.refs_5_.refs_4_ = bf16[192,512]{1,0:T(8,128)(2,1)S(1)} collective-permute-done((bf16[192,512]{1,0:T(8,128)(2,1)S(1)}, bf16[192,512]{1,0:T(8,128)(2,1)S(1)}, u32[]{:S(2)}, u32[]{:S(2)}) %collective-permute-start.12) | collective-permute-done | bytes 196640 | tf_op jit(solution)/shard_map/ppermute | solution.py:283
  76.5 6.2 %collective-permute-done.13.refs_6_.refs_5_ = bf16[192,512]{1,0:T(8,128)(2,1)S(1)} collective-permute-done((bf16[192,512]{1,0:T(8,128)(2,1)S(1)}, bf16[192,512]{1,0:T(8,128)(2,1)S(1)}, u32[]{:S(2)}, u32[]{:S(2)}) %collective-permute-start.13) | collective-permute-done | bytes 196640 | tf_op jit(solution)/shard_map/ppermute | solution.py:283
  82.7 4.2 %collective-permute-done.14.refs_7_.refs_6_ = bf16[192,512]{1,0:T(8,128)(2,1)S(1)} collective-permute-done((bf16[192,512]{1,0:T(8,128)(2,1)S(1)}, bf16[192,512]{1,0:T(8,128)(2,1)S(1)}, u32[]{:S(2)}, u32[]{:S(2)}) %collective-permute-start.14) | collective-permute-done | bytes 196640 | tf_op jit(solution)/shard_map/ppermute | solution.py:283
  86.9 1.8 packed.5
  90.8 3.7 %all-to-all-start.1 = ((bf16[8,192,512]{2,1,0:T(8,128)(2,1)}), bf16[8,192,512]{2,1,0:T(8,128)(2,1)S(1)}, u32[]{:S(2)}, u32[]{:S(2)}) async-start(bf16[8,192,512]{2,1,0:T(8,128)(2,1)} %packed.5), calls=%async_computation.1 | async-start | bytes 3145728 | tf_op jit(solution)/shard_map/all_to_all | solution.py:289
  99.6 12.7 %attend.2 = (bf16[1536,256]{1,0:T(8,128)(2,1)S(1)}, f32[1536,256]{1,0:T(8,128)S(1)}, bf16[1024,256]{1,0:T(8,128)(2,1)S(1)}) custom-call(s32[2]{0:T(128)S(1)} %pad_add_fusion.me_ref, s32[16]{0:T(128)S(1)} %copy-done.17, bf16[1024,512]{1,0:T(8,128)(2,1)S(1)} %collective-permute-done.7.halo_ref.refs_7_, bf16[1536,512]{1,0:T(8,128)(2,1)S(1)} %copy-done.15, ...), custom_call_target="tpu_custom_call" | custom-call | flops 5033164800 | bytes 4718592 | tf_op jit(solution)/shard_map/attend/pallas_call | solution.py:165
  112.2 1.9 collective-permute-start.15
  114.2 13.1 %collective-permute-done.15.refs_2_ = bf16[1024,256]{1,0:T(8,128)(2,1)S(1)} collective-permute-done((bf16[1024,256]{1,0:T(8,128)(2,1)S(1)}, bf16[1024,256]{1,0:T(8,128)(2,1)S(1)}, u32[]{:S(2)}, u32[]{:S(2)}) %collective-permute-start.15) | collective-permute-done | bytes 524320 | tf_op jit(solution)/shard_map/ppermute | solution.py:29
  127.3 1.8 settled.2
  129.1 6.6 %all-to-all-start = ((bf16[8,192,512]{2,1,0:T(8,128)(2,1)}), bf16[8,192,512]{2,1,0:T(8,128)(2,1)S(1)}, u32[]{:S(2)}, u32[]{:S(2)}) async-start(bf16[8,192,512]{2,1,0:T(8,128)(2,1)} %bitcast.2), calls=%async_computation | async-start | bytes 3145728 | tf_op jit(solution)/shard_map/all_to_all | solution.py:289
  138.4 12.4 %attend.3 = (bf16[1536,256]{1,0:T(8,128)(2,1)S(1)}, f32[1536,256]{1,0:T(8,128)S(1)}, bf16[1024,256]{1,0:T(8,128)(2,1)S(1)}) custom-call(s32[2]{0:T(128)S(1)} %pad_add_fusion.me_ref, s32[16]{0:T(128)S(1)} %copy-done.17, bf16[1024,512]{1,0:T(8,128)(2,1)S(1)} %copy-done.3, bf16[1536,512]{1,0:T(8,128)(2,1)S(1)} %copy-done.16, bf16[1536,512]{1,0:T(8,128)(2,1)S(1)} %bitcast.4), custom_call_target="tpu_custom_call" | custom-call | flops 5033164800 | bytes 4718592 | tf_op jit(solution)/shard_map/attend/pallas_call | solution.py:165
  150.8 1.9 collective-permute-start.16
  152.7 13.1 %collective-permute-done.16.refs_2_ = bf16[1024,256]{1,0:T(8,128)(2,1)S(1)} collective-permute-done((bf16[1024,256]{1,0:T(8,128)(2,1)S(1)}, bf16[1024,256]{1,0:T(8,128)(2,1)S(1)}, u32[]{:S(2)}, u32[]{:S(2)}) %collective-permute-start.16) | collective-permute-done | bytes 524320 | tf_op jit(solution)/shard_map/ppermute | solution.py:29
  165.9 1.6 settled.3
  168.7 1.6 collective-permute-start.19
  170.3 2.1 %collective-permute-start.20 = (bf16[192,512]{1,0:T(8,128)(2,1)}, bf16[192,512]{1,0:T(8,128)(2,1)S(1)}, u32[]{:S(2)}, u32[]{:S(2)}) collective-permute-start(bf16[192,512]{1,0:T(8,128)(2,1)} %get-tuple-element.63), channel_id=1, source_target_pairs={{0,4},{1,5},{2,6},{3,7},{4,0},{5,1},{6,2},{7,3},{8,12},{9,13},{10,... | collective-permute-start | bytes 589832 | tf_op jit(solution)/shard_map/ppermute | solution.py:283
  174.3 8.8 %collective-permute-done.18.refs_3_ = bf16[192,512]{1,0:T(8,128)(2,1)S(1)} collective-permute-done((bf16[192,512]{1,0:T(8,128)(2,1)S(1)}, bf16[192,512]{1,0:T(8,128)(2,1)S(1)}, u32[]{:S(2)}, u32[]{:S(2)}) %collective-permute-start.18) | collective-permute-done | bytes 196640 | tf_op jit(solution)/shard_map/ppermute | solution.py:283
  183.0 4.3 %collective-permute-done.19.refs_4_ = bf16[192,512]{1,0:T(8,128)(2,1)S(1)} collective-permute-done((bf16[192,512]{1,0:T(8,128)(2,1)}, bf16[192,512]{1,0:T(8,128)(2,1)S(1)}, u32[]{:S(2)}, u32[]{:S(2)}) %collective-permute-start.19) | collective-permute-done | bytes 196640 | tf_op jit(solution)/shard_map/ppermute | solution.py:283
  187.4 10.5 %collective-permute-done.21.refs_6_ = bf16[192,512]{1,0:T(8,128)(2,1)S(1)} collective-permute-done((bf16[192,512]{1,0:T(8,128)(2,1)}, bf16[192,512]{1,0:T(8,128)(2,1)S(1)}, u32[]{:S(2)}, u32[]{:S(2)}) %collective-permute-start.21) | collective-permute-done | bytes 196640 | tf_op jit(solution)/shard_map/ppermute | solution.py:283
  197.9 4.1 %collective-permute-done.22.refs_7_ = bf16[192,512]{1,0:T(8,128)(2,1)S(1)} collective-permute-done((bf16[192,512]{1,0:T(8,128)(2,1)S(1)}, bf16[192,512]{1,0:T(8,128)(2,1)S(1)}, u32[]{:S(2)}, u32[]{:S(2)}) %collective-permute-start.22) | collective-permute-done | bytes 196640 | tf_op jit(solution)/shard_map/ppermute | solution.py:283
  202.0 4.4 %collective-permute-done.23.refs_8_ = bf16[192,512]{1,0:T(8,128)(2,1)S(1)} collective-permute-done((bf16[192,512]{1,0:T(8,128)(2,1)S(1)}, bf16[192,512]{1,0:T(8,128)(2,1)S(1)}, u32[]{:S(2)}, u32[]{:S(2)}) %collective-permute-start.23) | collective-permute-done | bytes 196640 | tf_op jit(solution)/shard_map/ppermute | solution.py:283
  206.5 2.8 %unpacked.1 = (bf16[192,4096]{1,0:T(8,128)(2,1)}, bf16[192,2048]{1,0:T(8,128)(2,1)}, bf16[192,2048]{1,0:T(8,128)(2,1)}) custom-call(s32[2]{0:T(128)S(1)} %pad_add_fusion.me_ref, bf16[8,192,512]{2,1,0:T(8,128)(2,1)S(1)} %all-to-all-done.refs_0_, bf16[192,512]{1,0:T(8,128)(2,1)S(1)} %get-tuple-element.59.refs_1_, ...), custom_call_target="tpu_custom_call" | custom-call | bytes 6291456 | tf_op jit(solution)/shard_map/unpacked/pallas_call | solution.py:186
  (67 shorter events, 29.3 us)
Async XLA Ops:
  3.0 43.1 %copy-start = (bf16[192,4096]{1,0:T(8,128)(2,1)S(1)}, bf16[192,4096]{1,0:T(8,128)(2,1)}, u32[]{:S(2)}) copy-start(bf16[192,4096]{1,0:T(8,128)(2,1)} %refs_8_.1) | copy-start | bytes 4718596
  3.0 43.1 %copy-start.1 = (bf16[192,4096]{1,0:T(8,128)(2,1)S(1)}, bf16[192,4096]{1,0:T(8,128)(2,1)}, u32[]{:S(2)}) copy-start(bf16[192,4096]{1,0:T(8,128)(2,1)} %refs_9_.1) | copy-start | bytes 4718596
  3.7 5.2 %collective-permute-start = (bf16[192,512]{1,0:T(8,128)(2,1)S(1)}, bf16[192,512]{1,0:T(8,128)(2,1)S(1)}, u32[]{:S(2)}, u32[]{:S(2)}) collective-permute-start(bf16[192,512]{1,0:T(8,128)(2,1)S(1)} %get-tuple-element.36), channel_id=1, source_target_pairs={{0,1},{1,0},{2,3},{3,2},{4,5},{5,4},{6,7},{7,6},{8,9},{9,8},{10,11... | collective-permute-start | bytes 589832 | tf_op jit(solution)/shard_map/ppermute | solution.py:283
  4.5 12.2 %collective-permute-start.1 = (bf16[192,512]{1,0:T(8,128)(2,1)S(1)}, bf16[192,512]{1,0:T(8,128)(2,1)S(1)}, u32[]{:S(2)}, u32[]{:S(2)}) collective-permute-start(bf16[192,512]{1,0:T(8,128)(2,1)S(1)} %get-tuple-element.37), channel_id=1, source_target_pairs={{0,2},{1,3},{2,0},{3,1},{4,6},{5,7},{6,4},{7,5},{8,10},{9,11},{10,... | collective-permute-start | bytes 589832 | tf_op jit(solution)/shard_map/ppermute | solution.py:283
  4.7 16.4 %collective-permute-start.2 = (bf16[192,512]{1,0:T(8,128)(2,1)S(1)}, bf16[192,512]{1,0:T(8,128)(2,1)S(1)}, u32[]{:S(2)}, u32[]{:S(2)}) collective-permute-start(bf16[192,512]{1,0:T(8,128)(2,1)S(1)} %get-tuple-element.38), channel_id=1, source_target_pairs={{0,3},{1,2},{2,1},{3,0},{4,7},{5,6},{6,5},{7,4},{8,11},{9,10},{10,... | collective-permute-start | bytes 589832 | tf_op jit(solution)/shard_map/ppermute | solution.py:283
  6.2 14.8 %collective-permute-start.3 = (bf16[192,512]{1,0:T(8,128)(2,1)S(1)}, bf16[192,512]{1,0:T(8,128)(2,1)S(1)}, u32[]{:S(2)}, u32[]{:S(2)}) collective-permute-start(bf16[192,512]{1,0:T(8,128)(2,1)S(1)} %get-tuple-element.39), channel_id=1, source_target_pairs={{0,4},{1,5},{2,6},{3,7},{4,0},{5,1},{6,2},{7,3},{8,12},{9,13},{10,... | collective-permute-start | bytes 589832 | tf_op jit(solution)/shard_map/ppermute | solution.py:283
  8.5 25.3 %collective-permute-start.4 = (bf16[192,512]{1,0:T(8,128)(2,1)S(1)}, bf16[192,512]{1,0:T(8,128)(2,1)S(1)}, u32[]{:S(2)}, u32[]{:S(2)}) collective-permute-start(bf16[192,512]{1,0:T(8,128)(2,1)S(1)} %get-tuple-element.40), channel_id=1, source_target_pairs={{0,5},{1,4},{2,7},{3,6},{4,1},{5,0},{6,3},{7,2},{8,13},{9,12},{10,... | collective-permute-start | bytes 589832 | tf_op jit(solution)/shard_map/ppermute | solution.py:283
  8.9 29.1 %collective-permute-start.5 = (bf16[192,512]{1,0:T(8,128)(2,1)S(1)}, bf16[192,512]{1,0:T(8,128)(2,1)S(1)}, u32[]{:S(2)}, u32[]{:S(2)}) collective-permute-start(bf16[192,512]{1,0:T(8,128)(2,1)S(1)} %get-tuple-element.41), channel_id=1, source_target_pairs={{0,6},{1,7},{2,4},{3,5},{4,2},{5,3},{6,0},{7,1},{8,14},{9,15},{10,... | collective-permute-start | bytes 589832 | tf_op jit(solution)/shard_map/ppermute | solution.py:283
  16.7 25.6 %collective-permute-start.6 = (bf16[192,512]{1,0:T(8,128)(2,1)S(1)}, bf16[192,512]{1,0:T(8,128)(2,1)S(1)}, u32[]{:S(2)}, u32[]{:S(2)}) collective-permute-start(bf16[192,512]{1,0:T(8,128)(2,1)S(1)} %get-tuple-element.42), channel_id=1, source_target_pairs={{0,7},{1,6},{2,5},{3,4},{4,3},{5,2},{6,1},{7,0},{8,15},{9,14},{10,... | collective-permute-start | bytes 589832 | tf_op jit(solution)/shard_map/ppermute | solution.py:283
  43.0 3.9 %copy-start.14 = (bf16[1536,512]{1,0:T(8,128)(2,1)}, bf16[1536,512]{1,0:T(8,128)(2,1)S(1)}, u32[]{:S(2)}) copy-start(bf16[1536,512]{1,0:T(8,128)(2,1)S(1)} %get-tuple-element.44.kv_ref) | copy-start | bytes 4718596
  43.0 43.9 %collective-permute-start.7 = (bf16[1024,512]{1,0:T(8,128)(2,1)S(1)}, bf16[1024,512]{1,0:T(8,128)(2,1)S(1)}, u32[]{:S(2)}, u32[]{:S(2)}) collective-permute-start(bf16[1024,512]{1,0:T(8,128)(2,1)S(1)} %get-tuple-element.43), channel_id=1, source_target_pairs={{0,8},{8,16},{16,24},{1,9},{9,17},{17,25},{2,10},{10,18},{18,26},{... | collective-permute-start | bytes 3145736 | tf_op jit(solution)/shard_map/ppermute | solution.py:29
  47.6 4.1 %collective-permute-start.8 = (bf16[192,512]{1,0:T(8,128)(2,1)S(1)}, bf16[192,512]{1,0:T(8,128)(2,1)S(1)}, u32[]{:S(2)}, u32[]{:S(2)}) collective-permute-start(bf16[192,512]{1,0:T(8,128)(2,1)S(1)} %get-tuple-element.46), channel_id=1, source_target_pairs={{0,1},{1,0},{2,3},{3,2},{4,5},{5,4},{6,7},{7,6},{8,9},{9,8},{10,11... | collective-permute-start | bytes 589832 | tf_op jit(solution)/shard_map/ppermute | solution.py:283
  48.8 12.4 %collective-permute-start.9 = (bf16[192,512]{1,0:T(8,128)(2,1)S(1)}, bf16[192,512]{1,0:T(8,128)(2,1)S(1)}, u32[]{:S(2)}, u32[]{:S(2)}) collective-permute-start(bf16[192,512]{1,0:T(8,128)(2,1)S(1)} %get-tuple-element.47), channel_id=1, source_target_pairs={{0,2},{1,3},{2,0},{3,1},{4,6},{5,7},{6,4},{7,5},{8,10},{9,11},{10,... | collective-permute-start | bytes 589832 | tf_op jit(solution)/shard_map/ppermute | solution.py:283
  48.8 16.7 %collective-permute-start.10 = (bf16[192,512]{1,0:T(8,128)(2,1)S(1)}, bf16[192,512]{1,0:T(8,128)(2,1)S(1)}, u32[]{:S(2)}, u32[]{:S(2)}) collective-permute-start(bf16[192,512]{1,0:T(8,128)(2,1)S(1)} %get-tuple-element.48), channel_id=1, source_target_pairs={{0,3},{1,2},{2,1},{3,0},{4,7},{5,6},{6,5},{7,4},{8,11},{9,10},{10,... | collective-permute-start | bytes 589832 | tf_op jit(solution)/shard_map/ppermute | solution.py:283
  50.4 16.0 %collective-permute-start.11 = (bf16[192,512]{1,0:T(8,128)(2,1)S(1)}, bf16[192,512]{1,0:T(8,128)(2,1)S(1)}, u32[]{:S(2)}, u32[]{:S(2)}) collective-permute-start(bf16[192,512]{1,0:T(8,128)(2,1)S(1)} %get-tuple-element.49), channel_id=1, source_target_pairs={{0,4},{1,5},{2,6},{3,7},{4,0},{5,1},{6,2},{7,3},{8,12},{9,13},{10,... | collective-permute-start | bytes 589832 | tf_op jit(solution)/shard_map/ppermute | solution.py:283
  51.6 24.8 %collective-permute-start.12 = (bf16[192,512]{1,0:T(8,128)(2,1)S(1)}, bf16[192,512]{1,0:T(8,128)(2,1)S(1)}, u32[]{:S(2)}, u32[]{:S(2)}) collective-permute-start(bf16[192,512]{1,0:T(8,128)(2,1)S(1)} %get-tuple-element.50), channel_id=1, source_target_pairs={{0,5},{1,4},{2,7},{3,6},{4,1},{5,0},{6,3},{7,2},{8,13},{9,12},{10,... | collective-permute-start | bytes 589832 | tf_op jit(solution)/shard_map/ppermute | solution.py:283
  61.1 21.5 %collective-permute-start.13 = (bf16[192,512]{1,0:T(8,128)(2,1)S(1)}, bf16[192,512]{1,0:T(8,128)(2,1)S(1)}, u32[]{:S(2)}, u32[]{:S(2)}) collective-permute-start(bf16[192,512]{1,0:T(8,128)(2,1)S(1)} %get-tuple-element.51), channel_id=1, source_target_pairs={{0,6},{1,7},{2,4},{3,5},{4,2},{5,3},{6,0},{7,1},{8,14},{9,15},{10,... | collective-permute-start | bytes 589832 | tf_op jit(solution)/shard_map/ppermute | solution.py:283
  65.5 21.4 %collective-permute-start.14 = (bf16[192,512]{1,0:T(8,128)(2,1)S(1)}, bf16[192,512]{1,0:T(8,128)(2,1)S(1)}, u32[]{:S(2)}, u32[]{:S(2)}) collective-permute-start(bf16[192,512]{1,0:T(8,128)(2,1)S(1)} %get-tuple-element.52), channel_id=1, source_target_pairs={{0,7},{1,6},{2,5},{3,4},{4,3},{5,2},{6,1},{7,0},{8,15},{9,14},{10,... | collective-permute-start | bytes 589832 | tf_op jit(solution)/shard_map/ppermute | solution.py:283
  86.9 11.9 %copy-start.2 = (bf16[1024,512]{1,0:T(8,128)(2,1)}, bf16[1024,512]{1,0:T(8,128)(2,1)S(1)}, u32[]{:S(2)}) copy-start(bf16[1024,512]{1,0:T(8,128)(2,1)S(1)} %collective-permute-done.7.halo_ref.refs_7_) | copy-start | bytes 3145732
  90.8 38.4 %all-to-all-start.1 = ((bf16[8,192,512]{2,1,0:T(8,128)(2,1)}), bf16[8,192,512]{2,1,0:T(8,128)(2,1)S(1)}, u32[]{:S(2)}, u32[]{:S(2)}) async-start(bf16[8,192,512]{2,1,0:T(8,128)(2,1)} %packed.5), calls=%async_computation.1 | async-start | bytes 3145728 | tf_op jit(solution)/shard_map/all_to_all | solution.py:289
  98.2 1.4 copy-start.15
  98.2 1.4 copy-start.17
  112.2 15.0 %collective-permute-start.15 = (bf16[1024,256]{1,0:T(8,128)(2,1)S(1)}, bf16[1024,256]{1,0:T(8,128)(2,1)S(1)}, u32[]{:S(2)}, u32[]{:S(2)}) collective-permute-start(bf16[1024,256]{1,0:T(8,128)(2,1)S(1)} %get-tuple-element.55), channel_id=1, source_target_pairs={{8,0},{16,8},{24,16},{9,1},{17,9},{25,17},{10,2},{18,10},{26,18},{... | collective-permute-start | bytes 1572872 | tf_op jit(solution)/shard_map/ppermute | solution.py:29
  129.1 53.9 %all-to-all-start = ((bf16[8,192,512]{2,1,0:T(8,128)(2,1)}), bf16[8,192,512]{2,1,0:T(8,128)(2,1)S(1)}, u32[]{:S(2)}, u32[]{:S(2)}) async-start(bf16[8,192,512]{2,1,0:T(8,128)(2,1)} %bitcast.2), calls=%async_computation | async-start | bytes 3145728 | tf_op jit(solution)/shard_map/all_to_all | solution.py:289
  150.8 15.0 %collective-permute-start.16 = (bf16[1024,256]{1,0:T(8,128)(2,1)S(1)}, bf16[1024,256]{1,0:T(8,128)(2,1)S(1)}, u32[]{:S(2)}, u32[]{:S(2)}) collective-permute-start(bf16[1024,256]{1,0:T(8,128)(2,1)S(1)} %get-tuple-element.58), channel_id=1, source_target_pairs={{8,0},{16,8},{24,16},{9,1},{17,9},{25,17},{10,2},{18,10},{26,18},{... | collective-permute-start | bytes 1572872 | tf_op jit(solution)/shard_map/ppermute | solution.py:29
  167.5 5.6 %collective-permute-start.17 = (bf16[192,512]{1,0:T(8,128)(2,1)S(1)}, bf16[192,512]{1,0:T(8,128)(2,1)S(1)}, u32[]{:S(2)}, u32[]{:S(2)}) collective-permute-start(bf16[192,512]{1,0:T(8,128)(2,1)S(1)} %get-tuple-element.60), channel_id=1, source_target_pairs={{0,1},{1,0},{2,3},{3,2},{4,5},{5,4},{6,7},{7,6},{8,9},{9,8},{10,11... | collective-permute-start | bytes 589832 | tf_op jit(solution)/shard_map/ppermute | solution.py:283
  168.7 14.4 %collective-permute-start.18 = (bf16[192,512]{1,0:T(8,128)(2,1)S(1)}, bf16[192,512]{1,0:T(8,128)(2,1)S(1)}, u32[]{:S(2)}, u32[]{:S(2)}) collective-permute-start(bf16[192,512]{1,0:T(8,128)(2,1)S(1)} %get-tuple-element.61), channel_id=1, source_target_pairs={{0,2},{1,3},{2,0},{3,1},{4,6},{5,7},{6,4},{7,5},{8,10},{9,11},{10,... | collective-permute-start | bytes 589832 | tf_op jit(solution)/shard_map/ppermute | solution.py:283
  168.7 18.6 %collective-permute-start.19 = (bf16[192,512]{1,0:T(8,128)(2,1)}, bf16[192,512]{1,0:T(8,128)(2,1)S(1)}, u32[]{:S(2)}, u32[]{:S(2)}) collective-permute-start(bf16[192,512]{1,0:T(8,128)(2,1)} %get-tuple-element.62), channel_id=1, source_target_pairs={{0,3},{1,2},{2,1},{3,0},{4,7},{5,6},{6,5},{7,4},{8,11},{9,10},{10,... | collective-permute-start | bytes 589832 | tf_op jit(solution)/shard_map/ppermute | solution.py:283
  170.3 17.1 %collective-permute-start.20 = (bf16[192,512]{1,0:T(8,128)(2,1)}, bf16[192,512]{1,0:T(8,128)(2,1)S(1)}, u32[]{:S(2)}, u32[]{:S(2)}) collective-permute-start(bf16[192,512]{1,0:T(8,128)(2,1)} %get-tuple-element.63), channel_id=1, source_target_pairs={{0,4},{1,5},{2,6},{3,7},{4,0},{5,1},{6,2},{7,3},{8,12},{9,13},{10,... | collective-permute-start | bytes 589832 | tf_op jit(solution)/shard_map/ppermute | solution.py:283
  172.4 25.5 %collective-permute-start.21 = (bf16[192,512]{1,0:T(8,128)(2,1)}, bf16[192,512]{1,0:T(8,128)(2,1)S(1)}, u32[]{:S(2)}, u32[]{:S(2)}) collective-permute-start(bf16[192,512]{1,0:T(8,128)(2,1)} %get-tuple-element.64), channel_id=1, source_target_pairs={{0,5},{1,4},{2,7},{3,6},{4,1},{5,0},{6,3},{7,2},{8,13},{9,12},{10,... | collective-permute-start | bytes 589832 | tf_op jit(solution)/shard_map/ppermute | solution.py:283
  173.1 29.0 %collective-permute-start.22 = (bf16[192,512]{1,0:T(8,128)(2,1)S(1)}, bf16[192,512]{1,0:T(8,128)(2,1)S(1)}, u32[]{:S(2)}, u32[]{:S(2)}) collective-permute-start(bf16[192,512]{1,0:T(8,128)(2,1)S(1)} %get-tuple-element.65), channel_id=1, source_target_pairs={{0,6},{1,7},{2,4},{3,5},{4,2},{5,3},{6,0},{7,1},{8,14},{9,15},{10,... | collective-permute-start | bytes 589832 | tf_op jit(solution)/shard_map/ppermute | solution.py:283
  183.0 23.4 %collective-permute-start.23 = (bf16[192,512]{1,0:T(8,128)(2,1)S(1)}, bf16[192,512]{1,0:T(8,128)(2,1)S(1)}, u32[]{:S(2)}, u32[]{:S(2)}) collective-permute-start(bf16[192,512]{1,0:T(8,128)(2,1)S(1)} %get-tuple-element.66), channel_id=1, source_target_pairs={{0,7},{1,6},{2,5},{3,4},{4,3},{5,2},{6,1},{7,0},{8,15},{9,14},{10,... | collective-permute-start | bytes 589832 | tf_op jit(solution)/shard_map/ppermute | solution.py:283
  (12 other events, 11.3 us)
